TPU v7x, 32 devices: a whole 2x2x4 slice. The times are simulated.
32 devices in a mesh: groups: 1, tp: 8 (over z, core), dp: 4 (over y, x).
Axes of the slice: x: 2, y: 2, z: 4, core: 2. Of those that a mesh axis runs over, the one named last changes fastest.
Arguments:
- inputs: bfloat16 [512, 12288], P('groups', ('dp', 'tp')), may hold values from -6 to 6
- cotangent: bfloat16 [512, 12288], P('groups', ('dp', 'tp')), may hold values from -6 to 6
- gate_code: bfloat16 [12288, 16384], P('dp', 'tp'), may hold values from -0.0546875 to 0.0546875
- gate_scale: float32 [96, 128], P('dp', 'tp'), may hold values from 0.4 to 2.5
- up_code: bfloat16 [12288, 16384], P('dp', 'tp'), may hold values from -0.0546875 to 0.0546875
- up_scale: float32 [96, 128], P('dp', 'tp'), may hold values from 0.4 to 2.5
- down_code: bfloat16 [16384, 12288], P('tp', 'dp'), may hold values from -0.046875 to 0.046875
- down_scale: float32 [128, 96], P('tp', 'dp'), may hold values from 0.4 to 2.5
Outputs:
- input_grad: bfloat16 [512, 12288], P('groups', ('dp', 'tp'))
All inputs are finite; a program needn't handle non-finite values.
Results may differ from a plain program's by a relative error of at most 0.02.
Values may be sent and summed in bfloat16 or wider, within the bound.
No kernel may reach another device: no remote copies, remote signals or barrier semaphores. Data moves between devices by JAX's collectives and lax.ppermute only.
A program may use at most 256 MiB of HBM per device.

v0:
```python
import jax
import jax.numpy as jnp
from jax import lax
from jax.sharding import PartitionSpec as P

BLOCK = 128


def dequantize(code, scale):
    spread = jnp.repeat(jnp.repeat(scale, BLOCK, axis=0), BLOCK, axis=1)
    return (code.astype(jnp.float32) * spread).astype(jnp.bfloat16)


def transposed_dot(left, right):
    return lax.dot_general(
        left, right, (((1,), (1,)), ((), ())), preferred_element_type=jnp.float32
    )


def hidden_grads(sums, hidden_width):
    gate_pre = sums[:, :hidden_width]
    up_pre = sums[:, hidden_width : 2 * hidden_width]
    hidden_grad = sums[:, 2 * hidden_width :]
    gate_sig = jax.nn.sigmoid(gate_pre)
    gate_grad = (hidden_grad * up_pre * gate_sig * (1.0 + gate_pre * (1.0 - gate_sig))).astype(
        jnp.bfloat16
    )
    up_grad = (hidden_grad * gate_pre * gate_sig).astype(jnp.bfloat16)
    return (gate_grad, up_grad)


def local(inputs, cotangent, gate_code, gate_scale, up_code, up_scale, down_code, down_scale):
    gate_weight = dequantize(gate_code, gate_scale)
    up_weight = dequantize(up_code, up_scale)
    down_weight = dequantize(down_code, down_scale)
    hidden_width = gate_weight.shape[1]
    inputs_all, cotan_all = (
        lax.all_gather(inputs, "tp", axis=1, tiled=True),
        lax.all_gather(cotangent, "tp", axis=1, tiled=True),
    )
    gate_part = jnp.dot(inputs_all, gate_weight, preferred_element_type=jnp.float32)
    up_part = jnp.dot(inputs_all, up_weight, preferred_element_type=jnp.float32)
    hidden_part = transposed_dot(cotan_all, down_weight)
    sums = lax.psum_scatter(
        jnp.concatenate([gate_part, up_part, hidden_part], axis=1).astype(jnp.bfloat16),
        "dp",
        scatter_dimension=0,
        tiled=True,
    ).astype(jnp.float32)
    gate_grad, up_grad = hidden_grads(sums, hidden_width)
    gate_all, up_all = (
        lax.all_gather(gate_grad, "dp", axis=0, tiled=True),
        lax.all_gather(up_grad, "dp", axis=0, tiled=True),
    )
    grad_columns = lax.psum_scatter(
        (transposed_dot(gate_weight, gate_all) + transposed_dot(up_weight, up_all)).astype(
            jnp.bfloat16
        ),
        "tp",
        scatter_dimension=0,
        tiled=True,
    )
    return grad_columns.T


def solution(mesh):
    placed = (
        P("groups", ("dp", "tp")),
        P("groups", ("dp", "tp")),
        P("dp", "tp"),
        P("dp", "tp"),
        P("dp", "tp"),
        P("dp", "tp"),
        P("tp", "dp"),
        P("tp", "dp"),
    )
    return jax.shard_map(
        local, mesh=mesh, in_specs=placed, out_specs=P("groups", ("dp", "tp")), check_vma=False
    )
```

profile of v0, /device:TPU:0, one launch (start us, length us, event | category | flops | bytes accessed | tf_op | source)
XLA Modules:
  0.0 372.5 jit_solution(5849211101870880214)
XLA Ops:
  6.5 0.0 all-gather.5.cloned.1.call-start
  6.5 0.7 all-gather.5.cloned.1.call-update
  7.3 0.0 all-gather.7.cloned.1.call-start
  7.3 0.7 all-gather.7.cloned.1.call-update
  8.0 0.0 reduce-scatter.7.cloned.1.call-start
  8.1 0.8 copy.13
  8.8 0.8 copy.12
  9.6 40.4 %all-gather.5.cloned.1.call-done = bf16[512,3072]{1,0:T(8,128)(2,1)} async-done(((bf16[512,384]{1,0:T(8,128)(2,1)}), bf16[512,3072]{1,0:T(8,128)(2,1)}) %all-gather.5.cloned.1.call-update) | async-done | bytes 3145744 | tf_op jit(solution)/shard_map/all_gather | solution.py:38
  49.9 0.1 broadcast_in_dim.20
  50.0 9.0 %broadcast_in_dim.21 = f32[3072,16,128]{2,1,0:T(8,128)} broadcast(f32[3072,16]{1,0:T(8,128)S(1)} %bitcast.45), dimensions={0,1} | broadcast | bytes 25362432 | tf_op jit(solution)/shard_map/broadcast_in_dim | solution.py:10
  59.0 21.1 %fusion.9 = bf16[512,2048]{0,1:T(8,128)(2,1)S(1)} fusion(bf16[512,3072]{1,0:T(8,128)(2,1)} %all-gather.5.cloned.1.call-done, f32[384,8,16,128]{3,2,1,0:T(8,128)} %bitcast.40, bf16[3072,2048]{1,0:T(8,128)(2,1)} %param.12), kind=kOutput, calls=%fused_computation.13 | convolution fusion | flops 6462373888 | bytes 42991616 | tf_op jit(solution)/shard_map/dot_general | solution.py:42
  80.2 0.1 broadcast_in_dim.18
  80.3 8.9 %broadcast_in_dim.19 = f32[3072,16,128]{2,1,0:T(8,128)} broadcast(f32[3072,16]{1,0:T(8,128)S(1)} %bitcast.46), dimensions={0,1} | broadcast | bytes 25362432 | tf_op jit(solution)/shard_map/broadcast_in_dim | solution.py:10
  89.2 0.0 copy-start
  89.2 22.1 %fusion.8 = bf16[512,2048]{0,1:T(8,128)(2,1)} fusion(bf16[512,3072]{1,0:T(8,128)(2,1)} %all-gather.5.cloned.1.call-done, f32[384,8,16,128]{3,2,1,0:T(8,128)} %bitcast.42, bf16[3072,2048]{1,0:T(8,128)(2,1)} %param.10), kind=kOutput, calls=%fused_computation.12 | convolution fusion | flops 6462373888 | bytes 42991616 | tf_op jit(solution)/shard_map/dot_general | solution.py:41
  111.3 0.0 all-gather.7.cloned.1.call-done
  111.3 0.0 copy-done
  111.3 0.1 broadcast_in_dim.22
  111.4 8.9 %broadcast_in_dim.23 = f32[2048,24,128]{2,1,0:T(8,128)} broadcast(f32[2048,24]{1,0:T(8,128)S(1)} %bitcast.47), dimensions={0,1} | broadcast | bytes 25362432 | tf_op jit(solution)/shard_map/broadcast_in_dim | solution.py:10
  120.3 18.6 %fusion.10 = bf16[512,2048]{0,1:T(8,128)(2,1)} fusion(bf16[512,3072]{1,0:T(8,128)(2,1)} %all-gather.7.cloned.1.call-done, f32[256,8,24,128]{3,2,1,0:T(8,128)} %bitcast.44, bf16[2048,3072]{1,0:T(8,128)(2,1)} %param.14), kind=kOutput, calls=%fused_computation.14 | convolution fusion | flops 6462373888 | bytes 42991616 | tf_op jit(solution)/shard_map/dot_general | solution.py:15
  138.9 5.6 %pad_maximum_fusion = bf16[512,6144]{0,1:T(8,128)(2,1)} fusion(bf16[512,2048]{0,1:T(8,128)(2,1)} %fusion.10, bf16[512,2048]{0,1:T(8,128)(2,1)S(1)} %fusion.9, bf16[512,2048]{0,1:T(8,128)(2,1)} %fusion.8), kind=kLoop, calls=%fused_computation.7 | loop fusion | flops 18874368 | bytes 12582912 | tf_op jit(solution)/shard_map/concatenate | solution.py:45
  144.5 8.6 %copy.15 = bf16[512,6144]{1,0:T(8,128)(2,1)} copy(bf16[512,6144]{0,1:T(8,128)(2,1)} %pad_maximum_fusion) | data formatting | bytes 12582912
  153.1 0.0 reduce-scatter.7.cloned.1.call-update
  153.1 0.0 all-gather.9.cloned.1.call-start
  153.2 69.6 %reduce-scatter.7.cloned.1.call-done = bf16[128,6144]{1,0:T(8,128)(2,1)} async-done(((bf16[512,6144]{1,0:T(8,128)(2,1)}), bf16[128,6144]{1,0:T(8,128)(2,1)}) %reduce-scatter.7.cloned.1.call-update) | async-done | bytes 1572880
  222.8 1.9 copy.16
  224.8 0.2 convert_element_type.37
  225.0 1.5 multiply_convert_fusion
  226.4 0.0 all-gather.9.cloned.1.call-update
  226.5 0.0 all-gather.11.cloned.1.call-start
  226.5 0.5 all-gather.11.cloned.1.call-update
  227.1 0.0 reduce-scatter.5.cloned.1.call-start
  227.1 34.7 %all-gather.9.cloned.1.call-done = bf16[512,2048]{0,1:T(8,128)(2,1)} async-done(((bf16[128,2048]{0,1:T(8,128)(2,1)}), bf16[512,2048]{0,1:T(8,128)(2,1)}) %all-gather.9.cloned.1.call-update) | async-done | bytes 2097168 | tf_op jit(solution)/shard_map/all_gather | solution.py:52
  261.8 21.9 %fusion.16 = f32[3072,512]{1,0:T(8,128)} fusion(bf16[512,2048]{0,1:T(8,128)(2,1)} %all-gather.9.cloned.1.call-done, f32[384,8,16,128]{3,2,1,0:T(8,128)} %bitcast.43, bf16[3072,2048]{1,0:T(8,128)(2,1)} %param.10), kind=kOutput, calls=%fused_computation.21 | convolution fusion | flops 6461325312 | bytes 46137344 | tf_op jit(solution)/shard_map/dot_general | solution.py:15
  283.7 15.0 %all-gather.11.cloned.1.call-done = bf16[512,2048]{0,1:T(8,128)(2,1)} async-done(((bf16[128,2048]{0,1:T(8,128)(2,1)}), bf16[512,2048]{0,1:T(8,128)(2,1)}) %all-gather.11.cloned.1.call-update) | async-done | bytes 2097168 | tf_op jit(solution)/shard_map/all_gather | solution.py:53
  298.7 24.5 %add_convert_fusion = bf16[3072,512]{1,0:T(8,128)(2,1)} fusion(f32[3072,512]{1,0:T(8,128)} %fusion.16, bf16[512,2048]{0,1:T(8,128)(2,1)} %all-gather.11.cloned.1.call-done, f32[384,8,16,128]{3,2,1,0:T(8,128)} %bitcast.41, bf16[3072,2048]{1,0:T(8,128)(2,1)} %param.12), kind=kOutput, calls=%fused_computation.8 | convolution fusion | flops 6464471040 | bytes 49283072 | tf_op jit(solution)/shard_map/dot_general | solution.py:15
  323.2 0.0 reduce-scatter.5.cloned.1.call-update
  323.2 40.5 %reduce-scatter.5.cloned.1.call-done = bf16[384,512]{1,0:T(8,128)(2,1)} async-done(((bf16[3072,512]{1,0:T(8,128)(2,1)}), bf16[384,512]{1,0:T(8,128)(2,1)}) %reduce-scatter.5.cloned.1.call-update) | async-done | bytes 393232 | tf_op jit(solution)/shard_map/reduce_scatter | solution.py:55
  363.7 1.9 copy.14
Async XLA Ops:
  6.5 43.4 %all-gather.5.cloned.1.call-start = ((), (), s32[]{:S(2)}) async-start(), calls=%async_computation.2 | async-start | bytes 3538944 | tf_op jit(solution)/shard_map/all_gather | solution.py:38
  7.3 104.0 %all-gather.7.cloned.1.call-start = ((), (), s32[]{:S(2)}) async-start(), calls=%async_computation.3 | async-start | bytes 3538944 | tf_op jit(solution)/shard_map/all_gather | solution.py:39
  8.0 214.8 %reduce-scatter.7.cloned.1.call-start = ((), (), s32[]{:S(2)}) async-start(), calls=%async_computation.7 | async-start | bytes 7864320
  89.2 22.1 %copy-start = (f32[16,24]{1,0:T(8,128)S(1)}, f32[16,24]{1,0:T(8,128)}, u32[]{:S(2)}) copy-start(f32[16,24]{1,0:T(8,128)} %param.15) | copy-start | bytes 4612
  153.1 108.6 %all-gather.9.cloned.1.call-start = ((), (), s32[]{:S(2)}) async-start(), calls=%async_computation.4 | async-start | bytes 2621440 | tf_op jit(solution)/shard_map/all_gather | solution.py:52
  226.5 72.2 %all-gather.11.cloned.1.call-start = ((), (), s32[]{:S(2)}) async-start(), calls=%async_computation.5 | async-start | bytes 2621440 | tf_op jit(solution)/shard_map/all_gather | solution.py:53
  227.1 136.7 %reduce-scatter.5.cloned.1.call-start = ((), (), s32[]{:S(2)}) async-start(), calls=%async_computation.6 | async-start | bytes 3538944 | tf_op jit(solution)/shard_map/reduce_scatter | solution.py:55
Sparse Core Ops, SparseCore 0:
  9.0 40.9 all-gather.4
  51.6 37.1 all-gather.6
  153.3 69.5 reduce-scatter.6
  226.6 35.1 all-gather.8
  263.4 35.1 all-gather.10
  323.3 40.3 reduce-scatter.4
where the time goes:
time: 373 us; the launch traced here: 372 us
  waiting for transfers between devices  202 us (54%)
  matrix products  108 us (29%)
  local copies, waits for them, and re-layouts  41 us (11%)
  between operations  13.5 us (4%)
  other arithmetic  7.23 us (2%)
    unnamed x7, waiting for transfers between devices  71.6 us
    dot_general x3, matrix products, transposed_dot(): lax.dot_general(left, right, (((1,), (1,)), ((), ())), preferred_element_...  65.1 us
    reduce_scatter x1, waiting for transfers between devices, local(): lax.psum_scatter((transposed_dot(gate_weight, gate_all) + transposed_dot(...  40.5 us
    all_gather x1, waiting for transfers between devices, local(): lax.all_gather(inputs, 'tp', axis=1, tiled=True)  40.4 us
    all_gather x1, waiting for transfers between devices, local(): lax.all_gather(gate_grad, 'dp', axis=0, tiled=True)  34.7 us
    broadcast_in_dim x6, local copies, waits for them, and re-layouts, dequantize(): spread = jnp.repeat(jnp.repeat(scale, BLOCK, axis=0), BLOCK, axis=1)  27 us
    dot_general x1, matrix products, local(): jnp.dot(inputs_all, gate_weight, preferred_element_type=jnp.float32)  22.1 us
    dot_general x1, matrix products, local(): up_part = jnp.dot(inputs_all, up_weight, preferred_element_type=jnp.float32)  21.1 us
  transfers between devices with their start and end apart: 6, of which 5 were waited for; matrix products, arithmetic and copies ran while one was open for 23% of the time, Pallas kernels for 0%

commit v1 on v0

v1 whole, which is shorter than its diff:
```python
import functools

import jax
import jax.numpy as jnp
from jax import lax
from jax.experimental import pallas as pl
from jax.experimental.pallas import tpu as pltpu
from jax.sharding import PartitionSpec as P

BLOCK = 128
CORES = 2
CHUNKS = 2
BF16 = jnp.bfloat16
F32 = jnp.float32
PARAMS = pltpu.CompilerParams(vmem_limit_bytes=40 << 20)


def tile_of(extent, most):
    best = BLOCK
    for size in range(BLOCK, most + 1, BLOCK):
        if extent % size == 0:
            best = size
    return best


def weight_tile(code, scale_ref, row, column):
    rows = []
    for r in range(code.shape[0] // BLOCK):
        line = [
            (
                code[r * BLOCK : (r + 1) * BLOCK, c * BLOCK : (c + 1) * BLOCK].astype(F32)
                * scale_ref[row + r, column + c]
            ).astype(BF16)
            for c in range(code.shape[1] // BLOCK)
        ]
        rows.append(jnp.concatenate(line, axis=1))
    return jnp.concatenate(rows, axis=0)


def dot(left, right, contract):
    return lax.dot_general(
        left, right, (((1,), (contract,)), ((), ())), preferred_element_type=F32
    )


def prep_kernel(rows, where_ref, inputs_ref, cotangent_ref, *out_refs):
    count = inputs_ref.shape[0] // CHUNKS // rows
    for chunk in range(CHUNKS):
        for q in range(count):
            start = pl.multiple_of((chunk * count + (where_ref[0] ^ q)) * rows, rows)
            out_refs[2 * chunk][q * rows : (q + 1) * rows] = inputs_ref[pl.ds(start, rows)]
            out_refs[2 * chunk + 1][q * rows : (q + 1) * rows] = cotangent_ref[
                pl.ds(start, rows)
            ]


def prepare(where, inputs, cotangent, n_dp):
    seq, width = inputs.shape
    part = jax.ShapeDtypeStruct((seq // CHUNKS, width), inputs.dtype)
    return pl.pallas_call(
        functools.partial(prep_kernel, seq // CHUNKS // n_dp),
        grid_spec=pltpu.PrefetchScalarGridSpec(
            num_scalar_prefetch=1,
            grid=(),
            in_specs=[pl.BlockSpec(memory_space=pltpu.VMEM)] * 2,
            out_specs=[pl.BlockSpec(memory_space=pltpu.VMEM)] * (2 * CHUNKS),
        ),
        out_shape=[part] * (2 * CHUNKS),
        compiler_params=PARAMS,
        name="order_rows",
    )(where, inputs, cotangent)


def forward_kernel(groups, transposed, first, width, where_ref, scale_ref, *refs):
    *x_refs, code_ref, out_refs, x_all = refs[: len(refs) - len(groups) - 1] + (
        refs[len(refs) - len(groups) - 1 : -1],
        refs[-1],
    )
    n = pl.program_id(0)
    x = x_all
    if len(x_refs) == 2:

        @pl.when(n == 0)
        def _():
            count = x_all.shape[1] // (CORES * width)
            for j in range(count):
                for core, x_ref in enumerate(x_refs):
                    place = lax.rem(where_ref[1] + j, count) * CORES + (where_ref[2] ^ core)
                    x_all[:, pl.ds(pl.multiple_of(place * width, width), width)] = x_ref[
                        :, j * width : (j + 1) * width
                    ]
    else:
        x = x_refs[0]
    depth = x_all.shape[1]
    tile = code_ref.shape[0 if transposed else 1]
    step = tile_of(depth, 1024)
    block = (first + n * tile) // BLOCK
    total = None
    for k in range(0, depth, step):
        if transposed:
            weight = weight_tile(code_ref[:, k : k + step], scale_ref, block, k // BLOCK)
        else:
            weight = weight_tile(code_ref[k : k + step, :], scale_ref, k // BLOCK, block)
        term = dot(x[:, k : k + step], weight, 1 if transposed else 0)
        total = term if total is None else total + term
    rows = total.shape[0] // sum(len(group) for group in groups)
    for out_ref, group in zip(out_refs, groups):
        for place, q in enumerate(group):
            out_ref[place * rows : (place + 1) * rows] = total[
                q * rows : (q + 1) * rows
            ].astype(BF16)


def forward(where, scale, x, code, groups, transposed, first, count, width):
    rows = x[0].shape[0]
    depth = code.shape[1 if transposed else 0]
    blocks = sum(len(group) for group in groups)
    tile = tile_of(count, 512)
    base = first // tile
    code_spec = (
        pl.BlockSpec((tile, depth), lambda n, *_: (base + n, 0))
        if transposed
        else pl.BlockSpec((depth, tile), lambda n, *_: (0, base + n))
    )
    heights = [rows * len(group) // blocks for group in groups]
    return pl.pallas_call(
        functools.partial(forward_kernel, groups, transposed, first, width),
        grid_spec=pltpu.PrefetchScalarGridSpec(
            num_scalar_prefetch=2,
            grid=(count // tile,),
            in_specs=[pl.BlockSpec(part.shape, lambda n, *_: (0, 0)) for part in x] + [code_spec],
            out_specs=[pl.BlockSpec((height, tile), lambda n, *_: (0, n)) for height in heights],
            scratch_shapes=[pltpu.VMEM((rows, depth), BF16)],
        ),
        out_shape=[jax.ShapeDtypeStruct((height, count), BF16) for height in heights],
        compiler_params=PARAMS,
        cost_estimate=pl.CostEstimate(
            flops=2 * rows * depth * count, bytes_accessed=2 * depth * count, transcendentals=0
        ),
        name="forward_product",
    )(where, scale, *x, code)


def grads_kernel(pieces, *refs):
    *in_refs, gate_ref, up_ref = refs
    rows, width = gate_ref.shape
    at, sums = 0, []
    for piece in pieces:
        columns = []
        for terms in piece:
            total = None
            for term in in_refs[at : at + terms]:
                value = term[term.shape[0] - rows :].astype(F32)
                total = value if total is None else total + value
            at += terms
            columns.append(total)
        sums.append(columns[0] if len(columns) == 1 else jnp.concatenate(columns, axis=1))
    gate_pre, up_pre, hidden_grad = sums
    gate_sig = jax.nn.sigmoid(gate_pre)
    gate_ref[...] = (
        hidden_grad * up_pre * gate_sig * (1.0 + gate_pre * (1.0 - gate_sig))
    ).astype(BF16)
    up_ref[...] = (hidden_grad * gate_pre * gate_sig).astype(BF16)


def grads(pieces, rows, width):
    flat = [term for piece in pieces for part in piece for term in part]
    out = jax.ShapeDtypeStruct((rows, width), BF16)
    return pl.pallas_call(
        functools.partial(grads_kernel, [[len(part) for part in piece] for piece in pieces]),
        in_specs=[pl.BlockSpec(memory_space=pltpu.VMEM)] * len(flat),
        out_specs=[pl.BlockSpec(memory_space=pltpu.VMEM)] * 2,
        out_shape=[out, out],
        compiler_params=PARAMS,
        name="hidden_grads",
    )(*flat)


def backward_kernel(blocks, relative, where_ref, gate_scale_ref, up_scale_ref, *refs):
    gate_refs, up_refs = refs[:blocks], refs[blocks : 2 * blocks]
    gate_code_ref, up_code_ref = refs[2 * blocks : 2 * blocks + 2]
    *out_refs, gate_all, up_all, total_ref = refs[2 * blocks + 2 :]
    rows = gate_refs[0].shape[0]
    n = pl.program_id(0)

    @pl.when(n == 0)
    def _():
        for q in range(blocks):
            gate_all[q * rows : (q + 1) * rows] = gate_refs[q][...]
            up_all[q * rows : (q + 1) * rows] = up_refs[q][...]

    tile, depth = gate_code_ref.shape
    place = lax.rem(where_ref[1] + n, pl.num_programs(0)) if relative else n
    block = place * (tile // BLOCK)
    step = tile_of(depth, 1024)
    total = None
    for k in range(0, depth, step):
        for left, code_ref, scale_ref in (
            (gate_all, gate_code_ref, gate_scale_ref),
            (up_all, up_code_ref, up_scale_ref),
        ):
            weight = weight_tile(code_ref[:, k : k + step], scale_ref, block, k // BLOCK)
            term = dot(left[:, k : k + step], weight, 1)
            total = term if total is None else total + term
    if relative:
        width = tile // CORES
        total_ref[...] = total.astype(BF16)
        for out_ref, core in zip(out_refs, (where_ref[2], 1 - where_ref[2])):
            out_ref[...] = total_ref[:, pl.ds(pl.multiple_of(core * width, width), width)]
    else:
        out_refs[0][...] = total.astype(BF16)


def backward(where, gate_scale, up_scale, gate, up, gate_code, up_code, tiles):
    depth_rows, depth = gate_code.shape
    blocks, rows = len(gate), gate[0].shape[0] * len(gate)
    relative = tiles is not None
    tile = depth_rows // tiles if relative else tile_of(depth_rows, 512)
    steps = depth_rows // tile
    outs = CORES if relative else 1

    def code_place(n, where_ref, *_):
        return (lax.rem(where_ref[1] + n, steps) if relative else n, 0)

    return pl.pallas_call(
        functools.partial(backward_kernel, blocks, relative),
        grid_spec=pltpu.PrefetchScalarGridSpec(
            num_scalar_prefetch=3,
            grid=(steps,),
            in_specs=[pl.BlockSpec(part.shape, lambda n, *_: (0, 0)) for part in (*gate, *up)]
            + [pl.BlockSpec((tile, depth), code_place)] * 2,
            out_specs=[pl.BlockSpec((rows, tile // outs), lambda n, *_: (0, n))] * outs,
            scratch_shapes=[pltpu.VMEM((rows, depth), BF16)] * 2 + [pltpu.VMEM((rows, tile), BF16)],
        ),
        out_shape=[jax.ShapeDtypeStruct((rows, depth_rows // outs), BF16)] * outs,
        compiler_params=PARAMS,
        cost_estimate=pl.CostEstimate(
            flops=4 * rows * depth * depth_rows,
            bytes_accessed=4 * depth * depth_rows,
            transcendentals=0,
        ),
        name="backward_product",
    )(where, gate_scale, up_scale, *gate, *up, gate_code, up_code)


def pair_kernel(own_ref, other_ref, *out_refs):
    width = out_refs[0].shape[1]
    for j, out_ref in enumerate(out_refs):
        columns = slice((j + 1) * width, (j + 2) * width)
        out_ref[...] = (own_ref[:, columns].astype(F32) + other_ref[:, columns].astype(F32)).astype(BF16)


def pair_sums(own, other, count):
    rows, width = own.shape[0], own.shape[1] // count
    return pl.pallas_call(
        pair_kernel,
        in_specs=[pl.BlockSpec(memory_space=pltpu.VMEM)] * 2,
        out_specs=[pl.BlockSpec(memory_space=pltpu.VMEM)] * (count - 1),
        out_shape=[jax.ShapeDtypeStruct((rows, width), BF16)] * (count - 1),
        compiler_params=PARAMS,
        name="pair_sums",
    )(own, other)


def final_kernel(blocks, where_ref, *refs):
    *in_refs, out_ref = refs
    rows = in_refs[0].shape[0] // blocks
    width = out_ref.shape[1]
    for q in range(blocks):
        total = None
        for ref in in_refs:
            value = ref[q * rows : (q + 1) * rows, :width].astype(F32)
            total = value if total is None else total + value
        start = pl.multiple_of((where_ref[0] ^ q) * rows, rows)
        out_ref[pl.ds(start, rows)] = total.astype(BF16)


def final_sum(where, terms, blocks, width):
    rows = terms[0].shape[0]
    first = pl.BlockSpec((rows, width), lambda *_: (0, 0))
    return pl.pallas_call(
        functools.partial(final_kernel, blocks),
        grid_spec=pltpu.PrefetchScalarGridSpec(
            num_scalar_prefetch=1,
            grid=(1,),
            in_specs=[first] * len(terms),
            out_specs=first,
        ),
        out_shape=jax.ShapeDtypeStruct((rows, width), BF16),
        compiler_params=PARAMS,
        name="final_sum",
    )(where, *terms)


def local(
    n_tp, n_dp, inputs, cotangent, gate_code, gate_scale, up_code, up_scale, down_code, down_scale
):
    n_z = n_tp // CORES
    width = inputs.shape[1]
    hidden = gate_code.shape[1]
    bits = [1 << i for i in range(n_dp.bit_length() - 1)]
    by_blocks = width % BLOCK == 0 and n_tp % CORES == 0
    dp, tp = lax.axis_index("dp"), lax.axis_index("tp")
    place, core = tp // CORES, tp % CORES
    where = jnp.stack([dp, place, core]).astype(jnp.int32)

    def exchange(value, bit):
        return lax.ppermute(value, "dp", [(i, i ^ bit) for i in range(n_dp)])

    def swap_cores(value):
        return lax.ppermute(value, "tp", [(i, i ^ 1) for i in range(n_tp)])

    def gather(piece):
        if not by_blocks:
            return [lax.all_gather(piece, "tp", axis=1, tiled=True)]
        below, above = [piece], [piece]
        for s in range(1, n_z):
            ups = [z for z in range(n_z - 1) if z >= s - 1]
            downs = [z for z in range(1, n_z) if z <= n_z - s]
            pairs = lambda froms, by: [
                ((z * CORES + c), ((z + by) * CORES + c)) for z in froms for c in range(CORES)
            ]
            below.append(lax.ppermute(below[-1], "tp", pairs(ups, 1)))
            above.append(lax.ppermute(above[-1], "tp", pairs(downs, -1)))
        own = [piece] + [
            jnp.where(place + j < n_z, above[j], below[n_z - j]) for j in range(1, n_z)
        ]
        own = jnp.concatenate(own, axis=1)
        return [own, swap_cores(own)]

    def order_groups(order):
        rest, groups = list(range(n_dp)), []
        for bit in order:
            keep = [q for q in rest if not q & bit]
            groups.append((bit, keep))
            rest = keep
        stays, sends = [0], []
        for bit, _ in reversed(groups):
            sends.append([q | bit for q in stays])
            stays = sends[-1] + stays
        return sends[::-1] + [[0]]

    def reduce(parts, order):
        terms = []
        parts = list(parts)
        rows = parts[-1].shape[0]
        for step, bit in enumerate(order):
            got = exchange(parts[step], bit)
            at = 0
            for later in range(step + 1, len(parts) - 1):
                height = parts[later].shape[0]
                parts[later] = (
                    parts[later].astype(F32) + got[at : at + height].astype(F32)
                ).astype(BF16)
                at += height
            terms.append(got)
        return [parts[-1]] + terms

    def gather_rows(value, order):
        have = {0: value}
        for bit in order:
            for q in list(have):
                have[q | bit] = exchange(have[q], bit)
        return [have[q] for q in range(n_dp)]

    one, two = bits, bits[::-1]
    half = hidden // 2
    pieces = prepare(where, inputs, cotangent, n_dp)
    outs = []
    for chunk in range(CHUNKS):
        x_inputs = gather(pieces[2 * chunk])
        x_cotan = gather(pieces[2 * chunk + 1])
        product = lambda x, code, scale, order, transposed, first, count: reduce(
            forward(where, scale, x, code, order_groups(order), transposed, first, count, width),
            order,
        )
        gate_terms = [product(x_inputs, gate_code, gate_scale, one, False, 0, hidden)]
        up_terms = [product(x_inputs, up_code, up_scale, two, False, 0, hidden)]
        hidden_terms = [
            product(x_cotan, down_code, down_scale, one, True, 0, half),
            product(x_cotan, down_code, down_scale, two, True, half, half),
        ]
        rows = inputs.shape[0] // CHUNKS // n_dp
        gate_grad, up_grad = grads([gate_terms, up_terms, hidden_terms], rows, hidden)
        gate_all, up_all = gather_rows(gate_grad, one), gather_rows(up_grad, two)
        partial = backward(
            where, gate_scale, up_scale, gate_all, up_all, gate_code, up_code,
            n_z if by_blocks else None,
        )
        if by_blocks:
            own, other = partial
            other = swap_cores(other)
            sums = pair_sums(own, other, n_z)
            terms = [own, other] + [
                lax.ppermute(
                    part,
                    "tp",
                    [(i, (i + (j + 1) * CORES) % n_tp) for i in range(n_tp)],
                )
                for j, part in enumerate(sums)
            ]
            outs.append(final_sum(where, terms, n_dp, width))
        else:
            summed = lax.psum_scatter(partial[0], "tp", scatter_dimension=1, tiled=True)
            outs.append(final_sum(where, [summed], n_dp, width))
    return jnp.concatenate(outs, axis=0)


def solution(mesh):
    placed = (
        P("groups", ("dp", "tp")),
        P("groups", ("dp", "tp")),
        P("dp", "tp"),
        P("dp", "tp"),
        P("dp", "tp"),
        P("dp", "tp"),
        P("tp", "dp"),
        P("tp", "dp"),
    )
    return jax.shard_map(
        functools.partial(local, mesh.shape["tp"], mesh.shape["dp"]),
        mesh=mesh,
        in_specs=placed,
        out_specs=P("groups", ("dp", "tp")),
        check_vma=False,
    )
```

time: 373 us -> 258 us (0.69)
  waiting for transfers between devices: 202 us -> 77.7 us
  matrix products: 108 us -> 0 us
  starting transfers between devices: 0.2 us -> 90.4 us
  Pallas kernels: 0 us -> 80.7 us
  local copies, waits for them, and re-layouts: 41 us -> 3.54 us
  between operations: 13.5 us -> 0.75 us
  other arithmetic: 7.23 us -> 1.89 us
    dot_general x5 -> x0, matrix products: 108 us -> none  [the longest x3 65.1 us: transposed_dot(): lax.dot_general(left, right, (((1,), (1,)), ((), ())), preferred_element_...]
    ppermute x0 -> x64, starting transfers between devices: none -> 90.4 us  [the longest x28 37.3 us: exchange(): return lax.ppermute(value, 'dp', [(i, i ^ bit) for i in range(n_dp)])]
    all_gather x4 -> x0, waiting for transfers between devices: 90 us -> none  [the longest x1 40.4 us: local(): lax.all_gather(inputs, 'tp', axis=1, tiled=True)]
    pallas_call x0 -> x17, Pallas kernels: none -> 80.7 us  [the longest x8 51.9 us: forward(): pl.pallas_call(functools.partial(forward_kernel, groups, transposed, firs...]
    ppermute x0 -> x64, waiting for transfers between devices: none -> 77.7 us  [the longest x28 32.9 us: exchange(): return lax.ppermute(value, 'dp', [(i, i ^ bit) for i in range(n_dp)])]
    unnamed x7 -> x0, waiting for transfers between devices: 71.6 us -> none
    reduce_scatter x1 -> x0, waiting for transfers between devices: 40.5 us -> none  [local(): lax.psum_scatter((transposed_dot(gate_weight, gate_all) + transposed_dot(...]
    broadcast_in_dim x6 -> x0, local copies, waits for them, and re-layouts: 27 us -> none  [dequantize(): spread = jnp.repeat(jnp.repeat(scale, BLOCK, axis=0), BLOCK, axis=1)]
  transfers between devices with their start and end apart: 6 -> 64, of which waited for: 5 -> 21; matrix products, arithmetic and copies ran while one was open for 23% -> 1% of each run, Pallas kernels for 0% -> 31%
where the time goes in v1:
time: 258 us; the launch traced here: 255 us
  starting transfers between devices  90.4 us (35%)
  Pallas kernels  80.7 us (31%)
  waiting for transfers between devices  77.7 us (30%)
  local copies, waits for them, and re-layouts  3.54 us (1%)
    pallas_call x8, Pallas kernels, forward(): pl.pallas_call(functools.partial(forward_kernel, groups, transposed, firs...  51.9 us
    ppermute x28, starting transfers between devices, exchange(): return lax.ppermute(value, 'dp', [(i, i ^ bit) for i in range(n_dp)])  37.3 us
    ppermute x28, waiting for transfers between devices, exchange(): return lax.ppermute(value, 'dp', [(i, i ^ bit) for i in range(n_dp)])  32.9 us
    ppermute x12, starting transfers between devices, gather(): below.append(lax.ppermute(below[-1], 'tp', pairs(ups, 1)))  28.6 us
    pallas_call x2, Pallas kernels, backward(): pl.pallas_call(functools.partial(backward_kernel, blocks, relative), grid...  25.6 us
    ppermute x6, waiting for transfers between devices, local(): lax.ppermute(part, 'tp', [(i, (i + (j + 1) * CORES) % n_tp) for i in rang...  25.6 us
    ppermute x12, waiting for transfers between devices, gather(): above.append(lax.ppermute(above[-1], 'tp', pairs(downs, -1)))  19.2 us
    ppermute x12, starting transfers between devices, gather(): above.append(lax.ppermute(above[-1], 'tp', pairs(downs, -1)))  15.5 us
  transfers between devices with their start and end apart: 64, of which 21 were waited for; matrix products, arithmetic and copies ran while one was open for 1% of the time, Pallas kernels for 31%

profile of v1, /device:TPU:0, one launch (start us, length us, event | category | flops | bytes accessed | tf_op | source)
XLA Modules:
  0.0 255.0 jit_solution(2137606068269255504)
XLA Ops:
  4.0 5.6 %collective-permute-start.33 = (bf16[256,384]{1,0:T(8,128)(2,1)S(1)}, bf16[256,384]{1,0:T(8,128)(2,1)S(1)}, u32[]{:S(2)}, u32[]{:S(2)}) collective-permute-start(bf16[256,384]{1,0:T(8,128)(2,1)S(1)} %get-tuple-element.68), channel_id=1, source_target_pairs={{0,8},{4,12},{8,16},{12,20},{16,24},{20,28},{1,9},{5,13},{9,17},{1... | collective-permute-start | bytes 589832 | tf_op jit(solution)/shard_map/ppermute | solution.py:323
  10.9 4.6 %collective-permute-start.44 = (bf16[256,384]{1,0:T(8,128)(2,1)S(1)}, bf16[256,384]{1,0:T(8,128)(2,1)S(1)}, u32[]{:S(2)}, u32[]{:S(2)}) collective-permute-start(bf16[256,384]{1,0:T(8,128)(2,1)S(1)} %get-tuple-element.75), channel_id=1, source_target_pairs={{0,8},{4,12},{8,16},{12,20},{16,24},{20,28},{1,9},{5,13},{9,17},{1... | collective-permute-start | bytes 589832 | tf_op jit(solution)/shard_map/ppermute | solution.py:323
  20.3 8.4 %collective-permute-start.1 = (bf16[256,384]{1,0:T(8,128)(2,1)S(1)}, bf16[256,384]{1,0:T(8,128)(2,1)S(1)}, u32[]{:S(2)}, u32[]{:S(2)}) collective-permute-start(bf16[256,384]{1,0:T(8,128)(2,1)S(1)} %get-tuple-element.47), channel_id=1, source_target_pairs={{0,8},{4,12},{8,16},{12,20},{16,24},{20,28},{1,9},{5,13},{9,17},{1... | collective-permute-start | bytes 589832 | tf_op jit(solution)/shard_map/ppermute | solution.py:323
  30.0 4.6 %collective-permute-start.12 = (bf16[256,384]{1,0:T(8,128)(2,1)S(1)}, bf16[256,384]{1,0:T(8,128)(2,1)S(1)}, u32[]{:S(2)}, u32[]{:S(2)}) collective-permute-start(bf16[256,384]{1,0:T(8,128)(2,1)S(1)} %get-tuple-element.54), channel_id=1, source_target_pairs={{0,8},{4,12},{8,16},{12,20},{16,24},{20,28},{1,9},{5,13},{9,17},{1... | collective-permute-start | bytes 589832 | tf_op jit(solution)/shard_map/ppermute | solution.py:323
  40.0 4.0 %collective-permute-done.47 = bf16[256,384]{1,0:T(8,128)(2,1)S(1)} collective-permute-done((bf16[256,384]{1,0:T(8,128)(2,1)S(1)}, bf16[256,384]{1,0:T(8,128)(2,1)S(1)}, u32[]{:S(2)}, u32[]{:S(2)}) %collective-permute-start.47) | collective-permute-done | bytes 196640 | tf_op jit(solution)/shard_map/ppermute | solution.py:324
  49.1 5.1 %collective-permute-done.15 = bf16[256,384]{1,0:T(8,128)(2,1)S(1)} collective-permute-done((bf16[256,384]{1,0:T(8,128)(2,1)S(1)}, bf16[256,384]{1,0:T(8,128)(2,1)S(1)}, u32[]{:S(2)}, u32[]{:S(2)}) %collective-permute-start.15) | collective-permute-done | bytes 196640 | tf_op jit(solution)/shard_map/ppermute | solution.py:324
  56.2 3.5 %collective-permute-done.37 = bf16[256,384]{1,0:T(8,128)(2,1)S(1)} collective-permute-done((bf16[256,384]{1,0:T(8,128)(2,1)S(1)}, bf16[256,384]{1,0:T(8,128)(2,1)S(1)}, u32[]{:S(2)}, u32[]{:S(2)}) %collective-permute-start.37) | collective-permute-done | bytes 196640 | tf_op jit(solution)/shard_map/ppermute | solution.py:324
  61.9 2.1 collective-permute-done.48
  65.0 2.0 collective-permute-done.5
  69.4 8.1 %forward_product.12 = (bf16[128,2048]{1,0:T(8,128)(2,1)S(1)}, bf16[64,2048]{1,0:T(8,128)(2,1)S(1)}, bf16[64,2048]{1,0:T(8,128)(2,1)S(1)}) custom-call(s32[3]{0:T(128)S(1)} %pad_add_fusion.where_ref, f32[24,16]{1,0:T(8,128)S(1)} %copy.11.scale_ref.gate_scale_ref, bf16[256,1536]{1,0:T(8,128)(2,1)S(1)} %pad_maximum_fusion.2.refs_0_, ...), custom_call_target="tpu_custom_call" | custom-call | flops 3221225472 | bytes 12582912 | tf_op jit(solution)/shard_map/forward_product/pallas_call | solution.py:126
  77.5 1.7 collective-permute-start.39
  79.2 8.0 %forward_product.13 = (bf16[128,2048]{1,0:T(8,128)(2,1)S(1)}, bf16[64,2048]{1,0:T(8,128)(2,1)S(1)}, bf16[64,2048]{1,0:T(8,128)(2,1)S(1)}) custom-call(s32[3]{0:T(128)S(1)} %pad_add_fusion.where_ref, f32[24,16]{1,0:T(8,128)S(1)} %copy.12.scale_ref.up_scale_ref, bf16[256,1536]{1,0:T(8,128)(2,1)S(1)} %pad_maximum_fusion.2.refs_0_, ...), custom_call_target="tpu_custom_call" | custom-call | flops 3221225472 | bytes 12582912 | tf_op jit(solution)/shard_map/forward_product/pallas_call | solution.py:126
  87.2 1.6 collective-permute-start.41
  88.8 4.9 %forward_product.14 = (bf16[128,1024]{1,0:T(8,128)(2,1)S(1)}, bf16[64,1024]{1,0:T(8,128)(2,1)S(1)}, bf16[64,1024]{1,0:T(8,128)(2,1)S(1)}) custom-call(s32[3]{0:T(128)S(1)} %pad_add_fusion.where_ref, f32[16,24]{1,0:T(8,128)S(1)} %copy-done.2, bf16[256,1536]{1,0:T(8,128)(2,1)S(1)} %pad_maximum_fusion.3.refs_0_, ...), custom_call_target="tpu_custom_call" | custom-call | flops 1610612736 | bytes 6291456 | tf_op jit(solution)/shard_map/forward_product/pallas_call | solution.py:126
  94.3 4.9 %forward_product.15 = (bf16[128,1024]{1,0:T(8,128)(2,1)S(1)}, bf16[64,1024]{1,0:T(8,128)(2,1)S(1)}, bf16[64,1024]{1,0:T(8,128)(2,1)S(1)}) custom-call(s32[3]{0:T(128)S(1)} %pad_add_fusion.where_ref, f32[16,24]{1,0:T(8,128)S(1)} %copy-done.2, bf16[256,1536]{1,0:T(8,128)(2,1)S(1)} %pad_maximum_fusion.3.refs_0_, ...), custom_call_target="tpu_custom_call" | custom-call | flops 1610612736 | bytes 6291456 | tf_op jit(solution)/shard_map/forward_product/pallas_call | solution.py:126
  99.6 8.0 %forward_product.8 = (bf16[128,2048]{1,0:T(8,128)(2,1)S(1)}, bf16[64,2048]{1,0:T(8,128)(2,1)S(1)}, bf16[64,2048]{1,0:T(8,128)(2,1)S(1)}) custom-call(s32[3]{0:T(128)S(1)} %pad_add_fusion.where_ref, f32[24,16]{1,0:T(8,128)S(1)} %copy.11.scale_ref.gate_scale_ref, bf16[256,1536]{1,0:T(8,128)(2,1)S(1)} %pad_maximum_fusion.refs_0_, ...), custom_call_target="tpu_custom_call" | custom-call | flops 3221225472 | bytes 12582912 | tf_op jit(solution)/shard_map/forward_product/pallas_call | solution.py:126
  107.7 8.1 %forward_product.9 = (bf16[128,2048]{1,0:T(8,128)(2,1)S(1)}, bf16[64,2048]{1,0:T(8,128)(2,1)S(1)}, bf16[64,2048]{1,0:T(8,128)(2,1)S(1)}) custom-call(s32[3]{0:T(128)S(1)} %pad_add_fusion.where_ref, f32[24,16]{1,0:T(8,128)S(1)} %copy.12.scale_ref.up_scale_ref, bf16[256,1536]{1,0:T(8,128)(2,1)S(1)} %pad_maximum_fusion.refs_0_, ...), custom_call_target="tpu_custom_call" | custom-call | flops 3221225472 | bytes 12582912 | tf_op jit(solution)/shard_map/forward_product/pallas_call | solution.py:126
  115.7 1.7 collective-permute-start.7
  117.4 4.9 %forward_product.10 = (bf16[128,1024]{1,0:T(8,128)(2,1)S(1)}, bf16[64,1024]{1,0:T(8,128)(2,1)S(1)}, bf16[64,1024]{1,0:T(8,128)(2,1)S(1)}) custom-call(s32[3]{0:T(128)S(1)} %pad_add_fusion.where_ref, f32[16,24]{1,0:T(8,128)S(1)} %copy-done.2, bf16[256,1536]{1,0:T(8,128)(2,1)S(1)} %pad_maximum_fusion.1.refs_0_, ...), custom_call_target="tpu_custom_call" | custom-call | flops 1610612736 | bytes 6291456 | tf_op jit(solution)/shard_map/forward_product/pallas_call | solution.py:126
  122.3 5.1 %forward_product.11 = (bf16[128,1024]{1,0:T(8,128)(2,1)S(1)}, bf16[64,1024]{1,0:T(8,128)(2,1)S(1)}, bf16[64,1024]{1,0:T(8,128)(2,1)S(1)}) custom-call(s32[3]{0:T(128)S(1)} %pad_add_fusion.where_ref, f32[16,24]{1,0:T(8,128)S(1)} %copy-done.2, bf16[256,1536]{1,0:T(8,128)(2,1)S(1)} %pad_maximum_fusion.1.refs_0_, ...), custom_call_target="tpu_custom_call" | custom-call | flops 1610612736 | bytes 6291456 | tf_op jit(solution)/shard_map/forward_product/pallas_call | solution.py:126
  127.9 1.7 collective-permute-start.20
  129.7 5.2 %collective-permute-done.18.refs_7_ = bf16[128,1024]{1,0:T(8,128)(2,1)S(1)} collective-permute-done((bf16[128,1024]{1,0:T(8,128)(2,1)S(1)}, bf16[128,1024]{1,0:T(8,128)(2,1)S(1)}, u32[]{:S(2)}, u32[]{:S(2)}) %collective-permute-start.18) | collective-permute-done | bytes 262176 | tf_op jit(solution)/shard_map/ppermute | solution.py:308
  134.8 1.5 collective-permute-start.9
  138.6 1.6 collective-permute-start.19
  141.0 11.5 %collective-permute-done.51.refs_8_ = bf16[64,1024]{1,0:T(8,128)(2,1)S(1)} collective-permute-done((bf16[64,1024]{1,0:T(8,128)(2,1)S(1)}, bf16[64,1024]{1,0:T(8,128)(2,1)S(1)}, u32[]{:S(2)}, u32[]{:S(2)}) %collective-permute-start.51) | collective-permute-done | bytes 131104 | tf_op jit(solution)/shard_map/ppermute | solution.py:308
  156.1 4.9 %collective-permute-done.40.refs_2_ = bf16[64,2048]{1,0:T(8,128)(2,1)S(1)} collective-permute-done((bf16[64,2048]{1,0:T(8,128)(2,1)S(1)}, bf16[64,2048]{1,0:T(8,128)(2,1)S(1)}, u32[]{:S(2)}, u32[]{:S(2)}) %collective-permute-start.40) | collective-permute-done | bytes 262176 | tf_op jit(solution)/shard_map/ppermute | solution.py:308
  161.0 2.2 collective-permute-start.10
  163.8 1.6 collective-permute-start.55
  166.7 2.2 collective-permute-start.57
  168.8 1.6 collective-permute-done.10.refs_5_
  170.9 2.1 collective-permute-start.22
  173.0 3.1 %collective-permute-done.54.refs_1_ = bf16[64,2048]{1,0:T(8,128)(2,1)S(1)} collective-permute-done((bf16[64,2048]{1,0:T(8,128)(2,1)S(1)}, bf16[64,2048]{1,0:T(8,128)(2,1)S(1)}, u32[]{:S(2)}, u32[]{:S(2)}) %collective-permute-start.54) | collective-permute-done | bytes 262176 | tf_op jit(solution)/shard_map/ppermute | solution.py:308
  176.1 1.5 collective-permute-start.26
  178.7 1.9 collective-permute-start.59
  181.7 1.5 collective-permute-start.23
  183.2 4.1 %collective-permute-done.22.refs_1_ = bf16[64,2048]{1,0:T(8,128)(2,1)S(1)} collective-permute-done((bf16[64,2048]{1,0:T(8,128)(2,1)S(1)}, bf16[64,2048]{1,0:T(8,128)(2,1)S(1)}, u32[]{:S(2)}, u32[]{:S(2)}) %collective-permute-start.22) | collective-permute-done | bytes 262176 | tf_op jit(solution)/shard_map/ppermute | solution.py:308
  187.3 2.0 collective-permute-start.25
  189.3 1.5 collective-permute-start.24
  190.9 2.0 collective-permute-start.27
  192.9 12.8 %backward_product.3 = (bf16[256,1536]{1,0:T(8,128)(2,1)S(1)}, bf16[256,1536]{1,0:T(8,128)(2,1)S(1)}) custom-call(s32[3]{0:T(128)S(1)} %pad_add_fusion.where_ref, f32[24,16]{1,0:T(8,128)S(1)} %copy.11.scale_ref.gate_scale_ref, f32[24,16]{1,0:T(8,128)S(1)} %copy.12.scale_ref.up_scale_ref, bf16[64,2048]{1,0:T(8,128)(2,1)S(1)} %get-tuple-element.82.refs_0_, ...), custom_call_target="tpu_custom_call" | custom-call | flops 6442450944 | bytes 25165824 | tf_op jit(solution)/shard_map/backward_product/pallas_call | solution.py:225
  205.9 12.8 %backward_product.2 = (bf16[256,1536]{1,0:T(8,128)(2,1)S(1)}, bf16[256,1536]{1,0:T(8,128)(2,1)S(1)}) custom-call(s32[3]{0:T(128)S(1)} %pad_add_fusion.where_ref, f32[24,16]{1,0:T(8,128)S(1)} %copy.11.scale_ref.gate_scale_ref, f32[24,16]{1,0:T(8,128)S(1)} %copy.12.scale_ref.up_scale_ref, bf16[64,2048]{1,0:T(8,128)(2,1)S(1)} %get-tuple-element.61.refs_0_, ...), custom_call_target="tpu_custom_call" | custom-call | flops 6442450944 | bytes 25165824 | tf_op jit(solution)/shard_map/backward_product/pallas_call | solution.py:225
  219.4 3.7 %collective-permute-start.62 = (bf16[256,384]{1,0:T(8,128)(2,1)S(1)}, bf16[256,384]{1,0:T(8,128)(2,1)S(1)}, u32[]{:S(2)}, u32[]{:S(2)}) collective-permute-start(bf16[256,384]{1,0:T(8,128)(2,1)S(1)} %get-tuple-element.87), channel_id=1, source_target_pairs={{0,16},{4,20},{8,24},{12,28},{16,0},{20,4},{24,8},{28,12},{1,17},{... | collective-permute-start | bytes 589832 | tf_op jit(solution)/shard_map/ppermute | solution.py:395
  223.7 1.6 collective-permute-start.29
  225.6 3.6 %collective-permute-done.61.refs_2_ = bf16[256,384]{1,0:T(8,128)(2,1)S(1)} collective-permute-done((bf16[256,384]{1,0:T(8,128)(2,1)S(1)}, bf16[256,384]{1,0:T(8,128)(2,1)S(1)}, u32[]{:S(2)}, u32[]{:S(2)}) %collective-permute-start.61) | collective-permute-done | bytes 196640 | tf_op jit(solution)/shard_map/ppermute | solution.py:395
  229.1 1.7 collective-permute-start.31
  230.8 6.8 %collective-permute-done.62.refs_3_ = bf16[256,384]{1,0:T(8,128)(2,1)S(1)} collective-permute-done((bf16[256,384]{1,0:T(8,128)(2,1)S(1)}, bf16[256,384]{1,0:T(8,128)(2,1)S(1)}, u32[]{:S(2)}, u32[]{:S(2)}) %collective-permute-start.62) | collective-permute-done | bytes 196640 | tf_op jit(solution)/shard_map/ppermute | solution.py:395
  238.3 3.5 %collective-permute-done.29.refs_2_ = bf16[256,384]{1,0:T(8,128)(2,1)S(1)} collective-permute-done((bf16[256,384]{1,0:T(8,128)(2,1)S(1)}, bf16[256,384]{1,0:T(8,128)(2,1)S(1)}, u32[]{:S(2)}, u32[]{:S(2)}) %collective-permute-start.29) | collective-permute-done | bytes 196640 | tf_op jit(solution)/shard_map/ppermute | solution.py:395
  241.8 11.7 %collective-permute-done.30.refs_3_ = bf16[256,384]{1,0:T(8,128)(2,1)S(1)} collective-permute-done((bf16[256,384]{1,0:T(8,128)(2,1)S(1)}, bf16[256,384]{1,0:T(8,128)(2,1)S(1)}, u32[]{:S(2)}, u32[]{:S(2)}) %collective-permute-start.30) | collective-permute-done | bytes 196640 | tf_op jit(solution)/shard_map/ppermute | solution.py:395
  (131 shorter events, 45.6 us)
Async XLA Ops:
  2.7 14.0 %collective-permute-start.32 = (bf16[256,384]{1,0:T(8,128)(2,1)S(1)}, bf16[256,384]{1,0:T(8,128)(2,1)S(1)}, u32[]{:S(2)}, u32[]{:S(2)}) collective-permute-start(bf16[256,384]{1,0:T(8,128)(2,1)S(1)} %get-tuple-element.68), channel_id=1, source_target_pairs={{8,0},{12,4},{16,8},{20,12},{24,16},{28,20},{9,1},{13,5},{17,9},{2... | collective-permute-start | bytes 589832 | tf_op jit(solution)/shard_map/ppermute | solution.py:324
  4.0 14.1 %collective-permute-start.33 = (bf16[256,384]{1,0:T(8,128)(2,1)S(1)}, bf16[256,384]{1,0:T(8,128)(2,1)S(1)}, u32[]{:S(2)}, u32[]{:S(2)}) collective-permute-start(bf16[256,384]{1,0:T(8,128)(2,1)S(1)} %get-tuple-element.68), channel_id=1, source_target_pairs={{0,8},{4,12},{8,16},{12,20},{16,24},{20,28},{1,9},{5,13},{9,17},{1... | collective-permute-start | bytes 589832 | tf_op jit(solution)/shard_map/ppermute | solution.py:323
  9.6 10.7 %collective-permute-start.43 = (bf16[256,384]{1,0:T(8,128)(2,1)S(1)}, bf16[256,384]{1,0:T(8,128)(2,1)S(1)}, u32[]{:S(2)}, u32[]{:S(2)}) collective-permute-start(bf16[256,384]{1,0:T(8,128)(2,1)S(1)} %get-tuple-element.75), channel_id=1, source_target_pairs={{8,0},{12,4},{16,8},{20,12},{24,16},{28,20},{9,1},{13,5},{17,9},{2... | collective-permute-start | bytes 589832 | tf_op jit(solution)/shard_map/ppermute | solution.py:324
  10.9 17.9 %collective-permute-start.44 = (bf16[256,384]{1,0:T(8,128)(2,1)S(1)}, bf16[256,384]{1,0:T(8,128)(2,1)S(1)}, u32[]{:S(2)}, u32[]{:S(2)}) collective-permute-start(bf16[256,384]{1,0:T(8,128)(2,1)S(1)} %get-tuple-element.75), channel_id=1, source_target_pairs={{0,8},{4,12},{8,16},{12,20},{16,24},{20,28},{1,9},{5,13},{9,17},{1... | collective-permute-start | bytes 589832 | tf_op jit(solution)/shard_map/ppermute | solution.py:323
  15.4 14.6 %collective-permute-start = (bf16[256,384]{1,0:T(8,128)(2,1)S(1)}, bf16[256,384]{1,0:T(8,128)(2,1)S(1)}, u32[]{:S(2)}, u32[]{:S(2)}) collective-permute-start(bf16[256,384]{1,0:T(8,128)(2,1)S(1)} %get-tuple-element.47), channel_id=1, source_target_pairs={{8,0},{12,4},{16,8},{20,12},{24,16},{28,20},{9,1},{13,5},{17,9},{2... | collective-permute-start | bytes 589832 | tf_op jit(solution)/shard_map/ppermute | solution.py:324
  16.7 17.9 %collective-permute-start.36 = (bf16[256,384]{1,0:T(8,128)(2,1)S(1)}, bf16[256,384]{1,0:T(8,128)(2,1)S(1)}, u32[]{:S(2)}, u32[]{:S(2)}) collective-permute-start(bf16[256,384]{1,0:T(8,128)(2,1)S(1)} %collective-permute-done.32), channel_id=1, source_target_pairs={{8,0},{12,4},{16,8},{20,12},{9,1},{13,5},{17,9},{21,13},{10,2},{14... | collective-permute-start | bytes 589832 | tf_op jit(solution)/shard_map/ppermute | solution.py:324
  18.1 17.9 %collective-permute-start.34 = (bf16[256,384]{1,0:T(8,128)(2,1)S(1)}, bf16[256,384]{1,0:T(8,128)(2,1)S(1)}, u32[]{:S(2)}, u32[]{:S(2)}) collective-permute-start(bf16[256,384]{1,0:T(8,128)(2,1)S(1)} %collective-permute-done.33), channel_id=1, source_target_pairs={{8,16},{12,20},{16,24},{20,28},{9,17},{13,21},{17,25},{21,29},{10,... | collective-permute-start | bytes 589832 | tf_op jit(solution)/shard_map/ppermute | solution.py:323
  20.3 16.4 %collective-permute-start.1 = (bf16[256,384]{1,0:T(8,128)(2,1)S(1)}, bf16[256,384]{1,0:T(8,128)(2,1)S(1)}, u32[]{:S(2)}, u32[]{:S(2)}) collective-permute-start(bf16[256,384]{1,0:T(8,128)(2,1)S(1)} %get-tuple-element.47), channel_id=1, source_target_pairs={{0,8},{4,12},{8,16},{12,20},{16,24},{20,28},{1,9},{5,13},{9,17},{1... | collective-permute-start | bytes 589832 | tf_op jit(solution)/shard_map/ppermute | solution.py:323
  36.7 10.4 %collective-permute-start.4 = (bf16[256,384]{1,0:T(8,128)(2,1)S(1)}, bf16[256,384]{1,0:T(8,128)(2,1)S(1)}, u32[]{:S(2)}, u32[]{:S(2)}) collective-permute-start(bf16[256,384]{1,0:T(8,128)(2,1)S(1)} %collective-permute-done), channel_id=1, source_target_pairs={{8,0},{12,4},{16,8},{20,12},{9,1},{13,5},{17,9},{21,13},{10,2},{14... | collective-permute-start | bytes 589832 | tf_op jit(solution)/shard_map/ppermute | solution.py:324
  38.7 15.5 %collective-permute-start.15 = (bf16[256,384]{1,0:T(8,128)(2,1)S(1)}, bf16[256,384]{1,0:T(8,128)(2,1)S(1)}, u32[]{:S(2)}, u32[]{:S(2)}) collective-permute-start(bf16[256,384]{1,0:T(8,128)(2,1)S(1)} %collective-permute-done.11), channel_id=1, source_target_pairs={{8,0},{12,4},{16,8},{20,12},{9,1},{13,5},{17,9},{21,13},{10,2},{14... | collective-permute-start | bytes 589832 | tf_op jit(solution)/shard_map/ppermute | solution.py:324
  44.0 10.9 %collective-permute-start.13 = (bf16[256,384]{1,0:T(8,128)(2,1)S(1)}, bf16[256,384]{1,0:T(8,128)(2,1)S(1)}, u32[]{:S(2)}, u32[]{:S(2)}) collective-permute-start(bf16[256,384]{1,0:T(8,128)(2,1)S(1)} %collective-permute-done.12), channel_id=1, source_target_pairs={{8,16},{12,20},{16,24},{20,28},{9,17},{13,21},{17,25},{21,29},{10,... | collective-permute-start | bytes 589832 | tf_op jit(solution)/shard_map/ppermute | solution.py:323
  44.7 15.1 %collective-permute-start.37 = (bf16[256,384]{1,0:T(8,128)(2,1)S(1)}, bf16[256,384]{1,0:T(8,128)(2,1)S(1)}, u32[]{:S(2)}, u32[]{:S(2)}) collective-permute-start(bf16[256,384]{1,0:T(8,128)(2,1)S(1)} %collective-permute-done.36), channel_id=1, source_target_pairs={{8,0},{12,4},{9,1},{13,5},{10,2},{14,6},{11,3},{15,7}} | collective-permute-start | bytes 589832 | tf_op jit(solution)/shard_map/ppermute | solution.py:324
  47.1 13.4 %collective-permute-start.35 = (bf16[256,384]{1,0:T(8,128)(2,1)S(1)}, bf16[256,384]{1,0:T(8,128)(2,1)S(1)}, u32[]{:S(2)}, u32[]{:S(2)}) collective-permute-start(bf16[256,384]{1,0:T(8,128)(2,1)S(1)} %collective-permute-done.34), channel_id=1, source_target_pairs={{16,24},{20,28},{17,25},{21,29},{18,26},{22,30},{19,27},{23,31}} | collective-permute-start | bytes 589832 | tf_op jit(solution)/shard_map/ppermute | solution.py:323
  47.7 16.2 %collective-permute-start.48 = (bf16[256,384]{1,0:T(8,128)(2,1)S(1)}, bf16[256,384]{1,0:T(8,128)(2,1)S(1)}, u32[]{:S(2)}, u32[]{:S(2)}) collective-permute-start(bf16[256,384]{1,0:T(8,128)(2,1)S(1)} %collective-permute-done.47), channel_id=1, source_target_pairs={{8,0},{12,4},{9,1},{13,5},{10,2},{14,6},{11,3},{15,7}} | collective-permute-start | bytes 589832 | tf_op jit(solution)/shard_map/ppermute | solution.py:324
  54.2 10.6 %collective-permute-start.46 = (bf16[256,384]{1,0:T(8,128)(2,1)S(1)}, bf16[256,384]{1,0:T(8,128)(2,1)S(1)}, u32[]{:S(2)}, u32[]{:S(2)}) collective-permute-start(bf16[256,384]{1,0:T(8,128)(2,1)S(1)} %collective-permute-done.45), channel_id=1, source_target_pairs={{16,24},{20,28},{17,25},{21,29},{18,26},{22,30},{19,27},{23,31}} | collective-permute-start | bytes 589832 | tf_op jit(solution)/shard_map/ppermute | solution.py:323
  54.9 12.2 %collective-permute-start.5 = (bf16[256,384]{1,0:T(8,128)(2,1)S(1)}, bf16[256,384]{1,0:T(8,128)(2,1)S(1)}, u32[]{:S(2)}, u32[]{:S(2)}) collective-permute-start(bf16[256,384]{1,0:T(8,128)(2,1)S(1)} %collective-permute-done.4), channel_id=1, source_target_pairs={{8,0},{12,4},{9,1},{13,5},{10,2},{14,6},{11,3},{15,7}} | collective-permute-start | bytes 589832 | tf_op jit(solution)/shard_map/ppermute | solution.py:324
  67.1 21.8 %collective-permute-start.49 = (bf16[256,1536]{1,0:T(8,128)(2,1)S(1)}, bf16[256,1536]{1,0:T(8,128)(2,1)S(1)}, u32[]{:S(2)}, u32[]{:S(2)}) collective-permute-start(bf16[256,1536]{1,0:T(8,128)(2,1)S(1)} %pad_maximum_fusion.3.refs_0_), channel_id=1, source_target_pairs={{0,4},{4,0},{8,12},{12,8},{16,20},{20,16},{24,28},{28,24},{1,5},{5... | collective-permute-start | bytes 2359304 | tf_op jit(solution)/shard_map/ppermute | solution.py:311
  67.2 31.9 %collective-permute-start.6 = (bf16[256,1536]{1,0:T(8,128)(2,1)S(1)}, bf16[256,1536]{1,0:T(8,128)(2,1)S(1)}, u32[]{:S(2)}, u32[]{:S(2)}) collective-permute-start(bf16[256,1536]{1,0:T(8,128)(2,1)S(1)} %pad_maximum_fusion.refs_0_), channel_id=1, source_target_pairs={{0,4},{4,0},{8,12},{12,8},{16,20},{20,16},{24,28},{28,24},{1,5},{5... | collective-permute-start | bytes 2359304 | tf_op jit(solution)/shard_map/ppermute | solution.py:311
  69.3 46.4 %collective-permute-start.17 = (bf16[256,1536]{1,0:T(8,128)(2,1)S(1)}, bf16[256,1536]{1,0:T(8,128)(2,1)S(1)}, u32[]{:S(2)}, u32[]{:S(2)}) collective-permute-start(bf16[256,1536]{1,0:T(8,128)(2,1)S(1)} %pad_maximum_fusion.1.refs_0_), channel_id=1, source_target_pairs={{0,4},{4,0},{8,12},{12,8},{16,20},{20,16},{24,28},{28,24},{1,5},{5... | collective-permute-start | bytes 2359304 | tf_op jit(solution)/shard_map/ppermute | solution.py:311
  77.5 59.6 %collective-permute-start.39 = (bf16[128,2048]{1,0:T(8,128)(2,1)S(1)}, bf16[128,2048]{1,0:T(8,128)(2,1)S(1)}, u32[]{:S(2)}, u32[]{:S(2)}) collective-permute-start(bf16[128,2048]{1,0:T(8,128)(2,1)S(1)} %get-tuple-element.70), channel_id=1, source_target_pairs={{0,1},{1,0},{2,3},{3,2},{4,5},{5,4},{6,7},{7,6},{8,9},{9,8},{10,11... | collective-permute-start | bytes 1572872 | tf_op jit(solution)/shard_map/ppermute | solution.py:308
  87.2 51.4 %collective-permute-start.41 = (bf16[128,2048]{1,0:T(8,128)(2,1)S(1)}, bf16[128,2048]{1,0:T(8,128)(2,1)S(1)}, u32[]{:S(2)}, u32[]{:S(2)}) collective-permute-start(bf16[128,2048]{1,0:T(8,128)(2,1)S(1)} %get-tuple-element.73), channel_id=1, source_target_pairs={{0,2},{1,3},{2,0},{3,1},{4,6},{5,7},{6,4},{7,5},{8,10},{9,11},{10,... | collective-permute-start | bytes 1572872 | tf_op jit(solution)/shard_map/ppermute | solution.py:308
  93.7 33.7 %collective-permute-start.50 = (bf16[128,1024]{1,0:T(8,128)(2,1)S(1)}, bf16[128,1024]{1,0:T(8,128)(2,1)S(1)}, u32[]{:S(2)}, u32[]{:S(2)}) collective-permute-start(bf16[128,1024]{1,0:T(8,128)(2,1)S(1)} %get-tuple-element.77), channel_id=1, source_target_pairs={{0,1},{1,0},{2,3},{3,2},{4,5},{5,4},{6,7},{7,6},{8,9},{9,8},{10,11... | collective-permute-start | bytes 786440 | tf_op jit(solution)/shard_map/ppermute | solution.py:308
  99.2 28.8 %collective-permute-start.52 = (bf16[128,1024]{1,0:T(8,128)(2,1)S(1)}, bf16[128,1024]{1,0:T(8,128)(2,1)S(1)}, u32[]{:S(2)}, u32[]{:S(2)}) collective-permute-start(bf16[128,1024]{1,0:T(8,128)(2,1)S(1)} %get-tuple-element.80), channel_id=1, source_target_pairs={{0,2},{1,3},{2,0},{3,1},{4,6},{5,7},{6,4},{7,5},{8,10},{9,11},{10,... | collective-permute-start | bytes 786440 | tf_op jit(solution)/shard_map/ppermute | solution.py:308
  115.7 24.6 %collective-permute-start.7 = (bf16[128,2048]{1,0:T(8,128)(2,1)S(1)}, bf16[128,2048]{1,0:T(8,128)(2,1)S(1)}, u32[]{:S(2)}, u32[]{:S(2)}) collective-permute-start(bf16[128,2048]{1,0:T(8,128)(2,1)S(1)} %get-tuple-element.49), channel_id=1, source_target_pairs={{0,1},{1,0},{2,3},{3,2},{4,5},{5,4},{6,7},{7,6},{8,9},{9,8},{10,11... | collective-permute-start | bytes 1572872 | tf_op jit(solution)/shard_map/ppermute | solution.py:308
  134.8 19.2 %collective-permute-start.9 = (bf16[128,2048]{1,0:T(8,128)(2,1)S(1)}, bf16[128,2048]{1,0:T(8,128)(2,1)S(1)}, u32[]{:S(2)}, u32[]{:S(2)}) collective-permute-start(bf16[128,2048]{1,0:T(8,128)(2,1)S(1)} %get-tuple-element.52), channel_id=1, source_target_pairs={{0,2},{1,3},{2,0},{3,1},{4,6},{5,7},{6,4},{7,5},{8,10},{9,11},{10,... | collective-permute-start | bytes 1572872 | tf_op jit(solution)/shard_map/ppermute | solution.py:308
  136.4 16.1 %collective-permute-start.51 = (bf16[64,1024]{1,0:T(8,128)(2,1)S(1)}, bf16[64,1024]{1,0:T(8,128)(2,1)S(1)}, u32[]{:S(2)}, u32[]{:S(2)}) collective-permute-start(bf16[64,1024]{1,0:T(8,128)(2,1)S(1)} %add_convert_fusion.5), channel_id=1, source_target_pairs={{0,2},{1,3},{2,0},{3,1},{4,6},{5,7},{6,4},{7,5},{8,10},{9,11},{10,... | collective-permute-start | bytes 393224 | tf_op jit(solution)/shard_map/ppermute | solution.py:308
  137.0 18.5 %collective-permute-start.53 = (bf16[64,1024]{1,0:T(8,128)(2,1)S(1)}, bf16[64,1024]{1,0:T(8,128)(2,1)S(1)}, u32[]{:S(2)}, u32[]{:S(2)}) collective-permute-start(bf16[64,1024]{1,0:T(8,128)(2,1)S(1)} %add_convert_fusion.4), channel_id=1, source_target_pairs={{0,1},{1,0},{2,3},{3,2},{4,5},{5,4},{6,7},{7,6},{8,9},{9,8},{10,11... | collective-permute-start | bytes 393224 | tf_op jit(solution)/shard_map/ppermute | solution.py:308
  138.6 25.1 %collective-permute-start.19 = (bf16[64,1024]{1,0:T(8,128)(2,1)S(1)}, bf16[64,1024]{1,0:T(8,128)(2,1)S(1)}, u32[]{:S(2)}, u32[]{:S(2)}) collective-permute-start(bf16[64,1024]{1,0:T(8,128)(2,1)S(1)} %add_convert_fusion.7), channel_id=1, source_target_pairs={{0,2},{1,3},{2,0},{3,1},{4,6},{5,7},{6,4},{7,5},{8,10},{9,11},{10,... | collective-permute-start | bytes 393224 | tf_op jit(solution)/shard_map/ppermute | solution.py:308
  140.3 25.1 %collective-permute-start.21 = (bf16[64,1024]{1,0:T(8,128)(2,1)S(1)}, bf16[64,1024]{1,0:T(8,128)(2,1)S(1)}, u32[]{:S(2)}, u32[]{:S(2)}) collective-permute-start(bf16[64,1024]{1,0:T(8,128)(2,1)S(1)} %add_convert_fusion.6), channel_id=1, source_target_pairs={{0,1},{1,0},{2,3},{3,2},{4,5},{5,4},{6,7},{7,6},{8,9},{9,8},{10,11... | collective-permute-start | bytes 393224 | tf_op jit(solution)/shard_map/ppermute | solution.py:308
  155.6 11.1 %collective-permute-start.8 = (bf16[64,2048]{1,0:T(8,128)(2,1)S(1)}, bf16[64,2048]{1,0:T(8,128)(2,1)S(1)}, u32[]{:S(2)}, u32[]{:S(2)}) collective-permute-start(bf16[64,2048]{1,0:T(8,128)(2,1)S(1)} %add_convert_fusion.3), channel_id=1, source_target_pairs={{0,2},{1,3},{2,0},{3,1},{4,6},{5,7},{6,4},{7,5},{8,10},{9,11},{10,... | collective-permute-start | bytes 786440 | tf_op jit(solution)/shard_map/ppermute | solution.py:308
  163.7 12.4 %collective-permute-start.54 = (bf16[64,2048]{1,0:T(8,128)(2,1)S(1)}, bf16[64,2048]{1,0:T(8,128)(2,1)S(1)}, u32[]{:S(2)}, u32[]{:S(2)}) collective-permute-start(bf16[64,2048]{1,0:T(8,128)(2,1)S(1)} %get-tuple-element.82.refs_0_), channel_id=1, source_target_pairs={{0,1},{1,0},{2,3},{3,2},{4,5},{5,4},{6,7},{7,6},{8,9},{9,8},{10,11... | collective-permute-start | bytes 786440 | tf_op jit(solution)/shard_map/ppermute | solution.py:308
  163.8 13.8 %collective-permute-start.55 = (bf16[64,2048]{1,0:T(8,128)(2,1)S(1)}, bf16[64,2048]{1,0:T(8,128)(2,1)S(1)}, u32[]{:S(2)}, u32[]{:S(2)}) collective-permute-start(bf16[64,2048]{1,0:T(8,128)(2,1)S(1)} %get-tuple-element.82.refs_0_), channel_id=1, source_target_pairs={{0,2},{1,3},{2,0},{3,1},{4,6},{5,7},{6,4},{7,5},{8,10},{9,11},{10,... | collective-permute-start | bytes 786440 | tf_op jit(solution)/shard_map/ppermute | solution.py:308
  165.4 13.3 %collective-permute-start.58 = (bf16[64,2048]{1,0:T(8,128)(2,1)S(1)}, bf16[64,2048]{1,0:T(8,128)(2,1)S(1)}, u32[]{:S(2)}, u32[]{:S(2)}) collective-permute-start(bf16[64,2048]{1,0:T(8,128)(2,1)S(1)} %get-tuple-element.83.refs_4_), channel_id=1, source_target_pairs={{0,2},{1,3},{2,0},{3,1},{4,6},{5,7},{6,4},{7,5},{8,10},{9,11},{10,... | collective-permute-start | bytes 786440 | tf_op jit(solution)/shard_map/ppermute | solution.py:308
  166.7 15.0 %collective-permute-start.57 = (bf16[64,2048]{1,0:T(8,128)(2,1)S(1)}, bf16[64,2048]{1,0:T(8,128)(2,1)S(1)}, u32[]{:S(2)}, u32[]{:S(2)}) collective-permute-start(bf16[64,2048]{1,0:T(8,128)(2,1)S(1)} %get-tuple-element.83.refs_4_), channel_id=1, source_target_pairs={{0,1},{1,0},{2,3},{3,2},{4,5},{5,4},{6,7},{7,6},{8,9},{9,8},{10,11... | collective-permute-start | bytes 786440 | tf_op jit(solution)/shard_map/ppermute | solution.py:308
  170.9 16.4 %collective-permute-start.22 = (bf16[64,2048]{1,0:T(8,128)(2,1)S(1)}, bf16[64,2048]{1,0:T(8,128)(2,1)S(1)}, u32[]{:S(2)}, u32[]{:S(2)}) collective-permute-start(bf16[64,2048]{1,0:T(8,128)(2,1)S(1)} %get-tuple-element.61.refs_0_), channel_id=1, source_target_pairs={{0,1},{1,0},{2,3},{3,2},{4,5},{5,4},{6,7},{7,6},{8,9},{9,8},{10,11... | collective-permute-start | bytes 786440 | tf_op jit(solution)/shard_map/ppermute | solution.py:308
  176.1 13.3 %collective-permute-start.26 = (bf16[64,2048]{1,0:T(8,128)(2,1)S(1)}, bf16[64,2048]{1,0:T(8,128)(2,1)S(1)}, u32[]{:S(2)}, u32[]{:S(2)}) collective-permute-start(bf16[64,2048]{1,0:T(8,128)(2,1)S(1)} %get-tuple-element.62.refs_4_), channel_id=1, source_target_pairs={{0,2},{1,3},{2,0},{3,1},{4,6},{5,7},{6,4},{7,5},{8,10},{9,11},{10,... | collective-permute-start | bytes 786440 | tf_op jit(solution)/shard_map/ppermute | solution.py:308
  177.6 13.3 %collective-permute-start.56 = (bf16[64,2048]{1,0:T(8,128)(2,1)S(1)}, bf16[64,2048]{1,0:T(8,128)(2,1)S(1)}, u32[]{:S(2)}, u32[]{:S(2)}) collective-permute-start(bf16[64,2048]{1,0:T(8,128)(2,1)S(1)} %collective-permute-done.54.refs_1_), channel_id=1, source_target_pairs={{0,2},{1,3},{2,0},{3,1},{4,6},{5,7},{6,4},{7,5},{8,10},{9,11},{10,... | collective-permute-start | bytes 786440 | tf_op jit(solution)/shard_map/ppermute | solution.py:308
  178.7 14.2 %collective-permute-start.59 = (bf16[64,2048]{1,0:T(8,128)(2,1)S(1)}, bf16[64,2048]{1,0:T(8,128)(2,1)S(1)}, u32[]{:S(2)}, u32[]{:S(2)}) collective-permute-start(bf16[64,2048]{1,0:T(8,128)(2,1)S(1)} %collective-permute-done.58.refs_6_), channel_id=1, source_target_pairs={{0,1},{1,0},{2,3},{3,2},{4,5},{5,4},{6,7},{7,6},{8,9},{9,8},{10,11... | collective-permute-start | bytes 786440 | tf_op jit(solution)/shard_map/ppermute | solution.py:308
  181.7 24.2 %collective-permute-start.23 = (bf16[64,2048]{1,0:T(8,128)(2,1)S(1)}, bf16[64,2048]{1,0:T(8,128)(2,1)S(1)}, u32[]{:S(2)}, u32[]{:S(2)}) collective-permute-start(bf16[64,2048]{1,0:T(8,128)(2,1)S(1)} %get-tuple-element.61.refs_0_), channel_id=1, source_target_pairs={{0,2},{1,3},{2,0},{3,1},{4,6},{5,7},{6,4},{7,5},{8,10},{9,11},{10,... | collective-permute-start | bytes 786440 | tf_op jit(solution)/shard_map/ppermute | solution.py:308
  187.3 18.6 %collective-permute-start.25 = (bf16[64,2048]{1,0:T(8,128)(2,1)S(1)}, bf16[64,2048]{1,0:T(8,128)(2,1)S(1)}, u32[]{:S(2)}, u32[]{:S(2)}) collective-permute-start(bf16[64,2048]{1,0:T(8,128)(2,1)S(1)} %get-tuple-element.62.refs_4_), channel_id=1, source_target_pairs={{0,1},{1,0},{2,3},{3,2},{4,5},{5,4},{6,7},{7,6},{8,9},{9,8},{10,11... | collective-permute-start | bytes 786440 | tf_op jit(solution)/shard_map/ppermute | solution.py:308
  189.3 16.5 %collective-permute-start.24 = (bf16[64,2048]{1,0:T(8,128)(2,1)S(1)}, bf16[64,2048]{1,0:T(8,128)(2,1)S(1)}, u32[]{:S(2)}, u32[]{:S(2)}) collective-permute-start(bf16[64,2048]{1,0:T(8,128)(2,1)S(1)} %collective-permute-done.22.refs_1_), channel_id=1, source_target_pairs={{0,2},{1,3},{2,0},{3,1},{4,6},{5,7},{6,4},{7,5},{8,10},{9,11},{10,... | collective-permute-start | bytes 786440 | tf_op jit(solution)/shard_map/ppermute | solution.py:308
  190.9 14.9 %collective-permute-start.27 = (bf16[64,2048]{1,0:T(8,128)(2,1)S(1)}, bf16[64,2048]{1,0:T(8,128)(2,1)S(1)}, u32[]{:S(2)}, u32[]{:S(2)}) collective-permute-start(bf16[64,2048]{1,0:T(8,128)(2,1)S(1)} %collective-permute-done.26.refs_6_), channel_id=1, source_target_pairs={{0,1},{1,0},{2,3},{3,2},{4,5},{5,4},{6,7},{7,6},{8,9},{9,8},{10,11... | collective-permute-start | bytes 786440 | tf_op jit(solution)/shard_map/ppermute | solution.py:308
  205.8 13.5 %collective-permute-start.60 = (bf16[256,1536]{1,0:T(8,128)(2,1)S(1)}, bf16[256,1536]{1,0:T(8,128)(2,1)S(1)}, u32[]{:S(2)}, u32[]{:S(2)}) collective-permute-start(bf16[256,1536]{1,0:T(8,128)(2,1)S(1)} %get-tuple-element.85), channel_id=1, source_target_pairs={{0,4},{4,0},{8,12},{12,8},{16,20},{20,16},{24,28},{28,24},{1,5},{5... | collective-permute-start | bytes 2359304 | tf_op jit(solution)/shard_map/ppermute | solution.py:311
  219.4 18.2 %collective-permute-start.62 = (bf16[256,384]{1,0:T(8,128)(2,1)S(1)}, bf16[256,384]{1,0:T(8,128)(2,1)S(1)}, u32[]{:S(2)}, u32[]{:S(2)}) collective-permute-start(bf16[256,384]{1,0:T(8,128)(2,1)S(1)} %get-tuple-element.87), channel_id=1, source_target_pairs={{0,16},{4,20},{8,24},{12,28},{16,0},{20,4},{24,8},{28,12},{1,17},{... | collective-permute-start | bytes 589832 | tf_op jit(solution)/shard_map/ppermute | solution.py:395
  223.1 14.5 %collective-permute-start.63 = (bf16[256,384]{1,0:T(8,128)(2,1)S(1)}, bf16[256,384]{1,0:T(8,128)(2,1)S(1)}, u32[]{:S(2)}, u32[]{:S(2)}) collective-permute-start(bf16[256,384]{1,0:T(8,128)(2,1)S(1)} %get-tuple-element.88), channel_id=1, source_target_pairs={{0,24},{4,28},{8,0},{12,4},{16,8},{20,12},{24,16},{28,20},{1,25},{... | collective-permute-start | bytes 589832 | tf_op jit(solution)/shard_map/ppermute | solution.py:395
  223.7 18.1 %collective-permute-start.29 = (bf16[256,384]{1,0:T(8,128)(2,1)S(1)}, bf16[256,384]{1,0:T(8,128)(2,1)S(1)}, u32[]{:S(2)}, u32[]{:S(2)}) collective-permute-start(bf16[256,384]{1,0:T(8,128)(2,1)S(1)} %get-tuple-element.65), channel_id=1, source_target_pairs={{0,8},{4,12},{8,16},{12,20},{16,24},{20,28},{24,0},{28,4},{1,9},{5... | collective-permute-start | bytes 589832 | tf_op jit(solution)/shard_map/ppermute | solution.py:395
  225.4 28.2 %collective-permute-start.30 = (bf16[256,384]{1,0:T(8,128)(2,1)S(1)}, bf16[256,384]{1,0:T(8,128)(2,1)S(1)}, u32[]{:S(2)}, u32[]{:S(2)}) collective-permute-start(bf16[256,384]{1,0:T(8,128)(2,1)S(1)} %get-tuple-element.66), channel_id=1, source_target_pairs={{0,16},{4,20},{8,24},{12,28},{16,0},{20,4},{24,8},{28,12},{1,17},{... | collective-permute-start | bytes 589832 | tf_op jit(solution)/shard_map/ppermute | solution.py:395
  229.1 24.4 %collective-permute-start.31 = (bf16[256,384]{1,0:T(8,128)(2,1)S(1)}, bf16[256,384]{1,0:T(8,128)(2,1)S(1)}, u32[]{:S(2)}, u32[]{:S(2)}) collective-permute-start(bf16[256,384]{1,0:T(8,128)(2,1)S(1)} %get-tuple-element.67), channel_id=1, source_target_pairs={{0,24},{4,28},{8,0},{12,4},{16,8},{20,12},{24,16},{28,20},{1,25},{... | collective-permute-start | bytes 589832 | tf_op jit(solution)/shard_map/ppermute | solution.py:395
  (19 other events, 142.5 us)

commit v2 on v0

v2 whole, which is shorter than its diff:
```python
import functools

import jax
import jax.numpy as jnp
from jax import lax
from jax.experimental import pallas as pl
from jax.experimental.pallas import tpu as pltpu
from jax.sharding import PartitionSpec as P

BLOCK = 128
CORES = 2
CHUNKS = 2
BF16 = jnp.bfloat16
F32 = jnp.float32
PARAMS = pltpu.CompilerParams(vmem_limit_bytes=8 << 20)
VMEM = pl.BlockSpec(memory_space=pltpu.VMEM)
SMEM = pl.BlockSpec(memory_space=pltpu.SMEM)


def tile_of(extent, most):
    best = BLOCK
    for size in range(BLOCK, most + 1, BLOCK):
        if extent % size == 0:
            best = size
    return best


def dot(left, right, contract):
    return lax.dot_general(
        left, right, (((1,), (contract,)), ((), ())), preferred_element_type=F32
    )


def cost(rows, depth, columns):
    return pl.CostEstimate(
        flops=1024, bytes_accessed=1024, transcendentals=0
    )


def array(rows, columns):
    return jax.ShapeDtypeStruct((rows, columns), BF16)


def reversed_bits(q, count):
    width = count.bit_length() - 1
    return sum(((q >> i) & 1) << (width - 1 - i) for i in range(width))


def block_of(q, count, core):
    return q + core * (reversed_bits(q, count) - q)


def weight_kernel(turned, code_ref, scale_ref, weight_ref, buffer, sems):
    slots, rows = buffer.shape[:2]
    count = code_ref.shape[0] // rows

    def fetch(i):
        slot = lax.rem(i, slots)
        return pltpu.make_async_copy(
            code_ref.at[pl.ds(pl.multiple_of(i * rows, rows), rows)], buffer.at[slot], sems.at[slot]
        )

    for i in range(min(slots, count)):
        fetch(i).start()

    def body(i, carry):
        fetch(i).wait()
        slot = lax.rem(i, slots)
        start = pl.multiple_of(i * rows, rows)
        for c in range(code_ref.shape[1] // BLOCK):
            columns = slice(c * BLOCK, (c + 1) * BLOCK)
            weight_ref[pl.ds(start, rows), columns] = (
                buffer[slot, :, columns].astype(F32) * (scale_ref[c, i] if turned else scale_ref[i, c])
            ).astype(BF16)

        @pl.when(i + slots < count)
        def _():
            fetch(i + slots).start()

        return carry

    lax.fori_loop(0, count, body, 0)


def weight(code, scale, turned):
    slots = 6
    scale = scale.T if turned else scale
    return pl.pallas_call(
        functools.partial(weight_kernel, turned),
        in_specs=[pl.BlockSpec(memory_space=pltpu.HBM), SMEM],
        out_specs=VMEM,
        out_shape=pltpu.VMEM(code.shape, BF16),
        scratch_shapes=[
            pltpu.VMEM((slots, BLOCK, code.shape[1]), BF16),
            pltpu.SemaphoreType.DMA((slots,)),
        ],
        compiler_params=pltpu.CompilerParams(vmem_limit_bytes=10 << 20),
        cost_estimate=pl.CostEstimate(
            flops=0, bytes_accessed=code.size // 4096, transcendentals=0
        ),
        name="scaled_weight",
    )(pltpu.with_memory_space_constraint(code, pltpu.HBM), scale)


def prep_kernel(rows, where_ref, inputs_ref, cotangent_ref, *refs):
    *out_refs, sem = refs
    count = inputs_ref.shape[0] // CHUNKS // rows
    copies = []
    for at, out_ref in enumerate(out_refs):
        for q in range(count):
            start = pl.multiple_of((at // 2 * count + (where_ref[0] ^ q)) * rows, rows)
            copies.append(
                pltpu.make_async_copy(
                    (inputs_ref, cotangent_ref)[at % 2].at[pl.ds(start, rows)],
                    out_ref.at[pl.ds(q * rows, rows)],
                    sem.at[len(copies)],
                )
            )
            copies[-1].start()
    for copy in copies:
        copy.wait()


def prepare(where, inputs, cotangent, n_dp):
    seq, width = inputs.shape
    return pl.pallas_call(
        functools.partial(prep_kernel, seq // CHUNKS // n_dp),
        in_specs=[SMEM] + [pl.BlockSpec(memory_space=pltpu.HBM)] * 2,
        out_specs=[VMEM] * (2 * CHUNKS),
        out_shape=[array(seq // CHUNKS, width)] * (2 * CHUNKS),
        scratch_shapes=[pltpu.SemaphoreType.DMA((2 * CHUNKS * n_dp,))],
        compiler_params=PARAMS,
        name="order_rows",
    )(
        where,
        pltpu.with_memory_space_constraint(inputs, pltpu.HBM),
        pltpu.with_memory_space_constraint(cotangent, pltpu.HBM),
    )


def join_kernel(*refs):
    *part_refs, out_ref = refs
    width = part_refs[0].shape[1]
    for j, part_ref in enumerate(part_refs):
        out_ref[:, j * width : (j + 1) * width] = part_ref[...]


def join(parts):
    rows, width = parts[0].shape
    return pl.pallas_call(
        join_kernel,
        in_specs=[VMEM] * len(parts),
        out_specs=VMEM,
        out_shape=array(rows, width * len(parts)),
        compiler_params=PARAMS,
        name="join",
    )(*parts)


def join_four_kernel(where_ref, own_ref, two_ref, near_ref, middle_ref, passed_ref, out_ref):
    width = own_ref.shape[1]
    place = where_ref[1]
    out_ref[:, :width] = own_ref[...]
    out_ref[:, 2 * width : 3 * width] = two_ref[...]
    odd = lax.rem(place, 2)
    out_ref[:, pl.ds(pl.multiple_of((1 + 2 * odd) * width, width), width)] = near_ref[...]
    rest = pl.ds(pl.multiple_of((3 - 2 * odd) * width, width), width)
    inner = jnp.logical_or(place == 1, place == 2)

    @pl.when(inner)
    def _():
        out_ref[:, rest] = middle_ref[...]

    @pl.when(jnp.logical_not(inner))
    def _():
        out_ref[:, rest] = passed_ref[...]


def join_four(where, parts):
    rows, width = parts[0].shape
    return pl.pallas_call(
        join_four_kernel,
        in_specs=[SMEM] + [VMEM] * len(parts),
        out_specs=VMEM,
        out_shape=array(rows, 4 * width),
        compiler_params=PARAMS,
        name="join",
    )(where, *parts)


def assemble(width, blocks, where_ref, x_refs, x_all):
    rows = x_all.shape[0] // blocks
    for q in range(blocks):
        start = pl.multiple_of(block_of(q, blocks, where_ref[2]) * rows, rows)
        own = slice(q * rows, (q + 1) * rows)
        if len(x_refs) == 1:
            x_all[own] = x_refs[0][pl.ds(start, rows)]
            continue
        count = x_all.shape[1] // (CORES * width)
        for j in range(count):
            for core, x_ref in enumerate(x_refs):
                place = lax.rem(where_ref[1] + j, count) * CORES + (where_ref[2] ^ core)
                x_all[own, pl.ds(pl.multiple_of(place * width, width), width)] = x_ref[
                    pl.ds(start, rows), j * width : (j + 1) * width
                ]


def forward_kernel(groups, contract, width, count, where_ref, *refs):
    outs = len(groups)
    x_refs, weight_refs = refs[: -outs - 1 - count], refs[-outs - 1 - count : -outs - 1]
    out_refs, x_all = refs[-outs - 1 : -1], refs[-1]
    blocks = sum(len(group) for group in groups)
    assemble(width, blocks, where_ref, x_refs, x_all)
    columns = out_refs[0].shape[1] // count
    rows = x_all.shape[0] // blocks
    tile = tile_of(columns, 512)
    for at, weight_ref in enumerate(weight_refs):
        for n in range(0, columns, tile):
            part = weight_ref[n : n + tile, :] if contract else weight_ref[:, n : n + tile]
            total = dot(x_all[...], part, contract).astype(BF16)
            place = slice(at * columns + n, at * columns + n + tile)
            for out_ref, group in zip(out_refs, groups):
                for i, q in enumerate(group):
                    out_ref[i * rows : (i + 1) * rows, place] = total[q * rows : (q + 1) * rows]


def forward(where, x, weights, groups, contract, width):
    rows, blocks = x[0].shape[0], sum(len(group) for group in groups)
    depth, columns = weights[0].shape[contract], weights[0].shape[1 - contract]
    outs = [array(rows * len(group) // blocks, columns * len(weights)) for group in groups]
    return pl.pallas_call(
        functools.partial(forward_kernel, groups, contract, width, len(weights)),
        in_specs=[SMEM] + [VMEM] * (len(x) + len(weights)),
        out_specs=[VMEM] * len(outs),
        out_shape=outs,
        scratch_shapes=[pltpu.VMEM((rows, depth), BF16)],
        compiler_params=PARAMS,
        cost_estimate=cost(rows, depth, columns),
        name="forward_product",
    )(where, *x, *(pltpu.with_memory_space_constraint(part, pltpu.VMEM) for part in weights))


def streamed_kernel(groups, width, where_ref, scale_ref, *refs):
    outs = len(groups)
    x_refs, code_ref = refs[: -outs - 4], refs[-outs - 4]
    out_refs, (x_all, buffer, sems) = refs[-outs - 3 : -3], refs[-3:]
    slots, tile, depth = buffer.shape
    count = code_ref.shape[0] // tile
    blocks = sum(len(group) for group in groups)
    rows = x_all.shape[0] // blocks
    step = tile_of(depth, 512)

    def fetch(i):
        slot = lax.rem(i, slots)
        return pltpu.make_async_copy(
            code_ref.at[pl.ds(pl.multiple_of(i * tile, tile), tile)], buffer.at[slot], sems.at[slot]
        )

    for i in range(min(slots, count)):
        fetch(i).start()
    assemble(width, blocks, where_ref, x_refs, x_all)

    def body(i, carry):
        fetch(i).wait()
        slot = lax.rem(i, slots)
        total = None
        for k in range(0, depth, step):
            lines = []
            for r in range(tile // BLOCK):
                lines.append(
                    jnp.concatenate(
                        [
                            (
                                buffer[slot, r * BLOCK : (r + 1) * BLOCK, c : c + BLOCK].astype(F32)
                                * scale_ref[i * (tile // BLOCK) + r, c // BLOCK]
                            ).astype(BF16)
                            for c in range(k, k + step, BLOCK)
                        ],
                        axis=1,
                    )
                )
            term = dot(x_all[:, k : k + step], jnp.concatenate(lines, axis=0), 1)
            total = term if total is None else total + term
        total = total.astype(BF16)
        columns = pl.ds(pl.multiple_of(i * tile, tile), tile)
        for out_ref, group in zip(out_refs, groups):
            for at, q in enumerate(group):
                out_ref[at * rows : (at + 1) * rows, columns] = total[q * rows : (q + 1) * rows]

        @pl.when(i + slots < count)
        def _():
            fetch(i + slots).start()

        return carry

    lax.fori_loop(0, count, body, 0)


def forward_streamed(where, x, code, scale, groups, width):
    rows, blocks = x[0].shape[0], sum(len(group) for group in groups)
    columns, depth = code.shape
    tile, slots = tile_of(columns, 256), 3
    return pl.pallas_call(
        functools.partial(streamed_kernel, groups, width),
        in_specs=[SMEM] * 2 + [VMEM] * len(x) + [pl.BlockSpec(memory_space=pltpu.HBM)],
        out_specs=[VMEM] * len(groups),
        out_shape=[array(rows * len(group) // blocks, columns) for group in groups],
        scratch_shapes=[
            pltpu.VMEM((rows, depth), BF16),
            pltpu.VMEM((slots, tile, depth), BF16),
            pltpu.SemaphoreType.DMA((slots,)),
        ],
        compiler_params=pltpu.CompilerParams(vmem_limit_bytes=14 << 20),
        cost_estimate=cost(rows, depth, columns),
        name="forward_streamed",
    )(where, scale, *x, pltpu.with_memory_space_constraint(code, pltpu.HBM))


def grads_kernel(both, where_ref, *refs):
    *in_refs, out_ref = refs
    rows, width = out_ref.shape[0], out_ref.shape[1] // 2
    tile = tile_of(width, 512)

    def total(terms, n):
        values = [term[term.shape[0] - rows :, n : n + tile].astype(F32) for term in terms]
        return functools.reduce(lambda left, right: left + right, values)

    for n in range(0, width, tile):
        gate_pre = total(in_refs[:both], n)
        up_pre = total(in_refs[:both], width + n)
        hidden_grad = total(in_refs[both:], n)
        gate_sig = jax.nn.sigmoid(gate_pre)
        out_ref[:, n : n + tile] = (
            hidden_grad * up_pre * gate_sig * (1.0 + gate_pre * (1.0 - gate_sig))
        ).astype(BF16)
        out_ref[:, width + n : width + n + tile] = (hidden_grad * gate_pre * gate_sig).astype(BF16)


def grads(where, gate_up, hidden_terms, rows, width):
    return pl.pallas_call(
        functools.partial(grads_kernel, len(gate_up)),
        in_specs=[SMEM] + [VMEM] * (len(gate_up) + len(hidden_terms)),
        out_specs=VMEM,
        out_shape=array(rows, 2 * width),
        compiler_params=PARAMS,
        name="hidden_grads",
    )(where, *gate_up, *hidden_terms)


def backward_kernel(places, total_places, where_ref, *refs):
    outs = CORES if total_places else 1
    *grad_refs, gate_ref, up_ref = refs[: -3 - outs]
    *out_refs, gate_all, up_all, total_ref = refs[-3 - outs :]
    blocks, rows = len(grad_refs), grad_refs[0].shape[0]
    depth = gate_all.shape[1]
    for q, grad_ref in enumerate(grad_refs):
        start = pl.multiple_of(block_of(q, blocks, where_ref[2]) * rows, rows)
        gate_all[pl.ds(start, rows)] = grad_ref[:, :depth]
        up_all[pl.ds(start, rows)] = grad_ref[:, depth:]
    tile = total_ref.shape[1]
    for at, j in enumerate(places):
        place = lax.rem(where_ref[1] + j, total_places) if total_places else j
        part = pl.ds(pl.multiple_of(place * tile, tile), tile)
        total = dot(gate_all[...], gate_ref[part, :], 1) + dot(up_all[...], up_ref[part, :], 1)
        if total_places:
            width = tile // CORES
            total_ref[...] = total.astype(BF16)
            for out_ref, core in zip(out_refs, (where_ref[2], 1 - where_ref[2])):
                out_ref[:, at * width : (at + 1) * width] = total_ref[
                    :, pl.ds(pl.multiple_of(core * width, width), width)
                ]
        else:
            out_refs[0][:, at * tile : (at + 1) * tile] = total.astype(BF16)


def backward(where, grad_parts, gate_weight, up_weight, places, total_places):
    columns, depth = gate_weight.shape
    rows = grad_parts[0].shape[0] * len(grad_parts)
    outs = CORES if total_places else 1
    tile = columns // total_places if total_places else tile_of(columns, 512)
    places = places if total_places else range(columns // tile)
    return pl.pallas_call(
        functools.partial(backward_kernel, places, total_places),
        in_specs=[SMEM] + [VMEM] * (len(grad_parts) + 2),
        out_specs=[VMEM] * outs,
        out_shape=[array(rows, tile * len(places) // outs)] * outs,
        scratch_shapes=[pltpu.VMEM((rows, depth), BF16)] * 2 + [pltpu.VMEM((rows, tile), BF16)],
        compiler_params=PARAMS,
        cost_estimate=cost(rows, 2 * depth, tile * len(places)),
        name="backward_product",
    )(
        where,
        *grad_parts,
        pltpu.with_memory_space_constraint(gate_weight, pltpu.VMEM),
        pltpu.with_memory_space_constraint(up_weight, pltpu.VMEM),
    )


def pair_kernel(own_ref, other_ref, *out_refs):
    width = out_refs[0].shape[1]
    for j, out_ref in enumerate(out_refs):
        columns = slice(j * width, (j + 1) * width)
        out_ref[...] = (own_ref[:, columns].astype(F32) + other_ref[:, columns].astype(F32)).astype(
            BF16
        )


def pair_sums(own, other, count, width):
    rows = own.shape[0]
    return pl.pallas_call(
        pair_kernel,
        in_specs=[VMEM] * 2,
        out_specs=[VMEM] * count,
        out_shape=[array(rows, width)] * count,
        compiler_params=PARAMS,
        name="pair_sums",
    )(own, other)


def final_kernel(blocks, done, where_ref, *refs):
    done_refs, in_refs, out_ref = refs[:done], refs[done:-1], refs[-1]
    rows = in_refs[0].shape[0] // blocks
    width = out_ref.shape[1]
    at = 0
    for done_ref in done_refs:
        out_ref[at : at + done_ref.shape[0]] = done_ref[...]
        at += done_ref.shape[0]
    for q in range(blocks):
        total = None
        for ref in in_refs:
            value = ref[q * rows : (q + 1) * rows, ref.shape[1] - width :].astype(F32)
            total = value if total is None else total + value
        start = pl.multiple_of(at + (where_ref[0] ^ q) * rows, rows)
        out_ref[pl.ds(start, rows)] = total.astype(BF16)


def final_sum(where, done, terms, blocks, width):
    rows = terms[0].shape[0] + sum(part.shape[0] for part in done)
    return pl.pallas_call(
        functools.partial(final_kernel, blocks, len(done)),
        in_specs=[SMEM] + [VMEM] * (len(done) + len(terms)),
        out_specs=VMEM,
        out_shape=array(rows, width),
        compiler_params=PARAMS,
        name="final_sum",
    )(where, *done, *terms)


def local(
    n_tp, n_dp, inputs, cotangent, gate_code, gate_scale, up_code, up_scale, down_code, down_scale
):
    n_z = n_tp // CORES
    width = inputs.shape[1]
    hidden = gate_code.shape[1]
    steps = n_dp.bit_length() - 1
    by_blocks = width % BLOCK == 0
    tp = lax.axis_index("tp")
    where = jnp.stack([lax.axis_index("dp"), tp // CORES, tp % CORES]).astype(jnp.int32)

    def exchange(value, step):
        pairs = []
        for i in range(n_tp):
            bit = 1 << (step if i % CORES == 0 else steps - 1 - step)
            pairs += [(i * n_dp + k, i * n_dp + (k ^ bit)) for k in range(n_dp)]
        return lax.ppermute(value, ("tp", "dp"), pairs)

    def swap_cores(value):
        return lax.ppermute(value, "tp", [(i, i ^ 1) for i in range(n_tp)])

    def along(value, places):
        return lax.ppermute(
            value, "tp", [(i, (i + places * CORES) % n_tp) for i in range(n_tp)]
        )

    def between(value, pairs):
        return lax.ppermute(
            value,
            "tp",
            [(i * CORES + c, k * CORES + c) for i, k in pairs for c in range(CORES)],
        )

    hops = by_blocks and n_z == 4

    def set_out(piece):
        if not by_blocks:
            return [lax.all_gather(piece, "tp", axis=1, tiled=True)]
        if hops:
            return [along(piece, 2)]
        return [along(piece, n_z - j) for j in range(1, n_z)]

    def near(piece, got):
        return [*got, between(piece, [(0, 1), (1, 0), (2, 3), (3, 2)])] if hops else got

    def pass_on(piece, got):
        if not hops:
            return got
        return [*got, between(piece, [(1, 2), (2, 1)]), between(got[0], [(1, 0), (2, 3)])]

    def arrive(piece, got):
        if not by_blocks:
            return got
        own = join_four(where, (piece, *got)) if hops else join([piece, *got])
        return [own, swap_cores(own)]

    groups, stays = [[0]], [0]
    for step in reversed(range(steps)):
        groups.insert(0, [q | 1 << step for q in stays])
        stays = groups[0] + stays

    def send(parts, step=0):
        return [*parts, exchange(parts[step], step)]

    def take(parts, step=0):
        parts, at = list(parts), 0
        for later in range(step + 1, steps):
            height = parts[later].shape[0]
            came = parts[-1][at : at + height].astype(F32)
            parts[later] = (parts[later].astype(F32) + came).astype(BF16)
            at += height
        return parts

    def settle(parts):
        for step in range(1, steps):
            parts = send(take(parts, step - 1), step)
        return parts

    def terms_of(parts):
        return parts[steps:]

    def start_rows(value):
        return (
            {0: value, 1: exchange(value, 0)},
            {1 << step: exchange(value, step) for step in range(1, steps)},
        )

    def finish_rows(have, late):
        have = dict(have)
        for step in range(1, steps):
            for q in list(have):
                have[q | 1 << step] = exchange(have[q], step) if q else late[1 << step]
        return [have[q] for q in range(n_dp)]

    whole = [[*range(1, n_z), 0]]
    parts_of_z = [[2], [1, 3], [0]] if hops else whole

    def products(grad_parts, places):
        return backward(
            where, grad_parts, gate_weight, up_weight, places, n_z if by_blocks else 0
        )

    def swapped(partial):
        return [partial[0], swap_cores(partial[1])] if by_blocks else partial

    def scatter(partial, places):
        if not by_blocks:
            return [lax.psum_scatter(partial[0], "tp", scatter_dimension=1, tiled=True)]
        away = [j for j in places if j]
        if not away:
            return list(partial)
        sums = pair_sums(*partial, len(away), width)
        terms = [along(part, j) for j, part in zip(away, sums)]
        return terms + (list(partial) if 0 in places else [])

    rows = inputs.shape[0] // CHUNKS // n_dp

    def hold(values):
        nonlocal where
        values, where = lax.optimization_barrier((values, where))
        return values

    in_1, co_1, in_2, co_2 = prepare(where, inputs, cotangent, n_dp)
    got_in_1 = near(in_1, set_out(in_1))
    gate_weight = weight(gate_code, gate_scale, True)
    gate_weight, got_in_1, co_1 = hold((gate_weight, got_in_1, co_1))

    got_in_1 = pass_on(in_1, got_in_1)
    got_co_1 = near(co_1, set_out(co_1))
    up_weight = weight(up_code, up_scale, True)
    up_weight, got_in_1, got_co_1 = hold((up_weight, got_in_1, got_co_1))

    x = arrive(in_1, got_in_1)
    got_co_1 = pass_on(co_1, got_co_1)
    gate_up_1 = forward(where, x, [gate_weight, up_weight], groups, 0, width)
    gate_up_1, got_co_1, in_2 = hold((gate_up_1, got_co_1, in_2))

    gate_up_1 = send(gate_up_1)
    x = arrive(co_1, got_co_1)
    got_in_2 = near(in_2, set_out(in_2))
    hidden_1 = forward_streamed(where, x, down_code, down_scale, groups, width)
    hidden_1, gate_up_1, got_in_2 = hold((hidden_1, gate_up_1, got_in_2))

    hidden_1 = send(hidden_1)
    gate_up_1 = settle(gate_up_1)
    got_in_2 = hold(pass_on(in_2, got_in_2))

    x = arrive(in_2, got_in_2)
    x, co_2, hidden_1 = hold((x, co_2, hidden_1))

    hidden_1 = settle(hidden_1)
    got_co_2 = near(co_2, set_out(co_2))
    gate_up_2 = forward(where, x, [gate_weight, up_weight], groups, 0, width)
    gate_up_2, got_co_2, gate_up_1, hidden_1 = hold((gate_up_2, got_co_2, gate_up_1, hidden_1))

    got_co_2 = pass_on(co_2, got_co_2)
    gate_up_2 = send(gate_up_2)
    grad_1 = grads(where, terms_of(gate_up_1), terms_of(hidden_1), rows, hidden)
    got_co_2, grad_1 = hold((got_co_2, grad_1))

    early_1, late_1 = start_rows(grad_1)
    x = hold(arrive(co_2, got_co_2))

    hidden_2 = forward_streamed(where, x, down_code, down_scale, groups, width)
    hidden_2, gate_up_2 = hold((hidden_2, gate_up_2))

    hidden_2 = send(hidden_2)
    gate_up_2 = settle(gate_up_2)
    early_1 = hold(early_1)

    parts_1 = finish_rows(early_1, late_1)
    parts_1, hidden_2, gate_up_2 = hold((parts_1, hidden_2, gate_up_2))

    hidden_2 = settle(hidden_2)
    partial_1 = products(parts_1, whole[0])
    hidden_2, partial_1 = hold((hidden_2, partial_1))

    partial_1 = swapped(partial_1)
    grad_2 = grads(where, terms_of(gate_up_2), terms_of(hidden_2), rows, hidden)
    early_2, late_2 = start_rows(grad_2)
    terms_1 = scatter(partial_1, whole[0])
    early_2, early = hold((early_2, terms_1[:1]))
    parts_2 = finish_rows(early_2, late_2)
    parts_2, terms_1 = hold((parts_2, [*early, *terms_1[1:]]))

    terms_2 = []
    partial, before = products(parts_2, parts_of_z[0]), parts_of_z[0]
    for places in parts_of_z[1:]:
        following = products(parts_2, places)
        partial, following = hold((swapped(partial), following))
        terms_2 += scatter(partial, before)
        partial, before = following, places
    terms_2 += scatter(swapped(partial), before)
    done = [final_sum(where, [], terms_1, n_dp, width)]
    return final_sum(where, done, terms_2, n_dp, width)


def solution(mesh):
    placed = (
        P("groups", ("dp", "tp")),
        P("groups", ("dp", "tp")),
        P("dp", "tp"),
        P("dp", "tp"),
        P("dp", "tp"),
        P("dp", "tp"),
        P("tp", "dp"),
        P("tp", "dp"),
    )
    return jax.shard_map(
        functools.partial(local, mesh.shape["tp"], mesh.shape["dp"]),
        mesh=mesh,
        in_specs=placed,
        out_specs=P("groups", ("dp", "tp")),
        check_vma=False,
    )
```

time: 373 us -> 194 us (0.52)
  waiting for transfers between devices: 202 us -> 71.7 us
  matrix products: 108 us -> 0 us
  Pallas kernels: 0 us -> 68.6 us
  starting transfers between devices: 0.2 us -> 50.9 us
  local copies, waits for them, and re-layouts: 41 us -> 0.7 us
  between operations: 13.5 us -> 0.43 us
  other arithmetic: 7.23 us -> 0.45 us
    dot_general x5 -> x0, matrix products: 108 us -> none  [the longest x3 65.1 us: transposed_dot(): lax.dot_general(left, right, (((1,), (1,)), ((), ())), preferred_element_...]
    all_gather x4 -> x0, waiting for transfers between devices: 90 us -> none  [the longest x1 40.4 us: local(): lax.all_gather(inputs, 'tp', axis=1, tiled=True)]
    ppermute x0 -> x44, waiting for transfers between devices: none -> 71.7 us  [the longest x14 30.8 us: exchange(): return lax.ppermute(value, ('tp', 'dp'), pairs)]
    unnamed x7 -> x0, waiting for transfers between devices: 71.6 us -> none
    pallas_call x0 -> x22, Pallas kernels: none -> 68.6 us  [the longest x4 16.5 us: backward(): pl.pallas_call(functools.partial(backward_kernel, places, total_places),...]
    ppermute x0 -> x44, starting transfers between devices: none -> 50.9 us  [the longest x10 21.5 us: along(): lax.ppermute(value, 'tp', [(i, (i + places * CORES) % n_tp) for i in rang...]
    reduce_scatter x1 -> x0, waiting for transfers between devices: 40.5 us -> none  [local(): lax.psum_scatter((transposed_dot(gate_weight, gate_all) + transposed_dot(...]
    broadcast_in_dim x6 -> x0, local copies, waits for them, and re-layouts: 27 us -> none  [dequantize(): spread = jnp.repeat(jnp.repeat(scale, BLOCK, axis=0), BLOCK, axis=1)]
  transfers between devices with their start and end apart: 6 -> 44, of which waited for: 5 -> 19; matrix products, arithmetic and copies ran while one was open for 23% -> 0% of each run, Pallas kernels for 0% -> 32%
where the time goes in v2:
time: 194 us; the launch traced here: 193 us
  waiting for transfers between devices  71.7 us (37%)
  Pallas kernels  68.6 us (35%)
  starting transfers between devices  50.9 us (26%)
    ppermute x14, waiting for transfers between devices, exchange(): return lax.ppermute(value, ('tp', 'dp'), pairs)  30.8 us
    ppermute x10, waiting for transfers between devices, along(): lax.ppermute(value, 'tp', [(i, (i + places * CORES) % n_tp) for i in rang...  24.3 us
    ppermute x10, starting transfers between devices, along(): lax.ppermute(value, 'tp', [(i, (i + places * CORES) % n_tp) for i in rang...  21.5 us
    ppermute x14, starting transfers between devices, exchange(): return lax.ppermute(value, ('tp', 'dp'), pairs)  18.8 us
    pallas_call x4, Pallas kernels, backward(): pl.pallas_call(functools.partial(backward_kernel, places, total_places),...  16.5 us
    ppermute x12, waiting for transfers between devices, between(): lax.ppermute(value, 'tp', [(i * CORES + c, k * CORES + c) for i, k in pai...  15.6 us
    pallas_call x2, Pallas kernels, forward(): pl.pallas_call(functools.partial(forward_kernel, groups, contract, width,...  15 us
    pallas_call x2, Pallas kernels, forward_streamed(): pl.pallas_call(functools.partial(streamed_kernel, groups, width), in_spec...  14.8 us
  transfers between devices with their start and end apart: 44, of which 19 were waited for; matrix products, arithmetic and copies ran while one was open for 0% of the time, Pallas kernels for 32%

profile of v2, /device:TPU:0, one launch (start us, length us, event | category | flops | bytes accessed | tf_op | source)
XLA Modules:
  0.0 192.9 jit_solution(15183071543949507984)
XLA Ops:
  0.1 1.8 order_rows.1
  1.9 4.1 %collective-permute-start = (bf16[256,384]{1,0:T(8,128)(2,1)S(1)}, bf16[256,384]{1,0:T(8,128)(2,1)S(1)}, u32[]{:S(2)}, u32[]{:S(2)}) collective-permute-start(bf16[256,384]{1,0:T(8,128)(2,1)S(1)} %get-tuple-element.149.own_ref), channel_id=1, source_target_pairs={{0,16},{4,20},{8,24},{12,28},{16,0},{20,4},{24,8},{28,12},{1,17},{... | collective-permute-start | bytes 589832 | tf_op jit(solution)/shard_map/ppermute | solution.py:471
  6.0 1.6 collective-permute-start.1
  8.9 6.6 %scaled_weight.3.refs_2_.refs_4_ = bf16[3072,2048]{1,0:T(8,128)(2,1)S(1)} custom-call(bf16[3072,2048]{1,0:T(8,128)(2,1)} %code_ref.3, f32[16,24]{1,0:T(8,128)S(1)} %bitcast.5), custom_call_target="tpu_custom_call" | custom-call | bytes 1536 | tf_op jit(solution)/shard_map/scaled_weight/pallas_call | solution.py:88
  16.0 1.3 collective-permute-start.3
  17.3 4.0 %collective-permute-start.4 = (bf16[256,384]{1,0:T(8,128)(2,1)S(1)}, bf16[256,384]{1,0:T(8,128)(2,1)S(1)}, u32[]{:S(2)}, u32[]{:S(2)}) collective-permute-start(bf16[256,384]{1,0:T(8,128)(2,1)S(1)} %get-tuple-element.153.own_ref), channel_id=1, source_target_pairs={{0,16},{4,20},{8,24},{12,28},{16,0},{20,4},{24,8},{28,12},{1,17},{... | collective-permute-start | bytes 589832 | tf_op jit(solution)/shard_map/ppermute | solution.py:471
  21.3 6.6 %scaled_weight.2.refs_3_.refs_5_ = bf16[3072,2048]{1,0:T(8,128)(2,1)S(1)} custom-call(bf16[3072,2048]{1,0:T(8,128)(2,1)} %code_ref.2, f32[16,24]{1,0:T(8,128)S(1)} %bitcast.6), custom_call_target="tpu_custom_call" | custom-call | bytes 1536 | tf_op jit(solution)/shard_map/scaled_weight/pallas_call | solution.py:88
  27.9 2.1 %collective-permute-done.4.two_ref = bf16[256,384]{1,0:T(8,128)(2,1)S(1)} collective-permute-done((bf16[256,384]{1,0:T(8,128)(2,1)S(1)}, bf16[256,384]{1,0:T(8,128)(2,1)S(1)}, u32[]{:S(2)}, u32[]{:S(2)}) %collective-permute-start.4) | collective-permute-done | bytes 196640 | tf_op jit(solution)/shard_map/ppermute | solution.py:471
  30.0 2.0 %collective-permute-done.5.near_ref = bf16[256,384]{1,0:T(8,128)(2,1)S(1)} collective-permute-done((bf16[256,384]{1,0:T(8,128)(2,1)S(1)}, bf16[256,384]{1,0:T(8,128)(2,1)S(1)}, u32[]{:S(2)}, u32[]{:S(2)}) %collective-permute-start.5) | collective-permute-done | bytes 196640 | tf_op jit(solution)/shard_map/ppermute | solution.py:476
  33.4 1.3 collective-permute-start.8
  35.0 7.5 %forward_product.2 = (bf16[128,4096]{1,0:T(8,128)(2,1)S(1)}, bf16[64,4096]{1,0:T(8,128)(2,1)S(1)}, bf16[64,4096]{1,0:T(8,128)(2,1)S(1)}) custom-call(s32[3]{0:T(128)S(1)} %pad_add_fusion.where_ref, bf16[256,1536]{1,0:T(8,128)(2,1)S(1)} %join.4.refs_0_, bf16[256,1536]{1,0:T(8,128)(2,1)S(1)} %collective-permute-done.6.refs_1_, ...), custom_call_target="tpu_custom_call" | custom-call | flops 1024 | bytes 1024 | tf_op jit(solution)/shard_map/forward_product/pallas_call | solution.py:231
  42.5 1.1 collective-permute-done.8.passed_ref
  43.6 1.5 collective-permute-start.10
  45.8 3.7 %collective-permute-start.11 = (bf16[256,384]{1,0:T(8,128)(2,1)S(1)}, bf16[256,384]{1,0:T(8,128)(2,1)S(1)}, u32[]{:S(2)}, u32[]{:S(2)}) collective-permute-start(bf16[256,384]{1,0:T(8,128)(2,1)S(1)} %get-tuple-element.179.own_ref), channel_id=1, source_target_pairs={{0,16},{4,20},{8,24},{12,28},{16,0},{20,4},{24,8},{28,12},{1,17},{... | collective-permute-start | bytes 589832 | tf_op jit(solution)/shard_map/ppermute | solution.py:471
  50.3 7.4 %forward_streamed.2 = (bf16[128,2048]{1,0:T(8,128)(2,1)S(1)}, bf16[64,2048]{1,0:T(8,128)(2,1)S(1)}, bf16[64,2048]{1,0:T(8,128)(2,1)S(1)}) custom-call(s32[3]{0:T(128)S(1)} %pad_add_fusion.where_ref, f32[16,24]{1,0:T(8,128)S(1)} %copy-done, bf16[256,1536]{1,0:T(8,128)(2,1)S(1)} %join.5.refs_0_, bf16[256,1536]{1,0:T(8,128)(2,1)S(1)} %collective-permute-done.9.refs_1_, ...), custom_call_target="tpu_custom_call" | custom-call | flops 1024 | bytes 1024 | tf_op jit(solution)/shard_map/forward_streamed/pallas_call | solution.py:303
  57.7 1.9 collective-permute-done.11.two_ref
  59.9 1.3 collective-permute-start.14
  61.2 1.1 collective-permute-start.16
  62.2 5.6 %collective-permute-done.14.passed_ref = bf16[256,384]{1,0:T(8,128)(2,1)S(1)} collective-permute-done((bf16[256,384]{1,0:T(8,128)(2,1)S(1)}, bf16[256,384]{1,0:T(8,128)(2,1)S(1)}, u32[]{:S(2)}, u32[]{:S(2)}) %collective-permute-start.14) | collective-permute-done | bytes 196640 | tf_op jit(solution)/shard_map/ppermute | solution.py:476
  68.9 1.6 collective-permute-start.19
  71.1 1.6 collective-permute-start.20
  72.7 3.2 %collective-permute-start.17 = (bf16[256,384]{1,0:T(8,128)(2,1)S(1)}, bf16[256,384]{1,0:T(8,128)(2,1)S(1)}, u32[]{:S(2)}, u32[]{:S(2)}) collective-permute-start(bf16[256,384]{1,0:T(8,128)(2,1)S(1)} %get-tuple-element.198.own_ref), channel_id=1, source_target_pairs={{0,16},{4,20},{8,24},{12,28},{16,0},{20,4},{24,8},{28,12},{1,17},{... | collective-permute-start | bytes 589832 | tf_op jit(solution)/shard_map/ppermute | solution.py:471
  76.1 7.5 %forward_product.3 = (bf16[128,4096]{1,0:T(8,128)(2,1)S(1)}, bf16[64,4096]{1,0:T(8,128)(2,1)S(1)}, bf16[64,4096]{1,0:T(8,128)(2,1)S(1)}) custom-call(s32[3]{0:T(128)S(1)} %pad_add_fusion.where_ref, bf16[256,1536]{1,0:T(8,128)(2,1)S(1)} %join.6.refs_0_, bf16[256,1536]{1,0:T(8,128)(2,1)S(1)} %collective-permute-done.15.refs_1_, ...), custom_call_target="tpu_custom_call" | custom-call | flops 1024 | bytes 1024 | tf_op jit(solution)/shard_map/forward_product/pallas_call | solution.py:231
  83.7 1.4 collective-permute-start.25
  85.7 1.3 collective-permute-start.22
  87.0 1.0 hidden_grads.2.refs_0_
  88.0 6.5 %collective-permute-done.22.passed_ref = bf16[256,384]{1,0:T(8,128)(2,1)S(1)} collective-permute-done((bf16[256,384]{1,0:T(8,128)(2,1)S(1)}, bf16[256,384]{1,0:T(8,128)(2,1)S(1)}, u32[]{:S(2)}, u32[]{:S(2)}) %collective-permute-start.22) | collective-permute-done | bytes 196640 | tf_op jit(solution)/shard_map/ppermute | solution.py:476
  95.5 1.6 collective-permute-start.23
  97.8 7.4 %forward_streamed.3 = (bf16[128,2048]{1,0:T(8,128)(2,1)S(1)}, bf16[64,2048]{1,0:T(8,128)(2,1)S(1)}, bf16[64,2048]{1,0:T(8,128)(2,1)S(1)}) custom-call(s32[3]{0:T(128)S(1)} %pad_add_fusion.where_ref, f32[16,24]{1,0:T(8,128)S(1)} %copy-done, bf16[256,1536]{1,0:T(8,128)(2,1)S(1)} %join.7.refs_0_, bf16[256,1536]{1,0:T(8,128)(2,1)S(1)} %collective-permute-done.24.refs_1_, ...), custom_call_target="tpu_custom_call" | custom-call | flops 1024 | bytes 1024 | tf_op jit(solution)/shard_map/forward_streamed/pallas_call | solution.py:303
  105.2 4.7 %collective-permute-done.23.refs_1_ = bf16[64,4096]{1,0:T(8,128)(2,1)S(1)} collective-permute-done((bf16[64,4096]{1,0:T(8,128)(2,1)S(1)}, bf16[64,4096]{1,0:T(8,128)(2,1)S(1)}, u32[]{:S(2)}, u32[]{:S(2)}) %collective-permute-start.23) | collective-permute-done | bytes 524320 | tf_op jit(solution)/shard_map/ppermute | solution.py:465
  109.9 1.6 collective-permute-start.27
  111.8 1.9 %collective-permute-start.29 = (bf16[64,4096]{1,0:T(8,128)(2,1)S(1)}, bf16[64,4096]{1,0:T(8,128)(2,1)S(1)}, u32[]{:S(2)}, u32[]{:S(2)}) collective-permute-start(bf16[64,4096]{1,0:T(8,128)(2,1)S(1)} %add_convert_fusion), channel_id=1, source_target_pairs={{0,2},{1,3},{2,0},{3,1},{4,5},{5,4},{6,7},{7,6},{8,10},{9,11},{10,... | collective-permute-start | bytes 1572872 | tf_op jit(solution)/shard_map/ppermute | solution.py:465
  113.8 10.2 %collective-permute-done.27.refs_3_ = bf16[64,4096]{1,0:T(8,128)(2,1)S(1)} collective-permute-done((bf16[64,4096]{1,0:T(8,128)(2,1)S(1)}, bf16[64,4096]{1,0:T(8,128)(2,1)S(1)}, u32[]{:S(2)}, u32[]{:S(2)}) %collective-permute-start.27) | collective-permute-done | bytes 524320 | tf_op jit(solution)/shard_map/ppermute | solution.py:465
  124.0 2.5 %collective-permute-done.28.refs_4_ = bf16[128,2048]{1,0:T(8,128)(2,1)S(1)} collective-permute-done((bf16[128,2048]{1,0:T(8,128)(2,1)S(1)}, bf16[128,2048]{1,0:T(8,128)(2,1)S(1)}, u32[]{:S(2)}, u32[]{:S(2)}) %collective-permute-start.28) | collective-permute-done | bytes 524320 | tf_op jit(solution)/shard_map/ppermute | solution.py:465
  126.4 3.1 %collective-permute-done.29.refs_2_ = bf16[64,4096]{1,0:T(8,128)(2,1)S(1)} collective-permute-done((bf16[64,4096]{1,0:T(8,128)(2,1)S(1)}, bf16[64,4096]{1,0:T(8,128)(2,1)S(1)}, u32[]{:S(2)}, u32[]{:S(2)}) %collective-permute-start.29) | collective-permute-done | bytes 524320 | tf_op jit(solution)/shard_map/ppermute | solution.py:465
  130.0 7.4 %backward_product.4 = (bf16[256,1536]{1,0:T(8,128)(2,1)S(1)}, bf16[256,1536]{1,0:T(8,128)(2,1)S(1)}) custom-call(s32[3]{0:T(128)S(1)} %pad_add_fusion.where_ref, bf16[64,4096]{1,0:T(8,128)(2,1)S(1)} %hidden_grads.2.refs_0_, bf16[64,4096]{1,0:T(8,128)(2,1)S(1)} %collective-permute-done.23.refs_1_, bf16[64,4096]{1,0:T(8,128)(2,1)S(1)} %collective-permute-done.26.refs_2_, ...), custom_call_target="tpu_custom_call" | custom-call | flops 1024 | bytes 1024 | tf_op jit(solution)/shard_map/backward_product/pallas_call | solution.py:382
  138.5 1.4 collective-permute-start.31
  140.1 1.7 collective-permute-start.34
  141.8 10.3 %collective-permute-done.31.refs_1_ = bf16[64,4096]{1,0:T(8,128)(2,1)S(1)} collective-permute-done((bf16[64,4096]{1,0:T(8,128)(2,1)S(1)}, bf16[64,4096]{1,0:T(8,128)(2,1)S(1)}, u32[]{:S(2)}, u32[]{:S(2)}) %collective-permute-start.31) | collective-permute-done | bytes 524320 | tf_op jit(solution)/shard_map/ppermute | solution.py:465
  152.1 2.5 %collective-permute-start.35 = (bf16[64,4096]{1,0:T(8,128)(2,1)S(1)}, bf16[64,4096]{1,0:T(8,128)(2,1)S(1)}, u32[]{:S(2)}, u32[]{:S(2)}) collective-permute-start(bf16[64,4096]{1,0:T(8,128)(2,1)S(1)} %collective-permute-done.31.refs_1_), channel_id=1, source_target_pairs={{0,2},{1,3},{2,0},{3,1},{4,5},{5,4},{6,7},{7,6},{8,10},{9,11},{10,... | collective-permute-start | bytes 1572872 | tf_op jit(solution)/shard_map/ppermute | solution.py:465
  154.6 9.1 %collective-permute-done.36.refs_1_ = bf16[256,384]{1,0:T(8,128)(2,1)S(1)} collective-permute-done((bf16[256,384]{1,0:T(8,128)(2,1)S(1)}, bf16[256,384]{1,0:T(8,128)(2,1)S(1)}, u32[]{:S(2)}, u32[]{:S(2)}) %collective-permute-start.36) | collective-permute-done | bytes 196640 | tf_op jit(solution)/shard_map/ppermute | solution.py:471
  163.7 2.5 %backward_product.5 = (bf16[256,384]{1,0:T(8,128)(2,1)S(1)}, bf16[256,384]{1,0:T(8,128)(2,1)S(1)}) custom-call(s32[3]{0:T(128)S(1)} %pad_add_fusion.where_ref, bf16[64,4096]{1,0:T(8,128)(2,1)S(1)} %hidden_grads.3.refs_0_, bf16[64,4096]{1,0:T(8,128)(2,1)S(1)} %collective-permute-done.31.refs_1_, bf16[64,4096]{1,0:T(8,128)(2,1)S(1)} %collective-permute-done.34.refs_2_, ...), custom_call_target="tpu_custom_call" | custom-call | flops 1024 | bytes 1024 | tf_op jit(solution)/shard_map/backward_product/pallas_call | solution.py:382
  166.2 4.1 %backward_product.6 = (bf16[256,768]{1,0:T(8,128)(2,1)S(1)}, bf16[256,768]{1,0:T(8,128)(2,1)S(1)}) custom-call(s32[3]{0:T(128)S(1)} %pad_add_fusion.where_ref, bf16[64,4096]{1,0:T(8,128)(2,1)S(1)} %hidden_grads.3.refs_0_, bf16[64,4096]{1,0:T(8,128)(2,1)S(1)} %collective-permute-done.31.refs_1_, bf16[64,4096]{1,0:T(8,128)(2,1)S(1)} %collective-permute-done.34.refs_2_, ...), custom_call_target="tpu_custom_call" | custom-call | flops 1024 | bytes 1024 | tf_op jit(solution)/shard_map/backward_product/pallas_call | solution.py:382
  170.9 2.5 %backward_product.7 = (bf16[256,384]{1,0:T(8,128)(2,1)S(1)}, bf16[256,384]{1,0:T(8,128)(2,1)S(1)}) custom-call(s32[3]{0:T(128)S(1)} %pad_add_fusion.where_ref, bf16[64,4096]{1,0:T(8,128)(2,1)S(1)} %hidden_grads.3.refs_0_, bf16[64,4096]{1,0:T(8,128)(2,1)S(1)} %collective-permute-done.31.refs_1_, bf16[64,4096]{1,0:T(8,128)(2,1)S(1)} %collective-permute-done.34.refs_2_, ...), custom_call_target="tpu_custom_call" | custom-call | flops 1024 | bytes 1024 | tf_op jit(solution)/shard_map/backward_product/pallas_call | solution.py:382
  173.4 2.5 %collective-permute-start.40 = (bf16[256,384]{1,0:T(8,128)(2,1)S(1)}, bf16[256,384]{1,0:T(8,128)(2,1)S(1)}, u32[]{:S(2)}, u32[]{:S(2)}) collective-permute-start(bf16[256,384]{1,0:T(8,128)(2,1)S(1)} %pair_sums.4), channel_id=1, source_target_pairs={{0,16},{4,20},{8,24},{12,28},{16,0},{20,4},{24,8},{28,12},{1,17},{... | collective-permute-start | bytes 589832 | tf_op jit(solution)/shard_map/ppermute | solution.py:471
  176.0 3.7 %collective-permute-start.41 = (bf16[256,384]{1,0:T(8,128)(2,1)S(1)}, bf16[256,384]{1,0:T(8,128)(2,1)S(1)}, u32[]{:S(2)}, u32[]{:S(2)}) collective-permute-start(bf16[256,384]{1,0:T(8,128)(2,1)S(1)} %get-tuple-element.289), channel_id=1, source_target_pairs={{0,8},{4,12},{8,16},{12,20},{16,24},{20,28},{24,0},{28,4},{1,9},{5... | collective-permute-start | bytes 589832 | tf_op jit(solution)/shard_map/ppermute | solution.py:471
  180.6 10.0 %collective-permute-done.40.refs_1_ = bf16[256,384]{1,0:T(8,128)(2,1)S(1)} collective-permute-done((bf16[256,384]{1,0:T(8,128)(2,1)S(1)}, bf16[256,384]{1,0:T(8,128)(2,1)S(1)}, u32[]{:S(2)}, u32[]{:S(2)}) %collective-permute-start.40) | collective-permute-done | bytes 196640 | tf_op jit(solution)/shard_map/ppermute | solution.py:471
  191.5 1.4 final_sum.3
  (73 shorter events, 13.8 us)
Async XLA Ops:
  1.9 14.1 %collective-permute-start = (bf16[256,384]{1,0:T(8,128)(2,1)S(1)}, bf16[256,384]{1,0:T(8,128)(2,1)S(1)}, u32[]{:S(2)}, u32[]{:S(2)}) collective-permute-start(bf16[256,384]{1,0:T(8,128)(2,1)S(1)} %get-tuple-element.149.own_ref), channel_id=1, source_target_pairs={{0,16},{4,20},{8,24},{12,28},{16,0},{20,4},{24,8},{28,12},{1,17},{... | collective-permute-start | bytes 589832 | tf_op jit(solution)/shard_map/ppermute | solution.py:471
  6.0 10.0 %collective-permute-start.1 = (bf16[256,384]{1,0:T(8,128)(2,1)S(1)}, bf16[256,384]{1,0:T(8,128)(2,1)S(1)}, u32[]{:S(2)}, u32[]{:S(2)}) collective-permute-start(bf16[256,384]{1,0:T(8,128)(2,1)S(1)} %get-tuple-element.149.own_ref), channel_id=1, source_target_pairs={{0,8},{4,12},{8,0},{12,4},{16,24},{20,28},{24,16},{28,20},{1,9},{5... | collective-permute-start | bytes 589832 | tf_op jit(solution)/shard_map/ppermute | solution.py:476
  7.6 20.3 %collective-permute-start.2 = (bf16[256,384]{1,0:T(8,128)(2,1)S(1)}, bf16[256,384]{1,0:T(8,128)(2,1)S(1)}, u32[]{:S(2)}, u32[]{:S(2)}) collective-permute-start(bf16[256,384]{1,0:T(8,128)(2,1)S(1)} %get-tuple-element.149.own_ref), channel_id=1, source_target_pairs={{8,16},{12,20},{16,8},{20,12},{9,17},{13,21},{17,9},{21,13},{10,18... | collective-permute-start | bytes 589832 | tf_op jit(solution)/shard_map/ppermute | solution.py:476
  8.2 0.7 copy-start.1
  8.9 12.4 %copy-start.2 = (f32[24,16]{0,1:T(8,128)S(1)}, f32[24,16]{0,1:T(8,128)}, u32[]{:S(2)}) copy-start(f32[24,16]{0,1:T(8,128)} %param.13) | copy-start | bytes 4612
  16.0 11.9 %collective-permute-start.3 = (bf16[256,384]{1,0:T(8,128)(2,1)S(1)}, bf16[256,384]{1,0:T(8,128)(2,1)S(1)}, u32[]{:S(2)}, u32[]{:S(2)}) collective-permute-start(bf16[256,384]{1,0:T(8,128)(2,1)S(1)} %collective-permute-done.two_ref), channel_id=1, source_target_pairs={{8,0},{12,4},{16,24},{20,28},{9,1},{13,5},{17,25},{21,29},{10,2},{... | collective-permute-start | bytes 589832 | tf_op jit(solution)/shard_map/ppermute | solution.py:476
  17.3 12.7 %collective-permute-start.4 = (bf16[256,384]{1,0:T(8,128)(2,1)S(1)}, bf16[256,384]{1,0:T(8,128)(2,1)S(1)}, u32[]{:S(2)}, u32[]{:S(2)}) collective-permute-start(bf16[256,384]{1,0:T(8,128)(2,1)S(1)} %get-tuple-element.153.own_ref), channel_id=1, source_target_pairs={{0,16},{4,20},{8,24},{12,28},{16,0},{20,4},{24,8},{28,12},{1,17},{... | collective-permute-start | bytes 589832 | tf_op jit(solution)/shard_map/ppermute | solution.py:471
  21.3 10.7 %collective-permute-start.5 = (bf16[256,384]{1,0:T(8,128)(2,1)S(1)}, bf16[256,384]{1,0:T(8,128)(2,1)S(1)}, u32[]{:S(2)}, u32[]{:S(2)}) collective-permute-start(bf16[256,384]{1,0:T(8,128)(2,1)S(1)} %get-tuple-element.153.own_ref), channel_id=1, source_target_pairs={{0,8},{4,12},{8,0},{12,4},{16,24},{20,28},{24,16},{28,20},{1,9},{5... | collective-permute-start | bytes 589832 | tf_op jit(solution)/shard_map/ppermute | solution.py:476
  32.6 17.6 %copy-start = (f32[16,24]{1,0:T(8,128)S(1)}, f32[16,24]{1,0:T(8,128)}, u32[]{:S(2)}) copy-start(f32[16,24]{1,0:T(8,128)} %scale_ref.3) | copy-start | bytes 4612
  32.6 2.4 %collective-permute-start.6 = (bf16[256,1536]{1,0:T(8,128)(2,1)S(1)}, bf16[256,1536]{1,0:T(8,128)(2,1)S(1)}, u32[]{:S(2)}, u32[]{:S(2)}) collective-permute-start(bf16[256,1536]{1,0:T(8,128)(2,1)S(1)} %join.4.refs_0_), channel_id=1, source_target_pairs={{0,4},{4,0},{8,12},{12,8},{16,20},{20,16},{24,28},{28,24},{1,5},{5... | collective-permute-start | bytes 2359304 | tf_op jit(solution)/shard_map/ppermute | solution.py:468
  32.7 9.8 %collective-permute-start.7 = (bf16[256,384]{1,0:T(8,128)(2,1)S(1)}, bf16[256,384]{1,0:T(8,128)(2,1)S(1)}, u32[]{:S(2)}, u32[]{:S(2)}) collective-permute-start(bf16[256,384]{1,0:T(8,128)(2,1)S(1)} %get-tuple-element.153.own_ref), channel_id=1, source_target_pairs={{8,16},{12,20},{16,8},{20,12},{9,17},{13,21},{17,9},{21,13},{10,18... | collective-permute-start | bytes 589832 | tf_op jit(solution)/shard_map/ppermute | solution.py:476
  33.4 10.2 %collective-permute-start.8 = (bf16[256,384]{1,0:T(8,128)(2,1)S(1)}, bf16[256,384]{1,0:T(8,128)(2,1)S(1)}, u32[]{:S(2)}, u32[]{:S(2)}) collective-permute-start(bf16[256,384]{1,0:T(8,128)(2,1)S(1)} %collective-permute-done.4.two_ref), channel_id=1, source_target_pairs={{8,0},{12,4},{16,24},{20,28},{9,1},{13,5},{17,25},{21,29},{10,2},{... | collective-permute-start | bytes 589832 | tf_op jit(solution)/shard_map/ppermute | solution.py:476
  43.6 16.2 %collective-permute-start.10 = (bf16[128,4096]{1,0:T(8,128)(2,1)S(1)}, bf16[128,4096]{1,0:T(8,128)(2,1)S(1)}, u32[]{:S(2)}, u32[]{:S(2)}) collective-permute-start(bf16[128,4096]{1,0:T(8,128)(2,1)S(1)} %get-tuple-element.176), channel_id=1, source_target_pairs={{0,1},{1,0},{2,3},{3,2},{4,6},{5,7},{6,4},{7,5},{8,9},{9,8},{10,11... | collective-permute-start | bytes 3145736 | tf_op jit(solution)/shard_map/ppermute | solution.py:465
  45.7 4.5 %collective-permute-start.9 = (bf16[256,1536]{1,0:T(8,128)(2,1)S(1)}, bf16[256,1536]{1,0:T(8,128)(2,1)S(1)}, u32[]{:S(2)}, u32[]{:S(2)}) collective-permute-start(bf16[256,1536]{1,0:T(8,128)(2,1)S(1)} %join.5.refs_0_), channel_id=1, source_target_pairs={{0,4},{4,0},{8,12},{12,8},{16,20},{20,16},{24,28},{28,24},{1,5},{5... | collective-permute-start | bytes 2359304 | tf_op jit(solution)/shard_map/ppermute | solution.py:468
  45.8 13.7 %collective-permute-start.11 = (bf16[256,384]{1,0:T(8,128)(2,1)S(1)}, bf16[256,384]{1,0:T(8,128)(2,1)S(1)}, u32[]{:S(2)}, u32[]{:S(2)}) collective-permute-start(bf16[256,384]{1,0:T(8,128)(2,1)S(1)} %get-tuple-element.179.own_ref), channel_id=1, source_target_pairs={{0,16},{4,20},{8,24},{12,28},{16,0},{20,4},{24,8},{28,12},{1,17},{... | collective-permute-start | bytes 589832 | tf_op jit(solution)/shard_map/ppermute | solution.py:471
  49.6 10.3 %collective-permute-start.12 = (bf16[256,384]{1,0:T(8,128)(2,1)S(1)}, bf16[256,384]{1,0:T(8,128)(2,1)S(1)}, u32[]{:S(2)}, u32[]{:S(2)}) collective-permute-start(bf16[256,384]{1,0:T(8,128)(2,1)S(1)} %get-tuple-element.179.own_ref), channel_id=1, source_target_pairs={{0,8},{4,12},{8,0},{12,4},{16,24},{20,28},{24,16},{28,20},{1,9},{5... | collective-permute-start | bytes 589832 | tf_op jit(solution)/shard_map/ppermute | solution.py:476
  49.6 12.7 %collective-permute-start.13 = (bf16[256,384]{1,0:T(8,128)(2,1)S(1)}, bf16[256,384]{1,0:T(8,128)(2,1)S(1)}, u32[]{:S(2)}, u32[]{:S(2)}) collective-permute-start(bf16[256,384]{1,0:T(8,128)(2,1)S(1)} %get-tuple-element.179.own_ref), channel_id=1, source_target_pairs={{8,16},{12,20},{16,8},{20,12},{9,17},{13,21},{17,9},{21,13},{10,18... | collective-permute-start | bytes 589832 | tf_op jit(solution)/shard_map/ppermute | solution.py:476
  59.9 8.0 %collective-permute-start.14 = (bf16[256,384]{1,0:T(8,128)(2,1)S(1)}, bf16[256,384]{1,0:T(8,128)(2,1)S(1)}, u32[]{:S(2)}, u32[]{:S(2)}) collective-permute-start(bf16[256,384]{1,0:T(8,128)(2,1)S(1)} %collective-permute-done.11.two_ref), channel_id=1, source_target_pairs={{8,0},{12,4},{16,24},{20,28},{9,1},{13,5},{17,25},{21,29},{10,2},{... | collective-permute-start | bytes 589832 | tf_op jit(solution)/shard_map/ppermute | solution.py:476
  61.2 9.3 %collective-permute-start.16 = (bf16[128,2048]{1,0:T(8,128)(2,1)S(1)}, bf16[128,2048]{1,0:T(8,128)(2,1)S(1)}, u32[]{:S(2)}, u32[]{:S(2)}) collective-permute-start(bf16[128,2048]{1,0:T(8,128)(2,1)S(1)} %get-tuple-element.189), channel_id=1, source_target_pairs={{0,1},{1,0},{2,3},{3,2},{4,6},{5,7},{6,4},{7,5},{8,9},{9,8},{10,11... | collective-permute-start | bytes 1572872 | tf_op jit(solution)/shard_map/ppermute | solution.py:465
  68.7 2.4 %collective-permute-start.15 = (bf16[256,1536]{1,0:T(8,128)(2,1)S(1)}, bf16[256,1536]{1,0:T(8,128)(2,1)S(1)}, u32[]{:S(2)}, u32[]{:S(2)}) collective-permute-start(bf16[256,1536]{1,0:T(8,128)(2,1)S(1)} %join.6.refs_0_), channel_id=1, source_target_pairs={{0,4},{4,0},{8,12},{12,8},{16,20},{20,16},{24,28},{28,24},{1,5},{5... | collective-permute-start | bytes 2359304 | tf_op jit(solution)/shard_map/ppermute | solution.py:468
  68.9 14.7 %collective-permute-start.19 = (bf16[64,4096]{1,0:T(8,128)(2,1)S(1)}, bf16[64,4096]{1,0:T(8,128)(2,1)S(1)}, u32[]{:S(2)}, u32[]{:S(2)}) collective-permute-start(bf16[64,4096]{1,0:T(8,128)(2,1)S(1)} %add_convert_fusion.1), channel_id=1, source_target_pairs={{0,2},{1,3},{2,0},{3,1},{4,5},{5,4},{6,7},{7,6},{8,10},{9,11},{10,... | collective-permute-start | bytes 1572872 | tf_op jit(solution)/shard_map/ppermute | solution.py:465
  71.1 12.6 %collective-permute-start.20 = (bf16[64,2048]{1,0:T(8,128)(2,1)S(1)}, bf16[64,2048]{1,0:T(8,128)(2,1)S(1)}, u32[]{:S(2)}, u32[]{:S(2)}) collective-permute-start(bf16[64,2048]{1,0:T(8,128)(2,1)S(1)} %add_convert_fusion.3), channel_id=1, source_target_pairs={{0,2},{1,3},{2,0},{3,1},{4,5},{5,4},{6,7},{7,6},{8,10},{9,11},{10,... | collective-permute-start | bytes 786440 | tf_op jit(solution)/shard_map/ppermute | solution.py:465
  72.7 10.9 %collective-permute-start.17 = (bf16[256,384]{1,0:T(8,128)(2,1)S(1)}, bf16[256,384]{1,0:T(8,128)(2,1)S(1)}, u32[]{:S(2)}, u32[]{:S(2)}) collective-permute-start(bf16[256,384]{1,0:T(8,128)(2,1)S(1)} %get-tuple-element.198.own_ref), channel_id=1, source_target_pairs={{0,16},{4,20},{8,24},{12,28},{16,0},{20,4},{24,8},{28,12},{1,17},{... | collective-permute-start | bytes 589832 | tf_op jit(solution)/shard_map/ppermute | solution.py:471
  75.9 7.8 %collective-permute-start.18 = (bf16[256,384]{1,0:T(8,128)(2,1)S(1)}, bf16[256,384]{1,0:T(8,128)(2,1)S(1)}, u32[]{:S(2)}, u32[]{:S(2)}) collective-permute-start(bf16[256,384]{1,0:T(8,128)(2,1)S(1)} %get-tuple-element.198.own_ref), channel_id=1, source_target_pairs={{0,8},{4,12},{8,0},{12,4},{16,24},{20,28},{24,16},{28,20},{1,9},{5... | collective-permute-start | bytes 589832 | tf_op jit(solution)/shard_map/ppermute | solution.py:476
  83.7 21.5 %collective-permute-start.25 = (bf16[128,4096]{1,0:T(8,128)(2,1)S(1)}, bf16[128,4096]{1,0:T(8,128)(2,1)S(1)}, u32[]{:S(2)}, u32[]{:S(2)}) collective-permute-start(bf16[128,4096]{1,0:T(8,128)(2,1)S(1)} %get-tuple-element.226), channel_id=1, source_target_pairs={{0,1},{1,0},{2,3},{3,2},{4,6},{5,7},{6,4},{7,5},{8,9},{9,8},{10,11... | collective-permute-start | bytes 3145736 | tf_op jit(solution)/shard_map/ppermute | solution.py:465
  85.0 3.0 %collective-permute-start.21 = (bf16[256,384]{1,0:T(8,128)(2,1)S(1)}, bf16[256,384]{1,0:T(8,128)(2,1)S(1)}, u32[]{:S(2)}, u32[]{:S(2)}) collective-permute-start(bf16[256,384]{1,0:T(8,128)(2,1)S(1)} %get-tuple-element.198.own_ref), channel_id=1, source_target_pairs={{8,16},{12,20},{16,8},{20,12},{9,17},{13,21},{17,9},{21,13},{10,18... | collective-permute-start | bytes 589832 | tf_op jit(solution)/shard_map/ppermute | solution.py:476
  85.7 8.9 %collective-permute-start.22 = (bf16[256,384]{1,0:T(8,128)(2,1)S(1)}, bf16[256,384]{1,0:T(8,128)(2,1)S(1)}, u32[]{:S(2)}, u32[]{:S(2)}) collective-permute-start(bf16[256,384]{1,0:T(8,128)(2,1)S(1)} %collective-permute-done.17.two_ref), channel_id=1, source_target_pairs={{8,0},{12,4},{16,24},{20,28},{9,1},{13,5},{17,25},{21,29},{10,2},{... | collective-permute-start | bytes 589832 | tf_op jit(solution)/shard_map/ppermute | solution.py:476
  95.4 2.4 %collective-permute-start.24 = (bf16[256,1536]{1,0:T(8,128)(2,1)S(1)}, bf16[256,1536]{1,0:T(8,128)(2,1)S(1)}, u32[]{:S(2)}, u32[]{:S(2)}) collective-permute-start(bf16[256,1536]{1,0:T(8,128)(2,1)S(1)} %join.7.refs_0_), channel_id=1, source_target_pairs={{0,4},{4,0},{8,12},{12,8},{16,20},{20,16},{24,28},{28,24},{1,5},{5... | collective-permute-start | bytes 2359304 | tf_op jit(solution)/shard_map/ppermute | solution.py:468
  95.5 14.4 %collective-permute-start.23 = (bf16[64,4096]{1,0:T(8,128)(2,1)S(1)}, bf16[64,4096]{1,0:T(8,128)(2,1)S(1)}, u32[]{:S(2)}, u32[]{:S(2)}) collective-permute-start(bf16[64,4096]{1,0:T(8,128)(2,1)S(1)} %hidden_grads.2.refs_0_), channel_id=1, source_target_pairs={{0,1},{1,0},{2,3},{3,2},{4,6},{5,7},{6,4},{7,5},{8,9},{9,8},{10,11... | collective-permute-start | bytes 1572872 | tf_op jit(solution)/shard_map/ppermute | solution.py:465
  97.1 16.7 %collective-permute-start.26 = (bf16[64,4096]{1,0:T(8,128)(2,1)S(1)}, bf16[64,4096]{1,0:T(8,128)(2,1)S(1)}, u32[]{:S(2)}, u32[]{:S(2)}) collective-permute-start(bf16[64,4096]{1,0:T(8,128)(2,1)S(1)} %hidden_grads.2.refs_0_), channel_id=1, source_target_pairs={{0,2},{1,3},{2,0},{3,1},{4,5},{5,4},{6,7},{7,6},{8,10},{9,11},{10,... | collective-permute-start | bytes 1572872 | tf_op jit(solution)/shard_map/ppermute | solution.py:465
  109.9 14.0 %collective-permute-start.27 = (bf16[64,4096]{1,0:T(8,128)(2,1)S(1)}, bf16[64,4096]{1,0:T(8,128)(2,1)S(1)}, u32[]{:S(2)}, u32[]{:S(2)}) collective-permute-start(bf16[64,4096]{1,0:T(8,128)(2,1)S(1)} %collective-permute-done.23.refs_1_), channel_id=1, source_target_pairs={{0,2},{1,3},{2,0},{3,1},{4,5},{5,4},{6,7},{7,6},{8,10},{9,11},{10,... | collective-permute-start | bytes 1572872 | tf_op jit(solution)/shard_map/ppermute | solution.py:465
  111.6 14.9 %collective-permute-start.28 = (bf16[128,2048]{1,0:T(8,128)(2,1)S(1)}, bf16[128,2048]{1,0:T(8,128)(2,1)S(1)}, u32[]{:S(2)}, u32[]{:S(2)}) collective-permute-start(bf16[128,2048]{1,0:T(8,128)(2,1)S(1)} %get-tuple-element.232), channel_id=1, source_target_pairs={{0,1},{1,0},{2,3},{3,2},{4,6},{5,7},{6,4},{7,5},{8,9},{9,8},{10,11... | collective-permute-start | bytes 1572872 | tf_op jit(solution)/shard_map/ppermute | solution.py:465
  111.8 17.7 %collective-permute-start.29 = (bf16[64,4096]{1,0:T(8,128)(2,1)S(1)}, bf16[64,4096]{1,0:T(8,128)(2,1)S(1)}, u32[]{:S(2)}, u32[]{:S(2)}) collective-permute-start(bf16[64,4096]{1,0:T(8,128)(2,1)S(1)} %add_convert_fusion), channel_id=1, source_target_pairs={{0,2},{1,3},{2,0},{3,1},{4,5},{5,4},{6,7},{7,6},{8,10},{9,11},{10,... | collective-permute-start | bytes 1572872 | tf_op jit(solution)/shard_map/ppermute | solution.py:465
  129.6 7.8 %collective-permute-start.30 = (bf16[64,2048]{1,0:T(8,128)(2,1)S(1)}, bf16[64,2048]{1,0:T(8,128)(2,1)S(1)}, u32[]{:S(2)}, u32[]{:S(2)}) collective-permute-start(bf16[64,2048]{1,0:T(8,128)(2,1)S(1)} %add_convert_fusion.2), channel_id=1, source_target_pairs={{0,2},{1,3},{2,0},{3,1},{4,5},{5,4},{6,7},{7,6},{8,10},{9,11},{10,... | collective-permute-start | bytes 786440 | tf_op jit(solution)/shard_map/ppermute | solution.py:465
  137.4 2.5 %collective-permute-start.32 = (bf16[256,1536]{1,0:T(8,128)(2,1)S(1)}, bf16[256,1536]{1,0:T(8,128)(2,1)S(1)}, u32[]{:S(2)}, u32[]{:S(2)}) collective-permute-start(bf16[256,1536]{1,0:T(8,128)(2,1)S(1)} %get-tuple-element.257), channel_id=1, source_target_pairs={{0,4},{4,0},{8,12},{12,8},{16,20},{20,16},{24,28},{28,24},{1,5},{5... | collective-permute-start | bytes 2359304 | tf_op jit(solution)/shard_map/ppermute | solution.py:468
  138.5 13.6 %collective-permute-start.31 = (bf16[64,4096]{1,0:T(8,128)(2,1)S(1)}, bf16[64,4096]{1,0:T(8,128)(2,1)S(1)}, u32[]{:S(2)}, u32[]{:S(2)}) collective-permute-start(bf16[64,4096]{1,0:T(8,128)(2,1)S(1)} %hidden_grads.3.refs_0_), channel_id=1, source_target_pairs={{0,1},{1,0},{2,3},{3,2},{4,6},{5,7},{6,4},{7,5},{8,9},{9,8},{10,11... | collective-permute-start | bytes 1572872 | tf_op jit(solution)/shard_map/ppermute | solution.py:465
  140.0 12.0 %collective-permute-start.33 = (bf16[256,384]{1,0:T(8,128)(2,1)S(1)}, bf16[256,384]{1,0:T(8,128)(2,1)S(1)}, u32[]{:S(2)}, u32[]{:S(2)}) collective-permute-start(bf16[256,384]{1,0:T(8,128)(2,1)S(1)} %get-tuple-element.258), channel_id=1, source_target_pairs={{0,8},{4,12},{8,16},{12,20},{16,24},{20,28},{24,0},{28,4},{1,9},{5... | collective-permute-start | bytes 589832 | tf_op jit(solution)/shard_map/ppermute | solution.py:471
  140.1 14.5 %collective-permute-start.34 = (bf16[64,4096]{1,0:T(8,128)(2,1)S(1)}, bf16[64,4096]{1,0:T(8,128)(2,1)S(1)}, u32[]{:S(2)}, u32[]{:S(2)}) collective-permute-start(bf16[64,4096]{1,0:T(8,128)(2,1)S(1)} %hidden_grads.3.refs_0_), channel_id=1, source_target_pairs={{0,2},{1,3},{2,0},{3,1},{4,5},{5,4},{6,7},{7,6},{8,10},{9,11},{10,... | collective-permute-start | bytes 1572872 | tf_op jit(solution)/shard_map/ppermute | solution.py:465
  152.1 11.6 %collective-permute-start.35 = (bf16[64,4096]{1,0:T(8,128)(2,1)S(1)}, bf16[64,4096]{1,0:T(8,128)(2,1)S(1)}, u32[]{:S(2)}, u32[]{:S(2)}) collective-permute-start(bf16[64,4096]{1,0:T(8,128)(2,1)S(1)} %collective-permute-done.31.refs_1_), channel_id=1, source_target_pairs={{0,2},{1,3},{2,0},{3,1},{4,5},{5,4},{6,7},{7,6},{8,10},{9,11},{10,... | collective-permute-start | bytes 1572872 | tf_op jit(solution)/shard_map/ppermute | solution.py:465
  154.5 9.1 %collective-permute-start.36 = (bf16[256,384]{1,0:T(8,128)(2,1)S(1)}, bf16[256,384]{1,0:T(8,128)(2,1)S(1)}, u32[]{:S(2)}, u32[]{:S(2)}) collective-permute-start(bf16[256,384]{1,0:T(8,128)(2,1)S(1)} %get-tuple-element.262), channel_id=1, source_target_pairs={{0,16},{4,20},{8,24},{12,28},{16,0},{20,4},{24,8},{28,12},{1,17},{... | collective-permute-start | bytes 589832 | tf_op jit(solution)/shard_map/ppermute | solution.py:471
  154.5 9.1 %collective-permute-start.37 = (bf16[256,384]{1,0:T(8,128)(2,1)S(1)}, bf16[256,384]{1,0:T(8,128)(2,1)S(1)}, u32[]{:S(2)}, u32[]{:S(2)}) collective-permute-start(bf16[256,384]{1,0:T(8,128)(2,1)S(1)} %get-tuple-element.263), channel_id=1, source_target_pairs={{0,24},{4,28},{8,0},{12,4},{16,8},{20,12},{24,16},{28,20},{1,25},{... | collective-permute-start | bytes 589832 | tf_op jit(solution)/shard_map/ppermute | solution.py:471
  166.1 4.2 %collective-permute-start.38 = (bf16[256,384]{1,0:T(8,128)(2,1)S(1)}, bf16[256,384]{1,0:T(8,128)(2,1)S(1)}, u32[]{:S(2)}, u32[]{:S(2)}) collective-permute-start(bf16[256,384]{1,0:T(8,128)(2,1)S(1)} %get-tuple-element.271), channel_id=1, source_target_pairs={{0,4},{4,0},{8,12},{12,8},{16,20},{20,16},{24,28},{28,24},{1,5},{5... | collective-permute-start | bytes 589832 | tf_op jit(solution)/shard_map/ppermute | solution.py:468
  170.4 5.6 %collective-permute-start.39 = (bf16[256,768]{1,0:T(8,128)(2,1)S(1)}, bf16[256,768]{1,0:T(8,128)(2,1)S(1)}, u32[]{:S(2)}, u32[]{:S(2)}) collective-permute-start(bf16[256,768]{1,0:T(8,128)(2,1)S(1)} %get-tuple-element.275), channel_id=1, source_target_pairs={{0,4},{4,0},{8,12},{12,8},{16,20},{20,16},{24,28},{28,24},{1,5},{5... | collective-permute-start | bytes 1179656 | tf_op jit(solution)/shard_map/ppermute | solution.py:468
  173.4 17.2 %collective-permute-start.40 = (bf16[256,384]{1,0:T(8,128)(2,1)S(1)}, bf16[256,384]{1,0:T(8,128)(2,1)S(1)}, u32[]{:S(2)}, u32[]{:S(2)}) collective-permute-start(bf16[256,384]{1,0:T(8,128)(2,1)S(1)} %pair_sums.4), channel_id=1, source_target_pairs={{0,16},{4,20},{8,24},{12,28},{16,0},{20,4},{24,8},{28,12},{1,17},{... | collective-permute-start | bytes 589832 | tf_op jit(solution)/shard_map/ppermute | solution.py:471
  176.0 14.6 %collective-permute-start.41 = (bf16[256,384]{1,0:T(8,128)(2,1)S(1)}, bf16[256,384]{1,0:T(8,128)(2,1)S(1)}, u32[]{:S(2)}, u32[]{:S(2)}) collective-permute-start(bf16[256,384]{1,0:T(8,128)(2,1)S(1)} %get-tuple-element.289), channel_id=1, source_target_pairs={{0,8},{4,12},{8,16},{12,20},{16,24},{20,28},{24,0},{28,4},{1,9},{5... | collective-permute-start | bytes 589832 | tf_op jit(solution)/shard_map/ppermute | solution.py:471
  179.8 11.7 %collective-permute-start.42 = (bf16[256,384]{1,0:T(8,128)(2,1)S(1)}, bf16[256,384]{1,0:T(8,128)(2,1)S(1)}, u32[]{:S(2)}, u32[]{:S(2)}) collective-permute-start(bf16[256,384]{1,0:T(8,128)(2,1)S(1)} %get-tuple-element.290), channel_id=1, source_target_pairs={{0,24},{4,28},{8,0},{12,4},{16,8},{20,12},{24,16},{28,20},{1,25},{... | collective-permute-start | bytes 589832 | tf_op jit(solution)/shard_map/ppermute | solution.py:471
  179.9 11.5 %collective-permute-start.43 = (bf16[256,384]{1,0:T(8,128)(2,1)S(1)}, bf16[256,384]{1,0:T(8,128)(2,1)S(1)}, u32[]{:S(2)}, u32[]{:S(2)}) collective-permute-start(bf16[256,384]{1,0:T(8,128)(2,1)S(1)} %get-tuple-element.292), channel_id=1, source_target_pairs={{0,4},{4,0},{8,12},{12,8},{16,20},{20,16},{24,28},{28,24},{1,5},{5... | collective-permute-start | bytes 589832 | tf_op jit(solution)/shard_map/ppermute | solution.py:468

commit v3 on v2

--- a/solution.py
+++ b/solution.py
@@ -540,7 +540,7 @@
                 have[q | 1 << step] = exchange(have[q], step) if q else late[1 << step]
         return [have[q] for q in range(n_dp)]
 
-    whole = [[*range(1, n_z), 0]]
+    whole = [[2, 1, 3, 0] if hops else [*range(1, n_z), 0]]
     parts_of_z = [[2], [1, 3], [0]] if hops else whole
 
     def products(grad_parts, places):
@@ -551,15 +551,18 @@
     def swapped(partial):
         return [partial[0], swap_cores(partial[1])] if by_blocks else partial
 
-    def scatter(partial, places):
+    def sums_of(partial, places):
+        away = [j for j in places if j]
+        return pair_sums(*partial, len(away), width) if by_blocks and away else []
+
+    def spread(sums, partial, places):
         if not by_blocks:
             return [lax.psum_scatter(partial[0], "tp", scatter_dimension=1, tiled=True)]
-        away = [j for j in places if j]
-        if not away:
-            return list(partial)
-        sums = pair_sums(*partial, len(away), width)
-        terms = [along(part, j) for j, part in zip(away, sums)]
+        terms = [along(part, j) for j, part in zip([j for j in places if j], sums)]
         return terms + (list(partial) if 0 in places else [])
+
+    def scatter(partial, places):
+        return spread(sums_of(partial, places), partial, places)
 
     rows = inputs.shape[0] // CHUNKS // n_dp
 
@@ -613,15 +616,15 @@
     hidden_2, gate_up_2 = hold((hidden_2, gate_up_2))
 
     hidden_2 = send(hidden_2)
+    early_1 = hold(early_1)
+
+    parts_1 = finish_rows(early_1, late_1)
+    parts_1, hidden_2 = hold((parts_1, hidden_2))
+
+    hidden_2 = settle(hidden_2)
     gate_up_2 = settle(gate_up_2)
-    early_1 = hold(early_1)
-
-    parts_1 = finish_rows(early_1, late_1)
-    parts_1, hidden_2, gate_up_2 = hold((parts_1, hidden_2, gate_up_2))
-
-    hidden_2 = settle(hidden_2)
     partial_1 = products(parts_1, whole[0])
-    hidden_2, partial_1 = hold((hidden_2, partial_1))
+    hidden_2, gate_up_2, partial_1 = hold((hidden_2, gate_up_2, partial_1))
 
     partial_1 = swapped(partial_1)
     grad_2 = grads(where, terms_of(gate_up_2), terms_of(hidden_2), rows, hidden)
@@ -629,16 +632,20 @@
     terms_1 = scatter(partial_1, whole[0])
     early_2, early = hold((early_2, terms_1[:1]))
     parts_2 = finish_rows(early_2, late_2)
-    parts_2, terms_1 = hold((parts_2, [*early, *terms_1[1:]]))
+    parts_2, later = hold((parts_2, terms_1[1:2]))
+    terms_1 = [*early, *later, *terms_1[2:]]
 
     terms_2 = []
     partial, before = products(parts_2, parts_of_z[0]), parts_of_z[0]
     for places in parts_of_z[1:]:
-        following = products(parts_2, places)
-        partial, following = hold((swapped(partial), following))
-        terms_2 += scatter(partial, before)
-        partial, before = following, places
-    terms_2 += scatter(swapped(partial), before)
+        following = products(parts_2, places) if len(places) > 1 else None
+        partial, following, terms_1 = hold((swapped(partial), following, terms_1))
+        sums = hold(sums_of(partial, before))
+        terms_2 += spread(sums, partial, before)
+        partial = following or products(parts_2, places)
+        before = places
+    partial = swapped(partial)
+    terms_2 += spread(sums_of(partial, before), partial, before)
     done = [final_sum(where, [], terms_1, n_dp, width)]
     return final_sum(where, done, terms_2, n_dp, width)
 

time: 194 us -> 189 us (0.974)
  waiting for transfers between devices: 71.7 us -> 61.4 us
  starting transfers between devices: 50.9 us -> 55.7 us
    ppermute x14, waiting for transfers between devices: 30.8 us -> 22 us  [exchange(): return lax.ppermute(value, ('tp', 'dp'), pairs)]
    ppermute x10, starting transfers between devices: 21.5 us -> 28.6 us  [along(): lax.ppermute(value, 'tp', [(i, (i + places * CORES) % n_tp) for i in rang...]
    ppermute x14, starting transfers between devices: 18.8 us -> 16.4 us  [exchange(): return lax.ppermute(value, ('tp', 'dp'), pairs)]
  transfers between devices with their start and end apart: 44 -> 44, of which waited for: 19 -> 19; matrix products, arithmetic and copies ran while one was open for 0% -> 0% of each run, Pallas kernels for 32% -> 35%
where the time goes in v3:
time: 189 us; the launch traced here: 187 us
  Pallas kernels  68.6 us (36%)
  waiting for transfers between devices  61.4 us (32%)
  starting transfers between devices  55.7 us (29%)
    ppermute x10, starting transfers between devices, along(): lax.ppermute(value, 'tp', [(i, (i + places * CORES) % n_tp) for i in rang...  28.6 us
    ppermute x10, waiting for transfers between devices, along(): lax.ppermute(value, 'tp', [(i, (i + places * CORES) % n_tp) for i in rang...  22.9 us
    ppermute x14, waiting for transfers between devices, exchange(): return lax.ppermute(value, ('tp', 'dp'), pairs)  22 us
    pallas_call x4, Pallas kernels, backward(): pl.pallas_call(functools.partial(backward_kernel, places, total_places),...  16.4 us
    ppermute x14, starting transfers between devices, exchange(): return lax.ppermute(value, ('tp', 'dp'), pairs)  16.4 us
    ppermute x12, waiting for transfers between devices, between(): lax.ppermute(value, 'tp', [(i * CORES + c, k * CORES + c) for i, k in pai...  15.6 us
    pallas_call x2, Pallas kernels, forward(): pl.pallas_call(functools.partial(forward_kernel, groups, contract, width,...  15 us
    pallas_call x2, Pallas kernels, forward_streamed(): pl.pallas_call(functools.partial(streamed_kernel, groups, width), in_spec...  14.8 us
  transfers between devices with their start and end apart: 44, of which 19 were waited for; matrix products, arithmetic and copies ran while one was open for 0% of the time, Pallas kernels for 35%

profile of v3, /device:TPU:0, one launch (start us, length us, event | category | flops | bytes accessed | tf_op | source)
XLA Modules:
  0.0 187.3 jit_solution(11732071696309415338)
XLA Ops:
  0.1 1.8 order_rows.1
  1.9 4.1 %collective-permute-start = (bf16[256,384]{1,0:T(8,128)(2,1)S(1)}, bf16[256,384]{1,0:T(8,128)(2,1)S(1)}, u32[]{:S(2)}, u32[]{:S(2)}) collective-permute-start(bf16[256,384]{1,0:T(8,128)(2,1)S(1)} %get-tuple-element.158.own_ref), channel_id=1, source_target_pairs={{0,16},{4,20},{8,24},{12,28},{16,0},{20,4},{24,8},{28,12},{1,17},{... | collective-permute-start | bytes 589832 | tf_op jit(solution)/shard_map/ppermute | solution.py:471
  6.0 1.6 collective-permute-start.1
  8.9 6.6 %scaled_weight.3.refs_2_.refs_4_ = bf16[3072,2048]{1,0:T(8,128)(2,1)S(1)} custom-call(bf16[3072,2048]{1,0:T(8,128)(2,1)} %code_ref.3, f32[16,24]{1,0:T(8,128)S(1)} %bitcast.5), custom_call_target="tpu_custom_call" | custom-call | bytes 1536 | tf_op jit(solution)/shard_map/scaled_weight/pallas_call | solution.py:88
  16.0 1.3 collective-permute-start.3
  17.3 4.0 %collective-permute-start.4 = (bf16[256,384]{1,0:T(8,128)(2,1)S(1)}, bf16[256,384]{1,0:T(8,128)(2,1)S(1)}, u32[]{:S(2)}, u32[]{:S(2)}) collective-permute-start(bf16[256,384]{1,0:T(8,128)(2,1)S(1)} %get-tuple-element.162.own_ref), channel_id=1, source_target_pairs={{0,16},{4,20},{8,24},{12,28},{16,0},{20,4},{24,8},{28,12},{1,17},{... | collective-permute-start | bytes 589832 | tf_op jit(solution)/shard_map/ppermute | solution.py:471
  21.3 6.6 %scaled_weight.2.refs_3_.refs_5_ = bf16[3072,2048]{1,0:T(8,128)(2,1)S(1)} custom-call(bf16[3072,2048]{1,0:T(8,128)(2,1)} %code_ref.2, f32[16,24]{1,0:T(8,128)S(1)} %bitcast.6), custom_call_target="tpu_custom_call" | custom-call | bytes 1536 | tf_op jit(solution)/shard_map/scaled_weight/pallas_call | solution.py:88
  27.9 2.1 %collective-permute-done.4.two_ref = bf16[256,384]{1,0:T(8,128)(2,1)S(1)} collective-permute-done((bf16[256,384]{1,0:T(8,128)(2,1)S(1)}, bf16[256,384]{1,0:T(8,128)(2,1)S(1)}, u32[]{:S(2)}, u32[]{:S(2)}) %collective-permute-start.4) | collective-permute-done | bytes 196640 | tf_op jit(solution)/shard_map/ppermute | solution.py:471
  30.0 2.0 %collective-permute-done.5.near_ref = bf16[256,384]{1,0:T(8,128)(2,1)S(1)} collective-permute-done((bf16[256,384]{1,0:T(8,128)(2,1)S(1)}, bf16[256,384]{1,0:T(8,128)(2,1)S(1)}, u32[]{:S(2)}, u32[]{:S(2)}) %collective-permute-start.5) | collective-permute-done | bytes 196640 | tf_op jit(solution)/shard_map/ppermute | solution.py:476
  33.4 1.3 collective-permute-start.8
  35.0 7.5 %forward_product.2 = (bf16[128,4096]{1,0:T(8,128)(2,1)S(1)}, bf16[64,4096]{1,0:T(8,128)(2,1)S(1)}, bf16[64,4096]{1,0:T(8,128)(2,1)S(1)}) custom-call(s32[3]{0:T(128)S(1)} %pad_add_fusion.where_ref, bf16[256,1536]{1,0:T(8,128)(2,1)S(1)} %join.4.refs_0_, bf16[256,1536]{1,0:T(8,128)(2,1)S(1)} %collective-permute-done.6.refs_1_, ...), custom_call_target="tpu_custom_call" | custom-call | flops 1024 | bytes 1024 | tf_op jit(solution)/shard_map/forward_product/pallas_call | solution.py:231
  42.5 1.1 collective-permute-done.8.passed_ref
  43.6 1.5 collective-permute-start.10
  45.8 3.7 %collective-permute-start.11 = (bf16[256,384]{1,0:T(8,128)(2,1)S(1)}, bf16[256,384]{1,0:T(8,128)(2,1)S(1)}, u32[]{:S(2)}, u32[]{:S(2)}) collective-permute-start(bf16[256,384]{1,0:T(8,128)(2,1)S(1)} %get-tuple-element.188.own_ref), channel_id=1, source_target_pairs={{0,16},{4,20},{8,24},{12,28},{16,0},{20,4},{24,8},{28,12},{1,17},{... | collective-permute-start | bytes 589832 | tf_op jit(solution)/shard_map/ppermute | solution.py:471
  50.3 7.4 %forward_streamed.2 = (bf16[128,2048]{1,0:T(8,128)(2,1)S(1)}, bf16[64,2048]{1,0:T(8,128)(2,1)S(1)}, bf16[64,2048]{1,0:T(8,128)(2,1)S(1)}) custom-call(s32[3]{0:T(128)S(1)} %pad_add_fusion.where_ref, f32[16,24]{1,0:T(8,128)S(1)} %copy-done, bf16[256,1536]{1,0:T(8,128)(2,1)S(1)} %join.5.refs_0_, bf16[256,1536]{1,0:T(8,128)(2,1)S(1)} %collective-permute-done.9.refs_1_, ...), custom_call_target="tpu_custom_call" | custom-call | flops 1024 | bytes 1024 | tf_op jit(solution)/shard_map/forward_streamed/pallas_call | solution.py:303
  57.7 1.9 %collective-permute-done.11.two_ref = bf16[256,384]{1,0:T(8,128)(2,1)S(1)} collective-permute-done((bf16[256,384]{1,0:T(8,128)(2,1)S(1)}, bf16[256,384]{1,0:T(8,128)(2,1)S(1)}, u32[]{:S(2)}, u32[]{:S(2)}) %collective-permute-start.11) | collective-permute-done | bytes 196640 | tf_op jit(solution)/shard_map/ppermute | solution.py:471
  59.9 1.3 collective-permute-start.14
  61.2 1.1 collective-permute-start.16
  62.2 5.6 %collective-permute-done.14.passed_ref = bf16[256,384]{1,0:T(8,128)(2,1)S(1)} collective-permute-done((bf16[256,384]{1,0:T(8,128)(2,1)S(1)}, bf16[256,384]{1,0:T(8,128)(2,1)S(1)}, u32[]{:S(2)}, u32[]{:S(2)}) %collective-permute-start.14) | collective-permute-done | bytes 196640 | tf_op jit(solution)/shard_map/ppermute | solution.py:476
  68.9 1.6 collective-permute-start.19
  71.1 1.6 collective-permute-start.20
  72.7 3.2 %collective-permute-start.17 = (bf16[256,384]{1,0:T(8,128)(2,1)S(1)}, bf16[256,384]{1,0:T(8,128)(2,1)S(1)}, u32[]{:S(2)}, u32[]{:S(2)}) collective-permute-start(bf16[256,384]{1,0:T(8,128)(2,1)S(1)} %get-tuple-element.207.own_ref), channel_id=1, source_target_pairs={{0,16},{4,20},{8,24},{12,28},{16,0},{20,4},{24,8},{28,12},{1,17},{... | collective-permute-start | bytes 589832 | tf_op jit(solution)/shard_map/ppermute | solution.py:471
  76.1 7.5 %forward_product.3 = (bf16[128,4096]{1,0:T(8,128)(2,1)S(1)}, bf16[64,4096]{1,0:T(8,128)(2,1)S(1)}, bf16[64,4096]{1,0:T(8,128)(2,1)S(1)}) custom-call(s32[3]{0:T(128)S(1)} %pad_add_fusion.where_ref, bf16[256,1536]{1,0:T(8,128)(2,1)S(1)} %join.6.refs_0_, bf16[256,1536]{1,0:T(8,128)(2,1)S(1)} %collective-permute-done.15.refs_1_, ...), custom_call_target="tpu_custom_call" | custom-call | flops 1024 | bytes 1024 | tf_op jit(solution)/shard_map/forward_product/pallas_call | solution.py:231
  83.7 1.4 collective-permute-start.25
  85.7 1.3 collective-permute-start.22
  88.0 6.5 %collective-permute-done.22.passed_ref = bf16[256,384]{1,0:T(8,128)(2,1)S(1)} collective-permute-done((bf16[256,384]{1,0:T(8,128)(2,1)S(1)}, bf16[256,384]{1,0:T(8,128)(2,1)S(1)}, u32[]{:S(2)}, u32[]{:S(2)}) %collective-permute-start.22) | collective-permute-done | bytes 196640 | tf_op jit(solution)/shard_map/ppermute | solution.py:476
  95.5 1.6 collective-permute-start.23
  97.8 7.4 %forward_streamed.3 = (bf16[128,2048]{1,0:T(8,128)(2,1)S(1)}, bf16[64,2048]{1,0:T(8,128)(2,1)S(1)}, bf16[64,2048]{1,0:T(8,128)(2,1)S(1)}) custom-call(s32[3]{0:T(128)S(1)} %pad_add_fusion.where_ref, f32[16,24]{1,0:T(8,128)S(1)} %copy-done, bf16[256,1536]{1,0:T(8,128)(2,1)S(1)} %join.7.refs_0_, bf16[256,1536]{1,0:T(8,128)(2,1)S(1)} %collective-permute-done.24.refs_1_, ...), custom_call_target="tpu_custom_call" | custom-call | flops 1024 | bytes 1024 | tf_op jit(solution)/shard_map/forward_streamed/pallas_call | solution.py:303
  105.2 4.7 %collective-permute-done.23.refs_1_ = bf16[64,4096]{1,0:T(8,128)(2,1)S(1)} collective-permute-done((bf16[64,4096]{1,0:T(8,128)(2,1)S(1)}, bf16[64,4096]{1,0:T(8,128)(2,1)S(1)}, u32[]{:S(2)}, u32[]{:S(2)}) %collective-permute-start.23) | collective-permute-done | bytes 524320 | tf_op jit(solution)/shard_map/ppermute | solution.py:465
  109.9 1.6 collective-permute-start.27
  111.8 1.9 %collective-permute-start.30 = (bf16[64,4096]{1,0:T(8,128)(2,1)S(1)}, bf16[64,4096]{1,0:T(8,128)(2,1)S(1)}, u32[]{:S(2)}, u32[]{:S(2)}) collective-permute-start(bf16[64,4096]{1,0:T(8,128)(2,1)S(1)} %add_convert_fusion), channel_id=1, source_target_pairs={{0,2},{1,3},{2,0},{3,1},{4,5},{5,4},{6,7},{7,6},{8,10},{9,11},{10,... | collective-permute-start | bytes 1572872 | tf_op jit(solution)/shard_map/ppermute | solution.py:465
  113.8 10.2 %collective-permute-done.27.refs_3_ = bf16[64,4096]{1,0:T(8,128)(2,1)S(1)} collective-permute-done((bf16[64,4096]{1,0:T(8,128)(2,1)S(1)}, bf16[64,4096]{1,0:T(8,128)(2,1)S(1)}, u32[]{:S(2)}, u32[]{:S(2)}) %collective-permute-start.27) | collective-permute-done | bytes 524320 | tf_op jit(solution)/shard_map/ppermute | solution.py:465
  124.0 2.5 %collective-permute-done.28.refs_4_ = bf16[128,2048]{1,0:T(8,128)(2,1)S(1)} collective-permute-done((bf16[128,2048]{1,0:T(8,128)(2,1)S(1)}, bf16[128,2048]{1,0:T(8,128)(2,1)S(1)}, u32[]{:S(2)}, u32[]{:S(2)}) %collective-permute-start.28) | collective-permute-done | bytes 524320 | tf_op jit(solution)/shard_map/ppermute | solution.py:465
  126.9 7.4 %backward_product.4 = (bf16[256,1536]{1,0:T(8,128)(2,1)S(1)}, bf16[256,1536]{1,0:T(8,128)(2,1)S(1)}) custom-call(s32[3]{0:T(128)S(1)} %pad_add_fusion.where_ref, bf16[64,4096]{1,0:T(8,128)(2,1)S(1)} %hidden_grads.2.refs_0_, bf16[64,4096]{1,0:T(8,128)(2,1)S(1)} %collective-permute-done.23.refs_1_, bf16[64,4096]{1,0:T(8,128)(2,1)S(1)} %collective-permute-done.26.refs_2_, ...), custom_call_target="tpu_custom_call" | custom-call | flops 1024 | bytes 1024 | tf_op jit(solution)/shard_map/backward_product/pallas_call | solution.py:382
  135.5 1.7 collective-permute-start.31
  137.3 3.8 %collective-permute-start.33 = (bf16[256,384]{1,0:T(8,128)(2,1)S(1)}, bf16[256,384]{1,0:T(8,128)(2,1)S(1)}, u32[]{:S(2)}, u32[]{:S(2)}) collective-permute-start(bf16[256,384]{1,0:T(8,128)(2,1)S(1)} %get-tuple-element.267), channel_id=1, source_target_pairs={{0,16},{4,20},{8,24},{12,28},{16,0},{20,4},{24,8},{28,12},{1,17},{... | collective-permute-start | bytes 589832 | tf_op jit(solution)/shard_map/ppermute | solution.py:471
  141.5 4.6 %collective-permute-done.31.refs_1_ = bf16[64,4096]{1,0:T(8,128)(2,1)S(1)} collective-permute-done((bf16[64,4096]{1,0:T(8,128)(2,1)S(1)}, bf16[64,4096]{1,0:T(8,128)(2,1)S(1)}, u32[]{:S(2)}, u32[]{:S(2)}) %collective-permute-start.31) | collective-permute-done | bytes 524320 | tf_op jit(solution)/shard_map/ppermute | solution.py:465
  146.1 4.4 %collective-permute-done.33.refs_0_ = bf16[256,384]{1,0:T(8,128)(2,1)S(1)} collective-permute-done((bf16[256,384]{1,0:T(8,128)(2,1)S(1)}, bf16[256,384]{1,0:T(8,128)(2,1)S(1)}, u32[]{:S(2)}, u32[]{:S(2)}) %collective-permute-start.33) | collective-permute-done | bytes 196640 | tf_op jit(solution)/shard_map/ppermute | solution.py:471
  152.5 2.8 %collective-permute-start.38 = (bf16[256,384]{1,0:T(8,128)(2,1)S(1)}, bf16[256,384]{1,0:T(8,128)(2,1)S(1)}, u32[]{:S(2)}, u32[]{:S(2)}) collective-permute-start(bf16[256,384]{1,0:T(8,128)(2,1)S(1)} %get-tuple-element.283), channel_id=1, source_target_pairs={{0,24},{4,28},{8,0},{12,4},{16,8},{20,12},{24,16},{28,20},{1,25},{... | collective-permute-start | bytes 589832 | tf_op jit(solution)/shard_map/ppermute | solution.py:471
  155.3 5.8 %collective-permute-done.36.refs_1_ = bf16[256,384]{1,0:T(8,128)(2,1)S(1)} collective-permute-done((bf16[256,384]{1,0:T(8,128)(2,1)S(1)}, bf16[256,384]{1,0:T(8,128)(2,1)S(1)}, u32[]{:S(2)}, u32[]{:S(2)}) %collective-permute-start.36) | collective-permute-done | bytes 196640 | tf_op jit(solution)/shard_map/ppermute | solution.py:471
  161.1 2.5 %backward_product.5 = (bf16[256,384]{1,0:T(8,128)(2,1)S(1)}, bf16[256,384]{1,0:T(8,128)(2,1)S(1)}) custom-call(s32[3]{0:T(128)S(1)} %pad_add_fusion.where_ref, bf16[64,4096]{1,0:T(8,128)(2,1)S(1)} %hidden_grads.3.refs_0_, bf16[64,4096]{1,0:T(8,128)(2,1)S(1)} %collective-permute-done.31.refs_1_, bf16[64,4096]{1,0:T(8,128)(2,1)S(1)} %collective-permute-done.34.refs_2_, ...), custom_call_target="tpu_custom_call" | custom-call | flops 1024 | bytes 1024 | tf_op jit(solution)/shard_map/backward_product/pallas_call | solution.py:382
  163.6 4.1 %backward_product.6 = (bf16[256,768]{1,0:T(8,128)(2,1)S(1)}, bf16[256,768]{1,0:T(8,128)(2,1)S(1)}) custom-call(s32[3]{0:T(128)S(1)} %pad_add_fusion.where_ref, bf16[64,4096]{1,0:T(8,128)(2,1)S(1)} %hidden_grads.3.refs_0_, bf16[64,4096]{1,0:T(8,128)(2,1)S(1)} %collective-permute-done.31.refs_1_, bf16[64,4096]{1,0:T(8,128)(2,1)S(1)} %collective-permute-done.34.refs_2_, ...), custom_call_target="tpu_custom_call" | custom-call | flops 1024 | bytes 1024 | tf_op jit(solution)/shard_map/backward_product/pallas_call | solution.py:382
  168.4 2.1 %collective-permute-start.40 = (bf16[256,384]{1,0:T(8,128)(2,1)S(1)}, bf16[256,384]{1,0:T(8,128)(2,1)S(1)}, u32[]{:S(2)}, u32[]{:S(2)}) collective-permute-start(bf16[256,384]{1,0:T(8,128)(2,1)S(1)} %pair_sums.4), channel_id=1, source_target_pairs={{0,16},{4,20},{8,24},{12,28},{16,0},{20,4},{24,8},{28,12},{1,17},{... | collective-permute-start | bytes 589832 | tf_op jit(solution)/shard_map/ppermute | solution.py:471
  170.6 3.8 %collective-permute-start.42 = (bf16[256,384]{1,0:T(8,128)(2,1)S(1)}, bf16[256,384]{1,0:T(8,128)(2,1)S(1)}, u32[]{:S(2)}, u32[]{:S(2)}) collective-permute-start(bf16[256,384]{1,0:T(8,128)(2,1)S(1)} %get-tuple-element.308), channel_id=1, source_target_pairs={{0,24},{4,28},{8,0},{12,4},{16,8},{20,12},{24,16},{28,20},{1,25},{... | collective-permute-start | bytes 589832 | tf_op jit(solution)/shard_map/ppermute | solution.py:471
  174.4 2.5 %backward_product.7 = (bf16[256,384]{1,0:T(8,128)(2,1)S(1)}, bf16[256,384]{1,0:T(8,128)(2,1)S(1)}) custom-call(s32[3]{0:T(128)S(1)} %pad_add_fusion.where_ref, bf16[64,4096]{1,0:T(8,128)(2,1)S(1)} %hidden_grads.3.refs_0_, bf16[64,4096]{1,0:T(8,128)(2,1)S(1)} %collective-permute-done.31.refs_1_, bf16[64,4096]{1,0:T(8,128)(2,1)S(1)} %collective-permute-done.34.refs_2_, ...), custom_call_target="tpu_custom_call" | custom-call | flops 1024 | bytes 1024 | tf_op jit(solution)/shard_map/backward_product/pallas_call | solution.py:382
  177.6 6.1 %collective-permute-done.40.refs_1_ = bf16[256,384]{1,0:T(8,128)(2,1)S(1)} collective-permute-done((bf16[256,384]{1,0:T(8,128)(2,1)S(1)}, bf16[256,384]{1,0:T(8,128)(2,1)S(1)}, u32[]{:S(2)}, u32[]{:S(2)}) %collective-permute-start.40) | collective-permute-done | bytes 196640 | tf_op jit(solution)/shard_map/ppermute | solution.py:471
  183.7 2.2 %collective-permute-done.42.refs_3_ = bf16[256,384]{1,0:T(8,128)(2,1)S(1)} collective-permute-done((bf16[256,384]{1,0:T(8,128)(2,1)S(1)}, bf16[256,384]{1,0:T(8,128)(2,1)S(1)}, u32[]{:S(2)}, u32[]{:S(2)}) %collective-permute-start.42) | collective-permute-done | bytes 196640 | tf_op jit(solution)/shard_map/ppermute | solution.py:471
  185.9 1.4 final_sum.3
  (73 shorter events, 16.4 us)
Async XLA Ops:
  1.9 14.1 %collective-permute-start = (bf16[256,384]{1,0:T(8,128)(2,1)S(1)}, bf16[256,384]{1,0:T(8,128)(2,1)S(1)}, u32[]{:S(2)}, u32[]{:S(2)}) collective-permute-start(bf16[256,384]{1,0:T(8,128)(2,1)S(1)} %get-tuple-element.158.own_ref), channel_id=1, source_target_pairs={{0,16},{4,20},{8,24},{12,28},{16,0},{20,4},{24,8},{28,12},{1,17},{... | collective-permute-start | bytes 589832 | tf_op jit(solution)/shard_map/ppermute | solution.py:471
  6.0 10.0 %collective-permute-start.1 = (bf16[256,384]{1,0:T(8,128)(2,1)S(1)}, bf16[256,384]{1,0:T(8,128)(2,1)S(1)}, u32[]{:S(2)}, u32[]{:S(2)}) collective-permute-start(bf16[256,384]{1,0:T(8,128)(2,1)S(1)} %get-tuple-element.158.own_ref), channel_id=1, source_target_pairs={{0,8},{4,12},{8,0},{12,4},{16,24},{20,28},{24,16},{28,20},{1,9},{5... | collective-permute-start | bytes 589832 | tf_op jit(solution)/shard_map/ppermute | solution.py:476
  7.6 20.3 %collective-permute-start.2 = (bf16[256,384]{1,0:T(8,128)(2,1)S(1)}, bf16[256,384]{1,0:T(8,128)(2,1)S(1)}, u32[]{:S(2)}, u32[]{:S(2)}) collective-permute-start(bf16[256,384]{1,0:T(8,128)(2,1)S(1)} %get-tuple-element.158.own_ref), channel_id=1, source_target_pairs={{8,16},{12,20},{16,8},{20,12},{9,17},{13,21},{17,9},{21,13},{10,18... | collective-permute-start | bytes 589832 | tf_op jit(solution)/shard_map/ppermute | solution.py:476
  8.2 0.7 copy-start.1
  8.9 12.4 %copy-start.2 = (f32[24,16]{0,1:T(8,128)S(1)}, f32[24,16]{0,1:T(8,128)}, u32[]{:S(2)}) copy-start(f32[24,16]{0,1:T(8,128)} %param.13) | copy-start | bytes 4612
  16.0 11.9 %collective-permute-start.3 = (bf16[256,384]{1,0:T(8,128)(2,1)S(1)}, bf16[256,384]{1,0:T(8,128)(2,1)S(1)}, u32[]{:S(2)}, u32[]{:S(2)}) collective-permute-start(bf16[256,384]{1,0:T(8,128)(2,1)S(1)} %collective-permute-done.two_ref), channel_id=1, source_target_pairs={{8,0},{12,4},{16,24},{20,28},{9,1},{13,5},{17,25},{21,29},{10,2},{... | collective-permute-start | bytes 589832 | tf_op jit(solution)/shard_map/ppermute | solution.py:476
  17.3 12.7 %collective-permute-start.4 = (bf16[256,384]{1,0:T(8,128)(2,1)S(1)}, bf16[256,384]{1,0:T(8,128)(2,1)S(1)}, u32[]{:S(2)}, u32[]{:S(2)}) collective-permute-start(bf16[256,384]{1,0:T(8,128)(2,1)S(1)} %get-tuple-element.162.own_ref), channel_id=1, source_target_pairs={{0,16},{4,20},{8,24},{12,28},{16,0},{20,4},{24,8},{28,12},{1,17},{... | collective-permute-start | bytes 589832 | tf_op jit(solution)/shard_map/ppermute | solution.py:471
  21.3 10.7 %collective-permute-start.5 = (bf16[256,384]{1,0:T(8,128)(2,1)S(1)}, bf16[256,384]{1,0:T(8,128)(2,1)S(1)}, u32[]{:S(2)}, u32[]{:S(2)}) collective-permute-start(bf16[256,384]{1,0:T(8,128)(2,1)S(1)} %get-tuple-element.162.own_ref), channel_id=1, source_target_pairs={{0,8},{4,12},{8,0},{12,4},{16,24},{20,28},{24,16},{28,20},{1,9},{5... | collective-permute-start | bytes 589832 | tf_op jit(solution)/shard_map/ppermute | solution.py:476
  32.6 17.6 %copy-start = (f32[16,24]{1,0:T(8,128)S(1)}, f32[16,24]{1,0:T(8,128)}, u32[]{:S(2)}) copy-start(f32[16,24]{1,0:T(8,128)} %scale_ref.3) | copy-start | bytes 4612
  32.6 2.4 %collective-permute-start.6 = (bf16[256,1536]{1,0:T(8,128)(2,1)S(1)}, bf16[256,1536]{1,0:T(8,128)(2,1)S(1)}, u32[]{:S(2)}, u32[]{:S(2)}) collective-permute-start(bf16[256,1536]{1,0:T(8,128)(2,1)S(1)} %join.4.refs_0_), channel_id=1, source_target_pairs={{0,4},{4,0},{8,12},{12,8},{16,20},{20,16},{24,28},{28,24},{1,5},{5... | collective-permute-start | bytes 2359304 | tf_op jit(solution)/shard_map/ppermute | solution.py:468
  32.7 9.8 %collective-permute-start.7 = (bf16[256,384]{1,0:T(8,128)(2,1)S(1)}, bf16[256,384]{1,0:T(8,128)(2,1)S(1)}, u32[]{:S(2)}, u32[]{:S(2)}) collective-permute-start(bf16[256,384]{1,0:T(8,128)(2,1)S(1)} %get-tuple-element.162.own_ref), channel_id=1, source_target_pairs={{8,16},{12,20},{16,8},{20,12},{9,17},{13,21},{17,9},{21,13},{10,18... | collective-permute-start | bytes 589832 | tf_op jit(solution)/shard_map/ppermute | solution.py:476
  33.4 10.2 %collective-permute-start.8 = (bf16[256,384]{1,0:T(8,128)(2,1)S(1)}, bf16[256,384]{1,0:T(8,128)(2,1)S(1)}, u32[]{:S(2)}, u32[]{:S(2)}) collective-permute-start(bf16[256,384]{1,0:T(8,128)(2,1)S(1)} %collective-permute-done.4.two_ref), channel_id=1, source_target_pairs={{8,0},{12,4},{16,24},{20,28},{9,1},{13,5},{17,25},{21,29},{10,2},{... | collective-permute-start | bytes 589832 | tf_op jit(solution)/shard_map/ppermute | solution.py:476
  43.6 16.2 %collective-permute-start.10 = (bf16[128,4096]{1,0:T(8,128)(2,1)S(1)}, bf16[128,4096]{1,0:T(8,128)(2,1)S(1)}, u32[]{:S(2)}, u32[]{:S(2)}) collective-permute-start(bf16[128,4096]{1,0:T(8,128)(2,1)S(1)} %get-tuple-element.185), channel_id=1, source_target_pairs={{0,1},{1,0},{2,3},{3,2},{4,6},{5,7},{6,4},{7,5},{8,9},{9,8},{10,11... | collective-permute-start | bytes 3145736 | tf_op jit(solution)/shard_map/ppermute | solution.py:465
  45.7 4.5 %collective-permute-start.9 = (bf16[256,1536]{1,0:T(8,128)(2,1)S(1)}, bf16[256,1536]{1,0:T(8,128)(2,1)S(1)}, u32[]{:S(2)}, u32[]{:S(2)}) collective-permute-start(bf16[256,1536]{1,0:T(8,128)(2,1)S(1)} %join.5.refs_0_), channel_id=1, source_target_pairs={{0,4},{4,0},{8,12},{12,8},{16,20},{20,16},{24,28},{28,24},{1,5},{5... | collective-permute-start | bytes 2359304 | tf_op jit(solution)/shard_map/ppermute | solution.py:468
  45.8 13.7 %collective-permute-start.11 = (bf16[256,384]{1,0:T(8,128)(2,1)S(1)}, bf16[256,384]{1,0:T(8,128)(2,1)S(1)}, u32[]{:S(2)}, u32[]{:S(2)}) collective-permute-start(bf16[256,384]{1,0:T(8,128)(2,1)S(1)} %get-tuple-element.188.own_ref), channel_id=1, source_target_pairs={{0,16},{4,20},{8,24},{12,28},{16,0},{20,4},{24,8},{28,12},{1,17},{... | collective-permute-start | bytes 589832 | tf_op jit(solution)/shard_map/ppermute | solution.py:471
  49.6 10.3 %collective-permute-start.12 = (bf16[256,384]{1,0:T(8,128)(2,1)S(1)}, bf16[256,384]{1,0:T(8,128)(2,1)S(1)}, u32[]{:S(2)}, u32[]{:S(2)}) collective-permute-start(bf16[256,384]{1,0:T(8,128)(2,1)S(1)} %get-tuple-element.188.own_ref), channel_id=1, source_target_pairs={{0,8},{4,12},{8,0},{12,4},{16,24},{20,28},{24,16},{28,20},{1,9},{5... | collective-permute-start | bytes 589832 | tf_op jit(solution)/shard_map/ppermute | solution.py:476
  49.6 12.7 %collective-permute-start.13 = (bf16[256,384]{1,0:T(8,128)(2,1)S(1)}, bf16[256,384]{1,0:T(8,128)(2,1)S(1)}, u32[]{:S(2)}, u32[]{:S(2)}) collective-permute-start(bf16[256,384]{1,0:T(8,128)(2,1)S(1)} %get-tuple-element.188.own_ref), channel_id=1, source_target_pairs={{8,16},{12,20},{16,8},{20,12},{9,17},{13,21},{17,9},{21,13},{10,18... | collective-permute-start | bytes 589832 | tf_op jit(solution)/shard_map/ppermute | solution.py:476
  59.9 8.0 %collective-permute-start.14 = (bf16[256,384]{1,0:T(8,128)(2,1)S(1)}, bf16[256,384]{1,0:T(8,128)(2,1)S(1)}, u32[]{:S(2)}, u32[]{:S(2)}) collective-permute-start(bf16[256,384]{1,0:T(8,128)(2,1)S(1)} %collective-permute-done.11.two_ref), channel_id=1, source_target_pairs={{8,0},{12,4},{16,24},{20,28},{9,1},{13,5},{17,25},{21,29},{10,2},{... | collective-permute-start | bytes 589832 | tf_op jit(solution)/shard_map/ppermute | solution.py:476
  61.2 9.3 %collective-permute-start.16 = (bf16[128,2048]{1,0:T(8,128)(2,1)S(1)}, bf16[128,2048]{1,0:T(8,128)(2,1)S(1)}, u32[]{:S(2)}, u32[]{:S(2)}) collective-permute-start(bf16[128,2048]{1,0:T(8,128)(2,1)S(1)} %get-tuple-element.198), channel_id=1, source_target_pairs={{0,1},{1,0},{2,3},{3,2},{4,6},{5,7},{6,4},{7,5},{8,9},{9,8},{10,11... | collective-permute-start | bytes 1572872 | tf_op jit(solution)/shard_map/ppermute | solution.py:465
  68.7 2.4 %collective-permute-start.15 = (bf16[256,1536]{1,0:T(8,128)(2,1)S(1)}, bf16[256,1536]{1,0:T(8,128)(2,1)S(1)}, u32[]{:S(2)}, u32[]{:S(2)}) collective-permute-start(bf16[256,1536]{1,0:T(8,128)(2,1)S(1)} %join.6.refs_0_), channel_id=1, source_target_pairs={{0,4},{4,0},{8,12},{12,8},{16,20},{20,16},{24,28},{28,24},{1,5},{5... | collective-permute-start | bytes 2359304 | tf_op jit(solution)/shard_map/ppermute | solution.py:468
  68.9 14.7 %collective-permute-start.19 = (bf16[64,4096]{1,0:T(8,128)(2,1)S(1)}, bf16[64,4096]{1,0:T(8,128)(2,1)S(1)}, u32[]{:S(2)}, u32[]{:S(2)}) collective-permute-start(bf16[64,4096]{1,0:T(8,128)(2,1)S(1)} %add_convert_fusion.1), channel_id=1, source_target_pairs={{0,2},{1,3},{2,0},{3,1},{4,5},{5,4},{6,7},{7,6},{8,10},{9,11},{10,... | collective-permute-start | bytes 1572872 | tf_op jit(solution)/shard_map/ppermute | solution.py:465
  71.1 12.6 %collective-permute-start.20 = (bf16[64,2048]{1,0:T(8,128)(2,1)S(1)}, bf16[64,2048]{1,0:T(8,128)(2,1)S(1)}, u32[]{:S(2)}, u32[]{:S(2)}) collective-permute-start(bf16[64,2048]{1,0:T(8,128)(2,1)S(1)} %add_convert_fusion.3), channel_id=1, source_target_pairs={{0,2},{1,3},{2,0},{3,1},{4,5},{5,4},{6,7},{7,6},{8,10},{9,11},{10,... | collective-permute-start | bytes 786440 | tf_op jit(solution)/shard_map/ppermute | solution.py:465
  72.7 10.9 %collective-permute-start.17 = (bf16[256,384]{1,0:T(8,128)(2,1)S(1)}, bf16[256,384]{1,0:T(8,128)(2,1)S(1)}, u32[]{:S(2)}, u32[]{:S(2)}) collective-permute-start(bf16[256,384]{1,0:T(8,128)(2,1)S(1)} %get-tuple-element.207.own_ref), channel_id=1, source_target_pairs={{0,16},{4,20},{8,24},{12,28},{16,0},{20,4},{24,8},{28,12},{1,17},{... | collective-permute-start | bytes 589832 | tf_op jit(solution)/shard_map/ppermute | solution.py:471
  75.9 7.8 %collective-permute-start.18 = (bf16[256,384]{1,0:T(8,128)(2,1)S(1)}, bf16[256,384]{1,0:T(8,128)(2,1)S(1)}, u32[]{:S(2)}, u32[]{:S(2)}) collective-permute-start(bf16[256,384]{1,0:T(8,128)(2,1)S(1)} %get-tuple-element.207.own_ref), channel_id=1, source_target_pairs={{0,8},{4,12},{8,0},{12,4},{16,24},{20,28},{24,16},{28,20},{1,9},{5... | collective-permute-start | bytes 589832 | tf_op jit(solution)/shard_map/ppermute | solution.py:476
  83.7 21.5 %collective-permute-start.25 = (bf16[128,4096]{1,0:T(8,128)(2,1)S(1)}, bf16[128,4096]{1,0:T(8,128)(2,1)S(1)}, u32[]{:S(2)}, u32[]{:S(2)}) collective-permute-start(bf16[128,4096]{1,0:T(8,128)(2,1)S(1)} %get-tuple-element.235), channel_id=1, source_target_pairs={{0,1},{1,0},{2,3},{3,2},{4,6},{5,7},{6,4},{7,5},{8,9},{9,8},{10,11... | collective-permute-start | bytes 3145736 | tf_op jit(solution)/shard_map/ppermute | solution.py:465
  85.0 3.0 %collective-permute-start.21 = (bf16[256,384]{1,0:T(8,128)(2,1)S(1)}, bf16[256,384]{1,0:T(8,128)(2,1)S(1)}, u32[]{:S(2)}, u32[]{:S(2)}) collective-permute-start(bf16[256,384]{1,0:T(8,128)(2,1)S(1)} %get-tuple-element.207.own_ref), channel_id=1, source_target_pairs={{8,16},{12,20},{16,8},{20,12},{9,17},{13,21},{17,9},{21,13},{10,18... | collective-permute-start | bytes 589832 | tf_op jit(solution)/shard_map/ppermute | solution.py:476
  85.7 8.9 %collective-permute-start.22 = (bf16[256,384]{1,0:T(8,128)(2,1)S(1)}, bf16[256,384]{1,0:T(8,128)(2,1)S(1)}, u32[]{:S(2)}, u32[]{:S(2)}) collective-permute-start(bf16[256,384]{1,0:T(8,128)(2,1)S(1)} %collective-permute-done.17.two_ref), channel_id=1, source_target_pairs={{8,0},{12,4},{16,24},{20,28},{9,1},{13,5},{17,25},{21,29},{10,2},{... | collective-permute-start | bytes 589832 | tf_op jit(solution)/shard_map/ppermute | solution.py:476
  95.4 2.4 %collective-permute-start.24 = (bf16[256,1536]{1,0:T(8,128)(2,1)S(1)}, bf16[256,1536]{1,0:T(8,128)(2,1)S(1)}, u32[]{:S(2)}, u32[]{:S(2)}) collective-permute-start(bf16[256,1536]{1,0:T(8,128)(2,1)S(1)} %join.7.refs_0_), channel_id=1, source_target_pairs={{0,4},{4,0},{8,12},{12,8},{16,20},{20,16},{24,28},{28,24},{1,5},{5... | collective-permute-start | bytes 2359304 | tf_op jit(solution)/shard_map/ppermute | solution.py:468
  95.5 14.4 %collective-permute-start.23 = (bf16[64,4096]{1,0:T(8,128)(2,1)S(1)}, bf16[64,4096]{1,0:T(8,128)(2,1)S(1)}, u32[]{:S(2)}, u32[]{:S(2)}) collective-permute-start(bf16[64,4096]{1,0:T(8,128)(2,1)S(1)} %hidden_grads.2.refs_0_), channel_id=1, source_target_pairs={{0,1},{1,0},{2,3},{3,2},{4,6},{5,7},{6,4},{7,5},{8,9},{9,8},{10,11... | collective-permute-start | bytes 1572872 | tf_op jit(solution)/shard_map/ppermute | solution.py:465
  97.1 16.7 %collective-permute-start.26 = (bf16[64,4096]{1,0:T(8,128)(2,1)S(1)}, bf16[64,4096]{1,0:T(8,128)(2,1)S(1)}, u32[]{:S(2)}, u32[]{:S(2)}) collective-permute-start(bf16[64,4096]{1,0:T(8,128)(2,1)S(1)} %hidden_grads.2.refs_0_), channel_id=1, source_target_pairs={{0,2},{1,3},{2,0},{3,1},{4,5},{5,4},{6,7},{7,6},{8,10},{9,11},{10,... | collective-permute-start | bytes 1572872 | tf_op jit(solution)/shard_map/ppermute | solution.py:465
  109.9 14.0 %collective-permute-start.27 = (bf16[64,4096]{1,0:T(8,128)(2,1)S(1)}, bf16[64,4096]{1,0:T(8,128)(2,1)S(1)}, u32[]{:S(2)}, u32[]{:S(2)}) collective-permute-start(bf16[64,4096]{1,0:T(8,128)(2,1)S(1)} %collective-permute-done.23.refs_1_), channel_id=1, source_target_pairs={{0,2},{1,3},{2,0},{3,1},{4,5},{5,4},{6,7},{7,6},{8,10},{9,11},{10,... | collective-permute-start | bytes 1572872 | tf_op jit(solution)/shard_map/ppermute | solution.py:465
  111.6 14.9 %collective-permute-start.28 = (bf16[128,2048]{1,0:T(8,128)(2,1)S(1)}, bf16[128,2048]{1,0:T(8,128)(2,1)S(1)}, u32[]{:S(2)}, u32[]{:S(2)}) collective-permute-start(bf16[128,2048]{1,0:T(8,128)(2,1)S(1)} %get-tuple-element.241), channel_id=1, source_target_pairs={{0,1},{1,0},{2,3},{3,2},{4,6},{5,7},{6,4},{7,5},{8,9},{9,8},{10,11... | collective-permute-start | bytes 1572872 | tf_op jit(solution)/shard_map/ppermute | solution.py:465
  111.8 22.5 %collective-permute-start.30 = (bf16[64,4096]{1,0:T(8,128)(2,1)S(1)}, bf16[64,4096]{1,0:T(8,128)(2,1)S(1)}, u32[]{:S(2)}, u32[]{:S(2)}) collective-permute-start(bf16[64,4096]{1,0:T(8,128)(2,1)S(1)} %add_convert_fusion), channel_id=1, source_target_pairs={{0,2},{1,3},{2,0},{3,1},{4,5},{5,4},{6,7},{7,6},{8,10},{9,11},{10,... | collective-permute-start | bytes 1572872 | tf_op jit(solution)/shard_map/ppermute | solution.py:465
  126.5 7.9 %collective-permute-start.29 = (bf16[64,2048]{1,0:T(8,128)(2,1)S(1)}, bf16[64,2048]{1,0:T(8,128)(2,1)S(1)}, u32[]{:S(2)}, u32[]{:S(2)}) collective-permute-start(bf16[64,2048]{1,0:T(8,128)(2,1)S(1)} %add_convert_fusion.2), channel_id=1, source_target_pairs={{0,2},{1,3},{2,0},{3,1},{4,5},{5,4},{6,7},{7,6},{8,10},{9,11},{10,... | collective-permute-start | bytes 786440 | tf_op jit(solution)/shard_map/ppermute | solution.py:465
  134.4 2.8 %collective-permute-start.32 = (bf16[256,1536]{1,0:T(8,128)(2,1)S(1)}, bf16[256,1536]{1,0:T(8,128)(2,1)S(1)}, u32[]{:S(2)}, u32[]{:S(2)}) collective-permute-start(bf16[256,1536]{1,0:T(8,128)(2,1)S(1)} %get-tuple-element.266), channel_id=1, source_target_pairs={{0,4},{4,0},{8,12},{12,8},{16,20},{20,16},{24,28},{28,24},{1,5},{5... | collective-permute-start | bytes 2359304 | tf_op jit(solution)/shard_map/ppermute | solution.py:468
  135.5 10.6 %collective-permute-start.31 = (bf16[64,4096]{1,0:T(8,128)(2,1)S(1)}, bf16[64,4096]{1,0:T(8,128)(2,1)S(1)}, u32[]{:S(2)}, u32[]{:S(2)}) collective-permute-start(bf16[64,4096]{1,0:T(8,128)(2,1)S(1)} %hidden_grads.3.refs_0_), channel_id=1, source_target_pairs={{0,1},{1,0},{2,3},{3,2},{4,6},{5,7},{6,4},{7,5},{8,9},{9,8},{10,11... | collective-permute-start | bytes 1572872 | tf_op jit(solution)/shard_map/ppermute | solution.py:465
  137.3 13.2 %collective-permute-start.33 = (bf16[256,384]{1,0:T(8,128)(2,1)S(1)}, bf16[256,384]{1,0:T(8,128)(2,1)S(1)}, u32[]{:S(2)}, u32[]{:S(2)}) collective-permute-start(bf16[256,384]{1,0:T(8,128)(2,1)S(1)} %get-tuple-element.267), channel_id=1, source_target_pairs={{0,16},{4,20},{8,24},{12,28},{16,0},{20,4},{24,8},{28,12},{1,17},{... | collective-permute-start | bytes 589832 | tf_op jit(solution)/shard_map/ppermute | solution.py:471
  141.1 14.2 %collective-permute-start.34 = (bf16[64,4096]{1,0:T(8,128)(2,1)S(1)}, bf16[64,4096]{1,0:T(8,128)(2,1)S(1)}, u32[]{:S(2)}, u32[]{:S(2)}) collective-permute-start(bf16[64,4096]{1,0:T(8,128)(2,1)S(1)} %hidden_grads.3.refs_0_), channel_id=1, source_target_pairs={{0,2},{1,3},{2,0},{3,1},{4,5},{5,4},{6,7},{7,6},{8,10},{9,11},{10,... | collective-permute-start | bytes 1572872 | tf_op jit(solution)/shard_map/ppermute | solution.py:465
  150.5 10.5 %collective-permute-start.35 = (bf16[64,4096]{1,0:T(8,128)(2,1)S(1)}, bf16[64,4096]{1,0:T(8,128)(2,1)S(1)}, u32[]{:S(2)}, u32[]{:S(2)}) collective-permute-start(bf16[64,4096]{1,0:T(8,128)(2,1)S(1)} %collective-permute-done.31.refs_1_), channel_id=1, source_target_pairs={{0,2},{1,3},{2,0},{3,1},{4,5},{5,4},{6,7},{7,6},{8,10},{9,11},{10,... | collective-permute-start | bytes 1572872 | tf_op jit(solution)/shard_map/ppermute | solution.py:465
  151.4 9.6 %collective-permute-start.36 = (bf16[256,384]{1,0:T(8,128)(2,1)S(1)}, bf16[256,384]{1,0:T(8,128)(2,1)S(1)}, u32[]{:S(2)}, u32[]{:S(2)}) collective-permute-start(bf16[256,384]{1,0:T(8,128)(2,1)S(1)} %get-tuple-element.270), channel_id=1, source_target_pairs={{0,8},{4,12},{8,16},{12,20},{16,24},{20,28},{24,0},{28,4},{1,9},{5... | collective-permute-start | bytes 589832 | tf_op jit(solution)/shard_map/ppermute | solution.py:471
  152.5 15.3 %collective-permute-start.38 = (bf16[256,384]{1,0:T(8,128)(2,1)S(1)}, bf16[256,384]{1,0:T(8,128)(2,1)S(1)}, u32[]{:S(2)}, u32[]{:S(2)}) collective-permute-start(bf16[256,384]{1,0:T(8,128)(2,1)S(1)} %get-tuple-element.283), channel_id=1, source_target_pairs={{0,24},{4,28},{8,0},{12,4},{16,8},{20,12},{24,16},{28,20},{1,25},{... | collective-permute-start | bytes 589832 | tf_op jit(solution)/shard_map/ppermute | solution.py:471
  163.5 4.2 %collective-permute-start.37 = (bf16[256,384]{1,0:T(8,128)(2,1)S(1)}, bf16[256,384]{1,0:T(8,128)(2,1)S(1)}, u32[]{:S(2)}, u32[]{:S(2)}) collective-permute-start(bf16[256,384]{1,0:T(8,128)(2,1)S(1)} %get-tuple-element.278), channel_id=1, source_target_pairs={{0,4},{4,0},{8,12},{12,8},{16,20},{20,16},{24,28},{28,24},{1,5},{5... | collective-permute-start | bytes 589832 | tf_op jit(solution)/shard_map/ppermute | solution.py:468
  167.8 2.7 %collective-permute-start.39 = (bf16[256,768]{1,0:T(8,128)(2,1)S(1)}, bf16[256,768]{1,0:T(8,128)(2,1)S(1)}, u32[]{:S(2)}, u32[]{:S(2)}) collective-permute-start(bf16[256,768]{1,0:T(8,128)(2,1)S(1)} %get-tuple-element.285), channel_id=1, source_target_pairs={{0,4},{4,0},{8,12},{12,8},{16,20},{20,16},{24,28},{28,24},{1,5},{5... | collective-permute-start | bytes 1179656 | tf_op jit(solution)/shard_map/ppermute | solution.py:468
  168.4 15.3 %collective-permute-start.40 = (bf16[256,384]{1,0:T(8,128)(2,1)S(1)}, bf16[256,384]{1,0:T(8,128)(2,1)S(1)}, u32[]{:S(2)}, u32[]{:S(2)}) collective-permute-start(bf16[256,384]{1,0:T(8,128)(2,1)S(1)} %pair_sums.4), channel_id=1, source_target_pairs={{0,16},{4,20},{8,24},{12,28},{16,0},{20,4},{24,8},{28,12},{1,17},{... | collective-permute-start | bytes 589832 | tf_op jit(solution)/shard_map/ppermute | solution.py:471
  170.5 13.2 %collective-permute-start.41 = (bf16[256,384]{1,0:T(8,128)(2,1)S(1)}, bf16[256,384]{1,0:T(8,128)(2,1)S(1)}, u32[]{:S(2)}, u32[]{:S(2)}) collective-permute-start(bf16[256,384]{1,0:T(8,128)(2,1)S(1)} %get-tuple-element.307), channel_id=1, source_target_pairs={{0,8},{4,12},{8,16},{12,20},{16,24},{20,28},{24,0},{28,4},{1,9},{5... | collective-permute-start | bytes 589832 | tf_op jit(solution)/shard_map/ppermute | solution.py:471
  170.6 15.3 %collective-permute-start.42 = (bf16[256,384]{1,0:T(8,128)(2,1)S(1)}, bf16[256,384]{1,0:T(8,128)(2,1)S(1)}, u32[]{:S(2)}, u32[]{:S(2)}) collective-permute-start(bf16[256,384]{1,0:T(8,128)(2,1)S(1)} %get-tuple-element.308), channel_id=1, source_target_pairs={{0,24},{4,28},{8,0},{12,4},{16,8},{20,12},{24,16},{28,20},{1,25},{... | collective-permute-start | bytes 589832 | tf_op jit(solution)/shard_map/ppermute | solution.py:471
  176.9 9.0 %collective-permute-start.43 = (bf16[256,384]{1,0:T(8,128)(2,1)S(1)}, bf16[256,384]{1,0:T(8,128)(2,1)S(1)}, u32[]{:S(2)}, u32[]{:S(2)}) collective-permute-start(bf16[256,384]{1,0:T(8,128)(2,1)S(1)} %get-tuple-element.310), channel_id=1, source_target_pairs={{0,4},{4,0},{8,12},{12,8},{16,20},{20,16},{24,28},{28,24},{1,5},{5... | collective-permute-start | bytes 589832 | tf_op jit(solution)/shard_map/ppermute | solution.py:468

commit v4 on v3

--- a/solution.py
+++ b/solution.py
@@ -590,28 +590,26 @@
     x = arrive(co_1, got_co_1)
     got_in_2 = near(in_2, set_out(in_2))
     hidden_1 = forward_streamed(where, x, down_code, down_scale, groups, width)
-    hidden_1, gate_up_1, got_in_2 = hold((hidden_1, gate_up_1, got_in_2))
+    hidden_1, gate_up_1, got_in_2, co_2 = hold((hidden_1, gate_up_1, got_in_2, co_2))
 
     hidden_1 = send(hidden_1)
+    got_co_2 = near(co_2, set_out(co_2))
+    got_in_2 = hold(pass_on(in_2, got_in_2))
+
     gate_up_1 = settle(gate_up_1)
-    got_in_2 = hold(pass_on(in_2, got_in_2))
-
     x = arrive(in_2, got_in_2)
-    x, co_2, hidden_1 = hold((x, co_2, hidden_1))
+    x, hidden_1, got_co_2 = hold((x, hidden_1, got_co_2))
 
     hidden_1 = settle(hidden_1)
-    got_co_2 = near(co_2, set_out(co_2))
+    got_co_2 = pass_on(co_2, got_co_2)
     gate_up_2 = forward(where, x, [gate_weight, up_weight], groups, 0, width)
     gate_up_2, got_co_2, gate_up_1, hidden_1 = hold((gate_up_2, got_co_2, gate_up_1, hidden_1))
 
-    got_co_2 = pass_on(co_2, got_co_2)
     gate_up_2 = send(gate_up_2)
     grad_1 = grads(where, terms_of(gate_up_1), terms_of(hidden_1), rows, hidden)
-    got_co_2, grad_1 = hold((got_co_2, grad_1))
+    x, grad_1 = hold((arrive(co_2, got_co_2), grad_1))
 
     early_1, late_1 = start_rows(grad_1)
-    x = hold(arrive(co_2, got_co_2))
-
     hidden_2 = forward_streamed(where, x, down_code, down_scale, groups, width)
     hidden_2, gate_up_2 = hold((hidden_2, gate_up_2))
 
@@ -630,10 +628,10 @@
     grad_2 = grads(where, terms_of(gate_up_2), terms_of(hidden_2), rows, hidden)
     early_2, late_2 = start_rows(grad_2)
     terms_1 = scatter(partial_1, whole[0])
-    early_2, early = hold((early_2, terms_1[:1]))
+    early_2 = hold(early_2)
     parts_2 = finish_rows(early_2, late_2)
-    parts_2, later = hold((parts_2, terms_1[1:2]))
-    terms_1 = [*early, *later, *terms_1[2:]]
+    parts_2, early = hold((parts_2, terms_1[:1]))
+    terms_1 = [*early, *terms_1[1:]]
 
     terms_2 = []
     partial, before = products(parts_2, parts_of_z[0]), parts_of_z[0]

time: 189 us -> 193 us (1.021)
  waiting for transfers between devices: 61.4 us -> 72.3 us
  starting transfers between devices: 55.7 us -> 50.7 us
    ppermute x14, waiting for transfers between devices: 22 us -> 35.9 us  [exchange(): return lax.ppermute(value, ('tp', 'dp'), pairs)]
    ppermute x12, waiting for transfers between devices: 15.6 us -> 11.8 us  [between(): lax.ppermute(value, 'tp', [(i * CORES + c, k * CORES + c) for i, k in pai...]
    ppermute x10, starting transfers between devices: 28.6 us -> 25.5 us  [along(): lax.ppermute(value, 'tp', [(i, (i + places * CORES) % n_tp) for i in rang...]
  transfers between devices with their start and end apart: 44 -> 44, of which waited for: 19 -> 20; matrix products, arithmetic and copies ran while one was open for 0% -> 0% of each run, Pallas kernels for 35% -> 33%
where the time goes in v4:
time: 193 us
  waiting for transfers between devices  72.3 us (37%)
  Pallas kernels  68.2 us (35%)
  starting transfers between devices  50.7 us (26%)
    ppermute x14, waiting for transfers between devices, exchange(): return lax.ppermute(value, ('tp', 'dp'), pairs)  35.9 us
    ppermute x10, starting transfers between devices, along(): lax.ppermute(value, 'tp', [(i, (i + places * CORES) % n_tp) for i in rang...  25.5 us
    ppermute x10, waiting for transfers between devices, along(): lax.ppermute(value, 'tp', [(i, (i + places * CORES) % n_tp) for i in rang...  22.4 us
    pallas_call x4, Pallas kernels, backward(): pl.pallas_call(functools.partial(backward_kernel, places, total_places),...  16.4 us
    pallas_call x2, Pallas kernels, forward(): pl.pallas_call(functools.partial(forward_kernel, groups, contract, width,...  15 us
    pallas_call x2, Pallas kernels, forward_streamed(): pl.pallas_call(functools.partial(streamed_kernel, groups, width), in_spec...  14.8 us
    ppermute x14, starting transfers between devices, exchange(): return lax.ppermute(value, ('tp', 'dp'), pairs)  14.6 us
    pallas_call x2, Pallas kernels, weight(): pl.pallas_call(functools.partial(weight_kernel, turned), in_specs=[pl.Blo...  13.2 us
  transfers between devices with their start and end apart: 44, of which 20 were waited for; matrix products, arithmetic and copies ran while one was open for 0% of the time, Pallas kernels for 33%

profile of v4, /device:TPU:0, one launch (start us, length us, event | category | flops | bytes accessed | tf_op | source)
XLA Modules:
  0.0 192.8 jit_solution(6587220688568955346)
XLA Ops:
  0.1 1.8 order_rows.1
  1.9 4.1 %collective-permute-start = (bf16[256,384]{1,0:T(8,128)(2,1)S(1)}, bf16[256,384]{1,0:T(8,128)(2,1)S(1)}, u32[]{:S(2)}, u32[]{:S(2)}) collective-permute-start(bf16[256,384]{1,0:T(8,128)(2,1)S(1)} %get-tuple-element.156.own_ref), channel_id=1, source_target_pairs={{0,16},{4,20},{8,24},{12,28},{16,0},{20,4},{24,8},{28,12},{1,17},{... | collective-permute-start | bytes 589832 | tf_op jit(solution)/shard_map/ppermute | solution.py:471
  6.0 1.6 collective-permute-start.1
  8.9 6.6 %scaled_weight.3.refs_2_.refs_4_ = bf16[3072,2048]{1,0:T(8,128)(2,1)S(1)} custom-call(bf16[3072,2048]{1,0:T(8,128)(2,1)} %code_ref.3, f32[16,24]{1,0:T(8,128)S(1)} %bitcast.5), custom_call_target="tpu_custom_call" | custom-call | bytes 1536 | tf_op jit(solution)/shard_map/scaled_weight/pallas_call | solution.py:88
  16.0 1.3 collective-permute-start.3
  17.3 4.0 %collective-permute-start.4 = (bf16[256,384]{1,0:T(8,128)(2,1)S(1)}, bf16[256,384]{1,0:T(8,128)(2,1)S(1)}, u32[]{:S(2)}, u32[]{:S(2)}) collective-permute-start(bf16[256,384]{1,0:T(8,128)(2,1)S(1)} %get-tuple-element.160.own_ref), channel_id=1, source_target_pairs={{0,16},{4,20},{8,24},{12,28},{16,0},{20,4},{24,8},{28,12},{1,17},{... | collective-permute-start | bytes 589832 | tf_op jit(solution)/shard_map/ppermute | solution.py:471
  21.3 6.6 %scaled_weight.2.refs_3_.refs_5_ = bf16[3072,2048]{1,0:T(8,128)(2,1)S(1)} custom-call(bf16[3072,2048]{1,0:T(8,128)(2,1)} %code_ref.2, f32[16,24]{1,0:T(8,128)S(1)} %bitcast.6), custom_call_target="tpu_custom_call" | custom-call | bytes 1536 | tf_op jit(solution)/shard_map/scaled_weight/pallas_call | solution.py:88
  27.9 2.1 %collective-permute-done.4.two_ref = bf16[256,384]{1,0:T(8,128)(2,1)S(1)} collective-permute-done((bf16[256,384]{1,0:T(8,128)(2,1)S(1)}, bf16[256,384]{1,0:T(8,128)(2,1)S(1)}, u32[]{:S(2)}, u32[]{:S(2)}) %collective-permute-start.4) | collective-permute-done | bytes 196640 | tf_op jit(solution)/shard_map/ppermute | solution.py:471
  30.0 2.0 %collective-permute-done.5.near_ref = bf16[256,384]{1,0:T(8,128)(2,1)S(1)} collective-permute-done((bf16[256,384]{1,0:T(8,128)(2,1)S(1)}, bf16[256,384]{1,0:T(8,128)(2,1)S(1)}, u32[]{:S(2)}, u32[]{:S(2)}) %collective-permute-start.5) | collective-permute-done | bytes 196640 | tf_op jit(solution)/shard_map/ppermute | solution.py:476
  33.4 1.3 collective-permute-start.8
  35.0 7.5 %forward_product.2 = (bf16[128,4096]{1,0:T(8,128)(2,1)S(1)}, bf16[64,4096]{1,0:T(8,128)(2,1)S(1)}, bf16[64,4096]{1,0:T(8,128)(2,1)S(1)}) custom-call(s32[3]{0:T(128)S(1)} %pad_add_fusion.where_ref, bf16[256,1536]{1,0:T(8,128)(2,1)S(1)} %join.4.refs_0_, bf16[256,1536]{1,0:T(8,128)(2,1)S(1)} %collective-permute-done.6.refs_1_, ...), custom_call_target="tpu_custom_call" | custom-call | flops 1024 | bytes 1024 | tf_op jit(solution)/shard_map/forward_product/pallas_call | solution.py:231
  42.5 1.1 collective-permute-done.8.passed_ref
  43.6 1.5 collective-permute-start.10
  45.8 3.7 %collective-permute-start.11 = (bf16[256,384]{1,0:T(8,128)(2,1)S(1)}, bf16[256,384]{1,0:T(8,128)(2,1)S(1)}, u32[]{:S(2)}, u32[]{:S(2)}) collective-permute-start(bf16[256,384]{1,0:T(8,128)(2,1)S(1)} %get-tuple-element.186.own_ref), channel_id=1, source_target_pairs={{0,16},{4,20},{8,24},{12,28},{16,0},{20,4},{24,8},{28,12},{1,17},{... | collective-permute-start | bytes 589832 | tf_op jit(solution)/shard_map/ppermute | solution.py:471
  50.2 7.4 %forward_streamed.2 = (bf16[128,2048]{1,0:T(8,128)(2,1)S(1)}, bf16[64,2048]{1,0:T(8,128)(2,1)S(1)}, bf16[64,2048]{1,0:T(8,128)(2,1)S(1)}) custom-call(s32[3]{0:T(128)S(1)} %pad_add_fusion.where_ref, f32[16,24]{1,0:T(8,128)S(1)} %copy-done, bf16[256,1536]{1,0:T(8,128)(2,1)S(1)} %join.5.refs_0_, bf16[256,1536]{1,0:T(8,128)(2,1)S(1)} %collective-permute-done.9.refs_1_, ...), custom_call_target="tpu_custom_call" | custom-call | flops 1024 | bytes 1024 | tf_op jit(solution)/shard_map/forward_streamed/pallas_call | solution.py:303
  57.7 1.9 collective-permute-done.11.two_ref
  59.8 1.3 collective-permute-start.14
  61.1 2.9 %collective-permute-start.17 = (bf16[256,384]{1,0:T(8,128)(2,1)S(1)}, bf16[256,384]{1,0:T(8,128)(2,1)S(1)}, u32[]{:S(2)}, u32[]{:S(2)}) collective-permute-start(bf16[256,384]{1,0:T(8,128)(2,1)S(1)} %get-tuple-element.199.own_ref), channel_id=1, source_target_pairs={{0,16},{4,20},{8,24},{12,28},{16,0},{20,4},{24,8},{28,12},{1,17},{... | collective-permute-start | bytes 589832 | tf_op jit(solution)/shard_map/ppermute | solution.py:471
  64.0 1.4 collective-permute-start.16
  65.4 7.4 %collective-permute-done.14.passed_ref = bf16[256,384]{1,0:T(8,128)(2,1)S(1)} collective-permute-done((bf16[256,384]{1,0:T(8,128)(2,1)S(1)}, bf16[256,384]{1,0:T(8,128)(2,1)S(1)}, u32[]{:S(2)}, u32[]{:S(2)}) %collective-permute-start.14) | collective-permute-done | bytes 196640 | tf_op jit(solution)/shard_map/ppermute | solution.py:476
  73.7 1.6 collective-permute-start.21
  75.3 1.0 collective-permute-done.18.near_ref
  76.4 1.6 collective-permute-start.22
  78.6 1.5 collective-permute-start.20
  80.1 7.5 %forward_product.3 = (bf16[128,4096]{1,0:T(8,128)(2,1)S(1)}, bf16[64,4096]{1,0:T(8,128)(2,1)S(1)}, bf16[64,4096]{1,0:T(8,128)(2,1)S(1)}) custom-call(s32[3]{0:T(128)S(1)} %pad_add_fusion.where_ref, bf16[256,1536]{1,0:T(8,128)(2,1)S(1)} %join.6.refs_0_, bf16[256,1536]{1,0:T(8,128)(2,1)S(1)} %collective-permute-done.15.refs_1_, ...), custom_call_target="tpu_custom_call" | custom-call | flops 1024 | bytes 1024 | tf_op jit(solution)/shard_map/forward_product/pallas_call | solution.py:231
  89.0 1.0 hidden_grads.2.refs_0_
  92.0 7.4 %forward_streamed.3 = (bf16[128,2048]{1,0:T(8,128)(2,1)S(1)}, bf16[64,2048]{1,0:T(8,128)(2,1)S(1)}, bf16[64,2048]{1,0:T(8,128)(2,1)S(1)}) custom-call(s32[3]{0:T(128)S(1)} %pad_add_fusion.where_ref, f32[16,24]{1,0:T(8,128)S(1)} %copy-done, bf16[256,1536]{1,0:T(8,128)(2,1)S(1)} %join.7.refs_0_, bf16[256,1536]{1,0:T(8,128)(2,1)S(1)} %collective-permute-done.23.refs_1_, ...), custom_call_target="tpu_custom_call" | custom-call | flops 1024 | bytes 1024 | tf_op jit(solution)/shard_map/forward_streamed/pallas_call | solution.py:303
  99.5 9.4 %collective-permute-done.25.refs_1_ = bf16[128,4096]{1,0:T(8,128)(2,1)S(1)} collective-permute-done((bf16[128,4096]{1,0:T(8,128)(2,1)S(1)}, bf16[128,4096]{1,0:T(8,128)(2,1)S(1)}, u32[]{:S(2)}, u32[]{:S(2)}) %collective-permute-start.25) | collective-permute-done | bytes 1048608 | tf_op jit(solution)/shard_map/ppermute | solution.py:465
  109.4 5.1 %collective-permute-done.24.refs_1_ = bf16[64,4096]{1,0:T(8,128)(2,1)S(1)} collective-permute-done((bf16[64,4096]{1,0:T(8,128)(2,1)S(1)}, bf16[64,4096]{1,0:T(8,128)(2,1)S(1)}, u32[]{:S(2)}, u32[]{:S(2)}) %collective-permute-start.24) | collective-permute-done | bytes 524320 | tf_op jit(solution)/shard_map/ppermute | solution.py:465
  115.1 1.6 collective-permute-start.30
  116.7 6.8 %collective-permute-done.28.refs_4_ = bf16[128,2048]{1,0:T(8,128)(2,1)S(1)} collective-permute-done((bf16[128,2048]{1,0:T(8,128)(2,1)S(1)}, bf16[128,2048]{1,0:T(8,128)(2,1)S(1)}, u32[]{:S(2)}, u32[]{:S(2)}) %collective-permute-start.28) | collective-permute-done | bytes 524320 | tf_op jit(solution)/shard_map/ppermute | solution.py:465
  123.5 1.7 collective-permute-done.27.refs_3_
  125.8 7.4 %backward_product.4 = (bf16[256,1536]{1,0:T(8,128)(2,1)S(1)}, bf16[256,1536]{1,0:T(8,128)(2,1)S(1)}) custom-call(s32[3]{0:T(128)S(1)} %pad_add_fusion.where_ref, bf16[64,4096]{1,0:T(8,128)(2,1)S(1)} %hidden_grads.2.refs_0_, bf16[64,4096]{1,0:T(8,128)(2,1)S(1)} %collective-permute-done.24.refs_1_, bf16[64,4096]{1,0:T(8,128)(2,1)S(1)} %collective-permute-done.26.refs_2_, ...), custom_call_target="tpu_custom_call" | custom-call | flops 1024 | bytes 1024 | tf_op jit(solution)/shard_map/backward_product/pallas_call | solution.py:382
  133.6 1.0 hidden_grads.3.refs_0_
  135.3 1.5 collective-permute-start.32
  136.8 12.6 %collective-permute-done.31.refs_1_ = bf16[64,4096]{1,0:T(8,128)(2,1)S(1)} collective-permute-done((bf16[64,4096]{1,0:T(8,128)(2,1)S(1)}, bf16[64,4096]{1,0:T(8,128)(2,1)S(1)}, u32[]{:S(2)}, u32[]{:S(2)}) %collective-permute-start.31) | collective-permute-done | bytes 524320 | tf_op jit(solution)/shard_map/ppermute | solution.py:465
  149.4 1.2 collective-permute-start.33
  150.7 3.0 %collective-permute-start.35 = (bf16[256,384]{1,0:T(8,128)(2,1)S(1)}, bf16[256,384]{1,0:T(8,128)(2,1)S(1)}, u32[]{:S(2)}, u32[]{:S(2)}) collective-permute-start(bf16[256,384]{1,0:T(8,128)(2,1)S(1)} %get-tuple-element.266), channel_id=1, source_target_pairs={{0,16},{4,20},{8,24},{12,28},{16,0},{20,4},{24,8},{28,12},{1,17},{... | collective-permute-start | bytes 589832 | tf_op jit(solution)/shard_map/ppermute | solution.py:471
  153.7 3.8 %collective-permute-start.38 = (bf16[256,384]{1,0:T(8,128)(2,1)S(1)}, bf16[256,384]{1,0:T(8,128)(2,1)S(1)}, u32[]{:S(2)}, u32[]{:S(2)}) collective-permute-start(bf16[256,384]{1,0:T(8,128)(2,1)S(1)} %get-tuple-element.279), channel_id=1, source_target_pairs={{0,24},{4,28},{8,0},{12,4},{16,8},{20,12},{24,16},{28,20},{1,25},{... | collective-permute-start | bytes 589832 | tf_op jit(solution)/shard_map/ppermute | solution.py:471
  157.5 9.5 %collective-permute-done.35.refs_0_ = bf16[256,384]{1,0:T(8,128)(2,1)S(1)} collective-permute-done((bf16[256,384]{1,0:T(8,128)(2,1)S(1)}, bf16[256,384]{1,0:T(8,128)(2,1)S(1)}, u32[]{:S(2)}, u32[]{:S(2)}) %collective-permute-start.35) | collective-permute-done | bytes 196640 | tf_op jit(solution)/shard_map/ppermute | solution.py:471
  167.0 2.5 %backward_product.5 = (bf16[256,384]{1,0:T(8,128)(2,1)S(1)}, bf16[256,384]{1,0:T(8,128)(2,1)S(1)}) custom-call(s32[3]{0:T(128)S(1)} %pad_add_fusion.where_ref, bf16[64,4096]{1,0:T(8,128)(2,1)S(1)} %hidden_grads.3.refs_0_, bf16[64,4096]{1,0:T(8,128)(2,1)S(1)} %collective-permute-done.31.refs_1_, bf16[64,4096]{1,0:T(8,128)(2,1)S(1)} %collective-permute-done.32.refs_2_, ...), custom_call_target="tpu_custom_call" | custom-call | flops 1024 | bytes 1024 | tf_op jit(solution)/shard_map/backward_product/pallas_call | solution.py:382
  169.5 4.1 %backward_product.6 = (bf16[256,768]{1,0:T(8,128)(2,1)S(1)}, bf16[256,768]{1,0:T(8,128)(2,1)S(1)}) custom-call(s32[3]{0:T(128)S(1)} %pad_add_fusion.where_ref, bf16[64,4096]{1,0:T(8,128)(2,1)S(1)} %hidden_grads.3.refs_0_, bf16[64,4096]{1,0:T(8,128)(2,1)S(1)} %collective-permute-done.31.refs_1_, bf16[64,4096]{1,0:T(8,128)(2,1)S(1)} %collective-permute-done.32.refs_2_, ...), custom_call_target="tpu_custom_call" | custom-call | flops 1024 | bytes 1024 | tf_op jit(solution)/shard_map/backward_product/pallas_call | solution.py:382
  174.4 1.2 collective-permute-done.39.other_ref
  175.8 3.8 %collective-permute-start.42 = (bf16[256,384]{1,0:T(8,128)(2,1)S(1)}, bf16[256,384]{1,0:T(8,128)(2,1)S(1)}, u32[]{:S(2)}, u32[]{:S(2)}) collective-permute-start(bf16[256,384]{1,0:T(8,128)(2,1)S(1)} %get-tuple-element.304), channel_id=1, source_target_pairs={{0,24},{4,28},{8,0},{12,4},{16,8},{20,12},{24,16},{28,20},{1,25},{... | collective-permute-start | bytes 589832 | tf_op jit(solution)/shard_map/ppermute | solution.py:471
  179.6 2.5 %backward_product.7 = (bf16[256,384]{1,0:T(8,128)(2,1)S(1)}, bf16[256,384]{1,0:T(8,128)(2,1)S(1)}) custom-call(s32[3]{0:T(128)S(1)} %pad_add_fusion.where_ref, bf16[64,4096]{1,0:T(8,128)(2,1)S(1)} %hidden_grads.3.refs_0_, bf16[64,4096]{1,0:T(8,128)(2,1)S(1)} %collective-permute-done.31.refs_1_, bf16[64,4096]{1,0:T(8,128)(2,1)S(1)} %collective-permute-done.32.refs_2_, ...), custom_call_target="tpu_custom_call" | custom-call | flops 1024 | bytes 1024 | tf_op jit(solution)/shard_map/backward_product/pallas_call | solution.py:382
  182.8 5.1 %collective-permute-done.40.refs_1_ = bf16[256,384]{1,0:T(8,128)(2,1)S(1)} collective-permute-done((bf16[256,384]{1,0:T(8,128)(2,1)S(1)}, bf16[256,384]{1,0:T(8,128)(2,1)S(1)}, u32[]{:S(2)}, u32[]{:S(2)}) %collective-permute-start.40) | collective-permute-done | bytes 196640 | tf_op jit(solution)/shard_map/ppermute | solution.py:471
  187.9 3.4 %collective-permute-done.42.refs_3_ = bf16[256,384]{1,0:T(8,128)(2,1)S(1)} collective-permute-done((bf16[256,384]{1,0:T(8,128)(2,1)S(1)}, bf16[256,384]{1,0:T(8,128)(2,1)S(1)}, u32[]{:S(2)}, u32[]{:S(2)}) %collective-permute-start.42) | collective-permute-done | bytes 196640 | tf_op jit(solution)/shard_map/ppermute | solution.py:471
  191.3 1.4 final_sum.3
  (73 shorter events, 14.8 us)
Async XLA Ops:
  1.9 14.1 %collective-permute-start = (bf16[256,384]{1,0:T(8,128)(2,1)S(1)}, bf16[256,384]{1,0:T(8,128)(2,1)S(1)}, u32[]{:S(2)}, u32[]{:S(2)}) collective-permute-start(bf16[256,384]{1,0:T(8,128)(2,1)S(1)} %get-tuple-element.156.own_ref), channel_id=1, source_target_pairs={{0,16},{4,20},{8,24},{12,28},{16,0},{20,4},{24,8},{28,12},{1,17},{... | collective-permute-start | bytes 589832 | tf_op jit(solution)/shard_map/ppermute | solution.py:471
  6.0 10.0 %collective-permute-start.1 = (bf16[256,384]{1,0:T(8,128)(2,1)S(1)}, bf16[256,384]{1,0:T(8,128)(2,1)S(1)}, u32[]{:S(2)}, u32[]{:S(2)}) collective-permute-start(bf16[256,384]{1,0:T(8,128)(2,1)S(1)} %get-tuple-element.156.own_ref), channel_id=1, source_target_pairs={{0,8},{4,12},{8,0},{12,4},{16,24},{20,28},{24,16},{28,20},{1,9},{5... | collective-permute-start | bytes 589832 | tf_op jit(solution)/shard_map/ppermute | solution.py:476
  7.6 20.3 %collective-permute-start.2 = (bf16[256,384]{1,0:T(8,128)(2,1)S(1)}, bf16[256,384]{1,0:T(8,128)(2,1)S(1)}, u32[]{:S(2)}, u32[]{:S(2)}) collective-permute-start(bf16[256,384]{1,0:T(8,128)(2,1)S(1)} %get-tuple-element.156.own_ref), channel_id=1, source_target_pairs={{8,16},{12,20},{16,8},{20,12},{9,17},{13,21},{17,9},{21,13},{10,18... | collective-permute-start | bytes 589832 | tf_op jit(solution)/shard_map/ppermute | solution.py:476
  8.2 0.7 copy-start.1
  8.9 12.4 %copy-start.2 = (f32[24,16]{0,1:T(8,128)S(1)}, f32[24,16]{0,1:T(8,128)}, u32[]{:S(2)}) copy-start(f32[24,16]{0,1:T(8,128)} %param.13) | copy-start | bytes 4612
  16.0 11.9 %collective-permute-start.3 = (bf16[256,384]{1,0:T(8,128)(2,1)S(1)}, bf16[256,384]{1,0:T(8,128)(2,1)S(1)}, u32[]{:S(2)}, u32[]{:S(2)}) collective-permute-start(bf16[256,384]{1,0:T(8,128)(2,1)S(1)} %collective-permute-done.two_ref), channel_id=1, source_target_pairs={{8,0},{12,4},{16,24},{20,28},{9,1},{13,5},{17,25},{21,29},{10,2},{... | collective-permute-start | bytes 589832 | tf_op jit(solution)/shard_map/ppermute | solution.py:476
  17.3 12.7 %collective-permute-start.4 = (bf16[256,384]{1,0:T(8,128)(2,1)S(1)}, bf16[256,384]{1,0:T(8,128)(2,1)S(1)}, u32[]{:S(2)}, u32[]{:S(2)}) collective-permute-start(bf16[256,384]{1,0:T(8,128)(2,1)S(1)} %get-tuple-element.160.own_ref), channel_id=1, source_target_pairs={{0,16},{4,20},{8,24},{12,28},{16,0},{20,4},{24,8},{28,12},{1,17},{... | collective-permute-start | bytes 589832 | tf_op jit(solution)/shard_map/ppermute | solution.py:471
  21.3 10.7 %collective-permute-start.5 = (bf16[256,384]{1,0:T(8,128)(2,1)S(1)}, bf16[256,384]{1,0:T(8,128)(2,1)S(1)}, u32[]{:S(2)}, u32[]{:S(2)}) collective-permute-start(bf16[256,384]{1,0:T(8,128)(2,1)S(1)} %get-tuple-element.160.own_ref), channel_id=1, source_target_pairs={{0,8},{4,12},{8,0},{12,4},{16,24},{20,28},{24,16},{28,20},{1,9},{5... | collective-permute-start | bytes 589832 | tf_op jit(solution)/shard_map/ppermute | solution.py:476
  32.6 17.6 %copy-start = (f32[16,24]{1,0:T(8,128)S(1)}, f32[16,24]{1,0:T(8,128)}, u32[]{:S(2)}) copy-start(f32[16,24]{1,0:T(8,128)} %scale_ref.3) | copy-start | bytes 4612
  32.6 2.4 %collective-permute-start.6 = (bf16[256,1536]{1,0:T(8,128)(2,1)S(1)}, bf16[256,1536]{1,0:T(8,128)(2,1)S(1)}, u32[]{:S(2)}, u32[]{:S(2)}) collective-permute-start(bf16[256,1536]{1,0:T(8,128)(2,1)S(1)} %join.4.refs_0_), channel_id=1, source_target_pairs={{0,4},{4,0},{8,12},{12,8},{16,20},{20,16},{24,28},{28,24},{1,5},{5... | collective-permute-start | bytes 2359304 | tf_op jit(solution)/shard_map/ppermute | solution.py:468
  32.7 9.8 %collective-permute-start.7 = (bf16[256,384]{1,0:T(8,128)(2,1)S(1)}, bf16[256,384]{1,0:T(8,128)(2,1)S(1)}, u32[]{:S(2)}, u32[]{:S(2)}) collective-permute-start(bf16[256,384]{1,0:T(8,128)(2,1)S(1)} %get-tuple-element.160.own_ref), channel_id=1, source_target_pairs={{8,16},{12,20},{16,8},{20,12},{9,17},{13,21},{17,9},{21,13},{10,18... | collective-permute-start | bytes 589832 | tf_op jit(solution)/shard_map/ppermute | solution.py:476
  33.4 10.2 %collective-permute-start.8 = (bf16[256,384]{1,0:T(8,128)(2,1)S(1)}, bf16[256,384]{1,0:T(8,128)(2,1)S(1)}, u32[]{:S(2)}, u32[]{:S(2)}) collective-permute-start(bf16[256,384]{1,0:T(8,128)(2,1)S(1)} %collective-permute-done.4.two_ref), channel_id=1, source_target_pairs={{8,0},{12,4},{16,24},{20,28},{9,1},{13,5},{17,25},{21,29},{10,2},{... | collective-permute-start | bytes 589832 | tf_op jit(solution)/shard_map/ppermute | solution.py:476
  43.6 16.2 %collective-permute-start.10 = (bf16[128,4096]{1,0:T(8,128)(2,1)S(1)}, bf16[128,4096]{1,0:T(8,128)(2,1)S(1)}, u32[]{:S(2)}, u32[]{:S(2)}) collective-permute-start(bf16[128,4096]{1,0:T(8,128)(2,1)S(1)} %get-tuple-element.183), channel_id=1, source_target_pairs={{0,1},{1,0},{2,3},{3,2},{4,6},{5,7},{6,4},{7,5},{8,9},{9,8},{10,11... | collective-permute-start | bytes 3145736 | tf_op jit(solution)/shard_map/ppermute | solution.py:465
  45.7 4.5 %collective-permute-start.9 = (bf16[256,1536]{1,0:T(8,128)(2,1)S(1)}, bf16[256,1536]{1,0:T(8,128)(2,1)S(1)}, u32[]{:S(2)}, u32[]{:S(2)}) collective-permute-start(bf16[256,1536]{1,0:T(8,128)(2,1)S(1)} %join.5.refs_0_), channel_id=1, source_target_pairs={{0,4},{4,0},{8,12},{12,8},{16,20},{20,16},{24,28},{28,24},{1,5},{5... | collective-permute-start | bytes 2359304 | tf_op jit(solution)/shard_map/ppermute | solution.py:468
  45.8 13.7 %collective-permute-start.11 = (bf16[256,384]{1,0:T(8,128)(2,1)S(1)}, bf16[256,384]{1,0:T(8,128)(2,1)S(1)}, u32[]{:S(2)}, u32[]{:S(2)}) collective-permute-start(bf16[256,384]{1,0:T(8,128)(2,1)S(1)} %get-tuple-element.186.own_ref), channel_id=1, source_target_pairs={{0,16},{4,20},{8,24},{12,28},{16,0},{20,4},{24,8},{28,12},{1,17},{... | collective-permute-start | bytes 589832 | tf_op jit(solution)/shard_map/ppermute | solution.py:471
  49.5 10.3 %collective-permute-start.12 = (bf16[256,384]{1,0:T(8,128)(2,1)S(1)}, bf16[256,384]{1,0:T(8,128)(2,1)S(1)}, u32[]{:S(2)}, u32[]{:S(2)}) collective-permute-start(bf16[256,384]{1,0:T(8,128)(2,1)S(1)} %get-tuple-element.186.own_ref), channel_id=1, source_target_pairs={{0,8},{4,12},{8,0},{12,4},{16,24},{20,28},{24,16},{28,20},{1,9},{5... | collective-permute-start | bytes 589832 | tf_op jit(solution)/shard_map/ppermute | solution.py:476
  49.5 15.9 %collective-permute-start.13 = (bf16[256,384]{1,0:T(8,128)(2,1)S(1)}, bf16[256,384]{1,0:T(8,128)(2,1)S(1)}, u32[]{:S(2)}, u32[]{:S(2)}) collective-permute-start(bf16[256,384]{1,0:T(8,128)(2,1)S(1)} %get-tuple-element.186.own_ref), channel_id=1, source_target_pairs={{8,16},{12,20},{16,8},{20,12},{9,17},{13,21},{17,9},{21,13},{10,18... | collective-permute-start | bytes 589832 | tf_op jit(solution)/shard_map/ppermute | solution.py:476
  59.8 13.0 %collective-permute-start.14 = (bf16[256,384]{1,0:T(8,128)(2,1)S(1)}, bf16[256,384]{1,0:T(8,128)(2,1)S(1)}, u32[]{:S(2)}, u32[]{:S(2)}) collective-permute-start(bf16[256,384]{1,0:T(8,128)(2,1)S(1)} %collective-permute-done.11.two_ref), channel_id=1, source_target_pairs={{8,0},{12,4},{16,24},{20,28},{9,1},{13,5},{17,25},{21,29},{10,2},{... | collective-permute-start | bytes 589832 | tf_op jit(solution)/shard_map/ppermute | solution.py:476
  61.1 14.2 %collective-permute-start.17 = (bf16[256,384]{1,0:T(8,128)(2,1)S(1)}, bf16[256,384]{1,0:T(8,128)(2,1)S(1)}, u32[]{:S(2)}, u32[]{:S(2)}) collective-permute-start(bf16[256,384]{1,0:T(8,128)(2,1)S(1)} %get-tuple-element.199.own_ref), channel_id=1, source_target_pairs={{0,16},{4,20},{8,24},{12,28},{16,0},{20,4},{24,8},{28,12},{1,17},{... | collective-permute-start | bytes 589832 | tf_op jit(solution)/shard_map/ppermute | solution.py:471
  64.0 12.3 %collective-permute-start.18 = (bf16[256,384]{1,0:T(8,128)(2,1)S(1)}, bf16[256,384]{1,0:T(8,128)(2,1)S(1)}, u32[]{:S(2)}, u32[]{:S(2)}) collective-permute-start(bf16[256,384]{1,0:T(8,128)(2,1)S(1)} %get-tuple-element.199.own_ref), channel_id=1, source_target_pairs={{0,8},{4,12},{8,0},{12,4},{16,24},{20,28},{24,16},{28,20},{1,9},{5... | collective-permute-start | bytes 589832 | tf_op jit(solution)/shard_map/ppermute | solution.py:476
  64.0 12.3 %collective-permute-start.16 = (bf16[128,2048]{1,0:T(8,128)(2,1)S(1)}, bf16[128,2048]{1,0:T(8,128)(2,1)S(1)}, u32[]{:S(2)}, u32[]{:S(2)}) collective-permute-start(bf16[128,2048]{1,0:T(8,128)(2,1)S(1)} %get-tuple-element.196), channel_id=1, source_target_pairs={{0,1},{1,0},{2,3},{3,2},{4,6},{5,7},{6,4},{7,5},{8,9},{9,8},{10,11... | collective-permute-start | bytes 1572872 | tf_op jit(solution)/shard_map/ppermute | solution.py:465
  73.5 2.8 %collective-permute-start.15 = (bf16[256,1536]{1,0:T(8,128)(2,1)S(1)}, bf16[256,1536]{1,0:T(8,128)(2,1)S(1)}, u32[]{:S(2)}, u32[]{:S(2)}) collective-permute-start(bf16[256,1536]{1,0:T(8,128)(2,1)S(1)} %join.6.refs_0_), channel_id=1, source_target_pairs={{0,4},{4,0},{8,12},{12,8},{16,20},{20,16},{24,28},{28,24},{1,5},{5... | collective-permute-start | bytes 2359304 | tf_op jit(solution)/shard_map/ppermute | solution.py:468
  73.7 13.9 %collective-permute-start.21 = (bf16[64,4096]{1,0:T(8,128)(2,1)S(1)}, bf16[64,4096]{1,0:T(8,128)(2,1)S(1)}, u32[]{:S(2)}, u32[]{:S(2)}) collective-permute-start(bf16[64,4096]{1,0:T(8,128)(2,1)S(1)} %add_convert_fusion.1), channel_id=1, source_target_pairs={{0,2},{1,3},{2,0},{3,1},{4,5},{5,4},{6,7},{7,6},{8,10},{9,11},{10,... | collective-permute-start | bytes 1572872 | tf_op jit(solution)/shard_map/ppermute | solution.py:465
  76.4 11.3 %collective-permute-start.22 = (bf16[64,2048]{1,0:T(8,128)(2,1)S(1)}, bf16[64,2048]{1,0:T(8,128)(2,1)S(1)}, u32[]{:S(2)}, u32[]{:S(2)}) collective-permute-start(bf16[64,2048]{1,0:T(8,128)(2,1)S(1)} %add_convert_fusion.3), channel_id=1, source_target_pairs={{0,2},{1,3},{2,0},{3,1},{4,5},{5,4},{6,7},{7,6},{8,10},{9,11},{10,... | collective-permute-start | bytes 786440 | tf_op jit(solution)/shard_map/ppermute | solution.py:465
  77.9 9.7 %collective-permute-start.19 = (bf16[256,384]{1,0:T(8,128)(2,1)S(1)}, bf16[256,384]{1,0:T(8,128)(2,1)S(1)}, u32[]{:S(2)}, u32[]{:S(2)}) collective-permute-start(bf16[256,384]{1,0:T(8,128)(2,1)S(1)} %get-tuple-element.199.own_ref), channel_id=1, source_target_pairs={{8,16},{12,20},{16,8},{20,12},{9,17},{13,21},{17,9},{21,13},{10,18... | collective-permute-start | bytes 589832 | tf_op jit(solution)/shard_map/ppermute | solution.py:476
  78.6 9.0 %collective-permute-start.20 = (bf16[256,384]{1,0:T(8,128)(2,1)S(1)}, bf16[256,384]{1,0:T(8,128)(2,1)S(1)}, u32[]{:S(2)}, u32[]{:S(2)}) collective-permute-start(bf16[256,384]{1,0:T(8,128)(2,1)S(1)} %collective-permute-done.17.two_ref), channel_id=1, source_target_pairs={{8,0},{12,4},{16,24},{20,28},{9,1},{13,5},{17,25},{21,29},{10,2},{... | collective-permute-start | bytes 589832 | tf_op jit(solution)/shard_map/ppermute | solution.py:476
  88.3 2.4 %collective-permute-start.23 = (bf16[256,1536]{1,0:T(8,128)(2,1)S(1)}, bf16[256,1536]{1,0:T(8,128)(2,1)S(1)}, u32[]{:S(2)}, u32[]{:S(2)}) collective-permute-start(bf16[256,1536]{1,0:T(8,128)(2,1)S(1)} %join.7.refs_0_), channel_id=1, source_target_pairs={{0,4},{4,0},{8,12},{12,8},{16,20},{20,16},{24,28},{28,24},{1,5},{5... | collective-permute-start | bytes 2359304 | tf_op jit(solution)/shard_map/ppermute | solution.py:468
  88.4 20.5 %collective-permute-start.25 = (bf16[128,4096]{1,0:T(8,128)(2,1)S(1)}, bf16[128,4096]{1,0:T(8,128)(2,1)S(1)}, u32[]{:S(2)}, u32[]{:S(2)}) collective-permute-start(bf16[128,4096]{1,0:T(8,128)(2,1)S(1)} %get-tuple-element.232), channel_id=1, source_target_pairs={{0,1},{1,0},{2,3},{3,2},{4,6},{5,7},{6,4},{7,5},{8,9},{9,8},{10,11... | collective-permute-start | bytes 3145736 | tf_op jit(solution)/shard_map/ppermute | solution.py:465
  90.6 23.8 %collective-permute-start.24 = (bf16[64,4096]{1,0:T(8,128)(2,1)S(1)}, bf16[64,4096]{1,0:T(8,128)(2,1)S(1)}, u32[]{:S(2)}, u32[]{:S(2)}) collective-permute-start(bf16[64,4096]{1,0:T(8,128)(2,1)S(1)} %hidden_grads.2.refs_0_), channel_id=1, source_target_pairs={{0,1},{1,0},{2,3},{3,2},{4,6},{5,7},{6,4},{7,5},{8,9},{9,8},{10,11... | collective-permute-start | bytes 1572872 | tf_op jit(solution)/shard_map/ppermute | solution.py:465
  91.5 25.2 %collective-permute-start.26 = (bf16[64,4096]{1,0:T(8,128)(2,1)S(1)}, bf16[64,4096]{1,0:T(8,128)(2,1)S(1)}, u32[]{:S(2)}, u32[]{:S(2)}) collective-permute-start(bf16[64,4096]{1,0:T(8,128)(2,1)S(1)} %hidden_grads.2.refs_0_), channel_id=1, source_target_pairs={{0,2},{1,3},{2,0},{3,1},{4,5},{5,4},{6,7},{7,6},{8,10},{9,11},{10,... | collective-permute-start | bytes 1572872 | tf_op jit(solution)/shard_map/ppermute | solution.py:465
  108.8 14.6 %collective-permute-start.28 = (bf16[128,2048]{1,0:T(8,128)(2,1)S(1)}, bf16[128,2048]{1,0:T(8,128)(2,1)S(1)}, u32[]{:S(2)}, u32[]{:S(2)}) collective-permute-start(bf16[128,2048]{1,0:T(8,128)(2,1)S(1)} %get-tuple-element.238), channel_id=1, source_target_pairs={{0,1},{1,0},{2,3},{3,2},{4,6},{5,7},{6,4},{7,5},{8,9},{9,8},{10,11... | collective-permute-start | bytes 1572872 | tf_op jit(solution)/shard_map/ppermute | solution.py:465
  114.5 10.7 %collective-permute-start.27 = (bf16[64,4096]{1,0:T(8,128)(2,1)S(1)}, bf16[64,4096]{1,0:T(8,128)(2,1)S(1)}, u32[]{:S(2)}, u32[]{:S(2)}) collective-permute-start(bf16[64,4096]{1,0:T(8,128)(2,1)S(1)} %collective-permute-done.24.refs_1_), channel_id=1, source_target_pairs={{0,2},{1,3},{2,0},{3,1},{4,5},{5,4},{6,7},{7,6},{8,10},{9,11},{10,... | collective-permute-start | bytes 1572872 | tf_op jit(solution)/shard_map/ppermute | solution.py:465
  115.1 18.1 %collective-permute-start.30 = (bf16[64,4096]{1,0:T(8,128)(2,1)S(1)}, bf16[64,4096]{1,0:T(8,128)(2,1)S(1)}, u32[]{:S(2)}, u32[]{:S(2)}) collective-permute-start(bf16[64,4096]{1,0:T(8,128)(2,1)S(1)} %add_convert_fusion), channel_id=1, source_target_pairs={{0,2},{1,3},{2,0},{3,1},{4,5},{5,4},{6,7},{7,6},{8,10},{9,11},{10,... | collective-permute-start | bytes 1572872 | tf_op jit(solution)/shard_map/ppermute | solution.py:465
  125.2 8.4 %collective-permute-start.29 = (bf16[64,2048]{1,0:T(8,128)(2,1)S(1)}, bf16[64,2048]{1,0:T(8,128)(2,1)S(1)}, u32[]{:S(2)}, u32[]{:S(2)}) collective-permute-start(bf16[64,2048]{1,0:T(8,128)(2,1)S(1)} %add_convert_fusion.2), channel_id=1, source_target_pairs={{0,2},{1,3},{2,0},{3,1},{4,5},{5,4},{6,7},{7,6},{8,10},{9,11},{10,... | collective-permute-start | bytes 786440 | tf_op jit(solution)/shard_map/ppermute | solution.py:465
  134.6 14.8 %collective-permute-start.31 = (bf16[64,4096]{1,0:T(8,128)(2,1)S(1)}, bf16[64,4096]{1,0:T(8,128)(2,1)S(1)}, u32[]{:S(2)}, u32[]{:S(2)}) collective-permute-start(bf16[64,4096]{1,0:T(8,128)(2,1)S(1)} %hidden_grads.3.refs_0_), channel_id=1, source_target_pairs={{0,1},{1,0},{2,3},{3,2},{4,6},{5,7},{6,4},{7,5},{8,9},{9,8},{10,11... | collective-permute-start | bytes 1572872 | tf_op jit(solution)/shard_map/ppermute | solution.py:465
  135.2 15.4 %collective-permute-start.34 = (bf16[256,1536]{1,0:T(8,128)(2,1)S(1)}, bf16[256,1536]{1,0:T(8,128)(2,1)S(1)}, u32[]{:S(2)}, u32[]{:S(2)}) collective-permute-start(bf16[256,1536]{1,0:T(8,128)(2,1)S(1)} %get-tuple-element.265), channel_id=1, source_target_pairs={{0,4},{4,0},{8,12},{12,8},{16,20},{20,16},{24,28},{28,24},{1,5},{5... | collective-permute-start | bytes 2359304 | tf_op jit(solution)/shard_map/ppermute | solution.py:468
  135.3 22.2 %collective-permute-start.32 = (bf16[64,4096]{1,0:T(8,128)(2,1)S(1)}, bf16[64,4096]{1,0:T(8,128)(2,1)S(1)}, u32[]{:S(2)}, u32[]{:S(2)}) collective-permute-start(bf16[64,4096]{1,0:T(8,128)(2,1)S(1)} %hidden_grads.3.refs_0_), channel_id=1, source_target_pairs={{0,2},{1,3},{2,0},{3,1},{4,5},{5,4},{6,7},{7,6},{8,10},{9,11},{10,... | collective-permute-start | bytes 1572872 | tf_op jit(solution)/shard_map/ppermute | solution.py:465
  149.4 17.6 %collective-permute-start.33 = (bf16[64,4096]{1,0:T(8,128)(2,1)S(1)}, bf16[64,4096]{1,0:T(8,128)(2,1)S(1)}, u32[]{:S(2)}, u32[]{:S(2)}) collective-permute-start(bf16[64,4096]{1,0:T(8,128)(2,1)S(1)} %collective-permute-done.31.refs_1_), channel_id=1, source_target_pairs={{0,2},{1,3},{2,0},{3,1},{4,5},{5,4},{6,7},{7,6},{8,10},{9,11},{10,... | collective-permute-start | bytes 1572872 | tf_op jit(solution)/shard_map/ppermute | solution.py:465
  150.7 16.3 %collective-permute-start.35 = (bf16[256,384]{1,0:T(8,128)(2,1)S(1)}, bf16[256,384]{1,0:T(8,128)(2,1)S(1)}, u32[]{:S(2)}, u32[]{:S(2)}) collective-permute-start(bf16[256,384]{1,0:T(8,128)(2,1)S(1)} %get-tuple-element.266), channel_id=1, source_target_pairs={{0,16},{4,20},{8,24},{12,28},{16,0},{20,4},{24,8},{28,12},{1,17},{... | collective-permute-start | bytes 589832 | tf_op jit(solution)/shard_map/ppermute | solution.py:471
  153.7 20.0 %collective-permute-start.37 = (bf16[256,384]{1,0:T(8,128)(2,1)S(1)}, bf16[256,384]{1,0:T(8,128)(2,1)S(1)}, u32[]{:S(2)}, u32[]{:S(2)}) collective-permute-start(bf16[256,384]{1,0:T(8,128)(2,1)S(1)} %get-tuple-element.278), channel_id=1, source_target_pairs={{0,8},{4,12},{8,16},{12,20},{16,24},{20,28},{24,0},{28,4},{1,9},{5... | collective-permute-start | bytes 589832 | tf_op jit(solution)/shard_map/ppermute | solution.py:471
  153.7 20.0 %collective-permute-start.38 = (bf16[256,384]{1,0:T(8,128)(2,1)S(1)}, bf16[256,384]{1,0:T(8,128)(2,1)S(1)}, u32[]{:S(2)}, u32[]{:S(2)}) collective-permute-start(bf16[256,384]{1,0:T(8,128)(2,1)S(1)} %get-tuple-element.279), channel_id=1, source_target_pairs={{0,24},{4,28},{8,0},{12,4},{16,8},{20,12},{24,16},{28,20},{1,25},{... | collective-permute-start | bytes 589832 | tf_op jit(solution)/shard_map/ppermute | solution.py:471
  169.4 4.2 %collective-permute-start.36 = (bf16[256,384]{1,0:T(8,128)(2,1)S(1)}, bf16[256,384]{1,0:T(8,128)(2,1)S(1)}, u32[]{:S(2)}, u32[]{:S(2)}) collective-permute-start(bf16[256,384]{1,0:T(8,128)(2,1)S(1)} %get-tuple-element.274), channel_id=1, source_target_pairs={{0,4},{4,0},{8,12},{12,8},{16,20},{20,16},{24,28},{28,24},{1,5},{5... | collective-permute-start | bytes 589832 | tf_op jit(solution)/shard_map/ppermute | solution.py:468
  173.7 1.9 collective-permute-start.39
  174.3 13.6 %collective-permute-start.40 = (bf16[256,384]{1,0:T(8,128)(2,1)S(1)}, bf16[256,384]{1,0:T(8,128)(2,1)S(1)}, u32[]{:S(2)}, u32[]{:S(2)}) collective-permute-start(bf16[256,384]{1,0:T(8,128)(2,1)S(1)} %pair_sums.4), channel_id=1, source_target_pairs={{0,16},{4,20},{8,24},{12,28},{16,0},{20,4},{24,8},{28,12},{1,17},{... | collective-permute-start | bytes 589832 | tf_op jit(solution)/shard_map/ppermute | solution.py:471
  175.7 12.2 %collective-permute-start.41 = (bf16[256,384]{1,0:T(8,128)(2,1)S(1)}, bf16[256,384]{1,0:T(8,128)(2,1)S(1)}, u32[]{:S(2)}, u32[]{:S(2)}) collective-permute-start(bf16[256,384]{1,0:T(8,128)(2,1)S(1)} %get-tuple-element.303), channel_id=1, source_target_pairs={{0,8},{4,12},{8,16},{12,20},{16,24},{20,28},{24,0},{28,4},{1,9},{5... | collective-permute-start | bytes 589832 | tf_op jit(solution)/shard_map/ppermute | solution.py:471
  175.8 15.6 %collective-permute-start.42 = (bf16[256,384]{1,0:T(8,128)(2,1)S(1)}, bf16[256,384]{1,0:T(8,128)(2,1)S(1)}, u32[]{:S(2)}, u32[]{:S(2)}) collective-permute-start(bf16[256,384]{1,0:T(8,128)(2,1)S(1)} %get-tuple-element.304), channel_id=1, source_target_pairs={{0,24},{4,28},{8,0},{12,4},{16,8},{20,12},{24,16},{28,20},{1,25},{... | collective-permute-start | bytes 589832 | tf_op jit(solution)/shard_map/ppermute | solution.py:471
  182.0 9.3 %collective-permute-start.43 = (bf16[256,384]{1,0:T(8,128)(2,1)S(1)}, bf16[256,384]{1,0:T(8,128)(2,1)S(1)}, u32[]{:S(2)}, u32[]{:S(2)}) collective-permute-start(bf16[256,384]{1,0:T(8,128)(2,1)S(1)} %get-tuple-element.306), channel_id=1, source_target_pairs={{0,4},{4,0},{8,12},{12,8},{16,20},{20,16},{24,28},{28,24},{1,5},{5... | collective-permute-start | bytes 589832 | tf_op jit(solution)/shard_map/ppermute | solution.py:468

commit v5 on v4

--- a/solution.py
+++ b/solution.py
@@ -611,10 +611,10 @@
 
     early_1, late_1 = start_rows(grad_1)
     hidden_2 = forward_streamed(where, x, down_code, down_scale, groups, width)
-    hidden_2, gate_up_2 = hold((hidden_2, gate_up_2))
+    hidden_2 = hold(hidden_2)
 
     hidden_2 = send(hidden_2)
-    early_1 = hold(early_1)
+    early_1, gate_up_2 = hold((early_1, gate_up_2))
 
     parts_1 = finish_rows(early_1, late_1)
     parts_1, hidden_2 = hold((parts_1, hidden_2))
@@ -628,10 +628,10 @@
     grad_2 = grads(where, terms_of(gate_up_2), terms_of(hidden_2), rows, hidden)
     early_2, late_2 = start_rows(grad_2)
     terms_1 = scatter(partial_1, whole[0])
-    early_2 = hold(early_2)
+    early_2, early = hold((early_2, terms_1[:1]))
     parts_2 = finish_rows(early_2, late_2)
-    parts_2, early = hold((parts_2, terms_1[:1]))
-    terms_1 = [*early, *terms_1[1:]]
+    parts_2, later = hold((parts_2, terms_1[1:2]))
+    terms_1 = [*early, *later, *terms_1[2:]]
 
     terms_2 = []
     partial, before = products(parts_2, parts_of_z[0]), parts_of_z[0]

time: 193 us -> 187 us (0.969)
  waiting for transfers between devices: 72.3 us -> 61.8 us
  starting transfers between devices: 50.7 us -> 53.9 us
    ppermute x14, waiting for transfers between devices: 35.9 us -> 28.4 us  [exchange(): return lax.ppermute(value, ('tp', 'dp'), pairs)]
    ppermute x10, starting transfers between devices: 25.5 us -> 28 us  [along(): lax.ppermute(value, 'tp', [(i, (i + places * CORES) % n_tp) for i in rang...]
  transfers between devices with their start and end apart: 44 -> 44, of which waited for: 20 -> 19; matrix products, arithmetic and copies ran while one was open for 0% -> 0% of each run, Pallas kernels for 33% -> 34%
where the time goes in v5:
time: 187 us; the launch traced here: 186 us
  Pallas kernels  68.2 us (36%)
  waiting for transfers between devices  61.8 us (33%)
  starting transfers between devices  53.9 us (29%)
    ppermute x14, waiting for transfers between devices, exchange(): return lax.ppermute(value, ('tp', 'dp'), pairs)  28.4 us
    ppermute x10, starting transfers between devices, along(): lax.ppermute(value, 'tp', [(i, (i + places * CORES) % n_tp) for i in rang...  28 us
    ppermute x10, waiting for transfers between devices, along(): lax.ppermute(value, 'tp', [(i, (i + places * CORES) % n_tp) for i in rang...  20.6 us
    pallas_call x4, Pallas kernels, backward(): pl.pallas_call(functools.partial(backward_kernel, places, total_places),...  16.4 us
    ppermute x14, starting transfers between devices, exchange(): return lax.ppermute(value, ('tp', 'dp'), pairs)  15 us
    pallas_call x2, Pallas kernels, forward(): pl.pallas_call(functools.partial(forward_kernel, groups, contract, width,...  15 us
    pallas_call x2, Pallas kernels, forward_streamed(): pl.pallas_call(functools.partial(streamed_kernel, groups, width), in_spec...  14.8 us
    pallas_call x2, Pallas kernels, weight(): pl.pallas_call(functools.partial(weight_kernel, turned), in_specs=[pl.Blo...  13.2 us
  transfers between devices with their start and end apart: 44, of which 19 were waited for; matrix products, arithmetic and copies ran while one was open for 0% of the time, Pallas kernels for 34%

profile of v5, /device:TPU:0, one launch (start us, length us, event | category | flops | bytes accessed | tf_op | source)
XLA Modules:
  0.0 185.5 jit_solution(3399213704125250419)
XLA Ops:
  0.1 1.8 order_rows.1
  1.9 4.1 %collective-permute-start = (bf16[256,384]{1,0:T(8,128)(2,1)S(1)}, bf16[256,384]{1,0:T(8,128)(2,1)S(1)}, u32[]{:S(2)}, u32[]{:S(2)}) collective-permute-start(bf16[256,384]{1,0:T(8,128)(2,1)S(1)} %get-tuple-element.157.own_ref), channel_id=1, source_target_pairs={{0,16},{4,20},{8,24},{12,28},{16,0},{20,4},{24,8},{28,12},{1,17},{... | collective-permute-start | bytes 589832 | tf_op jit(solution)/shard_map/ppermute | solution.py:471
  6.0 1.6 collective-permute-start.1
  8.9 6.6 %scaled_weight.3.refs_2_.refs_4_ = bf16[3072,2048]{1,0:T(8,128)(2,1)S(1)} custom-call(bf16[3072,2048]{1,0:T(8,128)(2,1)} %code_ref.3, f32[16,24]{1,0:T(8,128)S(1)} %bitcast.5), custom_call_target="tpu_custom_call" | custom-call | bytes 1536 | tf_op jit(solution)/shard_map/scaled_weight/pallas_call | solution.py:88
  16.0 1.3 collective-permute-start.3
  17.3 4.0 %collective-permute-start.4 = (bf16[256,384]{1,0:T(8,128)(2,1)S(1)}, bf16[256,384]{1,0:T(8,128)(2,1)S(1)}, u32[]{:S(2)}, u32[]{:S(2)}) collective-permute-start(bf16[256,384]{1,0:T(8,128)(2,1)S(1)} %get-tuple-element.161.own_ref), channel_id=1, source_target_pairs={{0,16},{4,20},{8,24},{12,28},{16,0},{20,4},{24,8},{28,12},{1,17},{... | collective-permute-start | bytes 589832 | tf_op jit(solution)/shard_map/ppermute | solution.py:471
  21.3 6.6 %scaled_weight.2.refs_3_.refs_5_ = bf16[3072,2048]{1,0:T(8,128)(2,1)S(1)} custom-call(bf16[3072,2048]{1,0:T(8,128)(2,1)} %code_ref.2, f32[16,24]{1,0:T(8,128)S(1)} %bitcast.6), custom_call_target="tpu_custom_call" | custom-call | bytes 1536 | tf_op jit(solution)/shard_map/scaled_weight/pallas_call | solution.py:88
  27.9 2.1 %collective-permute-done.4.two_ref = bf16[256,384]{1,0:T(8,128)(2,1)S(1)} collective-permute-done((bf16[256,384]{1,0:T(8,128)(2,1)S(1)}, bf16[256,384]{1,0:T(8,128)(2,1)S(1)}, u32[]{:S(2)}, u32[]{:S(2)}) %collective-permute-start.4) | collective-permute-done | bytes 196640 | tf_op jit(solution)/shard_map/ppermute | solution.py:471
  30.0 2.0 %collective-permute-done.5.near_ref = bf16[256,384]{1,0:T(8,128)(2,1)S(1)} collective-permute-done((bf16[256,384]{1,0:T(8,128)(2,1)S(1)}, bf16[256,384]{1,0:T(8,128)(2,1)S(1)}, u32[]{:S(2)}, u32[]{:S(2)}) %collective-permute-start.5) | collective-permute-done | bytes 196640 | tf_op jit(solution)/shard_map/ppermute | solution.py:476
  33.4 1.3 collective-permute-start.8
  35.0 7.5 %forward_product.2 = (bf16[128,4096]{1,0:T(8,128)(2,1)S(1)}, bf16[64,4096]{1,0:T(8,128)(2,1)S(1)}, bf16[64,4096]{1,0:T(8,128)(2,1)S(1)}) custom-call(s32[3]{0:T(128)S(1)} %pad_add_fusion.where_ref, bf16[256,1536]{1,0:T(8,128)(2,1)S(1)} %join.4.refs_0_, bf16[256,1536]{1,0:T(8,128)(2,1)S(1)} %collective-permute-done.6.refs_1_, ...), custom_call_target="tpu_custom_call" | custom-call | flops 1024 | bytes 1024 | tf_op jit(solution)/shard_map/forward_product/pallas_call | solution.py:231
  42.5 1.1 collective-permute-done.8.passed_ref
  43.6 1.5 collective-permute-start.10
  45.8 3.7 %collective-permute-start.11 = (bf16[256,384]{1,0:T(8,128)(2,1)S(1)}, bf16[256,384]{1,0:T(8,128)(2,1)S(1)}, u32[]{:S(2)}, u32[]{:S(2)}) collective-permute-start(bf16[256,384]{1,0:T(8,128)(2,1)S(1)} %get-tuple-element.187.own_ref), channel_id=1, source_target_pairs={{0,16},{4,20},{8,24},{12,28},{16,0},{20,4},{24,8},{28,12},{1,17},{... | collective-permute-start | bytes 589832 | tf_op jit(solution)/shard_map/ppermute | solution.py:471
  50.2 7.4 %forward_streamed.2 = (bf16[128,2048]{1,0:T(8,128)(2,1)S(1)}, bf16[64,2048]{1,0:T(8,128)(2,1)S(1)}, bf16[64,2048]{1,0:T(8,128)(2,1)S(1)}) custom-call(s32[3]{0:T(128)S(1)} %pad_add_fusion.where_ref, f32[16,24]{1,0:T(8,128)S(1)} %copy-done, bf16[256,1536]{1,0:T(8,128)(2,1)S(1)} %join.5.refs_0_, bf16[256,1536]{1,0:T(8,128)(2,1)S(1)} %collective-permute-done.9.refs_1_, ...), custom_call_target="tpu_custom_call" | custom-call | flops 1024 | bytes 1024 | tf_op jit(solution)/shard_map/forward_streamed/pallas_call | solution.py:303
  57.7 1.9 %collective-permute-done.11.two_ref = bf16[256,384]{1,0:T(8,128)(2,1)S(1)} collective-permute-done((bf16[256,384]{1,0:T(8,128)(2,1)S(1)}, bf16[256,384]{1,0:T(8,128)(2,1)S(1)}, u32[]{:S(2)}, u32[]{:S(2)}) %collective-permute-start.11) | collective-permute-done | bytes 196640 | tf_op jit(solution)/shard_map/ppermute | solution.py:471
  59.8 1.3 collective-permute-start.14
  61.1 2.9 %collective-permute-start.17 = (bf16[256,384]{1,0:T(8,128)(2,1)S(1)}, bf16[256,384]{1,0:T(8,128)(2,1)S(1)}, u32[]{:S(2)}, u32[]{:S(2)}) collective-permute-start(bf16[256,384]{1,0:T(8,128)(2,1)S(1)} %get-tuple-element.200.own_ref), channel_id=1, source_target_pairs={{0,16},{4,20},{8,24},{12,28},{16,0},{20,4},{24,8},{28,12},{1,17},{... | collective-permute-start | bytes 589832 | tf_op jit(solution)/shard_map/ppermute | solution.py:471
  64.0 1.4 collective-permute-start.16
  65.4 7.4 %collective-permute-done.14.passed_ref = bf16[256,384]{1,0:T(8,128)(2,1)S(1)} collective-permute-done((bf16[256,384]{1,0:T(8,128)(2,1)S(1)}, bf16[256,384]{1,0:T(8,128)(2,1)S(1)}, u32[]{:S(2)}, u32[]{:S(2)}) %collective-permute-start.14) | collective-permute-done | bytes 196640 | tf_op jit(solution)/shard_map/ppermute | solution.py:476
  73.7 1.6 collective-permute-start.21
  75.3 1.0 collective-permute-done.18.near_ref
  76.4 1.6 collective-permute-start.22
  78.6 1.5 collective-permute-start.20
  80.1 7.5 %forward_product.3 = (bf16[128,4096]{1,0:T(8,128)(2,1)S(1)}, bf16[64,4096]{1,0:T(8,128)(2,1)S(1)}, bf16[64,4096]{1,0:T(8,128)(2,1)S(1)}) custom-call(s32[3]{0:T(128)S(1)} %pad_add_fusion.where_ref, bf16[256,1536]{1,0:T(8,128)(2,1)S(1)} %join.6.refs_0_, bf16[256,1536]{1,0:T(8,128)(2,1)S(1)} %collective-permute-done.15.refs_1_, ...), custom_call_target="tpu_custom_call" | custom-call | flops 1024 | bytes 1024 | tf_op jit(solution)/shard_map/forward_product/pallas_call | solution.py:231
  89.0 1.0 hidden_grads.2.refs_0_
  92.0 7.4 %forward_streamed.3 = (bf16[128,2048]{1,0:T(8,128)(2,1)S(1)}, bf16[64,2048]{1,0:T(8,128)(2,1)S(1)}, bf16[64,2048]{1,0:T(8,128)(2,1)S(1)}) custom-call(s32[3]{0:T(128)S(1)} %pad_add_fusion.where_ref, f32[16,24]{1,0:T(8,128)S(1)} %copy-done, bf16[256,1536]{1,0:T(8,128)(2,1)S(1)} %join.7.refs_0_, bf16[256,1536]{1,0:T(8,128)(2,1)S(1)} %collective-permute-done.23.refs_1_, ...), custom_call_target="tpu_custom_call" | custom-call | flops 1024 | bytes 1024 | tf_op jit(solution)/shard_map/forward_streamed/pallas_call | solution.py:303
  99.5 1.2 collective-permute-start.28
  100.7 8.2 %collective-permute-done.25.refs_1_ = bf16[128,4096]{1,0:T(8,128)(2,1)S(1)} collective-permute-done((bf16[128,4096]{1,0:T(8,128)(2,1)S(1)}, bf16[128,4096]{1,0:T(8,128)(2,1)S(1)}, u32[]{:S(2)}, u32[]{:S(2)}) %collective-permute-start.25) | collective-permute-done | bytes 1048608 | tf_op jit(solution)/shard_map/ppermute | solution.py:465
  108.8 5.6 %collective-permute-done.24.refs_1_ = bf16[64,4096]{1,0:T(8,128)(2,1)S(1)} collective-permute-done((bf16[64,4096]{1,0:T(8,128)(2,1)S(1)}, bf16[64,4096]{1,0:T(8,128)(2,1)S(1)}, u32[]{:S(2)}, u32[]{:S(2)}) %collective-permute-start.24) | collective-permute-done | bytes 524320 | tf_op jit(solution)/shard_map/ppermute | solution.py:465
  115.1 1.6 collective-permute-start.30
  116.7 6.8 %collective-permute-done.28.refs_4_ = bf16[128,2048]{1,0:T(8,128)(2,1)S(1)} collective-permute-done((bf16[128,2048]{1,0:T(8,128)(2,1)S(1)}, bf16[128,2048]{1,0:T(8,128)(2,1)S(1)}, u32[]{:S(2)}, u32[]{:S(2)}) %collective-permute-start.28) | collective-permute-done | bytes 524320 | tf_op jit(solution)/shard_map/ppermute | solution.py:465
  123.5 1.7 collective-permute-done.27.refs_3_
  125.8 7.4 %backward_product.4 = (bf16[256,1536]{1,0:T(8,128)(2,1)S(1)}, bf16[256,1536]{1,0:T(8,128)(2,1)S(1)}) custom-call(s32[3]{0:T(128)S(1)} %pad_add_fusion.where_ref, bf16[64,4096]{1,0:T(8,128)(2,1)S(1)} %hidden_grads.2.refs_0_, bf16[64,4096]{1,0:T(8,128)(2,1)S(1)} %collective-permute-done.24.refs_1_, bf16[64,4096]{1,0:T(8,128)(2,1)S(1)} %collective-permute-done.26.refs_2_, ...), custom_call_target="tpu_custom_call" | custom-call | flops 1024 | bytes 1024 | tf_op jit(solution)/shard_map/backward_product/pallas_call | solution.py:382
  133.9 1.0 hidden_grads.3.refs_0_
  134.9 1.3 collective-permute-start.31
  136.4 3.2 %collective-permute-start.33 = (bf16[256,384]{1,0:T(8,128)(2,1)S(1)}, bf16[256,384]{1,0:T(8,128)(2,1)S(1)}, u32[]{:S(2)}, u32[]{:S(2)}) collective-permute-start(bf16[256,384]{1,0:T(8,128)(2,1)S(1)} %get-tuple-element.265), channel_id=1, source_target_pairs={{0,16},{4,20},{8,24},{12,28},{16,0},{20,4},{24,8},{28,12},{1,17},{... | collective-permute-start | bytes 589832 | tf_op jit(solution)/shard_map/ppermute | solution.py:471
  140.5 5.8 %collective-permute-done.31.refs_1_ = bf16[64,4096]{1,0:T(8,128)(2,1)S(1)} collective-permute-done((bf16[64,4096]{1,0:T(8,128)(2,1)S(1)}, bf16[64,4096]{1,0:T(8,128)(2,1)S(1)}, u32[]{:S(2)}, u32[]{:S(2)}) %collective-permute-start.31) | collective-permute-done | bytes 524320 | tf_op jit(solution)/shard_map/ppermute | solution.py:465
  146.3 2.7 %collective-permute-done.33.refs_0_ = bf16[256,384]{1,0:T(8,128)(2,1)S(1)} collective-permute-done((bf16[256,384]{1,0:T(8,128)(2,1)S(1)}, bf16[256,384]{1,0:T(8,128)(2,1)S(1)}, u32[]{:S(2)}, u32[]{:S(2)}) %collective-permute-start.33) | collective-permute-done | bytes 196640 | tf_op jit(solution)/shard_map/ppermute | solution.py:471
  149.9 2.9 %collective-permute-start.36 = (bf16[256,384]{1,0:T(8,128)(2,1)S(1)}, bf16[256,384]{1,0:T(8,128)(2,1)S(1)}, u32[]{:S(2)}, u32[]{:S(2)}) collective-permute-start(bf16[256,384]{1,0:T(8,128)(2,1)S(1)} %get-tuple-element.268), channel_id=1, source_target_pairs={{0,8},{4,12},{8,16},{12,20},{16,24},{20,28},{24,0},{28,4},{1,9},{5... | collective-permute-start | bytes 589832 | tf_op jit(solution)/shard_map/ppermute | solution.py:471
  153.7 5.8 %collective-permute-done.36.refs_1_ = bf16[256,384]{1,0:T(8,128)(2,1)S(1)} collective-permute-done((bf16[256,384]{1,0:T(8,128)(2,1)S(1)}, bf16[256,384]{1,0:T(8,128)(2,1)S(1)}, u32[]{:S(2)}, u32[]{:S(2)}) %collective-permute-start.36) | collective-permute-done | bytes 196640 | tf_op jit(solution)/shard_map/ppermute | solution.py:471
  159.5 2.5 %backward_product.5 = (bf16[256,384]{1,0:T(8,128)(2,1)S(1)}, bf16[256,384]{1,0:T(8,128)(2,1)S(1)}) custom-call(s32[3]{0:T(128)S(1)} %pad_add_fusion.where_ref, bf16[64,4096]{1,0:T(8,128)(2,1)S(1)} %hidden_grads.3.refs_0_, bf16[64,4096]{1,0:T(8,128)(2,1)S(1)} %collective-permute-done.31.refs_1_, bf16[64,4096]{1,0:T(8,128)(2,1)S(1)} %collective-permute-done.34.refs_2_, ...), custom_call_target="tpu_custom_call" | custom-call | flops 1024 | bytes 1024 | tf_op jit(solution)/shard_map/backward_product/pallas_call | solution.py:382
  162.1 4.1 %backward_product.6 = (bf16[256,768]{1,0:T(8,128)(2,1)S(1)}, bf16[256,768]{1,0:T(8,128)(2,1)S(1)}) custom-call(s32[3]{0:T(128)S(1)} %pad_add_fusion.where_ref, bf16[64,4096]{1,0:T(8,128)(2,1)S(1)} %hidden_grads.3.refs_0_, bf16[64,4096]{1,0:T(8,128)(2,1)S(1)} %collective-permute-done.31.refs_1_, bf16[64,4096]{1,0:T(8,128)(2,1)S(1)} %collective-permute-done.34.refs_2_, ...), custom_call_target="tpu_custom_call" | custom-call | flops 1024 | bytes 1024 | tf_op jit(solution)/shard_map/backward_product/pallas_call | solution.py:382
  166.8 2.4 %collective-permute-start.40 = (bf16[256,384]{1,0:T(8,128)(2,1)S(1)}, bf16[256,384]{1,0:T(8,128)(2,1)S(1)}, u32[]{:S(2)}, u32[]{:S(2)}) collective-permute-start(bf16[256,384]{1,0:T(8,128)(2,1)S(1)} %pair_sums.4), channel_id=1, source_target_pairs={{0,16},{4,20},{8,24},{12,28},{16,0},{20,4},{24,8},{28,12},{1,17},{... | collective-permute-start | bytes 589832 | tf_op jit(solution)/shard_map/ppermute | solution.py:471
  169.9 3.2 %collective-permute-start.42 = (bf16[256,384]{1,0:T(8,128)(2,1)S(1)}, bf16[256,384]{1,0:T(8,128)(2,1)S(1)}, u32[]{:S(2)}, u32[]{:S(2)}) collective-permute-start(bf16[256,384]{1,0:T(8,128)(2,1)S(1)} %get-tuple-element.306), channel_id=1, source_target_pairs={{0,24},{4,28},{8,0},{12,4},{16,8},{20,12},{24,16},{28,20},{1,25},{... | collective-permute-start | bytes 589832 | tf_op jit(solution)/shard_map/ppermute | solution.py:471
  173.2 2.5 %backward_product.7 = (bf16[256,384]{1,0:T(8,128)(2,1)S(1)}, bf16[256,384]{1,0:T(8,128)(2,1)S(1)}) custom-call(s32[3]{0:T(128)S(1)} %pad_add_fusion.where_ref, bf16[64,4096]{1,0:T(8,128)(2,1)S(1)} %hidden_grads.3.refs_0_, bf16[64,4096]{1,0:T(8,128)(2,1)S(1)} %collective-permute-done.31.refs_1_, bf16[64,4096]{1,0:T(8,128)(2,1)S(1)} %collective-permute-done.34.refs_2_, ...), custom_call_target="tpu_custom_call" | custom-call | flops 1024 | bytes 1024 | tf_op jit(solution)/shard_map/backward_product/pallas_call | solution.py:382
  176.4 7.6 %collective-permute-done.40.refs_1_ = bf16[256,384]{1,0:T(8,128)(2,1)S(1)} collective-permute-done((bf16[256,384]{1,0:T(8,128)(2,1)S(1)}, bf16[256,384]{1,0:T(8,128)(2,1)S(1)}, u32[]{:S(2)}, u32[]{:S(2)}) %collective-permute-start.40) | collective-permute-done | bytes 196640 | tf_op jit(solution)/shard_map/ppermute | solution.py:471
  184.1 1.4 final_sum.3
  (73 shorter events, 17.2 us)
Async XLA Ops:
  1.9 14.1 %collective-permute-start = (bf16[256,384]{1,0:T(8,128)(2,1)S(1)}, bf16[256,384]{1,0:T(8,128)(2,1)S(1)}, u32[]{:S(2)}, u32[]{:S(2)}) collective-permute-start(bf16[256,384]{1,0:T(8,128)(2,1)S(1)} %get-tuple-element.157.own_ref), channel_id=1, source_target_pairs={{0,16},{4,20},{8,24},{12,28},{16,0},{20,4},{24,8},{28,12},{1,17},{... | collective-permute-start | bytes 589832 | tf_op jit(solution)/shard_map/ppermute | solution.py:471
  6.0 10.0 %collective-permute-start.1 = (bf16[256,384]{1,0:T(8,128)(2,1)S(1)}, bf16[256,384]{1,0:T(8,128)(2,1)S(1)}, u32[]{:S(2)}, u32[]{:S(2)}) collective-permute-start(bf16[256,384]{1,0:T(8,128)(2,1)S(1)} %get-tuple-element.157.own_ref), channel_id=1, source_target_pairs={{0,8},{4,12},{8,0},{12,4},{16,24},{20,28},{24,16},{28,20},{1,9},{5... | collective-permute-start | bytes 589832 | tf_op jit(solution)/shard_map/ppermute | solution.py:476
  7.6 20.3 %collective-permute-start.2 = (bf16[256,384]{1,0:T(8,128)(2,1)S(1)}, bf16[256,384]{1,0:T(8,128)(2,1)S(1)}, u32[]{:S(2)}, u32[]{:S(2)}) collective-permute-start(bf16[256,384]{1,0:T(8,128)(2,1)S(1)} %get-tuple-element.157.own_ref), channel_id=1, source_target_pairs={{8,16},{12,20},{16,8},{20,12},{9,17},{13,21},{17,9},{21,13},{10,18... | collective-permute-start | bytes 589832 | tf_op jit(solution)/shard_map/ppermute | solution.py:476
  8.2 0.7 copy-start.1
  8.9 12.4 %copy-start.2 = (f32[24,16]{0,1:T(8,128)S(1)}, f32[24,16]{0,1:T(8,128)}, u32[]{:S(2)}) copy-start(f32[24,16]{0,1:T(8,128)} %param.13) | copy-start | bytes 4612
  16.0 11.9 %collective-permute-start.3 = (bf16[256,384]{1,0:T(8,128)(2,1)S(1)}, bf16[256,384]{1,0:T(8,128)(2,1)S(1)}, u32[]{:S(2)}, u32[]{:S(2)}) collective-permute-start(bf16[256,384]{1,0:T(8,128)(2,1)S(1)} %collective-permute-done.two_ref), channel_id=1, source_target_pairs={{8,0},{12,4},{16,24},{20,28},{9,1},{13,5},{17,25},{21,29},{10,2},{... | collective-permute-start | bytes 589832 | tf_op jit(solution)/shard_map/ppermute | solution.py:476
  17.3 12.7 %collective-permute-start.4 = (bf16[256,384]{1,0:T(8,128)(2,1)S(1)}, bf16[256,384]{1,0:T(8,128)(2,1)S(1)}, u32[]{:S(2)}, u32[]{:S(2)}) collective-permute-start(bf16[256,384]{1,0:T(8,128)(2,1)S(1)} %get-tuple-element.161.own_ref), channel_id=1, source_target_pairs={{0,16},{4,20},{8,24},{12,28},{16,0},{20,4},{24,8},{28,12},{1,17},{... | collective-permute-start | bytes 589832 | tf_op jit(solution)/shard_map/ppermute | solution.py:471
  21.3 10.7 %collective-permute-start.5 = (bf16[256,384]{1,0:T(8,128)(2,1)S(1)}, bf16[256,384]{1,0:T(8,128)(2,1)S(1)}, u32[]{:S(2)}, u32[]{:S(2)}) collective-permute-start(bf16[256,384]{1,0:T(8,128)(2,1)S(1)} %get-tuple-element.161.own_ref), channel_id=1, source_target_pairs={{0,8},{4,12},{8,0},{12,4},{16,24},{20,28},{24,16},{28,20},{1,9},{5... | collective-permute-start | bytes 589832 | tf_op jit(solution)/shard_map/ppermute | solution.py:476
  32.6 17.6 %copy-start = (f32[16,24]{1,0:T(8,128)S(1)}, f32[16,24]{1,0:T(8,128)}, u32[]{:S(2)}) copy-start(f32[16,24]{1,0:T(8,128)} %scale_ref.3) | copy-start | bytes 4612
  32.6 2.4 %collective-permute-start.6 = (bf16[256,1536]{1,0:T(8,128)(2,1)S(1)}, bf16[256,1536]{1,0:T(8,128)(2,1)S(1)}, u32[]{:S(2)}, u32[]{:S(2)}) collective-permute-start(bf16[256,1536]{1,0:T(8,128)(2,1)S(1)} %join.4.refs_0_), channel_id=1, source_target_pairs={{0,4},{4,0},{8,12},{12,8},{16,20},{20,16},{24,28},{28,24},{1,5},{5... | collective-permute-start | bytes 2359304 | tf_op jit(solution)/shard_map/ppermute | solution.py:468
  32.7 9.8 %collective-permute-start.7 = (bf16[256,384]{1,0:T(8,128)(2,1)S(1)}, bf16[256,384]{1,0:T(8,128)(2,1)S(1)}, u32[]{:S(2)}, u32[]{:S(2)}) collective-permute-start(bf16[256,384]{1,0:T(8,128)(2,1)S(1)} %get-tuple-element.161.own_ref), channel_id=1, source_target_pairs={{8,16},{12,20},{16,8},{20,12},{9,17},{13,21},{17,9},{21,13},{10,18... | collective-permute-start | bytes 589832 | tf_op jit(solution)/shard_map/ppermute | solution.py:476
  33.4 10.2 %collective-permute-start.8 = (bf16[256,384]{1,0:T(8,128)(2,1)S(1)}, bf16[256,384]{1,0:T(8,128)(2,1)S(1)}, u32[]{:S(2)}, u32[]{:S(2)}) collective-permute-start(bf16[256,384]{1,0:T(8,128)(2,1)S(1)} %collective-permute-done.4.two_ref), channel_id=1, source_target_pairs={{8,0},{12,4},{16,24},{20,28},{9,1},{13,5},{17,25},{21,29},{10,2},{... | collective-permute-start | bytes 589832 | tf_op jit(solution)/shard_map/ppermute | solution.py:476
  43.6 16.2 %collective-permute-start.10 = (bf16[128,4096]{1,0:T(8,128)(2,1)S(1)}, bf16[128,4096]{1,0:T(8,128)(2,1)S(1)}, u32[]{:S(2)}, u32[]{:S(2)}) collective-permute-start(bf16[128,4096]{1,0:T(8,128)(2,1)S(1)} %get-tuple-element.184), channel_id=1, source_target_pairs={{0,1},{1,0},{2,3},{3,2},{4,6},{5,7},{6,4},{7,5},{8,9},{9,8},{10,11... | collective-permute-start | bytes 3145736 | tf_op jit(solution)/shard_map/ppermute | solution.py:465
  45.7 4.5 %collective-permute-start.9 = (bf16[256,1536]{1,0:T(8,128)(2,1)S(1)}, bf16[256,1536]{1,0:T(8,128)(2,1)S(1)}, u32[]{:S(2)}, u32[]{:S(2)}) collective-permute-start(bf16[256,1536]{1,0:T(8,128)(2,1)S(1)} %join.5.refs_0_), channel_id=1, source_target_pairs={{0,4},{4,0},{8,12},{12,8},{16,20},{20,16},{24,28},{28,24},{1,5},{5... | collective-permute-start | bytes 2359304 | tf_op jit(solution)/shard_map/ppermute | solution.py:468
  45.8 13.7 %collective-permute-start.11 = (bf16[256,384]{1,0:T(8,128)(2,1)S(1)}, bf16[256,384]{1,0:T(8,128)(2,1)S(1)}, u32[]{:S(2)}, u32[]{:S(2)}) collective-permute-start(bf16[256,384]{1,0:T(8,128)(2,1)S(1)} %get-tuple-element.187.own_ref), channel_id=1, source_target_pairs={{0,16},{4,20},{8,24},{12,28},{16,0},{20,4},{24,8},{28,12},{1,17},{... | collective-permute-start | bytes 589832 | tf_op jit(solution)/shard_map/ppermute | solution.py:471
  49.5 10.3 %collective-permute-start.12 = (bf16[256,384]{1,0:T(8,128)(2,1)S(1)}, bf16[256,384]{1,0:T(8,128)(2,1)S(1)}, u32[]{:S(2)}, u32[]{:S(2)}) collective-permute-start(bf16[256,384]{1,0:T(8,128)(2,1)S(1)} %get-tuple-element.187.own_ref), channel_id=1, source_target_pairs={{0,8},{4,12},{8,0},{12,4},{16,24},{20,28},{24,16},{28,20},{1,9},{5... | collective-permute-start | bytes 589832 | tf_op jit(solution)/shard_map/ppermute | solution.py:476
  49.5 15.9 %collective-permute-start.13 = (bf16[256,384]{1,0:T(8,128)(2,1)S(1)}, bf16[256,384]{1,0:T(8,128)(2,1)S(1)}, u32[]{:S(2)}, u32[]{:S(2)}) collective-permute-start(bf16[256,384]{1,0:T(8,128)(2,1)S(1)} %get-tuple-element.187.own_ref), channel_id=1, source_target_pairs={{8,16},{12,20},{16,8},{20,12},{9,17},{13,21},{17,9},{21,13},{10,18... | collective-permute-start | bytes 589832 | tf_op jit(solution)/shard_map/ppermute | solution.py:476
  59.8 13.0 %collective-permute-start.14 = (bf16[256,384]{1,0:T(8,128)(2,1)S(1)}, bf16[256,384]{1,0:T(8,128)(2,1)S(1)}, u32[]{:S(2)}, u32[]{:S(2)}) collective-permute-start(bf16[256,384]{1,0:T(8,128)(2,1)S(1)} %collective-permute-done.11.two_ref), channel_id=1, source_target_pairs={{8,0},{12,4},{16,24},{20,28},{9,1},{13,5},{17,25},{21,29},{10,2},{... | collective-permute-start | bytes 589832 | tf_op jit(solution)/shard_map/ppermute | solution.py:476
  61.1 14.2 %collective-permute-start.17 = (bf16[256,384]{1,0:T(8,128)(2,1)S(1)}, bf16[256,384]{1,0:T(8,128)(2,1)S(1)}, u32[]{:S(2)}, u32[]{:S(2)}) collective-permute-start(bf16[256,384]{1,0:T(8,128)(2,1)S(1)} %get-tuple-element.200.own_ref), channel_id=1, source_target_pairs={{0,16},{4,20},{8,24},{12,28},{16,0},{20,4},{24,8},{28,12},{1,17},{... | collective-permute-start | bytes 589832 | tf_op jit(solution)/shard_map/ppermute | solution.py:471
  64.0 12.3 %collective-permute-start.18 = (bf16[256,384]{1,0:T(8,128)(2,1)S(1)}, bf16[256,384]{1,0:T(8,128)(2,1)S(1)}, u32[]{:S(2)}, u32[]{:S(2)}) collective-permute-start(bf16[256,384]{1,0:T(8,128)(2,1)S(1)} %get-tuple-element.200.own_ref), channel_id=1, source_target_pairs={{0,8},{4,12},{8,0},{12,4},{16,24},{20,28},{24,16},{28,20},{1,9},{5... | collective-permute-start | bytes 589832 | tf_op jit(solution)/shard_map/ppermute | solution.py:476
  64.0 12.3 %collective-permute-start.16 = (bf16[128,2048]{1,0:T(8,128)(2,1)S(1)}, bf16[128,2048]{1,0:T(8,128)(2,1)S(1)}, u32[]{:S(2)}, u32[]{:S(2)}) collective-permute-start(bf16[128,2048]{1,0:T(8,128)(2,1)S(1)} %get-tuple-element.197), channel_id=1, source_target_pairs={{0,1},{1,0},{2,3},{3,2},{4,6},{5,7},{6,4},{7,5},{8,9},{9,8},{10,11... | collective-permute-start | bytes 1572872 | tf_op jit(solution)/shard_map/ppermute | solution.py:465
  73.5 2.8 %collective-permute-start.15 = (bf16[256,1536]{1,0:T(8,128)(2,1)S(1)}, bf16[256,1536]{1,0:T(8,128)(2,1)S(1)}, u32[]{:S(2)}, u32[]{:S(2)}) collective-permute-start(bf16[256,1536]{1,0:T(8,128)(2,1)S(1)} %join.6.refs_0_), channel_id=1, source_target_pairs={{0,4},{4,0},{8,12},{12,8},{16,20},{20,16},{24,28},{28,24},{1,5},{5... | collective-permute-start | bytes 2359304 | tf_op jit(solution)/shard_map/ppermute | solution.py:468
  73.7 13.9 %collective-permute-start.21 = (bf16[64,4096]{1,0:T(8,128)(2,1)S(1)}, bf16[64,4096]{1,0:T(8,128)(2,1)S(1)}, u32[]{:S(2)}, u32[]{:S(2)}) collective-permute-start(bf16[64,4096]{1,0:T(8,128)(2,1)S(1)} %add_convert_fusion.1), channel_id=1, source_target_pairs={{0,2},{1,3},{2,0},{3,1},{4,5},{5,4},{6,7},{7,6},{8,10},{9,11},{10,... | collective-permute-start | bytes 1572872 | tf_op jit(solution)/shard_map/ppermute | solution.py:465
  76.4 11.3 %collective-permute-start.22 = (bf16[64,2048]{1,0:T(8,128)(2,1)S(1)}, bf16[64,2048]{1,0:T(8,128)(2,1)S(1)}, u32[]{:S(2)}, u32[]{:S(2)}) collective-permute-start(bf16[64,2048]{1,0:T(8,128)(2,1)S(1)} %add_convert_fusion.3), channel_id=1, source_target_pairs={{0,2},{1,3},{2,0},{3,1},{4,5},{5,4},{6,7},{7,6},{8,10},{9,11},{10,... | collective-permute-start | bytes 786440 | tf_op jit(solution)/shard_map/ppermute | solution.py:465
  77.9 9.7 %collective-permute-start.19 = (bf16[256,384]{1,0:T(8,128)(2,1)S(1)}, bf16[256,384]{1,0:T(8,128)(2,1)S(1)}, u32[]{:S(2)}, u32[]{:S(2)}) collective-permute-start(bf16[256,384]{1,0:T(8,128)(2,1)S(1)} %get-tuple-element.200.own_ref), channel_id=1, source_target_pairs={{8,16},{12,20},{16,8},{20,12},{9,17},{13,21},{17,9},{21,13},{10,18... | collective-permute-start | bytes 589832 | tf_op jit(solution)/shard_map/ppermute | solution.py:476
  78.6 9.0 %collective-permute-start.20 = (bf16[256,384]{1,0:T(8,128)(2,1)S(1)}, bf16[256,384]{1,0:T(8,128)(2,1)S(1)}, u32[]{:S(2)}, u32[]{:S(2)}) collective-permute-start(bf16[256,384]{1,0:T(8,128)(2,1)S(1)} %collective-permute-done.17.two_ref), channel_id=1, source_target_pairs={{8,0},{12,4},{16,24},{20,28},{9,1},{13,5},{17,25},{21,29},{10,2},{... | collective-permute-start | bytes 589832 | tf_op jit(solution)/shard_map/ppermute | solution.py:476
  88.3 2.4 %collective-permute-start.23 = (bf16[256,1536]{1,0:T(8,128)(2,1)S(1)}, bf16[256,1536]{1,0:T(8,128)(2,1)S(1)}, u32[]{:S(2)}, u32[]{:S(2)}) collective-permute-start(bf16[256,1536]{1,0:T(8,128)(2,1)S(1)} %join.7.refs_0_), channel_id=1, source_target_pairs={{0,4},{4,0},{8,12},{12,8},{16,20},{20,16},{24,28},{28,24},{1,5},{5... | collective-permute-start | bytes 2359304 | tf_op jit(solution)/shard_map/ppermute | solution.py:468
  88.4 20.5 %collective-permute-start.25 = (bf16[128,4096]{1,0:T(8,128)(2,1)S(1)}, bf16[128,4096]{1,0:T(8,128)(2,1)S(1)}, u32[]{:S(2)}, u32[]{:S(2)}) collective-permute-start(bf16[128,4096]{1,0:T(8,128)(2,1)S(1)} %get-tuple-element.227), channel_id=1, source_target_pairs={{0,1},{1,0},{2,3},{3,2},{4,6},{5,7},{6,4},{7,5},{8,9},{9,8},{10,11... | collective-permute-start | bytes 3145736 | tf_op jit(solution)/shard_map/ppermute | solution.py:465
  90.6 23.8 %collective-permute-start.24 = (bf16[64,4096]{1,0:T(8,128)(2,1)S(1)}, bf16[64,4096]{1,0:T(8,128)(2,1)S(1)}, u32[]{:S(2)}, u32[]{:S(2)}) collective-permute-start(bf16[64,4096]{1,0:T(8,128)(2,1)S(1)} %hidden_grads.2.refs_0_), channel_id=1, source_target_pairs={{0,1},{1,0},{2,3},{3,2},{4,6},{5,7},{6,4},{7,5},{8,9},{9,8},{10,11... | collective-permute-start | bytes 1572872 | tf_op jit(solution)/shard_map/ppermute | solution.py:465
  91.5 25.2 %collective-permute-start.26 = (bf16[64,4096]{1,0:T(8,128)(2,1)S(1)}, bf16[64,4096]{1,0:T(8,128)(2,1)S(1)}, u32[]{:S(2)}, u32[]{:S(2)}) collective-permute-start(bf16[64,4096]{1,0:T(8,128)(2,1)S(1)} %hidden_grads.2.refs_0_), channel_id=1, source_target_pairs={{0,2},{1,3},{2,0},{3,1},{4,5},{5,4},{6,7},{7,6},{8,10},{9,11},{10,... | collective-permute-start | bytes 1572872 | tf_op jit(solution)/shard_map/ppermute | solution.py:465
  99.5 24.0 %collective-permute-start.28 = (bf16[128,2048]{1,0:T(8,128)(2,1)S(1)}, bf16[128,2048]{1,0:T(8,128)(2,1)S(1)}, u32[]{:S(2)}, u32[]{:S(2)}) collective-permute-start(bf16[128,2048]{1,0:T(8,128)(2,1)S(1)} %get-tuple-element.239), channel_id=1, source_target_pairs={{0,1},{1,0},{2,3},{3,2},{4,6},{5,7},{6,4},{7,5},{8,9},{9,8},{10,11... | collective-permute-start | bytes 1572872 | tf_op jit(solution)/shard_map/ppermute | solution.py:465
  114.5 10.7 %collective-permute-start.27 = (bf16[64,4096]{1,0:T(8,128)(2,1)S(1)}, bf16[64,4096]{1,0:T(8,128)(2,1)S(1)}, u32[]{:S(2)}, u32[]{:S(2)}) collective-permute-start(bf16[64,4096]{1,0:T(8,128)(2,1)S(1)} %collective-permute-done.24.refs_1_), channel_id=1, source_target_pairs={{0,2},{1,3},{2,0},{3,1},{4,5},{5,4},{6,7},{7,6},{8,10},{9,11},{10,... | collective-permute-start | bytes 1572872 | tf_op jit(solution)/shard_map/ppermute | solution.py:465
  115.1 18.1 %collective-permute-start.30 = (bf16[64,4096]{1,0:T(8,128)(2,1)S(1)}, bf16[64,4096]{1,0:T(8,128)(2,1)S(1)}, u32[]{:S(2)}, u32[]{:S(2)}) collective-permute-start(bf16[64,4096]{1,0:T(8,128)(2,1)S(1)} %add_convert_fusion), channel_id=1, source_target_pairs={{0,2},{1,3},{2,0},{3,1},{4,5},{5,4},{6,7},{7,6},{8,10},{9,11},{10,... | collective-permute-start | bytes 1572872 | tf_op jit(solution)/shard_map/ppermute | solution.py:465
  125.2 8.4 %collective-permute-start.29 = (bf16[64,2048]{1,0:T(8,128)(2,1)S(1)}, bf16[64,2048]{1,0:T(8,128)(2,1)S(1)}, u32[]{:S(2)}, u32[]{:S(2)}) collective-permute-start(bf16[64,2048]{1,0:T(8,128)(2,1)S(1)} %add_convert_fusion.2), channel_id=1, source_target_pairs={{0,2},{1,3},{2,0},{3,1},{4,5},{5,4},{6,7},{7,6},{8,10},{9,11},{10,... | collective-permute-start | bytes 786440 | tf_op jit(solution)/shard_map/ppermute | solution.py:465
  133.6 2.7 %collective-permute-start.32 = (bf16[256,1536]{1,0:T(8,128)(2,1)S(1)}, bf16[256,1536]{1,0:T(8,128)(2,1)S(1)}, u32[]{:S(2)}, u32[]{:S(2)}) collective-permute-start(bf16[256,1536]{1,0:T(8,128)(2,1)S(1)} %get-tuple-element.264), channel_id=1, source_target_pairs={{0,4},{4,0},{8,12},{12,8},{16,20},{20,16},{24,28},{28,24},{1,5},{5... | collective-permute-start | bytes 2359304 | tf_op jit(solution)/shard_map/ppermute | solution.py:468
  134.9 11.3 %collective-permute-start.31 = (bf16[64,4096]{1,0:T(8,128)(2,1)S(1)}, bf16[64,4096]{1,0:T(8,128)(2,1)S(1)}, u32[]{:S(2)}, u32[]{:S(2)}) collective-permute-start(bf16[64,4096]{1,0:T(8,128)(2,1)S(1)} %hidden_grads.3.refs_0_), channel_id=1, source_target_pairs={{0,1},{1,0},{2,3},{3,2},{4,6},{5,7},{6,4},{7,5},{8,9},{9,8},{10,11... | collective-permute-start | bytes 1572872 | tf_op jit(solution)/shard_map/ppermute | solution.py:465
  136.4 12.6 %collective-permute-start.33 = (bf16[256,384]{1,0:T(8,128)(2,1)S(1)}, bf16[256,384]{1,0:T(8,128)(2,1)S(1)}, u32[]{:S(2)}, u32[]{:S(2)}) collective-permute-start(bf16[256,384]{1,0:T(8,128)(2,1)S(1)} %get-tuple-element.265), channel_id=1, source_target_pairs={{0,16},{4,20},{8,24},{12,28},{16,0},{20,4},{24,8},{28,12},{1,17},{... | collective-permute-start | bytes 589832 | tf_op jit(solution)/shard_map/ppermute | solution.py:471
  139.7 14.1 %collective-permute-start.34 = (bf16[64,4096]{1,0:T(8,128)(2,1)S(1)}, bf16[64,4096]{1,0:T(8,128)(2,1)S(1)}, u32[]{:S(2)}, u32[]{:S(2)}) collective-permute-start(bf16[64,4096]{1,0:T(8,128)(2,1)S(1)} %hidden_grads.3.refs_0_), channel_id=1, source_target_pairs={{0,2},{1,3},{2,0},{3,1},{4,5},{5,4},{6,7},{7,6},{8,10},{9,11},{10,... | collective-permute-start | bytes 1572872 | tf_op jit(solution)/shard_map/ppermute | solution.py:465
  149.0 10.5 %collective-permute-start.35 = (bf16[64,4096]{1,0:T(8,128)(2,1)S(1)}, bf16[64,4096]{1,0:T(8,128)(2,1)S(1)}, u32[]{:S(2)}, u32[]{:S(2)}) collective-permute-start(bf16[64,4096]{1,0:T(8,128)(2,1)S(1)} %collective-permute-done.31.refs_1_), channel_id=1, source_target_pairs={{0,2},{1,3},{2,0},{3,1},{4,5},{5,4},{6,7},{7,6},{8,10},{9,11},{10,... | collective-permute-start | bytes 1572872 | tf_op jit(solution)/shard_map/ppermute | solution.py:465
  149.9 9.6 %collective-permute-start.36 = (bf16[256,384]{1,0:T(8,128)(2,1)S(1)}, bf16[256,384]{1,0:T(8,128)(2,1)S(1)}, u32[]{:S(2)}, u32[]{:S(2)}) collective-permute-start(bf16[256,384]{1,0:T(8,128)(2,1)S(1)} %get-tuple-element.268), channel_id=1, source_target_pairs={{0,8},{4,12},{8,16},{12,20},{16,24},{20,28},{24,0},{28,4},{1,9},{5... | collective-permute-start | bytes 589832 | tf_op jit(solution)/shard_map/ppermute | solution.py:471
  152.8 13.4 %collective-permute-start.38 = (bf16[256,384]{1,0:T(8,128)(2,1)S(1)}, bf16[256,384]{1,0:T(8,128)(2,1)S(1)}, u32[]{:S(2)}, u32[]{:S(2)}) collective-permute-start(bf16[256,384]{1,0:T(8,128)(2,1)S(1)} %get-tuple-element.281), channel_id=1, source_target_pairs={{0,24},{4,28},{8,0},{12,4},{16,8},{20,12},{24,16},{28,20},{1,25},{... | collective-permute-start | bytes 589832 | tf_op jit(solution)/shard_map/ppermute | solution.py:471
  162.0 4.2 %collective-permute-start.37 = (bf16[256,384]{1,0:T(8,128)(2,1)S(1)}, bf16[256,384]{1,0:T(8,128)(2,1)S(1)}, u32[]{:S(2)}, u32[]{:S(2)}) collective-permute-start(bf16[256,384]{1,0:T(8,128)(2,1)S(1)} %get-tuple-element.276), channel_id=1, source_target_pairs={{0,4},{4,0},{8,12},{12,8},{16,20},{20,16},{24,28},{28,24},{1,5},{5... | collective-permute-start | bytes 589832 | tf_op jit(solution)/shard_map/ppermute | solution.py:468
  166.2 3.0 %collective-permute-start.39 = (bf16[256,768]{1,0:T(8,128)(2,1)S(1)}, bf16[256,768]{1,0:T(8,128)(2,1)S(1)}, u32[]{:S(2)}, u32[]{:S(2)}) collective-permute-start(bf16[256,768]{1,0:T(8,128)(2,1)S(1)} %get-tuple-element.283), channel_id=1, source_target_pairs={{0,4},{4,0},{8,12},{12,8},{16,20},{20,16},{24,28},{28,24},{1,5},{5... | collective-permute-start | bytes 1179656 | tf_op jit(solution)/shard_map/ppermute | solution.py:468
  166.8 17.2 %collective-permute-start.40 = (bf16[256,384]{1,0:T(8,128)(2,1)S(1)}, bf16[256,384]{1,0:T(8,128)(2,1)S(1)}, u32[]{:S(2)}, u32[]{:S(2)}) collective-permute-start(bf16[256,384]{1,0:T(8,128)(2,1)S(1)} %pair_sums.4), channel_id=1, source_target_pairs={{0,16},{4,20},{8,24},{12,28},{16,0},{20,4},{24,8},{28,12},{1,17},{... | collective-permute-start | bytes 589832 | tf_op jit(solution)/shard_map/ppermute | solution.py:471
  169.3 14.7 %collective-permute-start.41 = (bf16[256,384]{1,0:T(8,128)(2,1)S(1)}, bf16[256,384]{1,0:T(8,128)(2,1)S(1)}, u32[]{:S(2)}, u32[]{:S(2)}) collective-permute-start(bf16[256,384]{1,0:T(8,128)(2,1)S(1)} %get-tuple-element.305), channel_id=1, source_target_pairs={{0,8},{4,12},{8,16},{12,20},{16,24},{20,28},{24,0},{28,4},{1,9},{5... | collective-permute-start | bytes 589832 | tf_op jit(solution)/shard_map/ppermute | solution.py:471
  169.9 14.1 %collective-permute-start.42 = (bf16[256,384]{1,0:T(8,128)(2,1)S(1)}, bf16[256,384]{1,0:T(8,128)(2,1)S(1)}, u32[]{:S(2)}, u32[]{:S(2)}) collective-permute-start(bf16[256,384]{1,0:T(8,128)(2,1)S(1)} %get-tuple-element.306), channel_id=1, source_target_pairs={{0,24},{4,28},{8,0},{12,4},{16,8},{20,12},{24,16},{28,20},{1,25},{... | collective-permute-start | bytes 589832 | tf_op jit(solution)/shard_map/ppermute | solution.py:471
  175.6 8.4 %collective-permute-start.43 = (bf16[256,384]{1,0:T(8,128)(2,1)S(1)}, bf16[256,384]{1,0:T(8,128)(2,1)S(1)}, u32[]{:S(2)}, u32[]{:S(2)}) collective-permute-start(bf16[256,384]{1,0:T(8,128)(2,1)S(1)} %get-tuple-element.308), channel_id=1, source_target_pairs={{0,4},{4,0},{8,12},{12,8},{16,20},{20,16},{24,28},{28,24},{1,5},{5... | collective-permute-start | bytes 589832 | tf_op jit(solution)/shard_map/ppermute | solution.py:468

commit v6 on v5

--- a/solution.py
+++ b/solution.py
@@ -614,24 +614,28 @@
     hidden_2 = hold(hidden_2)
 
     hidden_2 = send(hidden_2)
-    early_1, gate_up_2 = hold((early_1, gate_up_2))
-
+    gate_up_2 = hold(gate_up_2)
+
+    gate_up_2 = settle(gate_up_2)
+    early_1, hidden_2 = hold((early_1, hidden_2))
+
+    hidden_2 = settle(hidden_2)
     parts_1 = finish_rows(early_1, late_1)
-    parts_1, hidden_2 = hold((parts_1, hidden_2))
-
-    hidden_2 = settle(hidden_2)
-    gate_up_2 = settle(gate_up_2)
-    partial_1 = products(parts_1, whole[0])
-    hidden_2, gate_up_2, partial_1 = hold((hidden_2, gate_up_2, partial_1))
-
-    partial_1 = swapped(partial_1)
+    hidden_2, gate_up_2 = hold((hidden_2, gate_up_2))
+
     grad_2 = grads(where, terms_of(gate_up_2), terms_of(hidden_2), rows, hidden)
     early_2, late_2 = start_rows(grad_2)
+    parts_1, grad_2 = hold((parts_1, grad_2))
+
+    partial_1 = products(parts_1, whole[0])
+    partial_1, early_2 = hold((partial_1, early_2))
+
+    parts_2 = finish_rows(early_2, late_2)
+    partial_1 = hold(swapped(partial_1))
+
     terms_1 = scatter(partial_1, whole[0])
-    early_2, early = hold((early_2, terms_1[:1]))
-    parts_2 = finish_rows(early_2, late_2)
-    parts_2, later = hold((parts_2, terms_1[1:2]))
-    terms_1 = [*early, *later, *terms_1[2:]]
+    parts_2, early = hold((parts_2, terms_1[:1]))
+    terms_1 = [*early, *terms_1[1:]]
 
     terms_2 = []
     partial, before = products(parts_2, parts_of_z[0]), parts_of_z[0]

time: 187 us -> 196 us (1.048)
  waiting for transfers between devices: 61.8 us -> 74.8 us
  starting transfers between devices: 53.9 us -> 51 us
    ppermute x14, waiting for transfers between devices: 28.4 us -> 42.2 us  [exchange(): return lax.ppermute(value, ('tp', 'dp'), pairs)]
    ppermute x10, waiting for transfers between devices: 20.6 us -> 17.8 us  [along(): lax.ppermute(value, 'tp', [(i, (i + places * CORES) % n_tp) for i in rang...]
    ppermute x10, starting transfers between devices: 28 us -> 25.7 us  [along(): lax.ppermute(value, 'tp', [(i, (i + places * CORES) % n_tp) for i in rang...]
    ppermute x8, waiting for transfers between devices: 0.97 us -> 2.96 us  [swap_cores(): return lax.ppermute(value, 'tp', [(i, i ^ 1) for i in range(n_tp)])]
  transfers between devices with their start and end apart: 44 -> 44, of which waited for: 19 -> 22; matrix products, arithmetic and copies ran while one was open for 0% -> 0% of each run, Pallas kernels for 34% -> 33%
where the time goes in v6:
time: 196 us
  waiting for transfers between devices  74.8 us (38%)
  Pallas kernels  68.5 us (35%)
  starting transfers between devices  51 us (26%)
    ppermute x14, waiting for transfers between devices, exchange(): return lax.ppermute(value, ('tp', 'dp'), pairs)  42.2 us
    ppermute x10, starting transfers between devices, along(): lax.ppermute(value, 'tp', [(i, (i + places * CORES) % n_tp) for i in rang...  25.7 us
    ppermute x10, waiting for transfers between devices, along(): lax.ppermute(value, 'tp', [(i, (i + places * CORES) % n_tp) for i in rang...  17.8 us
    pallas_call x4, Pallas kernels, backward(): pl.pallas_call(functools.partial(backward_kernel, places, total_places),...  16.5 us
    pallas_call x2, Pallas kernels, forward(): pl.pallas_call(functools.partial(forward_kernel, groups, contract, width,...  15 us
    pallas_call x2, Pallas kernels, forward_streamed(): pl.pallas_call(functools.partial(streamed_kernel, groups, width), in_spec...  14.8 us
    ppermute x14, starting transfers between devices, exchange(): return lax.ppermute(value, ('tp', 'dp'), pairs)  14.6 us
    pallas_call x2, Pallas kernels, weight(): pl.pallas_call(functools.partial(weight_kernel, turned), in_specs=[pl.Blo...  13.2 us
  transfers between devices with their start and end apart: 44, of which 22 were waited for; matrix products, arithmetic and copies ran while one was open for 0% of the time, Pallas kernels for 33%

profile of v6, /device:TPU:0, one launch (start us, length us, event | category | flops | bytes accessed | tf_op | source)
XLA Modules:
  0.0 195.8 jit_solution(7478751575832279323)
XLA Ops:
  0.1 1.8 order_rows.1
  1.9 4.1 %collective-permute-start = (bf16[256,384]{1,0:T(8,128)(2,1)S(1)}, bf16[256,384]{1,0:T(8,128)(2,1)S(1)}, u32[]{:S(2)}, u32[]{:S(2)}) collective-permute-start(bf16[256,384]{1,0:T(8,128)(2,1)S(1)} %get-tuple-element.160.own_ref), channel_id=1, source_target_pairs={{0,16},{4,20},{8,24},{12,28},{16,0},{20,4},{24,8},{28,12},{1,17},{... | collective-permute-start | bytes 589832 | tf_op jit(solution)/shard_map/ppermute | solution.py:471
  6.0 1.6 collective-permute-start.1
  8.9 6.6 %scaled_weight.3.refs_2_.refs_4_ = bf16[3072,2048]{1,0:T(8,128)(2,1)S(1)} custom-call(bf16[3072,2048]{1,0:T(8,128)(2,1)} %code_ref.3, f32[16,24]{1,0:T(8,128)S(1)} %bitcast.5), custom_call_target="tpu_custom_call" | custom-call | bytes 1536 | tf_op jit(solution)/shard_map/scaled_weight/pallas_call | solution.py:88
  16.0 1.3 collective-permute-start.3
  17.3 4.0 %collective-permute-start.4 = (bf16[256,384]{1,0:T(8,128)(2,1)S(1)}, bf16[256,384]{1,0:T(8,128)(2,1)S(1)}, u32[]{:S(2)}, u32[]{:S(2)}) collective-permute-start(bf16[256,384]{1,0:T(8,128)(2,1)S(1)} %get-tuple-element.164.own_ref), channel_id=1, source_target_pairs={{0,16},{4,20},{8,24},{12,28},{16,0},{20,4},{24,8},{28,12},{1,17},{... | collective-permute-start | bytes 589832 | tf_op jit(solution)/shard_map/ppermute | solution.py:471
  21.3 6.6 %scaled_weight.2.refs_3_.refs_5_ = bf16[3072,2048]{1,0:T(8,128)(2,1)S(1)} custom-call(bf16[3072,2048]{1,0:T(8,128)(2,1)} %code_ref.2, f32[16,24]{1,0:T(8,128)S(1)} %bitcast.6), custom_call_target="tpu_custom_call" | custom-call | bytes 1536 | tf_op jit(solution)/shard_map/scaled_weight/pallas_call | solution.py:88
  27.9 2.1 %collective-permute-done.4.two_ref = bf16[256,384]{1,0:T(8,128)(2,1)S(1)} collective-permute-done((bf16[256,384]{1,0:T(8,128)(2,1)S(1)}, bf16[256,384]{1,0:T(8,128)(2,1)S(1)}, u32[]{:S(2)}, u32[]{:S(2)}) %collective-permute-start.4) | collective-permute-done | bytes 196640 | tf_op jit(solution)/shard_map/ppermute | solution.py:471
  30.0 2.0 %collective-permute-done.5.near_ref = bf16[256,384]{1,0:T(8,128)(2,1)S(1)} collective-permute-done((bf16[256,384]{1,0:T(8,128)(2,1)S(1)}, bf16[256,384]{1,0:T(8,128)(2,1)S(1)}, u32[]{:S(2)}, u32[]{:S(2)}) %collective-permute-start.5) | collective-permute-done | bytes 196640 | tf_op jit(solution)/shard_map/ppermute | solution.py:476
  33.4 1.3 collective-permute-start.8
  35.0 7.5 %forward_product.2 = (bf16[128,4096]{1,0:T(8,128)(2,1)S(1)}, bf16[64,4096]{1,0:T(8,128)(2,1)S(1)}, bf16[64,4096]{1,0:T(8,128)(2,1)S(1)}) custom-call(s32[3]{0:T(128)S(1)} %pad_add_fusion.where_ref, bf16[256,1536]{1,0:T(8,128)(2,1)S(1)} %join.4.refs_0_, bf16[256,1536]{1,0:T(8,128)(2,1)S(1)} %collective-permute-done.6.refs_1_, ...), custom_call_target="tpu_custom_call" | custom-call | flops 1024 | bytes 1024 | tf_op jit(solution)/shard_map/forward_product/pallas_call | solution.py:231
  42.5 1.1 collective-permute-done.8.passed_ref
  43.6 1.5 collective-permute-start.10
  45.8 3.7 %collective-permute-start.11 = (bf16[256,384]{1,0:T(8,128)(2,1)S(1)}, bf16[256,384]{1,0:T(8,128)(2,1)S(1)}, u32[]{:S(2)}, u32[]{:S(2)}) collective-permute-start(bf16[256,384]{1,0:T(8,128)(2,1)S(1)} %get-tuple-element.190.own_ref), channel_id=1, source_target_pairs={{0,16},{4,20},{8,24},{12,28},{16,0},{20,4},{24,8},{28,12},{1,17},{... | collective-permute-start | bytes 589832 | tf_op jit(solution)/shard_map/ppermute | solution.py:471
  50.2 7.4 %forward_streamed.2 = (bf16[128,2048]{1,0:T(8,128)(2,1)S(1)}, bf16[64,2048]{1,0:T(8,128)(2,1)S(1)}, bf16[64,2048]{1,0:T(8,128)(2,1)S(1)}) custom-call(s32[3]{0:T(128)S(1)} %pad_add_fusion.where_ref, f32[16,24]{1,0:T(8,128)S(1)} %copy-done, bf16[256,1536]{1,0:T(8,128)(2,1)S(1)} %join.5.refs_0_, bf16[256,1536]{1,0:T(8,128)(2,1)S(1)} %collective-permute-done.9.refs_1_, ...), custom_call_target="tpu_custom_call" | custom-call | flops 1024 | bytes 1024 | tf_op jit(solution)/shard_map/forward_streamed/pallas_call | solution.py:303
  57.6 1.9 collective-permute-done.11.two_ref
  59.8 1.3 collective-permute-start.14
  61.1 2.9 %collective-permute-start.17 = (bf16[256,384]{1,0:T(8,128)(2,1)S(1)}, bf16[256,384]{1,0:T(8,128)(2,1)S(1)}, u32[]{:S(2)}, u32[]{:S(2)}) collective-permute-start(bf16[256,384]{1,0:T(8,128)(2,1)S(1)} %get-tuple-element.203.own_ref), channel_id=1, source_target_pairs={{0,16},{4,20},{8,24},{12,28},{16,0},{20,4},{24,8},{28,12},{1,17},{... | collective-permute-start | bytes 589832 | tf_op jit(solution)/shard_map/ppermute | solution.py:471
  64.0 1.4 collective-permute-start.16
  65.4 7.4 %collective-permute-done.14.passed_ref = bf16[256,384]{1,0:T(8,128)(2,1)S(1)} collective-permute-done((bf16[256,384]{1,0:T(8,128)(2,1)S(1)}, bf16[256,384]{1,0:T(8,128)(2,1)S(1)}, u32[]{:S(2)}, u32[]{:S(2)}) %collective-permute-start.14) | collective-permute-done | bytes 196640 | tf_op jit(solution)/shard_map/ppermute | solution.py:476
  73.7 1.6 collective-permute-start.21
  76.4 1.6 collective-permute-start.22
  78.6 1.5 collective-permute-start.20
  80.1 7.5 %forward_product.3 = (bf16[128,4096]{1,0:T(8,128)(2,1)S(1)}, bf16[64,4096]{1,0:T(8,128)(2,1)S(1)}, bf16[64,4096]{1,0:T(8,128)(2,1)S(1)}) custom-call(s32[3]{0:T(128)S(1)} %pad_add_fusion.where_ref, bf16[256,1536]{1,0:T(8,128)(2,1)S(1)} %join.6.refs_0_, bf16[256,1536]{1,0:T(8,128)(2,1)S(1)} %collective-permute-done.15.refs_1_, ...), custom_call_target="tpu_custom_call" | custom-call | flops 1024 | bytes 1024 | tf_op jit(solution)/shard_map/forward_product/pallas_call | solution.py:231
  90.2 1.3 collective-permute-done.23.refs_1_
  91.5 1.5 collective-permute-start.24
  92.9 7.4 %forward_streamed.3 = (bf16[128,2048]{1,0:T(8,128)(2,1)S(1)}, bf16[64,2048]{1,0:T(8,128)(2,1)S(1)}, bf16[64,2048]{1,0:T(8,128)(2,1)S(1)}) custom-call(s32[3]{0:T(128)S(1)} %pad_add_fusion.where_ref, f32[16,24]{1,0:T(8,128)S(1)} %copy-done, bf16[256,1536]{1,0:T(8,128)(2,1)S(1)} %join.7.refs_0_, bf16[256,1536]{1,0:T(8,128)(2,1)S(1)} %collective-permute-done.23.refs_1_, ...), custom_call_target="tpu_custom_call" | custom-call | flops 1024 | bytes 1024 | tf_op jit(solution)/shard_map/forward_streamed/pallas_call | solution.py:303
  101.0 1.5 collective-permute-done.26.refs_1_
  103.2 9.6 %collective-permute-done.24.refs_1_ = bf16[64,4096]{1,0:T(8,128)(2,1)S(1)} collective-permute-done((bf16[64,4096]{1,0:T(8,128)(2,1)S(1)}, bf16[64,4096]{1,0:T(8,128)(2,1)S(1)}, u32[]{:S(2)}, u32[]{:S(2)}) %collective-permute-start.24) | collective-permute-done | bytes 524320 | tf_op jit(solution)/shard_map/ppermute | solution.py:465
  112.9 6.5 %collective-permute-done.25.refs_4_ = bf16[128,2048]{1,0:T(8,128)(2,1)S(1)} collective-permute-done((bf16[128,2048]{1,0:T(8,128)(2,1)S(1)}, bf16[128,2048]{1,0:T(8,128)(2,1)S(1)}, u32[]{:S(2)}, u32[]{:S(2)}) %collective-permute-start.25) | collective-permute-done | bytes 524320 | tf_op jit(solution)/shard_map/ppermute | solution.py:465
  120.0 1.5 collective-permute-start.27
  122.0 3.8 %collective-permute-done.29.refs_5_ = bf16[64,2048]{1,0:T(8,128)(2,1)S(1)} collective-permute-done((bf16[64,2048]{1,0:T(8,128)(2,1)S(1)}, bf16[64,2048]{1,0:T(8,128)(2,1)S(1)}, u32[]{:S(2)}, u32[]{:S(2)}) %collective-permute-start.29) | collective-permute-done | bytes 262176 | tf_op jit(solution)/shard_map/ppermute | solution.py:465
  127.5 9.1 %collective-permute-done.27.refs_2_ = bf16[64,4096]{1,0:T(8,128)(2,1)S(1)} collective-permute-done((bf16[64,4096]{1,0:T(8,128)(2,1)S(1)}, bf16[64,4096]{1,0:T(8,128)(2,1)S(1)}, u32[]{:S(2)}, u32[]{:S(2)}) %collective-permute-start.27) | collective-permute-done | bytes 524320 | tf_op jit(solution)/shard_map/ppermute | solution.py:465
  136.5 6.2 %collective-permute-done.28.refs_3_ = bf16[64,4096]{1,0:T(8,128)(2,1)S(1)} collective-permute-done((bf16[64,4096]{1,0:T(8,128)(2,1)S(1)}, bf16[64,4096]{1,0:T(8,128)(2,1)S(1)}, u32[]{:S(2)}, u32[]{:S(2)}) %collective-permute-start.28) | collective-permute-done | bytes 524320 | tf_op jit(solution)/shard_map/ppermute | solution.py:465
  142.7 7.4 %backward_product.4 = (bf16[256,1536]{1,0:T(8,128)(2,1)S(1)}, bf16[256,1536]{1,0:T(8,128)(2,1)S(1)}) custom-call(s32[3]{0:T(128)S(1)} %pad_add_fusion.where_ref, bf16[64,4096]{1,0:T(8,128)(2,1)S(1)} %hidden_grads.2.refs_0_, bf16[64,4096]{1,0:T(8,128)(2,1)S(1)} %collective-permute-done.24.refs_1_, bf16[64,4096]{1,0:T(8,128)(2,1)S(1)} %collective-permute-done.27.refs_2_, ...), custom_call_target="tpu_custom_call" | custom-call | flops 1024 | bytes 1024 | tf_op jit(solution)/shard_map/backward_product/pallas_call | solution.py:382
  150.8 1.5 collective-permute-start.33
  152.7 3.2 %collective-permute-start.35 = (bf16[256,384]{1,0:T(8,128)(2,1)S(1)}, bf16[256,384]{1,0:T(8,128)(2,1)S(1)}, u32[]{:S(2)}, u32[]{:S(2)}) collective-permute-start(bf16[256,384]{1,0:T(8,128)(2,1)S(1)} %get-tuple-element.274), channel_id=1, source_target_pairs={{0,16},{4,20},{8,24},{12,28},{16,0},{20,4},{24,8},{28,12},{1,17},{... | collective-permute-start | bytes 589832 | tf_op jit(solution)/shard_map/ppermute | solution.py:471
  155.9 3.8 %collective-permute-start.38 = (bf16[256,384]{1,0:T(8,128)(2,1)S(1)}, bf16[256,384]{1,0:T(8,128)(2,1)S(1)}, u32[]{:S(2)}, u32[]{:S(2)}) collective-permute-start(bf16[256,384]{1,0:T(8,128)(2,1)S(1)} %get-tuple-element.287), channel_id=1, source_target_pairs={{0,24},{4,28},{8,0},{12,4},{16,8},{20,12},{24,16},{28,20},{1,25},{... | collective-permute-start | bytes 589832 | tf_op jit(solution)/shard_map/ppermute | solution.py:471
  159.7 5.4 %collective-permute-done.33.refs_3_ = bf16[64,4096]{1,0:T(8,128)(2,1)S(1)} collective-permute-done((bf16[64,4096]{1,0:T(8,128)(2,1)S(1)}, bf16[64,4096]{1,0:T(8,128)(2,1)S(1)}, u32[]{:S(2)}, u32[]{:S(2)}) %collective-permute-start.33) | collective-permute-done | bytes 524320 | tf_op jit(solution)/shard_map/ppermute | solution.py:465
  165.1 4.9 %collective-permute-done.35.refs_0_ = bf16[256,384]{1,0:T(8,128)(2,1)S(1)} collective-permute-done((bf16[256,384]{1,0:T(8,128)(2,1)S(1)}, bf16[256,384]{1,0:T(8,128)(2,1)S(1)}, u32[]{:S(2)}, u32[]{:S(2)}) %collective-permute-start.35) | collective-permute-done | bytes 196640 | tf_op jit(solution)/shard_map/ppermute | solution.py:471
  170.0 2.5 %backward_product.5 = (bf16[256,384]{1,0:T(8,128)(2,1)S(1)}, bf16[256,384]{1,0:T(8,128)(2,1)S(1)}) custom-call(s32[3]{0:T(128)S(1)} %pad_add_fusion.where_ref, bf16[64,4096]{1,0:T(8,128)(2,1)S(1)} %hidden_grads.3.refs_0_, bf16[64,4096]{1,0:T(8,128)(2,1)S(1)} %collective-permute-done.31.refs_1_, bf16[64,4096]{1,0:T(8,128)(2,1)S(1)} %collective-permute-done.32.refs_2_, ...), custom_call_target="tpu_custom_call" | custom-call | flops 1024 | bytes 1024 | tf_op jit(solution)/shard_map/backward_product/pallas_call | solution.py:382
  172.6 4.1 %backward_product.6 = (bf16[256,768]{1,0:T(8,128)(2,1)S(1)}, bf16[256,768]{1,0:T(8,128)(2,1)S(1)}) custom-call(s32[3]{0:T(128)S(1)} %pad_add_fusion.where_ref, bf16[64,4096]{1,0:T(8,128)(2,1)S(1)} %hidden_grads.3.refs_0_, bf16[64,4096]{1,0:T(8,128)(2,1)S(1)} %collective-permute-done.31.refs_1_, bf16[64,4096]{1,0:T(8,128)(2,1)S(1)} %collective-permute-done.32.refs_2_, ...), custom_call_target="tpu_custom_call" | custom-call | flops 1024 | bytes 1024 | tf_op jit(solution)/shard_map/backward_product/pallas_call | solution.py:382
  177.4 1.2 collective-permute-done.39.other_ref
  178.8 3.8 %collective-permute-start.42 = (bf16[256,384]{1,0:T(8,128)(2,1)S(1)}, bf16[256,384]{1,0:T(8,128)(2,1)S(1)}, u32[]{:S(2)}, u32[]{:S(2)}) collective-permute-start(bf16[256,384]{1,0:T(8,128)(2,1)S(1)} %get-tuple-element.312), channel_id=1, source_target_pairs={{0,24},{4,28},{8,0},{12,4},{16,8},{20,12},{24,16},{28,20},{1,25},{... | collective-permute-start | bytes 589832 | tf_op jit(solution)/shard_map/ppermute | solution.py:471
  182.6 2.5 %backward_product.7 = (bf16[256,384]{1,0:T(8,128)(2,1)S(1)}, bf16[256,384]{1,0:T(8,128)(2,1)S(1)}) custom-call(s32[3]{0:T(128)S(1)} %pad_add_fusion.where_ref, bf16[64,4096]{1,0:T(8,128)(2,1)S(1)} %hidden_grads.3.refs_0_, bf16[64,4096]{1,0:T(8,128)(2,1)S(1)} %collective-permute-done.31.refs_1_, bf16[64,4096]{1,0:T(8,128)(2,1)S(1)} %collective-permute-done.32.refs_2_, ...), custom_call_target="tpu_custom_call" | custom-call | flops 1024 | bytes 1024 | tf_op jit(solution)/shard_map/backward_product/pallas_call | solution.py:382
  185.9 5.1 %collective-permute-done.40.refs_1_ = bf16[256,384]{1,0:T(8,128)(2,1)S(1)} collective-permute-done((bf16[256,384]{1,0:T(8,128)(2,1)S(1)}, bf16[256,384]{1,0:T(8,128)(2,1)S(1)}, u32[]{:S(2)}, u32[]{:S(2)}) %collective-permute-start.40) | collective-permute-done | bytes 196640 | tf_op jit(solution)/shard_map/ppermute | solution.py:471
  190.9 3.5 %collective-permute-done.42.refs_3_ = bf16[256,384]{1,0:T(8,128)(2,1)S(1)} collective-permute-done((bf16[256,384]{1,0:T(8,128)(2,1)S(1)}, bf16[256,384]{1,0:T(8,128)(2,1)S(1)}, u32[]{:S(2)}, u32[]{:S(2)}) %collective-permute-start.42) | collective-permute-done | bytes 196640 | tf_op jit(solution)/shard_map/ppermute | solution.py:471
  194.4 1.4 final_sum.3
  (73 shorter events, 17.0 us)
Async XLA Ops:
  1.9 14.1 %collective-permute-start = (bf16[256,384]{1,0:T(8,128)(2,1)S(1)}, bf16[256,384]{1,0:T(8,128)(2,1)S(1)}, u32[]{:S(2)}, u32[]{:S(2)}) collective-permute-start(bf16[256,384]{1,0:T(8,128)(2,1)S(1)} %get-tuple-element.160.own_ref), channel_id=1, source_target_pairs={{0,16},{4,20},{8,24},{12,28},{16,0},{20,4},{24,8},{28,12},{1,17},{... | collective-permute-start | bytes 589832 | tf_op jit(solution)/shard_map/ppermute | solution.py:471
  6.0 10.0 %collective-permute-start.1 = (bf16[256,384]{1,0:T(8,128)(2,1)S(1)}, bf16[256,384]{1,0:T(8,128)(2,1)S(1)}, u32[]{:S(2)}, u32[]{:S(2)}) collective-permute-start(bf16[256,384]{1,0:T(8,128)(2,1)S(1)} %get-tuple-element.160.own_ref), channel_id=1, source_target_pairs={{0,8},{4,12},{8,0},{12,4},{16,24},{20,28},{24,16},{28,20},{1,9},{5... | collective-permute-start | bytes 589832 | tf_op jit(solution)/shard_map/ppermute | solution.py:476
  7.6 20.3 %collective-permute-start.2 = (bf16[256,384]{1,0:T(8,128)(2,1)S(1)}, bf16[256,384]{1,0:T(8,128)(2,1)S(1)}, u32[]{:S(2)}, u32[]{:S(2)}) collective-permute-start(bf16[256,384]{1,0:T(8,128)(2,1)S(1)} %get-tuple-element.160.own_ref), channel_id=1, source_target_pairs={{8,16},{12,20},{16,8},{20,12},{9,17},{13,21},{17,9},{21,13},{10,18... | collective-permute-start | bytes 589832 | tf_op jit(solution)/shard_map/ppermute | solution.py:476
  8.2 0.7 copy-start.1
  8.9 12.4 %copy-start.2 = (f32[24,16]{0,1:T(8,128)S(1)}, f32[24,16]{0,1:T(8,128)}, u32[]{:S(2)}) copy-start(f32[24,16]{0,1:T(8,128)} %param.13) | copy-start | bytes 4612
  16.0 11.9 %collective-permute-start.3 = (bf16[256,384]{1,0:T(8,128)(2,1)S(1)}, bf16[256,384]{1,0:T(8,128)(2,1)S(1)}, u32[]{:S(2)}, u32[]{:S(2)}) collective-permute-start(bf16[256,384]{1,0:T(8,128)(2,1)S(1)} %collective-permute-done.two_ref), channel_id=1, source_target_pairs={{8,0},{12,4},{16,24},{20,28},{9,1},{13,5},{17,25},{21,29},{10,2},{... | collective-permute-start | bytes 589832 | tf_op jit(solution)/shard_map/ppermute | solution.py:476
  17.3 12.7 %collective-permute-start.4 = (bf16[256,384]{1,0:T(8,128)(2,1)S(1)}, bf16[256,384]{1,0:T(8,128)(2,1)S(1)}, u32[]{:S(2)}, u32[]{:S(2)}) collective-permute-start(bf16[256,384]{1,0:T(8,128)(2,1)S(1)} %get-tuple-element.164.own_ref), channel_id=1, source_target_pairs={{0,16},{4,20},{8,24},{12,28},{16,0},{20,4},{24,8},{28,12},{1,17},{... | collective-permute-start | bytes 589832 | tf_op jit(solution)/shard_map/ppermute | solution.py:471
  21.3 10.7 %collective-permute-start.5 = (bf16[256,384]{1,0:T(8,128)(2,1)S(1)}, bf16[256,384]{1,0:T(8,128)(2,1)S(1)}, u32[]{:S(2)}, u32[]{:S(2)}) collective-permute-start(bf16[256,384]{1,0:T(8,128)(2,1)S(1)} %get-tuple-element.164.own_ref), channel_id=1, source_target_pairs={{0,8},{4,12},{8,0},{12,4},{16,24},{20,28},{24,16},{28,20},{1,9},{5... | collective-permute-start | bytes 589832 | tf_op jit(solution)/shard_map/ppermute | solution.py:476
  32.6 17.6 %copy-start = (f32[16,24]{1,0:T(8,128)S(1)}, f32[16,24]{1,0:T(8,128)}, u32[]{:S(2)}) copy-start(f32[16,24]{1,0:T(8,128)} %scale_ref.3) | copy-start | bytes 4612
  32.6 2.4 %collective-permute-start.6 = (bf16[256,1536]{1,0:T(8,128)(2,1)S(1)}, bf16[256,1536]{1,0:T(8,128)(2,1)S(1)}, u32[]{:S(2)}, u32[]{:S(2)}) collective-permute-start(bf16[256,1536]{1,0:T(8,128)(2,1)S(1)} %join.4.refs_0_), channel_id=1, source_target_pairs={{0,4},{4,0},{8,12},{12,8},{16,20},{20,16},{24,28},{28,24},{1,5},{5... | collective-permute-start | bytes 2359304 | tf_op jit(solution)/shard_map/ppermute | solution.py:468
  32.7 9.8 %collective-permute-start.7 = (bf16[256,384]{1,0:T(8,128)(2,1)S(1)}, bf16[256,384]{1,0:T(8,128)(2,1)S(1)}, u32[]{:S(2)}, u32[]{:S(2)}) collective-permute-start(bf16[256,384]{1,0:T(8,128)(2,1)S(1)} %get-tuple-element.164.own_ref), channel_id=1, source_target_pairs={{8,16},{12,20},{16,8},{20,12},{9,17},{13,21},{17,9},{21,13},{10,18... | collective-permute-start | bytes 589832 | tf_op jit(solution)/shard_map/ppermute | solution.py:476
  33.4 10.2 %collective-permute-start.8 = (bf16[256,384]{1,0:T(8,128)(2,1)S(1)}, bf16[256,384]{1,0:T(8,128)(2,1)S(1)}, u32[]{:S(2)}, u32[]{:S(2)}) collective-permute-start(bf16[256,384]{1,0:T(8,128)(2,1)S(1)} %collective-permute-done.4.two_ref), channel_id=1, source_target_pairs={{8,0},{12,4},{16,24},{20,28},{9,1},{13,5},{17,25},{21,29},{10,2},{... | collective-permute-start | bytes 589832 | tf_op jit(solution)/shard_map/ppermute | solution.py:476
  43.6 16.2 %collective-permute-start.10 = (bf16[128,4096]{1,0:T(8,128)(2,1)S(1)}, bf16[128,4096]{1,0:T(8,128)(2,1)S(1)}, u32[]{:S(2)}, u32[]{:S(2)}) collective-permute-start(bf16[128,4096]{1,0:T(8,128)(2,1)S(1)} %get-tuple-element.187), channel_id=1, source_target_pairs={{0,1},{1,0},{2,3},{3,2},{4,6},{5,7},{6,4},{7,5},{8,9},{9,8},{10,11... | collective-permute-start | bytes 3145736 | tf_op jit(solution)/shard_map/ppermute | solution.py:465
  45.7 4.5 %collective-permute-start.9 = (bf16[256,1536]{1,0:T(8,128)(2,1)S(1)}, bf16[256,1536]{1,0:T(8,128)(2,1)S(1)}, u32[]{:S(2)}, u32[]{:S(2)}) collective-permute-start(bf16[256,1536]{1,0:T(8,128)(2,1)S(1)} %join.5.refs_0_), channel_id=1, source_target_pairs={{0,4},{4,0},{8,12},{12,8},{16,20},{20,16},{24,28},{28,24},{1,5},{5... | collective-permute-start | bytes 2359304 | tf_op jit(solution)/shard_map/ppermute | solution.py:468
  45.8 13.7 %collective-permute-start.11 = (bf16[256,384]{1,0:T(8,128)(2,1)S(1)}, bf16[256,384]{1,0:T(8,128)(2,1)S(1)}, u32[]{:S(2)}, u32[]{:S(2)}) collective-permute-start(bf16[256,384]{1,0:T(8,128)(2,1)S(1)} %get-tuple-element.190.own_ref), channel_id=1, source_target_pairs={{0,16},{4,20},{8,24},{12,28},{16,0},{20,4},{24,8},{28,12},{1,17},{... | collective-permute-start | bytes 589832 | tf_op jit(solution)/shard_map/ppermute | solution.py:471
  49.5 10.3 %collective-permute-start.12 = (bf16[256,384]{1,0:T(8,128)(2,1)S(1)}, bf16[256,384]{1,0:T(8,128)(2,1)S(1)}, u32[]{:S(2)}, u32[]{:S(2)}) collective-permute-start(bf16[256,384]{1,0:T(8,128)(2,1)S(1)} %get-tuple-element.190.own_ref), channel_id=1, source_target_pairs={{0,8},{4,12},{8,0},{12,4},{16,24},{20,28},{24,16},{28,20},{1,9},{5... | collective-permute-start | bytes 589832 | tf_op jit(solution)/shard_map/ppermute | solution.py:476
  49.5 15.9 %collective-permute-start.13 = (bf16[256,384]{1,0:T(8,128)(2,1)S(1)}, bf16[256,384]{1,0:T(8,128)(2,1)S(1)}, u32[]{:S(2)}, u32[]{:S(2)}) collective-permute-start(bf16[256,384]{1,0:T(8,128)(2,1)S(1)} %get-tuple-element.190.own_ref), channel_id=1, source_target_pairs={{8,16},{12,20},{16,8},{20,12},{9,17},{13,21},{17,9},{21,13},{10,18... | collective-permute-start | bytes 589832 | tf_op jit(solution)/shard_map/ppermute | solution.py:476
  59.8 13.0 %collective-permute-start.14 = (bf16[256,384]{1,0:T(8,128)(2,1)S(1)}, bf16[256,384]{1,0:T(8,128)(2,1)S(1)}, u32[]{:S(2)}, u32[]{:S(2)}) collective-permute-start(bf16[256,384]{1,0:T(8,128)(2,1)S(1)} %collective-permute-done.11.two_ref), channel_id=1, source_target_pairs={{8,0},{12,4},{16,24},{20,28},{9,1},{13,5},{17,25},{21,29},{10,2},{... | collective-permute-start | bytes 589832 | tf_op jit(solution)/shard_map/ppermute | solution.py:476
  61.1 14.2 %collective-permute-start.17 = (bf16[256,384]{1,0:T(8,128)(2,1)S(1)}, bf16[256,384]{1,0:T(8,128)(2,1)S(1)}, u32[]{:S(2)}, u32[]{:S(2)}) collective-permute-start(bf16[256,384]{1,0:T(8,128)(2,1)S(1)} %get-tuple-element.203.own_ref), channel_id=1, source_target_pairs={{0,16},{4,20},{8,24},{12,28},{16,0},{20,4},{24,8},{28,12},{1,17},{... | collective-permute-start | bytes 589832 | tf_op jit(solution)/shard_map/ppermute | solution.py:471
  64.0 12.3 %collective-permute-start.18 = (bf16[256,384]{1,0:T(8,128)(2,1)S(1)}, bf16[256,384]{1,0:T(8,128)(2,1)S(1)}, u32[]{:S(2)}, u32[]{:S(2)}) collective-permute-start(bf16[256,384]{1,0:T(8,128)(2,1)S(1)} %get-tuple-element.203.own_ref), channel_id=1, source_target_pairs={{0,8},{4,12},{8,0},{12,4},{16,24},{20,28},{24,16},{28,20},{1,9},{5... | collective-permute-start | bytes 589832 | tf_op jit(solution)/shard_map/ppermute | solution.py:476
  64.0 12.3 %collective-permute-start.16 = (bf16[128,2048]{1,0:T(8,128)(2,1)S(1)}, bf16[128,2048]{1,0:T(8,128)(2,1)S(1)}, u32[]{:S(2)}, u32[]{:S(2)}) collective-permute-start(bf16[128,2048]{1,0:T(8,128)(2,1)S(1)} %get-tuple-element.200), channel_id=1, source_target_pairs={{0,1},{1,0},{2,3},{3,2},{4,6},{5,7},{6,4},{7,5},{8,9},{9,8},{10,11... | collective-permute-start | bytes 1572872 | tf_op jit(solution)/shard_map/ppermute | solution.py:465
  73.5 2.8 %collective-permute-start.15 = (bf16[256,1536]{1,0:T(8,128)(2,1)S(1)}, bf16[256,1536]{1,0:T(8,128)(2,1)S(1)}, u32[]{:S(2)}, u32[]{:S(2)}) collective-permute-start(bf16[256,1536]{1,0:T(8,128)(2,1)S(1)} %join.6.refs_0_), channel_id=1, source_target_pairs={{0,4},{4,0},{8,12},{12,8},{16,20},{20,16},{24,28},{28,24},{1,5},{5... | collective-permute-start | bytes 2359304 | tf_op jit(solution)/shard_map/ppermute | solution.py:468
  73.7 13.9 %collective-permute-start.21 = (bf16[64,4096]{1,0:T(8,128)(2,1)S(1)}, bf16[64,4096]{1,0:T(8,128)(2,1)S(1)}, u32[]{:S(2)}, u32[]{:S(2)}) collective-permute-start(bf16[64,4096]{1,0:T(8,128)(2,1)S(1)} %add_convert_fusion.1), channel_id=1, source_target_pairs={{0,2},{1,3},{2,0},{3,1},{4,5},{5,4},{6,7},{7,6},{8,10},{9,11},{10,... | collective-permute-start | bytes 1572872 | tf_op jit(solution)/shard_map/ppermute | solution.py:465
  76.4 11.3 %collective-permute-start.22 = (bf16[64,2048]{1,0:T(8,128)(2,1)S(1)}, bf16[64,2048]{1,0:T(8,128)(2,1)S(1)}, u32[]{:S(2)}, u32[]{:S(2)}) collective-permute-start(bf16[64,2048]{1,0:T(8,128)(2,1)S(1)} %add_convert_fusion.3), channel_id=1, source_target_pairs={{0,2},{1,3},{2,0},{3,1},{4,5},{5,4},{6,7},{7,6},{8,10},{9,11},{10,... | collective-permute-start | bytes 786440 | tf_op jit(solution)/shard_map/ppermute | solution.py:465
  77.9 9.7 %collective-permute-start.19 = (bf16[256,384]{1,0:T(8,128)(2,1)S(1)}, bf16[256,384]{1,0:T(8,128)(2,1)S(1)}, u32[]{:S(2)}, u32[]{:S(2)}) collective-permute-start(bf16[256,384]{1,0:T(8,128)(2,1)S(1)} %get-tuple-element.203.own_ref), channel_id=1, source_target_pairs={{8,16},{12,20},{16,8},{20,12},{9,17},{13,21},{17,9},{21,13},{10,18... | collective-permute-start | bytes 589832 | tf_op jit(solution)/shard_map/ppermute | solution.py:476
  78.6 9.0 %collective-permute-start.20 = (bf16[256,384]{1,0:T(8,128)(2,1)S(1)}, bf16[256,384]{1,0:T(8,128)(2,1)S(1)}, u32[]{:S(2)}, u32[]{:S(2)}) collective-permute-start(bf16[256,384]{1,0:T(8,128)(2,1)S(1)} %collective-permute-done.17.two_ref), channel_id=1, source_target_pairs={{8,0},{12,4},{16,24},{20,28},{9,1},{13,5},{17,25},{21,29},{10,2},{... | collective-permute-start | bytes 589832 | tf_op jit(solution)/shard_map/ppermute | solution.py:476
  87.6 14.9 %collective-permute-start.26 = (bf16[128,4096]{1,0:T(8,128)(2,1)S(1)}, bf16[128,4096]{1,0:T(8,128)(2,1)S(1)}, u32[]{:S(2)}, u32[]{:S(2)}) collective-permute-start(bf16[128,4096]{1,0:T(8,128)(2,1)S(1)} %get-tuple-element.239), channel_id=1, source_target_pairs={{0,1},{1,0},{2,3},{3,2},{4,6},{5,7},{6,4},{7,5},{8,9},{9,8},{10,11... | collective-permute-start | bytes 3145736 | tf_op jit(solution)/shard_map/ppermute | solution.py:465
  89.1 2.4 %collective-permute-start.23 = (bf16[256,1536]{1,0:T(8,128)(2,1)S(1)}, bf16[256,1536]{1,0:T(8,128)(2,1)S(1)}, u32[]{:S(2)}, u32[]{:S(2)}) collective-permute-start(bf16[256,1536]{1,0:T(8,128)(2,1)S(1)} %join.7.refs_0_), channel_id=1, source_target_pairs={{0,4},{4,0},{8,12},{12,8},{16,20},{20,16},{24,28},{28,24},{1,5},{5... | collective-permute-start | bytes 2359304 | tf_op jit(solution)/shard_map/ppermute | solution.py:468
  91.5 21.4 %collective-permute-start.24 = (bf16[64,4096]{1,0:T(8,128)(2,1)S(1)}, bf16[64,4096]{1,0:T(8,128)(2,1)S(1)}, u32[]{:S(2)}, u32[]{:S(2)}) collective-permute-start(bf16[64,4096]{1,0:T(8,128)(2,1)S(1)} %hidden_grads.2.refs_0_), channel_id=1, source_target_pairs={{0,1},{1,0},{2,3},{3,2},{4,6},{5,7},{6,4},{7,5},{8,9},{9,8},{10,11... | collective-permute-start | bytes 1572872 | tf_op jit(solution)/shard_map/ppermute | solution.py:465
  100.4 19.0 %collective-permute-start.25 = (bf16[128,2048]{1,0:T(8,128)(2,1)S(1)}, bf16[128,2048]{1,0:T(8,128)(2,1)S(1)}, u32[]{:S(2)}, u32[]{:S(2)}) collective-permute-start(bf16[128,2048]{1,0:T(8,128)(2,1)S(1)} %get-tuple-element.236), channel_id=1, source_target_pairs={{0,1},{1,0},{2,3},{3,2},{4,6},{5,7},{6,4},{7,5},{8,9},{9,8},{10,11... | collective-permute-start | bytes 1572872 | tf_op jit(solution)/shard_map/ppermute | solution.py:465
  102.6 23.2 %collective-permute-start.30 = (bf16[64,4096]{1,0:T(8,128)(2,1)S(1)}, bf16[64,4096]{1,0:T(8,128)(2,1)S(1)}, u32[]{:S(2)}, u32[]{:S(2)}) collective-permute-start(bf16[64,4096]{1,0:T(8,128)(2,1)S(1)} %add_convert_fusion), channel_id=1, source_target_pairs={{0,2},{1,3},{2,0},{3,1},{4,5},{5,4},{6,7},{7,6},{8,10},{9,11},{10,... | collective-permute-start | bytes 1572872 | tf_op jit(solution)/shard_map/ppermute | solution.py:465
  119.4 6.4 %collective-permute-start.29 = (bf16[64,2048]{1,0:T(8,128)(2,1)S(1)}, bf16[64,2048]{1,0:T(8,128)(2,1)S(1)}, u32[]{:S(2)}, u32[]{:S(2)}) collective-permute-start(bf16[64,2048]{1,0:T(8,128)(2,1)S(1)} %add_convert_fusion.2), channel_id=1, source_target_pairs={{0,2},{1,3},{2,0},{3,1},{4,5},{5,4},{6,7},{7,6},{8,10},{9,11},{10,... | collective-permute-start | bytes 786440 | tf_op jit(solution)/shard_map/ppermute | solution.py:465
  120.0 16.5 %collective-permute-start.27 = (bf16[64,4096]{1,0:T(8,128)(2,1)S(1)}, bf16[64,4096]{1,0:T(8,128)(2,1)S(1)}, u32[]{:S(2)}, u32[]{:S(2)}) collective-permute-start(bf16[64,4096]{1,0:T(8,128)(2,1)S(1)} %hidden_grads.2.refs_0_), channel_id=1, source_target_pairs={{0,2},{1,3},{2,0},{3,1},{4,5},{5,4},{6,7},{7,6},{8,10},{9,11},{10,... | collective-permute-start | bytes 1572872 | tf_op jit(solution)/shard_map/ppermute | solution.py:465
  121.5 21.2 %collective-permute-start.28 = (bf16[64,4096]{1,0:T(8,128)(2,1)S(1)}, bf16[64,4096]{1,0:T(8,128)(2,1)S(1)}, u32[]{:S(2)}, u32[]{:S(2)}) collective-permute-start(bf16[64,4096]{1,0:T(8,128)(2,1)S(1)} %collective-permute-done.24.refs_1_), channel_id=1, source_target_pairs={{0,2},{1,3},{2,0},{3,1},{4,5},{5,4},{6,7},{7,6},{8,10},{9,11},{10,... | collective-permute-start | bytes 1572872 | tf_op jit(solution)/shard_map/ppermute | solution.py:465
  126.9 23.3 %collective-permute-start.31 = (bf16[64,4096]{1,0:T(8,128)(2,1)S(1)}, bf16[64,4096]{1,0:T(8,128)(2,1)S(1)}, u32[]{:S(2)}, u32[]{:S(2)}) collective-permute-start(bf16[64,4096]{1,0:T(8,128)(2,1)S(1)} %hidden_grads.3.refs_0_), channel_id=1, source_target_pairs={{0,1},{1,0},{2,3},{3,2},{4,6},{5,7},{6,4},{7,5},{8,9},{9,8},{10,11... | collective-permute-start | bytes 1572872 | tf_op jit(solution)/shard_map/ppermute | solution.py:465
  150.2 2.4 %collective-permute-start.34 = (bf16[256,1536]{1,0:T(8,128)(2,1)S(1)}, bf16[256,1536]{1,0:T(8,128)(2,1)S(1)}, u32[]{:S(2)}, u32[]{:S(2)}) collective-permute-start(bf16[256,1536]{1,0:T(8,128)(2,1)S(1)} %get-tuple-element.270), channel_id=1, source_target_pairs={{0,4},{4,0},{8,12},{12,8},{16,20},{20,16},{24,28},{28,24},{1,5},{5... | collective-permute-start | bytes 2359304 | tf_op jit(solution)/shard_map/ppermute | solution.py:468
  150.2 9.5 %collective-permute-start.32 = (bf16[64,4096]{1,0:T(8,128)(2,1)S(1)}, bf16[64,4096]{1,0:T(8,128)(2,1)S(1)}, u32[]{:S(2)}, u32[]{:S(2)}) collective-permute-start(bf16[64,4096]{1,0:T(8,128)(2,1)S(1)} %hidden_grads.3.refs_0_), channel_id=1, source_target_pairs={{0,2},{1,3},{2,0},{3,1},{4,5},{5,4},{6,7},{7,6},{8,10},{9,11},{10,... | collective-permute-start | bytes 1572872 | tf_op jit(solution)/shard_map/ppermute | solution.py:465
  150.8 14.3 %collective-permute-start.33 = (bf16[64,4096]{1,0:T(8,128)(2,1)S(1)}, bf16[64,4096]{1,0:T(8,128)(2,1)S(1)}, u32[]{:S(2)}, u32[]{:S(2)}) collective-permute-start(bf16[64,4096]{1,0:T(8,128)(2,1)S(1)} %collective-permute-done.31.refs_1_), channel_id=1, source_target_pairs={{0,2},{1,3},{2,0},{3,1},{4,5},{5,4},{6,7},{7,6},{8,10},{9,11},{10,... | collective-permute-start | bytes 1572872 | tf_op jit(solution)/shard_map/ppermute | solution.py:465
  152.7 17.3 %collective-permute-start.35 = (bf16[256,384]{1,0:T(8,128)(2,1)S(1)}, bf16[256,384]{1,0:T(8,128)(2,1)S(1)}, u32[]{:S(2)}, u32[]{:S(2)}) collective-permute-start(bf16[256,384]{1,0:T(8,128)(2,1)S(1)} %get-tuple-element.274), channel_id=1, source_target_pairs={{0,16},{4,20},{8,24},{12,28},{16,0},{20,4},{24,8},{28,12},{1,17},{... | collective-permute-start | bytes 589832 | tf_op jit(solution)/shard_map/ppermute | solution.py:471
  155.9 20.8 %collective-permute-start.37 = (bf16[256,384]{1,0:T(8,128)(2,1)S(1)}, bf16[256,384]{1,0:T(8,128)(2,1)S(1)}, u32[]{:S(2)}, u32[]{:S(2)}) collective-permute-start(bf16[256,384]{1,0:T(8,128)(2,1)S(1)} %get-tuple-element.286), channel_id=1, source_target_pairs={{0,8},{4,12},{8,16},{12,20},{16,24},{20,28},{24,0},{28,4},{1,9},{5... | collective-permute-start | bytes 589832 | tf_op jit(solution)/shard_map/ppermute | solution.py:471
  155.9 20.8 %collective-permute-start.38 = (bf16[256,384]{1,0:T(8,128)(2,1)S(1)}, bf16[256,384]{1,0:T(8,128)(2,1)S(1)}, u32[]{:S(2)}, u32[]{:S(2)}) collective-permute-start(bf16[256,384]{1,0:T(8,128)(2,1)S(1)} %get-tuple-element.287), channel_id=1, source_target_pairs={{0,24},{4,28},{8,0},{12,4},{16,8},{20,12},{24,16},{28,20},{1,25},{... | collective-permute-start | bytes 589832 | tf_op jit(solution)/shard_map/ppermute | solution.py:471
  172.5 4.2 %collective-permute-start.36 = (bf16[256,384]{1,0:T(8,128)(2,1)S(1)}, bf16[256,384]{1,0:T(8,128)(2,1)S(1)}, u32[]{:S(2)}, u32[]{:S(2)}) collective-permute-start(bf16[256,384]{1,0:T(8,128)(2,1)S(1)} %get-tuple-element.282), channel_id=1, source_target_pairs={{0,4},{4,0},{8,12},{12,8},{16,20},{20,16},{24,28},{28,24},{1,5},{5... | collective-permute-start | bytes 589832 | tf_op jit(solution)/shard_map/ppermute | solution.py:468
  176.7 1.9 collective-permute-start.39
  177.3 13.6 %collective-permute-start.40 = (bf16[256,384]{1,0:T(8,128)(2,1)S(1)}, bf16[256,384]{1,0:T(8,128)(2,1)S(1)}, u32[]{:S(2)}, u32[]{:S(2)}) collective-permute-start(bf16[256,384]{1,0:T(8,128)(2,1)S(1)} %pair_sums.4), channel_id=1, source_target_pairs={{0,16},{4,20},{8,24},{12,28},{16,0},{20,4},{24,8},{28,12},{1,17},{... | collective-permute-start | bytes 589832 | tf_op jit(solution)/shard_map/ppermute | solution.py:471
  178.7 12.2 %collective-permute-start.41 = (bf16[256,384]{1,0:T(8,128)(2,1)S(1)}, bf16[256,384]{1,0:T(8,128)(2,1)S(1)}, u32[]{:S(2)}, u32[]{:S(2)}) collective-permute-start(bf16[256,384]{1,0:T(8,128)(2,1)S(1)} %get-tuple-element.311), channel_id=1, source_target_pairs={{0,8},{4,12},{8,16},{12,20},{16,24},{20,28},{24,0},{28,4},{1,9},{5... | collective-permute-start | bytes 589832 | tf_op jit(solution)/shard_map/ppermute | solution.py:471
  178.8 15.6 %collective-permute-start.42 = (bf16[256,384]{1,0:T(8,128)(2,1)S(1)}, bf16[256,384]{1,0:T(8,128)(2,1)S(1)}, u32[]{:S(2)}, u32[]{:S(2)}) collective-permute-start(bf16[256,384]{1,0:T(8,128)(2,1)S(1)} %get-tuple-element.312), channel_id=1, source_target_pairs={{0,24},{4,28},{8,0},{12,4},{16,8},{20,12},{24,16},{28,20},{1,25},{... | collective-permute-start | bytes 589832 | tf_op jit(solution)/shard_map/ppermute | solution.py:471
  185.1 9.3 %collective-permute-start.43 = (bf16[256,384]{1,0:T(8,128)(2,1)S(1)}, bf16[256,384]{1,0:T(8,128)(2,1)S(1)}, u32[]{:S(2)}, u32[]{:S(2)}) collective-permute-start(bf16[256,384]{1,0:T(8,128)(2,1)S(1)} %get-tuple-element.314), channel_id=1, source_target_pairs={{0,4},{4,0},{8,12},{12,8},{16,20},{20,16},{24,28},{28,24},{1,5},{5... | collective-permute-start | bytes 589832 | tf_op jit(solution)/shard_map/ppermute | solution.py:468

commit v7 on v5

--- a/solution.py
+++ b/solution.py
@@ -540,7 +540,7 @@
                 have[q | 1 << step] = exchange(have[q], step) if q else late[1 << step]
         return [have[q] for q in range(n_dp)]
 
-    whole = [[2, 1, 3, 0] if hops else [*range(1, n_z), 0]]
+    whole = [[*range(1, n_z), 0]]
     parts_of_z = [[2], [1, 3], [0]] if hops else whole
 
     def products(grad_parts, places):

time: 187 us -> 189 us (1.011)
  transfers between devices with their start and end apart: 44 -> 44, of which waited for: 19 -> 20; matrix products, arithmetic and copies ran while one was open for 0% -> 0% of each run, Pallas kernels for 34% -> 34%
where the time goes in v7:
time: 189 us; the launch traced here: 188 us
  Pallas kernels  68.2 us (36%)
  waiting for transfers between devices  62.9 us (33%)
  starting transfers between devices  55.3 us (29%)
    ppermute x14, waiting for transfers between devices, exchange(): return lax.ppermute(value, ('tp', 'dp'), pairs)  29.6 us
    ppermute x10, starting transfers between devices, along(): lax.ppermute(value, 'tp', [(i, (i + places * CORES) % n_tp) for i in rang...  29.4 us
    ppermute x10, waiting for transfers between devices, along(): lax.ppermute(value, 'tp', [(i, (i + places * CORES) % n_tp) for i in rang...  19.9 us
    pallas_call x4, Pallas kernels, backward(): pl.pallas_call(functools.partial(backward_kernel, places, total_places),...  16.4 us
    pallas_call x2, Pallas kernels, forward(): pl.pallas_call(functools.partial(forward_kernel, groups, contract, width,...  15 us
    ppermute x14, starting transfers between devices, exchange(): return lax.ppermute(value, ('tp', 'dp'), pairs)  14.9 us
    pallas_call x2, Pallas kernels, forward_streamed(): pl.pallas_call(functools.partial(streamed_kernel, groups, width), in_spec...  14.8 us
    pallas_call x2, Pallas kernels, weight(): pl.pallas_call(functools.partial(weight_kernel, turned), in_specs=[pl.Blo...  13.2 us
  transfers between devices with their start and end apart: 44, of which 20 were waited for; matrix products, arithmetic and copies ran while one was open for 0% of the time, Pallas kernels for 34%

profile of v7, /device:TPU:0, one launch (start us, length us, event | category | flops | bytes accessed | tf_op | source)
XLA Modules:
  0.0 188.0 jit_solution(9510449055220974641)
XLA Ops:
  0.1 1.8 order_rows.1
  1.9 4.1 %collective-permute-start = (bf16[256,384]{1,0:T(8,128)(2,1)S(1)}, bf16[256,384]{1,0:T(8,128)(2,1)S(1)}, u32[]{:S(2)}, u32[]{:S(2)}) collective-permute-start(bf16[256,384]{1,0:T(8,128)(2,1)S(1)} %get-tuple-element.157.own_ref), channel_id=1, source_target_pairs={{0,16},{4,20},{8,24},{12,28},{16,0},{20,4},{24,8},{28,12},{1,17},{... | collective-permute-start | bytes 589832 | tf_op jit(solution)/shard_map/ppermute | solution.py:471
  6.0 1.6 collective-permute-start.1
  8.9 6.6 %scaled_weight.3.refs_2_.refs_4_ = bf16[3072,2048]{1,0:T(8,128)(2,1)S(1)} custom-call(bf16[3072,2048]{1,0:T(8,128)(2,1)} %code_ref.3, f32[16,24]{1,0:T(8,128)S(1)} %bitcast.5), custom_call_target="tpu_custom_call" | custom-call | bytes 1536 | tf_op jit(solution)/shard_map/scaled_weight/pallas_call | solution.py:88
  16.0 1.3 collective-permute-start.3
  17.3 4.0 %collective-permute-start.4 = (bf16[256,384]{1,0:T(8,128)(2,1)S(1)}, bf16[256,384]{1,0:T(8,128)(2,1)S(1)}, u32[]{:S(2)}, u32[]{:S(2)}) collective-permute-start(bf16[256,384]{1,0:T(8,128)(2,1)S(1)} %get-tuple-element.161.own_ref), channel_id=1, source_target_pairs={{0,16},{4,20},{8,24},{12,28},{16,0},{20,4},{24,8},{28,12},{1,17},{... | collective-permute-start | bytes 589832 | tf_op jit(solution)/shard_map/ppermute | solution.py:471
  21.3 6.6 %scaled_weight.2.refs_3_.refs_5_ = bf16[3072,2048]{1,0:T(8,128)(2,1)S(1)} custom-call(bf16[3072,2048]{1,0:T(8,128)(2,1)} %code_ref.2, f32[16,24]{1,0:T(8,128)S(1)} %bitcast.6), custom_call_target="tpu_custom_call" | custom-call | bytes 1536 | tf_op jit(solution)/shard_map/scaled_weight/pallas_call | solution.py:88
  27.9 2.1 %collective-permute-done.4.two_ref = bf16[256,384]{1,0:T(8,128)(2,1)S(1)} collective-permute-done((bf16[256,384]{1,0:T(8,128)(2,1)S(1)}, bf16[256,384]{1,0:T(8,128)(2,1)S(1)}, u32[]{:S(2)}, u32[]{:S(2)}) %collective-permute-start.4) | collective-permute-done | bytes 196640 | tf_op jit(solution)/shard_map/ppermute | solution.py:471
  30.0 2.0 %collective-permute-done.5.near_ref = bf16[256,384]{1,0:T(8,128)(2,1)S(1)} collective-permute-done((bf16[256,384]{1,0:T(8,128)(2,1)S(1)}, bf16[256,384]{1,0:T(8,128)(2,1)S(1)}, u32[]{:S(2)}, u32[]{:S(2)}) %collective-permute-start.5) | collective-permute-done | bytes 196640 | tf_op jit(solution)/shard_map/ppermute | solution.py:476
  33.4 1.3 collective-permute-start.8
  35.0 7.5 %forward_product.2 = (bf16[128,4096]{1,0:T(8,128)(2,1)S(1)}, bf16[64,4096]{1,0:T(8,128)(2,1)S(1)}, bf16[64,4096]{1,0:T(8,128)(2,1)S(1)}) custom-call(s32[3]{0:T(128)S(1)} %pad_add_fusion.where_ref, bf16[256,1536]{1,0:T(8,128)(2,1)S(1)} %join.4.refs_0_, bf16[256,1536]{1,0:T(8,128)(2,1)S(1)} %collective-permute-done.6.refs_1_, ...), custom_call_target="tpu_custom_call" | custom-call | flops 1024 | bytes 1024 | tf_op jit(solution)/shard_map/forward_product/pallas_call | solution.py:231
  42.5 1.1 collective-permute-done.8.passed_ref
  43.6 1.5 collective-permute-start.10
  45.8 3.7 %collective-permute-start.11 = (bf16[256,384]{1,0:T(8,128)(2,1)S(1)}, bf16[256,384]{1,0:T(8,128)(2,1)S(1)}, u32[]{:S(2)}, u32[]{:S(2)}) collective-permute-start(bf16[256,384]{1,0:T(8,128)(2,1)S(1)} %get-tuple-element.187.own_ref), channel_id=1, source_target_pairs={{0,16},{4,20},{8,24},{12,28},{16,0},{20,4},{24,8},{28,12},{1,17},{... | collective-permute-start | bytes 589832 | tf_op jit(solution)/shard_map/ppermute | solution.py:471
  50.2 7.4 %forward_streamed.2 = (bf16[128,2048]{1,0:T(8,128)(2,1)S(1)}, bf16[64,2048]{1,0:T(8,128)(2,1)S(1)}, bf16[64,2048]{1,0:T(8,128)(2,1)S(1)}) custom-call(s32[3]{0:T(128)S(1)} %pad_add_fusion.where_ref, f32[16,24]{1,0:T(8,128)S(1)} %copy-done, bf16[256,1536]{1,0:T(8,128)(2,1)S(1)} %join.5.refs_0_, bf16[256,1536]{1,0:T(8,128)(2,1)S(1)} %collective-permute-done.9.refs_1_, ...), custom_call_target="tpu_custom_call" | custom-call | flops 1024 | bytes 1024 | tf_op jit(solution)/shard_map/forward_streamed/pallas_call | solution.py:303
  57.7 1.9 %collective-permute-done.11.two_ref = bf16[256,384]{1,0:T(8,128)(2,1)S(1)} collective-permute-done((bf16[256,384]{1,0:T(8,128)(2,1)S(1)}, bf16[256,384]{1,0:T(8,128)(2,1)S(1)}, u32[]{:S(2)}, u32[]{:S(2)}) %collective-permute-start.11) | collective-permute-done | bytes 196640 | tf_op jit(solution)/shard_map/ppermute | solution.py:471
  59.8 1.3 collective-permute-start.14
  61.1 2.9 %collective-permute-start.17 = (bf16[256,384]{1,0:T(8,128)(2,1)S(1)}, bf16[256,384]{1,0:T(8,128)(2,1)S(1)}, u32[]{:S(2)}, u32[]{:S(2)}) collective-permute-start(bf16[256,384]{1,0:T(8,128)(2,1)S(1)} %get-tuple-element.200.own_ref), channel_id=1, source_target_pairs={{0,16},{4,20},{8,24},{12,28},{16,0},{20,4},{24,8},{28,12},{1,17},{... | collective-permute-start | bytes 589832 | tf_op jit(solution)/shard_map/ppermute | solution.py:471
  64.0 1.4 collective-permute-start.16
  65.4 7.4 %collective-permute-done.14.passed_ref = bf16[256,384]{1,0:T(8,128)(2,1)S(1)} collective-permute-done((bf16[256,384]{1,0:T(8,128)(2,1)S(1)}, bf16[256,384]{1,0:T(8,128)(2,1)S(1)}, u32[]{:S(2)}, u32[]{:S(2)}) %collective-permute-start.14) | collective-permute-done | bytes 196640 | tf_op jit(solution)/shard_map/ppermute | solution.py:476
  73.7 1.6 collective-permute-start.21
  75.3 1.0 collective-permute-done.18.near_ref
  76.4 1.6 collective-permute-start.22
  78.6 1.5 collective-permute-start.20
  80.1 7.5 %forward_product.3 = (bf16[128,4096]{1,0:T(8,128)(2,1)S(1)}, bf16[64,4096]{1,0:T(8,128)(2,1)S(1)}, bf16[64,4096]{1,0:T(8,128)(2,1)S(1)}) custom-call(s32[3]{0:T(128)S(1)} %pad_add_fusion.where_ref, bf16[256,1536]{1,0:T(8,128)(2,1)S(1)} %join.6.refs_0_, bf16[256,1536]{1,0:T(8,128)(2,1)S(1)} %collective-permute-done.15.refs_1_, ...), custom_call_target="tpu_custom_call" | custom-call | flops 1024 | bytes 1024 | tf_op jit(solution)/shard_map/forward_product/pallas_call | solution.py:231
  89.0 1.0 hidden_grads.2.refs_0_
  90.6 0.9 collective-permute-start.24
  92.0 7.4 %forward_streamed.3 = (bf16[128,2048]{1,0:T(8,128)(2,1)S(1)}, bf16[64,2048]{1,0:T(8,128)(2,1)S(1)}, bf16[64,2048]{1,0:T(8,128)(2,1)S(1)}) custom-call(s32[3]{0:T(128)S(1)} %pad_add_fusion.where_ref, f32[16,24]{1,0:T(8,128)S(1)} %copy-done, bf16[256,1536]{1,0:T(8,128)(2,1)S(1)} %join.7.refs_0_, bf16[256,1536]{1,0:T(8,128)(2,1)S(1)} %collective-permute-done.23.refs_1_, ...), custom_call_target="tpu_custom_call" | custom-call | flops 1024 | bytes 1024 | tf_op jit(solution)/shard_map/forward_streamed/pallas_call | solution.py:303
  99.5 1.2 collective-permute-start.28
  100.7 8.2 %collective-permute-done.25.refs_1_ = bf16[128,4096]{1,0:T(8,128)(2,1)S(1)} collective-permute-done((bf16[128,4096]{1,0:T(8,128)(2,1)S(1)}, bf16[128,4096]{1,0:T(8,128)(2,1)S(1)}, u32[]{:S(2)}, u32[]{:S(2)}) %collective-permute-start.25) | collective-permute-done | bytes 1048608 | tf_op jit(solution)/shard_map/ppermute | solution.py:465
  108.8 5.6 %collective-permute-done.24.refs_1_ = bf16[64,4096]{1,0:T(8,128)(2,1)S(1)} collective-permute-done((bf16[64,4096]{1,0:T(8,128)(2,1)S(1)}, bf16[64,4096]{1,0:T(8,128)(2,1)S(1)}, u32[]{:S(2)}, u32[]{:S(2)}) %collective-permute-start.24) | collective-permute-done | bytes 524320 | tf_op jit(solution)/shard_map/ppermute | solution.py:465
  115.1 1.6 collective-permute-start.30
  116.7 6.8 %collective-permute-done.28.refs_4_ = bf16[128,2048]{1,0:T(8,128)(2,1)S(1)} collective-permute-done((bf16[128,2048]{1,0:T(8,128)(2,1)S(1)}, bf16[128,2048]{1,0:T(8,128)(2,1)S(1)}, u32[]{:S(2)}, u32[]{:S(2)}) %collective-permute-start.28) | collective-permute-done | bytes 524320 | tf_op jit(solution)/shard_map/ppermute | solution.py:465
  123.5 1.7 collective-permute-done.27.refs_3_
  125.8 7.4 %backward_product.4 = (bf16[256,1536]{1,0:T(8,128)(2,1)S(1)}, bf16[256,1536]{1,0:T(8,128)(2,1)S(1)}) custom-call(s32[3]{0:T(128)S(1)} %pad_add_fusion.where_ref, bf16[64,4096]{1,0:T(8,128)(2,1)S(1)} %hidden_grads.2.refs_0_, bf16[64,4096]{1,0:T(8,128)(2,1)S(1)} %collective-permute-done.24.refs_1_, bf16[64,4096]{1,0:T(8,128)(2,1)S(1)} %collective-permute-done.26.refs_2_, ...), custom_call_target="tpu_custom_call" | custom-call | flops 1024 | bytes 1024 | tf_op jit(solution)/shard_map/backward_product/pallas_call | solution.py:382
  133.9 1.0 hidden_grads.3.refs_0_
  134.9 1.3 collective-permute-start.31
  136.4 2.7 %collective-permute-start.33 = (bf16[256,384]{1,0:T(8,128)(2,1)S(1)}, bf16[256,384]{1,0:T(8,128)(2,1)S(1)}, u32[]{:S(2)}, u32[]{:S(2)}) collective-permute-start(bf16[256,384]{1,0:T(8,128)(2,1)S(1)} %get-tuple-element.265), channel_id=1, source_target_pairs={{0,8},{4,12},{8,16},{12,20},{16,24},{20,28},{24,0},{28,4},{1,9},{5... | collective-permute-start | bytes 589832 | tf_op jit(solution)/shard_map/ppermute | solution.py:471
  140.0 6.9 %collective-permute-done.31.refs_1_ = bf16[64,4096]{1,0:T(8,128)(2,1)S(1)} collective-permute-done((bf16[64,4096]{1,0:T(8,128)(2,1)S(1)}, bf16[64,4096]{1,0:T(8,128)(2,1)S(1)}, u32[]{:S(2)}, u32[]{:S(2)}) %collective-permute-start.31) | collective-permute-done | bytes 524320 | tf_op jit(solution)/shard_map/ppermute | solution.py:465
  147.7 5.6 %collective-permute-start.36 = (bf16[256,384]{1,0:T(8,128)(2,1)S(1)}, bf16[256,384]{1,0:T(8,128)(2,1)S(1)}, u32[]{:S(2)}, u32[]{:S(2)}) collective-permute-start(bf16[256,384]{1,0:T(8,128)(2,1)S(1)} %get-tuple-element.268), channel_id=1, source_target_pairs={{0,16},{4,20},{8,24},{12,28},{16,0},{20,4},{24,8},{28,12},{1,17},{... | collective-permute-start | bytes 589832 | tf_op jit(solution)/shard_map/ppermute | solution.py:471
  153.3 1.0 collective-permute-start.38
  154.3 6.9 %collective-permute-done.36.refs_1_ = bf16[256,384]{1,0:T(8,128)(2,1)S(1)} collective-permute-done((bf16[256,384]{1,0:T(8,128)(2,1)S(1)}, bf16[256,384]{1,0:T(8,128)(2,1)S(1)}, u32[]{:S(2)}, u32[]{:S(2)}) %collective-permute-start.36) | collective-permute-done | bytes 196640 | tf_op jit(solution)/shard_map/ppermute | solution.py:471
  161.3 2.5 %backward_product.5 = (bf16[256,384]{1,0:T(8,128)(2,1)S(1)}, bf16[256,384]{1,0:T(8,128)(2,1)S(1)}) custom-call(s32[3]{0:T(128)S(1)} %pad_add_fusion.where_ref, bf16[64,4096]{1,0:T(8,128)(2,1)S(1)} %hidden_grads.3.refs_0_, bf16[64,4096]{1,0:T(8,128)(2,1)S(1)} %collective-permute-done.31.refs_1_, bf16[64,4096]{1,0:T(8,128)(2,1)S(1)} %collective-permute-done.34.refs_2_, ...), custom_call_target="tpu_custom_call" | custom-call | flops 1024 | bytes 1024 | tf_op jit(solution)/shard_map/backward_product/pallas_call | solution.py:382
  163.8 4.1 %backward_product.6 = (bf16[256,768]{1,0:T(8,128)(2,1)S(1)}, bf16[256,768]{1,0:T(8,128)(2,1)S(1)}) custom-call(s32[3]{0:T(128)S(1)} %pad_add_fusion.where_ref, bf16[64,4096]{1,0:T(8,128)(2,1)S(1)} %hidden_grads.3.refs_0_, bf16[64,4096]{1,0:T(8,128)(2,1)S(1)} %collective-permute-done.31.refs_1_, bf16[64,4096]{1,0:T(8,128)(2,1)S(1)} %collective-permute-done.34.refs_2_, ...), custom_call_target="tpu_custom_call" | custom-call | flops 1024 | bytes 1024 | tf_op jit(solution)/shard_map/backward_product/pallas_call | solution.py:382
  170.0 4.0 %collective-permute-start.41 = (bf16[256,384]{1,0:T(8,128)(2,1)S(1)}, bf16[256,384]{1,0:T(8,128)(2,1)S(1)}, u32[]{:S(2)}, u32[]{:S(2)}) collective-permute-start(bf16[256,384]{1,0:T(8,128)(2,1)S(1)} %get-tuple-element.305), channel_id=1, source_target_pairs={{0,8},{4,12},{8,16},{12,20},{16,24},{20,28},{24,0},{28,4},{1,9},{5... | collective-permute-start | bytes 589832 | tf_op jit(solution)/shard_map/ppermute | solution.py:471
  174.7 2.4 %backward_product.7 = (bf16[256,384]{1,0:T(8,128)(2,1)S(1)}, bf16[256,384]{1,0:T(8,128)(2,1)S(1)}) custom-call(s32[3]{0:T(128)S(1)} %pad_add_fusion.where_ref, bf16[64,4096]{1,0:T(8,128)(2,1)S(1)} %hidden_grads.3.refs_0_, bf16[64,4096]{1,0:T(8,128)(2,1)S(1)} %collective-permute-done.31.refs_1_, bf16[64,4096]{1,0:T(8,128)(2,1)S(1)} %collective-permute-done.34.refs_2_, ...), custom_call_target="tpu_custom_call" | custom-call | flops 1024 | bytes 1024 | tf_op jit(solution)/shard_map/backward_product/pallas_call | solution.py:382
  178.0 7.8 %collective-permute-done.40.refs_1_ = bf16[256,384]{1,0:T(8,128)(2,1)S(1)} collective-permute-done((bf16[256,384]{1,0:T(8,128)(2,1)S(1)}, bf16[256,384]{1,0:T(8,128)(2,1)S(1)}, u32[]{:S(2)}, u32[]{:S(2)}) %collective-permute-start.40) | collective-permute-done | bytes 196640 | tf_op jit(solution)/shard_map/ppermute | solution.py:471
  186.6 1.4 final_sum.3
  (73 shorter events, 17.5 us)
Async XLA Ops:
  1.9 14.1 %collective-permute-start = (bf16[256,384]{1,0:T(8,128)(2,1)S(1)}, bf16[256,384]{1,0:T(8,128)(2,1)S(1)}, u32[]{:S(2)}, u32[]{:S(2)}) collective-permute-start(bf16[256,384]{1,0:T(8,128)(2,1)S(1)} %get-tuple-element.157.own_ref), channel_id=1, source_target_pairs={{0,16},{4,20},{8,24},{12,28},{16,0},{20,4},{24,8},{28,12},{1,17},{... | collective-permute-start | bytes 589832 | tf_op jit(solution)/shard_map/ppermute | solution.py:471
  6.0 10.0 %collective-permute-start.1 = (bf16[256,384]{1,0:T(8,128)(2,1)S(1)}, bf16[256,384]{1,0:T(8,128)(2,1)S(1)}, u32[]{:S(2)}, u32[]{:S(2)}) collective-permute-start(bf16[256,384]{1,0:T(8,128)(2,1)S(1)} %get-tuple-element.157.own_ref), channel_id=1, source_target_pairs={{0,8},{4,12},{8,0},{12,4},{16,24},{20,28},{24,16},{28,20},{1,9},{5... | collective-permute-start | bytes 589832 | tf_op jit(solution)/shard_map/ppermute | solution.py:476
  7.6 20.3 %collective-permute-start.2 = (bf16[256,384]{1,0:T(8,128)(2,1)S(1)}, bf16[256,384]{1,0:T(8,128)(2,1)S(1)}, u32[]{:S(2)}, u32[]{:S(2)}) collective-permute-start(bf16[256,384]{1,0:T(8,128)(2,1)S(1)} %get-tuple-element.157.own_ref), channel_id=1, source_target_pairs={{8,16},{12,20},{16,8},{20,12},{9,17},{13,21},{17,9},{21,13},{10,18... | collective-permute-start | bytes 589832 | tf_op jit(solution)/shard_map/ppermute | solution.py:476
  8.2 0.7 copy-start.1
  8.9 12.4 %copy-start.2 = (f32[24,16]{0,1:T(8,128)S(1)}, f32[24,16]{0,1:T(8,128)}, u32[]{:S(2)}) copy-start(f32[24,16]{0,1:T(8,128)} %param.13) | copy-start | bytes 4612
  16.0 11.9 %collective-permute-start.3 = (bf16[256,384]{1,0:T(8,128)(2,1)S(1)}, bf16[256,384]{1,0:T(8,128)(2,1)S(1)}, u32[]{:S(2)}, u32[]{:S(2)}) collective-permute-start(bf16[256,384]{1,0:T(8,128)(2,1)S(1)} %collective-permute-done.two_ref), channel_id=1, source_target_pairs={{8,0},{12,4},{16,24},{20,28},{9,1},{13,5},{17,25},{21,29},{10,2},{... | collective-permute-start | bytes 589832 | tf_op jit(solution)/shard_map/ppermute | solution.py:476
  17.3 12.7 %collective-permute-start.4 = (bf16[256,384]{1,0:T(8,128)(2,1)S(1)}, bf16[256,384]{1,0:T(8,128)(2,1)S(1)}, u32[]{:S(2)}, u32[]{:S(2)}) collective-permute-start(bf16[256,384]{1,0:T(8,128)(2,1)S(1)} %get-tuple-element.161.own_ref), channel_id=1, source_target_pairs={{0,16},{4,20},{8,24},{12,28},{16,0},{20,4},{24,8},{28,12},{1,17},{... | collective-permute-start | bytes 589832 | tf_op jit(solution)/shard_map/ppermute | solution.py:471
  21.3 10.7 %collective-permute-start.5 = (bf16[256,384]{1,0:T(8,128)(2,1)S(1)}, bf16[256,384]{1,0:T(8,128)(2,1)S(1)}, u32[]{:S(2)}, u32[]{:S(2)}) collective-permute-start(bf16[256,384]{1,0:T(8,128)(2,1)S(1)} %get-tuple-element.161.own_ref), channel_id=1, source_target_pairs={{0,8},{4,12},{8,0},{12,4},{16,24},{20,28},{24,16},{28,20},{1,9},{5... | collective-permute-start | bytes 589832 | tf_op jit(solution)/shard_map/ppermute | solution.py:476
  32.6 17.6 %copy-start = (f32[16,24]{1,0:T(8,128)S(1)}, f32[16,24]{1,0:T(8,128)}, u32[]{:S(2)}) copy-start(f32[16,24]{1,0:T(8,128)} %scale_ref.3) | copy-start | bytes 4612
  32.6 2.4 %collective-permute-start.6 = (bf16[256,1536]{1,0:T(8,128)(2,1)S(1)}, bf16[256,1536]{1,0:T(8,128)(2,1)S(1)}, u32[]{:S(2)}, u32[]{:S(2)}) collective-permute-start(bf16[256,1536]{1,0:T(8,128)(2,1)S(1)} %join.4.refs_0_), channel_id=1, source_target_pairs={{0,4},{4,0},{8,12},{12,8},{16,20},{20,16},{24,28},{28,24},{1,5},{5... | collective-permute-start | bytes 2359304 | tf_op jit(solution)/shard_map/ppermute | solution.py:468
  32.7 9.8 %collective-permute-start.7 = (bf16[256,384]{1,0:T(8,128)(2,1)S(1)}, bf16[256,384]{1,0:T(8,128)(2,1)S(1)}, u32[]{:S(2)}, u32[]{:S(2)}) collective-permute-start(bf16[256,384]{1,0:T(8,128)(2,1)S(1)} %get-tuple-element.161.own_ref), channel_id=1, source_target_pairs={{8,16},{12,20},{16,8},{20,12},{9,17},{13,21},{17,9},{21,13},{10,18... | collective-permute-start | bytes 589832 | tf_op jit(solution)/shard_map/ppermute | solution.py:476
  33.4 10.2 %collective-permute-start.8 = (bf16[256,384]{1,0:T(8,128)(2,1)S(1)}, bf16[256,384]{1,0:T(8,128)(2,1)S(1)}, u32[]{:S(2)}, u32[]{:S(2)}) collective-permute-start(bf16[256,384]{1,0:T(8,128)(2,1)S(1)} %collective-permute-done.4.two_ref), channel_id=1, source_target_pairs={{8,0},{12,4},{16,24},{20,28},{9,1},{13,5},{17,25},{21,29},{10,2},{... | collective-permute-start | bytes 589832 | tf_op jit(solution)/shard_map/ppermute | solution.py:476
  43.6 16.2 %collective-permute-start.10 = (bf16[128,4096]{1,0:T(8,128)(2,1)S(1)}, bf16[128,4096]{1,0:T(8,128)(2,1)S(1)}, u32[]{:S(2)}, u32[]{:S(2)}) collective-permute-start(bf16[128,4096]{1,0:T(8,128)(2,1)S(1)} %get-tuple-element.184), channel_id=1, source_target_pairs={{0,1},{1,0},{2,3},{3,2},{4,6},{5,7},{6,4},{7,5},{8,9},{9,8},{10,11... | collective-permute-start | bytes 3145736 | tf_op jit(solution)/shard_map/ppermute | solution.py:465
  45.7 4.5 %collective-permute-start.9 = (bf16[256,1536]{1,0:T(8,128)(2,1)S(1)}, bf16[256,1536]{1,0:T(8,128)(2,1)S(1)}, u32[]{:S(2)}, u32[]{:S(2)}) collective-permute-start(bf16[256,1536]{1,0:T(8,128)(2,1)S(1)} %join.5.refs_0_), channel_id=1, source_target_pairs={{0,4},{4,0},{8,12},{12,8},{16,20},{20,16},{24,28},{28,24},{1,5},{5... | collective-permute-start | bytes 2359304 | tf_op jit(solution)/shard_map/ppermute | solution.py:468
  45.8 13.7 %collective-permute-start.11 = (bf16[256,384]{1,0:T(8,128)(2,1)S(1)}, bf16[256,384]{1,0:T(8,128)(2,1)S(1)}, u32[]{:S(2)}, u32[]{:S(2)}) collective-permute-start(bf16[256,384]{1,0:T(8,128)(2,1)S(1)} %get-tuple-element.187.own_ref), channel_id=1, source_target_pairs={{0,16},{4,20},{8,24},{12,28},{16,0},{20,4},{24,8},{28,12},{1,17},{... | collective-permute-start | bytes 589832 | tf_op jit(solution)/shard_map/ppermute | solution.py:471
  49.5 10.3 %collective-permute-start.12 = (bf16[256,384]{1,0:T(8,128)(2,1)S(1)}, bf16[256,384]{1,0:T(8,128)(2,1)S(1)}, u32[]{:S(2)}, u32[]{:S(2)}) collective-permute-start(bf16[256,384]{1,0:T(8,128)(2,1)S(1)} %get-tuple-element.187.own_ref), channel_id=1, source_target_pairs={{0,8},{4,12},{8,0},{12,4},{16,24},{20,28},{24,16},{28,20},{1,9},{5... | collective-permute-start | bytes 589832 | tf_op jit(solution)/shard_map/ppermute | solution.py:476
  49.5 15.9 %collective-permute-start.13 = (bf16[256,384]{1,0:T(8,128)(2,1)S(1)}, bf16[256,384]{1,0:T(8,128)(2,1)S(1)}, u32[]{:S(2)}, u32[]{:S(2)}) collective-permute-start(bf16[256,384]{1,0:T(8,128)(2,1)S(1)} %get-tuple-element.187.own_ref), channel_id=1, source_target_pairs={{8,16},{12,20},{16,8},{20,12},{9,17},{13,21},{17,9},{21,13},{10,18... | collective-permute-start | bytes 589832 | tf_op jit(solution)/shard_map/ppermute | solution.py:476
  59.8 13.0 %collective-permute-start.14 = (bf16[256,384]{1,0:T(8,128)(2,1)S(1)}, bf16[256,384]{1,0:T(8,128)(2,1)S(1)}, u32[]{:S(2)}, u32[]{:S(2)}) collective-permute-start(bf16[256,384]{1,0:T(8,128)(2,1)S(1)} %collective-permute-done.11.two_ref), channel_id=1, source_target_pairs={{8,0},{12,4},{16,24},{20,28},{9,1},{13,5},{17,25},{21,29},{10,2},{... | collective-permute-start | bytes 589832 | tf_op jit(solution)/shard_map/ppermute | solution.py:476
  61.1 14.2 %collective-permute-start.17 = (bf16[256,384]{1,0:T(8,128)(2,1)S(1)}, bf16[256,384]{1,0:T(8,128)(2,1)S(1)}, u32[]{:S(2)}, u32[]{:S(2)}) collective-permute-start(bf16[256,384]{1,0:T(8,128)(2,1)S(1)} %get-tuple-element.200.own_ref), channel_id=1, source_target_pairs={{0,16},{4,20},{8,24},{12,28},{16,0},{20,4},{24,8},{28,12},{1,17},{... | collective-permute-start | bytes 589832 | tf_op jit(solution)/shard_map/ppermute | solution.py:471
  64.0 12.3 %collective-permute-start.18 = (bf16[256,384]{1,0:T(8,128)(2,1)S(1)}, bf16[256,384]{1,0:T(8,128)(2,1)S(1)}, u32[]{:S(2)}, u32[]{:S(2)}) collective-permute-start(bf16[256,384]{1,0:T(8,128)(2,1)S(1)} %get-tuple-element.200.own_ref), channel_id=1, source_target_pairs={{0,8},{4,12},{8,0},{12,4},{16,24},{20,28},{24,16},{28,20},{1,9},{5... | collective-permute-start | bytes 589832 | tf_op jit(solution)/shard_map/ppermute | solution.py:476
  64.0 12.3 %collective-permute-start.16 = (bf16[128,2048]{1,0:T(8,128)(2,1)S(1)}, bf16[128,2048]{1,0:T(8,128)(2,1)S(1)}, u32[]{:S(2)}, u32[]{:S(2)}) collective-permute-start(bf16[128,2048]{1,0:T(8,128)(2,1)S(1)} %get-tuple-element.197), channel_id=1, source_target_pairs={{0,1},{1,0},{2,3},{3,2},{4,6},{5,7},{6,4},{7,5},{8,9},{9,8},{10,11... | collective-permute-start | bytes 1572872 | tf_op jit(solution)/shard_map/ppermute | solution.py:465
  73.5 2.8 %collective-permute-start.15 = (bf16[256,1536]{1,0:T(8,128)(2,1)S(1)}, bf16[256,1536]{1,0:T(8,128)(2,1)S(1)}, u32[]{:S(2)}, u32[]{:S(2)}) collective-permute-start(bf16[256,1536]{1,0:T(8,128)(2,1)S(1)} %join.6.refs_0_), channel_id=1, source_target_pairs={{0,4},{4,0},{8,12},{12,8},{16,20},{20,16},{24,28},{28,24},{1,5},{5... | collective-permute-start | bytes 2359304 | tf_op jit(solution)/shard_map/ppermute | solution.py:468
  73.7 13.9 %collective-permute-start.21 = (bf16[64,4096]{1,0:T(8,128)(2,1)S(1)}, bf16[64,4096]{1,0:T(8,128)(2,1)S(1)}, u32[]{:S(2)}, u32[]{:S(2)}) collective-permute-start(bf16[64,4096]{1,0:T(8,128)(2,1)S(1)} %add_convert_fusion.1), channel_id=1, source_target_pairs={{0,2},{1,3},{2,0},{3,1},{4,5},{5,4},{6,7},{7,6},{8,10},{9,11},{10,... | collective-permute-start | bytes 1572872 | tf_op jit(solution)/shard_map/ppermute | solution.py:465
  76.4 11.3 %collective-permute-start.22 = (bf16[64,2048]{1,0:T(8,128)(2,1)S(1)}, bf16[64,2048]{1,0:T(8,128)(2,1)S(1)}, u32[]{:S(2)}, u32[]{:S(2)}) collective-permute-start(bf16[64,2048]{1,0:T(8,128)(2,1)S(1)} %add_convert_fusion.3), channel_id=1, source_target_pairs={{0,2},{1,3},{2,0},{3,1},{4,5},{5,4},{6,7},{7,6},{8,10},{9,11},{10,... | collective-permute-start | bytes 786440 | tf_op jit(solution)/shard_map/ppermute | solution.py:465
  77.9 9.7 %collective-permute-start.19 = (bf16[256,384]{1,0:T(8,128)(2,1)S(1)}, bf16[256,384]{1,0:T(8,128)(2,1)S(1)}, u32[]{:S(2)}, u32[]{:S(2)}) collective-permute-start(bf16[256,384]{1,0:T(8,128)(2,1)S(1)} %get-tuple-element.200.own_ref), channel_id=1, source_target_pairs={{8,16},{12,20},{16,8},{20,12},{9,17},{13,21},{17,9},{21,13},{10,18... | collective-permute-start | bytes 589832 | tf_op jit(solution)/shard_map/ppermute | solution.py:476
  78.6 9.0 %collective-permute-start.20 = (bf16[256,384]{1,0:T(8,128)(2,1)S(1)}, bf16[256,384]{1,0:T(8,128)(2,1)S(1)}, u32[]{:S(2)}, u32[]{:S(2)}) collective-permute-start(bf16[256,384]{1,0:T(8,128)(2,1)S(1)} %collective-permute-done.17.two_ref), channel_id=1, source_target_pairs={{8,0},{12,4},{16,24},{20,28},{9,1},{13,5},{17,25},{21,29},{10,2},{... | collective-permute-start | bytes 589832 | tf_op jit(solution)/shard_map/ppermute | solution.py:476
  88.3 2.4 %collective-permute-start.23 = (bf16[256,1536]{1,0:T(8,128)(2,1)S(1)}, bf16[256,1536]{1,0:T(8,128)(2,1)S(1)}, u32[]{:S(2)}, u32[]{:S(2)}) collective-permute-start(bf16[256,1536]{1,0:T(8,128)(2,1)S(1)} %join.7.refs_0_), channel_id=1, source_target_pairs={{0,4},{4,0},{8,12},{12,8},{16,20},{20,16},{24,28},{28,24},{1,5},{5... | collective-permute-start | bytes 2359304 | tf_op jit(solution)/shard_map/ppermute | solution.py:468
  88.4 20.5 %collective-permute-start.25 = (bf16[128,4096]{1,0:T(8,128)(2,1)S(1)}, bf16[128,4096]{1,0:T(8,128)(2,1)S(1)}, u32[]{:S(2)}, u32[]{:S(2)}) collective-permute-start(bf16[128,4096]{1,0:T(8,128)(2,1)S(1)} %get-tuple-element.227), channel_id=1, source_target_pairs={{0,1},{1,0},{2,3},{3,2},{4,6},{5,7},{6,4},{7,5},{8,9},{9,8},{10,11... | collective-permute-start | bytes 3145736 | tf_op jit(solution)/shard_map/ppermute | solution.py:465
  90.6 23.8 %collective-permute-start.24 = (bf16[64,4096]{1,0:T(8,128)(2,1)S(1)}, bf16[64,4096]{1,0:T(8,128)(2,1)S(1)}, u32[]{:S(2)}, u32[]{:S(2)}) collective-permute-start(bf16[64,4096]{1,0:T(8,128)(2,1)S(1)} %hidden_grads.2.refs_0_), channel_id=1, source_target_pairs={{0,1},{1,0},{2,3},{3,2},{4,6},{5,7},{6,4},{7,5},{8,9},{9,8},{10,11... | collective-permute-start | bytes 1572872 | tf_op jit(solution)/shard_map/ppermute | solution.py:465
  91.5 25.2 %collective-permute-start.26 = (bf16[64,4096]{1,0:T(8,128)(2,1)S(1)}, bf16[64,4096]{1,0:T(8,128)(2,1)S(1)}, u32[]{:S(2)}, u32[]{:S(2)}) collective-permute-start(bf16[64,4096]{1,0:T(8,128)(2,1)S(1)} %hidden_grads.2.refs_0_), channel_id=1, source_target_pairs={{0,2},{1,3},{2,0},{3,1},{4,5},{5,4},{6,7},{7,6},{8,10},{9,11},{10,... | collective-permute-start | bytes 1572872 | tf_op jit(solution)/shard_map/ppermute | solution.py:465
  99.5 24.0 %collective-permute-start.28 = (bf16[128,2048]{1,0:T(8,128)(2,1)S(1)}, bf16[128,2048]{1,0:T(8,128)(2,1)S(1)}, u32[]{:S(2)}, u32[]{:S(2)}) collective-permute-start(bf16[128,2048]{1,0:T(8,128)(2,1)S(1)} %get-tuple-element.239), channel_id=1, source_target_pairs={{0,1},{1,0},{2,3},{3,2},{4,6},{5,7},{6,4},{7,5},{8,9},{9,8},{10,11... | collective-permute-start | bytes 1572872 | tf_op jit(solution)/shard_map/ppermute | solution.py:465
  114.5 10.7 %collective-permute-start.27 = (bf16[64,4096]{1,0:T(8,128)(2,1)S(1)}, bf16[64,4096]{1,0:T(8,128)(2,1)S(1)}, u32[]{:S(2)}, u32[]{:S(2)}) collective-permute-start(bf16[64,4096]{1,0:T(8,128)(2,1)S(1)} %collective-permute-done.24.refs_1_), channel_id=1, source_target_pairs={{0,2},{1,3},{2,0},{3,1},{4,5},{5,4},{6,7},{7,6},{8,10},{9,11},{10,... | collective-permute-start | bytes 1572872 | tf_op jit(solution)/shard_map/ppermute | solution.py:465
  115.1 18.1 %collective-permute-start.30 = (bf16[64,4096]{1,0:T(8,128)(2,1)S(1)}, bf16[64,4096]{1,0:T(8,128)(2,1)S(1)}, u32[]{:S(2)}, u32[]{:S(2)}) collective-permute-start(bf16[64,4096]{1,0:T(8,128)(2,1)S(1)} %add_convert_fusion), channel_id=1, source_target_pairs={{0,2},{1,3},{2,0},{3,1},{4,5},{5,4},{6,7},{7,6},{8,10},{9,11},{10,... | collective-permute-start | bytes 1572872 | tf_op jit(solution)/shard_map/ppermute | solution.py:465
  125.2 8.4 %collective-permute-start.29 = (bf16[64,2048]{1,0:T(8,128)(2,1)S(1)}, bf16[64,2048]{1,0:T(8,128)(2,1)S(1)}, u32[]{:S(2)}, u32[]{:S(2)}) collective-permute-start(bf16[64,2048]{1,0:T(8,128)(2,1)S(1)} %add_convert_fusion.2), channel_id=1, source_target_pairs={{0,2},{1,3},{2,0},{3,1},{4,5},{5,4},{6,7},{7,6},{8,10},{9,11},{10,... | collective-permute-start | bytes 786440 | tf_op jit(solution)/shard_map/ppermute | solution.py:465
  133.6 2.7 %collective-permute-start.32 = (bf16[256,1536]{1,0:T(8,128)(2,1)S(1)}, bf16[256,1536]{1,0:T(8,128)(2,1)S(1)}, u32[]{:S(2)}, u32[]{:S(2)}) collective-permute-start(bf16[256,1536]{1,0:T(8,128)(2,1)S(1)} %get-tuple-element.264), channel_id=1, source_target_pairs={{0,4},{4,0},{8,12},{12,8},{16,20},{20,16},{24,28},{28,24},{1,5},{5... | collective-permute-start | bytes 2359304 | tf_op jit(solution)/shard_map/ppermute | solution.py:468
  134.9 12.0 %collective-permute-start.31 = (bf16[64,4096]{1,0:T(8,128)(2,1)S(1)}, bf16[64,4096]{1,0:T(8,128)(2,1)S(1)}, u32[]{:S(2)}, u32[]{:S(2)}) collective-permute-start(bf16[64,4096]{1,0:T(8,128)(2,1)S(1)} %hidden_grads.3.refs_0_), channel_id=1, source_target_pairs={{0,1},{1,0},{2,3},{3,2},{4,6},{5,7},{6,4},{7,5},{8,9},{9,8},{10,11... | collective-permute-start | bytes 1572872 | tf_op jit(solution)/shard_map/ppermute | solution.py:465
  136.4 10.5 %collective-permute-start.33 = (bf16[256,384]{1,0:T(8,128)(2,1)S(1)}, bf16[256,384]{1,0:T(8,128)(2,1)S(1)}, u32[]{:S(2)}, u32[]{:S(2)}) collective-permute-start(bf16[256,384]{1,0:T(8,128)(2,1)S(1)} %get-tuple-element.265), channel_id=1, source_target_pairs={{0,8},{4,12},{8,16},{12,20},{16,24},{20,28},{24,0},{28,4},{1,9},{5... | collective-permute-start | bytes 589832 | tf_op jit(solution)/shard_map/ppermute | solution.py:471
  139.1 15.2 %collective-permute-start.34 = (bf16[64,4096]{1,0:T(8,128)(2,1)S(1)}, bf16[64,4096]{1,0:T(8,128)(2,1)S(1)}, u32[]{:S(2)}, u32[]{:S(2)}) collective-permute-start(bf16[64,4096]{1,0:T(8,128)(2,1)S(1)} %hidden_grads.3.refs_0_), channel_id=1, source_target_pairs={{0,2},{1,3},{2,0},{3,1},{4,5},{5,4},{6,7},{7,6},{8,10},{9,11},{10,... | collective-permute-start | bytes 1572872 | tf_op jit(solution)/shard_map/ppermute | solution.py:465
  146.9 14.3 %collective-permute-start.35 = (bf16[64,4096]{1,0:T(8,128)(2,1)S(1)}, bf16[64,4096]{1,0:T(8,128)(2,1)S(1)}, u32[]{:S(2)}, u32[]{:S(2)}) collective-permute-start(bf16[64,4096]{1,0:T(8,128)(2,1)S(1)} %collective-permute-done.31.refs_1_), channel_id=1, source_target_pairs={{0,2},{1,3},{2,0},{3,1},{4,5},{5,4},{6,7},{7,6},{8,10},{9,11},{10,... | collective-permute-start | bytes 1572872 | tf_op jit(solution)/shard_map/ppermute | solution.py:465
  147.7 13.5 %collective-permute-start.36 = (bf16[256,384]{1,0:T(8,128)(2,1)S(1)}, bf16[256,384]{1,0:T(8,128)(2,1)S(1)}, u32[]{:S(2)}, u32[]{:S(2)}) collective-permute-start(bf16[256,384]{1,0:T(8,128)(2,1)S(1)} %get-tuple-element.268), channel_id=1, source_target_pairs={{0,16},{4,20},{8,24},{12,28},{16,0},{20,4},{24,8},{28,12},{1,17},{... | collective-permute-start | bytes 589832 | tf_op jit(solution)/shard_map/ppermute | solution.py:471
  153.3 14.6 %collective-permute-start.38 = (bf16[256,384]{1,0:T(8,128)(2,1)S(1)}, bf16[256,384]{1,0:T(8,128)(2,1)S(1)}, u32[]{:S(2)}, u32[]{:S(2)}) collective-permute-start(bf16[256,384]{1,0:T(8,128)(2,1)S(1)} %get-tuple-element.281), channel_id=1, source_target_pairs={{0,24},{4,28},{8,0},{12,4},{16,8},{20,12},{24,16},{28,20},{1,25},{... | collective-permute-start | bytes 589832 | tf_op jit(solution)/shard_map/ppermute | solution.py:471
  163.7 4.2 %collective-permute-start.37 = (bf16[256,384]{1,0:T(8,128)(2,1)S(1)}, bf16[256,384]{1,0:T(8,128)(2,1)S(1)}, u32[]{:S(2)}, u32[]{:S(2)}) collective-permute-start(bf16[256,384]{1,0:T(8,128)(2,1)S(1)} %get-tuple-element.276), channel_id=1, source_target_pairs={{0,4},{4,0},{8,12},{12,8},{16,20},{20,16},{24,28},{28,24},{1,5},{5... | collective-permute-start | bytes 589832 | tf_op jit(solution)/shard_map/ppermute | solution.py:468
  168.0 1.9 %collective-permute-start.39 = (bf16[256,768]{1,0:T(8,128)(2,1)S(1)}, bf16[256,768]{1,0:T(8,128)(2,1)S(1)}, u32[]{:S(2)}, u32[]{:S(2)}) collective-permute-start(bf16[256,768]{1,0:T(8,128)(2,1)S(1)} %get-tuple-element.283), channel_id=1, source_target_pairs={{0,4},{4,0},{8,12},{12,8},{16,20},{20,16},{24,28},{28,24},{1,5},{5... | collective-permute-start | bytes 1179656 | tf_op jit(solution)/shard_map/ppermute | solution.py:468
  168.6 17.2 %collective-permute-start.40 = (bf16[256,384]{1,0:T(8,128)(2,1)S(1)}, bf16[256,384]{1,0:T(8,128)(2,1)S(1)}, u32[]{:S(2)}, u32[]{:S(2)}) collective-permute-start(bf16[256,384]{1,0:T(8,128)(2,1)S(1)} %pair_sums.4), channel_id=1, source_target_pairs={{0,16},{4,20},{8,24},{12,28},{16,0},{20,4},{24,8},{28,12},{1,17},{... | collective-permute-start | bytes 589832 | tf_op jit(solution)/shard_map/ppermute | solution.py:471
  170.0 15.8 %collective-permute-start.41 = (bf16[256,384]{1,0:T(8,128)(2,1)S(1)}, bf16[256,384]{1,0:T(8,128)(2,1)S(1)}, u32[]{:S(2)}, u32[]{:S(2)}) collective-permute-start(bf16[256,384]{1,0:T(8,128)(2,1)S(1)} %get-tuple-element.305), channel_id=1, source_target_pairs={{0,8},{4,12},{8,16},{12,20},{16,24},{20,28},{24,0},{28,4},{1,9},{5... | collective-permute-start | bytes 589832 | tf_op jit(solution)/shard_map/ppermute | solution.py:471
  174.0 12.6 %collective-permute-start.42 = (bf16[256,384]{1,0:T(8,128)(2,1)S(1)}, bf16[256,384]{1,0:T(8,128)(2,1)S(1)}, u32[]{:S(2)}, u32[]{:S(2)}) collective-permute-start(bf16[256,384]{1,0:T(8,128)(2,1)S(1)} %get-tuple-element.306), channel_id=1, source_target_pairs={{0,24},{4,28},{8,0},{12,4},{16,8},{20,12},{24,16},{28,20},{1,25},{... | collective-permute-start | bytes 589832 | tf_op jit(solution)/shard_map/ppermute | solution.py:471
  177.2 9.4 %collective-permute-start.43 = (bf16[256,384]{1,0:T(8,128)(2,1)S(1)}, bf16[256,384]{1,0:T(8,128)(2,1)S(1)}, u32[]{:S(2)}, u32[]{:S(2)}) collective-permute-start(bf16[256,384]{1,0:T(8,128)(2,1)S(1)} %get-tuple-element.308), channel_id=1, source_target_pairs={{0,4},{4,0},{8,12},{12,8},{16,20},{20,16},{24,28},{28,24},{1,5},{5... | collective-permute-start | bytes 589832 | tf_op jit(solution)/shard_map/ppermute | solution.py:468

commit v8 on v5

--- a/solution.py
+++ b/solution.py
@@ -614,13 +614,14 @@
     hidden_2 = hold(hidden_2)
 
     hidden_2 = send(hidden_2)
-    early_1, gate_up_2 = hold((early_1, gate_up_2))
+    gate_up_2 = hold(gate_up_2)
+    gate_up_2 = settle(gate_up_2)
+    early_1 = hold(early_1)
 
     parts_1 = finish_rows(early_1, late_1)
     parts_1, hidden_2 = hold((parts_1, hidden_2))
 
     hidden_2 = settle(hidden_2)
-    gate_up_2 = settle(gate_up_2)
     partial_1 = products(parts_1, whole[0])
     hidden_2, gate_up_2, partial_1 = hold((hidden_2, gate_up_2, partial_1))
 

time: 187 us -> 187 us (level)
  no operation moved by 1% of the time
where the time goes in v8:
time: 187 us; the launch traced here: 186 us
  Pallas kernels  68.2 us (36%)
  waiting for transfers between devices  61.8 us (33%)
  starting transfers between devices  53.9 us (29%)
    ppermute x14, waiting for transfers between devices, exchange(): return lax.ppermute(value, ('tp', 'dp'), pairs)  28.4 us
    ppermute x10, starting transfers between devices, along(): lax.ppermute(value, 'tp', [(i, (i + places * CORES) % n_tp) for i in rang...  28 us
    ppermute x10, waiting for transfers between devices, along(): lax.ppermute(value, 'tp', [(i, (i + places * CORES) % n_tp) for i in rang...  20.6 us
    pallas_call x4, Pallas kernels, backward(): pl.pallas_call(functools.partial(backward_kernel, places, total_places),...  16.4 us
    ppermute x14, starting transfers between devices, exchange(): return lax.ppermute(value, ('tp', 'dp'), pairs)  15 us
    pallas_call x2, Pallas kernels, forward(): pl.pallas_call(functools.partial(forward_kernel, groups, contract, width,...  15 us
    pallas_call x2, Pallas kernels, forward_streamed(): pl.pallas_call(functools.partial(streamed_kernel, groups, width), in_spec...  14.8 us
    pallas_call x2, Pallas kernels, weight(): pl.pallas_call(functools.partial(weight_kernel, turned), in_specs=[pl.Blo...  13.2 us
  transfers between devices with their start and end apart: 44, of which 19 were waited for; matrix products, arithmetic and copies ran while one was open for 0% of the time, Pallas kernels for 34%

profile of v8, /device:TPU:0, one launch (start us, length us, event | category | flops | bytes accessed | tf_op | source)
XLA Modules:
  0.0 185.5 jit_solution(3399213704125250419)
XLA Ops:
  0.1 1.8 order_rows.1
  1.9 4.1 %collective-permute-start = (bf16[256,384]{1,0:T(8,128)(2,1)S(1)}, bf16[256,384]{1,0:T(8,128)(2,1)S(1)}, u32[]{:S(2)}, u32[]{:S(2)}) collective-permute-start(bf16[256,384]{1,0:T(8,128)(2,1)S(1)} %get-tuple-element.158.own_ref), channel_id=1, source_target_pairs={{0,16},{4,20},{8,24},{12,28},{16,0},{20,4},{24,8},{28,12},{1,17},{... | collective-permute-start | bytes 589832 | tf_op jit(solution)/shard_map/ppermute | solution.py:471
  6.0 1.6 collective-permute-start.1
  8.9 6.6 %scaled_weight.3.refs_2_.refs_4_ = bf16[3072,2048]{1,0:T(8,128)(2,1)S(1)} custom-call(bf16[3072,2048]{1,0:T(8,128)(2,1)} %code_ref.3, f32[16,24]{1,0:T(8,128)S(1)} %bitcast.5), custom_call_target="tpu_custom_call" | custom-call | bytes 1536 | tf_op jit(solution)/shard_map/scaled_weight/pallas_call | solution.py:88
  16.0 1.3 collective-permute-start.3
  17.3 4.0 %collective-permute-start.4 = (bf16[256,384]{1,0:T(8,128)(2,1)S(1)}, bf16[256,384]{1,0:T(8,128)(2,1)S(1)}, u32[]{:S(2)}, u32[]{:S(2)}) collective-permute-start(bf16[256,384]{1,0:T(8,128)(2,1)S(1)} %get-tuple-element.162.own_ref), channel_id=1, source_target_pairs={{0,16},{4,20},{8,24},{12,28},{16,0},{20,4},{24,8},{28,12},{1,17},{... | collective-permute-start | bytes 589832 | tf_op jit(solution)/shard_map/ppermute | solution.py:471
  21.3 6.6 %scaled_weight.2.refs_3_.refs_5_ = bf16[3072,2048]{1,0:T(8,128)(2,1)S(1)} custom-call(bf16[3072,2048]{1,0:T(8,128)(2,1)} %code_ref.2, f32[16,24]{1,0:T(8,128)S(1)} %bitcast.6), custom_call_target="tpu_custom_call" | custom-call | bytes 1536 | tf_op jit(solution)/shard_map/scaled_weight/pallas_call | solution.py:88
  27.9 2.1 %collective-permute-done.4.two_ref = bf16[256,384]{1,0:T(8,128)(2,1)S(1)} collective-permute-done((bf16[256,384]{1,0:T(8,128)(2,1)S(1)}, bf16[256,384]{1,0:T(8,128)(2,1)S(1)}, u32[]{:S(2)}, u32[]{:S(2)}) %collective-permute-start.4) | collective-permute-done | bytes 196640 | tf_op jit(solution)/shard_map/ppermute | solution.py:471
  30.0 2.0 %collective-permute-done.5.near_ref = bf16[256,384]{1,0:T(8,128)(2,1)S(1)} collective-permute-done((bf16[256,384]{1,0:T(8,128)(2,1)S(1)}, bf16[256,384]{1,0:T(8,128)(2,1)S(1)}, u32[]{:S(2)}, u32[]{:S(2)}) %collective-permute-start.5) | collective-permute-done | bytes 196640 | tf_op jit(solution)/shard_map/ppermute | solution.py:476
  33.4 1.3 collective-permute-start.8
  35.0 7.5 %forward_product.2 = (bf16[128,4096]{1,0:T(8,128)(2,1)S(1)}, bf16[64,4096]{1,0:T(8,128)(2,1)S(1)}, bf16[64,4096]{1,0:T(8,128)(2,1)S(1)}) custom-call(s32[3]{0:T(128)S(1)} %pad_add_fusion.where_ref, bf16[256,1536]{1,0:T(8,128)(2,1)S(1)} %join.4.refs_0_, bf16[256,1536]{1,0:T(8,128)(2,1)S(1)} %collective-permute-done.6.refs_1_, ...), custom_call_target="tpu_custom_call" | custom-call | flops 1024 | bytes 1024 | tf_op jit(solution)/shard_map/forward_product/pallas_call | solution.py:231
  42.5 1.1 collective-permute-done.8.passed_ref
  43.6 1.5 collective-permute-start.10
  45.8 3.7 %collective-permute-start.11 = (bf16[256,384]{1,0:T(8,128)(2,1)S(1)}, bf16[256,384]{1,0:T(8,128)(2,1)S(1)}, u32[]{:S(2)}, u32[]{:S(2)}) collective-permute-start(bf16[256,384]{1,0:T(8,128)(2,1)S(1)} %get-tuple-element.188.own_ref), channel_id=1, source_target_pairs={{0,16},{4,20},{8,24},{12,28},{16,0},{20,4},{24,8},{28,12},{1,17},{... | collective-permute-start | bytes 589832 | tf_op jit(solution)/shard_map/ppermute | solution.py:471
  50.2 7.4 %forward_streamed.2 = (bf16[128,2048]{1,0:T(8,128)(2,1)S(1)}, bf16[64,2048]{1,0:T(8,128)(2,1)S(1)}, bf16[64,2048]{1,0:T(8,128)(2,1)S(1)}) custom-call(s32[3]{0:T(128)S(1)} %pad_add_fusion.where_ref, f32[16,24]{1,0:T(8,128)S(1)} %copy-done, bf16[256,1536]{1,0:T(8,128)(2,1)S(1)} %join.5.refs_0_, bf16[256,1536]{1,0:T(8,128)(2,1)S(1)} %collective-permute-done.9.refs_1_, ...), custom_call_target="tpu_custom_call" | custom-call | flops 1024 | bytes 1024 | tf_op jit(solution)/shard_map/forward_streamed/pallas_call | solution.py:303
  57.7 1.9 %collective-permute-done.11.two_ref = bf16[256,384]{1,0:T(8,128)(2,1)S(1)} collective-permute-done((bf16[256,384]{1,0:T(8,128)(2,1)S(1)}, bf16[256,384]{1,0:T(8,128)(2,1)S(1)}, u32[]{:S(2)}, u32[]{:S(2)}) %collective-permute-start.11) | collective-permute-done | bytes 196640 | tf_op jit(solution)/shard_map/ppermute | solution.py:471
  59.8 1.3 collective-permute-start.14
  61.1 2.9 %collective-permute-start.17 = (bf16[256,384]{1,0:T(8,128)(2,1)S(1)}, bf16[256,384]{1,0:T(8,128)(2,1)S(1)}, u32[]{:S(2)}, u32[]{:S(2)}) collective-permute-start(bf16[256,384]{1,0:T(8,128)(2,1)S(1)} %get-tuple-element.201.own_ref), channel_id=1, source_target_pairs={{0,16},{4,20},{8,24},{12,28},{16,0},{20,4},{24,8},{28,12},{1,17},{... | collective-permute-start | bytes 589832 | tf_op jit(solution)/shard_map/ppermute | solution.py:471
  64.0 1.4 collective-permute-start.16
  65.4 7.4 %collective-permute-done.14.passed_ref = bf16[256,384]{1,0:T(8,128)(2,1)S(1)} collective-permute-done((bf16[256,384]{1,0:T(8,128)(2,1)S(1)}, bf16[256,384]{1,0:T(8,128)(2,1)S(1)}, u32[]{:S(2)}, u32[]{:S(2)}) %collective-permute-start.14) | collective-permute-done | bytes 196640 | tf_op jit(solution)/shard_map/ppermute | solution.py:476
  73.7 1.6 collective-permute-start.21
  75.3 1.0 collective-permute-done.18.near_ref
  76.4 1.6 collective-permute-start.22
  78.6 1.5 collective-permute-start.20
  80.1 7.5 %forward_product.3 = (bf16[128,4096]{1,0:T(8,128)(2,1)S(1)}, bf16[64,4096]{1,0:T(8,128)(2,1)S(1)}, bf16[64,4096]{1,0:T(8,128)(2,1)S(1)}) custom-call(s32[3]{0:T(128)S(1)} %pad_add_fusion.where_ref, bf16[256,1536]{1,0:T(8,128)(2,1)S(1)} %join.6.refs_0_, bf16[256,1536]{1,0:T(8,128)(2,1)S(1)} %collective-permute-done.15.refs_1_, ...), custom_call_target="tpu_custom_call" | custom-call | flops 1024 | bytes 1024 | tf_op jit(solution)/shard_map/forward_product/pallas_call | solution.py:231
  89.0 1.0 hidden_grads.2.refs_0_
  92.0 7.4 %forward_streamed.3 = (bf16[128,2048]{1,0:T(8,128)(2,1)S(1)}, bf16[64,2048]{1,0:T(8,128)(2,1)S(1)}, bf16[64,2048]{1,0:T(8,128)(2,1)S(1)}) custom-call(s32[3]{0:T(128)S(1)} %pad_add_fusion.where_ref, f32[16,24]{1,0:T(8,128)S(1)} %copy-done, bf16[256,1536]{1,0:T(8,128)(2,1)S(1)} %join.7.refs_0_, bf16[256,1536]{1,0:T(8,128)(2,1)S(1)} %collective-permute-done.23.refs_1_, ...), custom_call_target="tpu_custom_call" | custom-call | flops 1024 | bytes 1024 | tf_op jit(solution)/shard_map/forward_streamed/pallas_call | solution.py:303
  99.5 1.2 collective-permute-start.28
  100.7 8.2 %collective-permute-done.25.refs_1_ = bf16[128,4096]{1,0:T(8,128)(2,1)S(1)} collective-permute-done((bf16[128,4096]{1,0:T(8,128)(2,1)S(1)}, bf16[128,4096]{1,0:T(8,128)(2,1)S(1)}, u32[]{:S(2)}, u32[]{:S(2)}) %collective-permute-start.25) | collective-permute-done | bytes 1048608 | tf_op jit(solution)/shard_map/ppermute | solution.py:465
  108.8 5.6 %collective-permute-done.24.refs_1_ = bf16[64,4096]{1,0:T(8,128)(2,1)S(1)} collective-permute-done((bf16[64,4096]{1,0:T(8,128)(2,1)S(1)}, bf16[64,4096]{1,0:T(8,128)(2,1)S(1)}, u32[]{:S(2)}, u32[]{:S(2)}) %collective-permute-start.24) | collective-permute-done | bytes 524320 | tf_op jit(solution)/shard_map/ppermute | solution.py:465
  115.1 1.6 collective-permute-start.30
  116.7 6.8 %collective-permute-done.28.refs_4_ = bf16[128,2048]{1,0:T(8,128)(2,1)S(1)} collective-permute-done((bf16[128,2048]{1,0:T(8,128)(2,1)S(1)}, bf16[128,2048]{1,0:T(8,128)(2,1)S(1)}, u32[]{:S(2)}, u32[]{:S(2)}) %collective-permute-start.28) | collective-permute-done | bytes 524320 | tf_op jit(solution)/shard_map/ppermute | solution.py:465
  123.5 1.7 collective-permute-done.27.refs_3_
  125.8 7.4 %backward_product.4 = (bf16[256,1536]{1,0:T(8,128)(2,1)S(1)}, bf16[256,1536]{1,0:T(8,128)(2,1)S(1)}) custom-call(s32[3]{0:T(128)S(1)} %pad_add_fusion.where_ref, bf16[64,4096]{1,0:T(8,128)(2,1)S(1)} %hidden_grads.2.refs_0_, bf16[64,4096]{1,0:T(8,128)(2,1)S(1)} %collective-permute-done.24.refs_1_, bf16[64,4096]{1,0:T(8,128)(2,1)S(1)} %collective-permute-done.26.refs_2_, ...), custom_call_target="tpu_custom_call" | custom-call | flops 1024 | bytes 1024 | tf_op jit(solution)/shard_map/backward_product/pallas_call | solution.py:382
  133.9 1.0 hidden_grads.3.refs_0_
  134.9 1.3 collective-permute-start.31
  136.4 3.2 %collective-permute-start.33 = (bf16[256,384]{1,0:T(8,128)(2,1)S(1)}, bf16[256,384]{1,0:T(8,128)(2,1)S(1)}, u32[]{:S(2)}, u32[]{:S(2)}) collective-permute-start(bf16[256,384]{1,0:T(8,128)(2,1)S(1)} %get-tuple-element.267), channel_id=1, source_target_pairs={{0,16},{4,20},{8,24},{12,28},{16,0},{20,4},{24,8},{28,12},{1,17},{... | collective-permute-start | bytes 589832 | tf_op jit(solution)/shard_map/ppermute | solution.py:471
  140.5 5.8 %collective-permute-done.31.refs_1_ = bf16[64,4096]{1,0:T(8,128)(2,1)S(1)} collective-permute-done((bf16[64,4096]{1,0:T(8,128)(2,1)S(1)}, bf16[64,4096]{1,0:T(8,128)(2,1)S(1)}, u32[]{:S(2)}, u32[]{:S(2)}) %collective-permute-start.31) | collective-permute-done | bytes 524320 | tf_op jit(solution)/shard_map/ppermute | solution.py:465
  146.3 2.7 %collective-permute-done.33.refs_0_ = bf16[256,384]{1,0:T(8,128)(2,1)S(1)} collective-permute-done((bf16[256,384]{1,0:T(8,128)(2,1)S(1)}, bf16[256,384]{1,0:T(8,128)(2,1)S(1)}, u32[]{:S(2)}, u32[]{:S(2)}) %collective-permute-start.33) | collective-permute-done | bytes 196640 | tf_op jit(solution)/shard_map/ppermute | solution.py:471
  149.9 2.9 %collective-permute-start.36 = (bf16[256,384]{1,0:T(8,128)(2,1)S(1)}, bf16[256,384]{1,0:T(8,128)(2,1)S(1)}, u32[]{:S(2)}, u32[]{:S(2)}) collective-permute-start(bf16[256,384]{1,0:T(8,128)(2,1)S(1)} %get-tuple-element.270), channel_id=1, source_target_pairs={{0,8},{4,12},{8,16},{12,20},{16,24},{20,28},{24,0},{28,4},{1,9},{5... | collective-permute-start | bytes 589832 | tf_op jit(solution)/shard_map/ppermute | solution.py:471
  153.7 5.8 %collective-permute-done.36.refs_1_ = bf16[256,384]{1,0:T(8,128)(2,1)S(1)} collective-permute-done((bf16[256,384]{1,0:T(8,128)(2,1)S(1)}, bf16[256,384]{1,0:T(8,128)(2,1)S(1)}, u32[]{:S(2)}, u32[]{:S(2)}) %collective-permute-start.36) | collective-permute-done | bytes 196640 | tf_op jit(solution)/shard_map/ppermute | solution.py:471
  159.5 2.5 %backward_product.5 = (bf16[256,384]{1,0:T(8,128)(2,1)S(1)}, bf16[256,384]{1,0:T(8,128)(2,1)S(1)}) custom-call(s32[3]{0:T(128)S(1)} %pad_add_fusion.where_ref, bf16[64,4096]{1,0:T(8,128)(2,1)S(1)} %hidden_grads.3.refs_0_, bf16[64,4096]{1,0:T(8,128)(2,1)S(1)} %collective-permute-done.31.refs_1_, bf16[64,4096]{1,0:T(8,128)(2,1)S(1)} %collective-permute-done.34.refs_2_, ...), custom_call_target="tpu_custom_call" | custom-call | flops 1024 | bytes 1024 | tf_op jit(solution)/shard_map/backward_product/pallas_call | solution.py:382
  162.1 4.1 %backward_product.6 = (bf16[256,768]{1,0:T(8,128)(2,1)S(1)}, bf16[256,768]{1,0:T(8,128)(2,1)S(1)}) custom-call(s32[3]{0:T(128)S(1)} %pad_add_fusion.where_ref, bf16[64,4096]{1,0:T(8,128)(2,1)S(1)} %hidden_grads.3.refs_0_, bf16[64,4096]{1,0:T(8,128)(2,1)S(1)} %collective-permute-done.31.refs_1_, bf16[64,4096]{1,0:T(8,128)(2,1)S(1)} %collective-permute-done.34.refs_2_, ...), custom_call_target="tpu_custom_call" | custom-call | flops 1024 | bytes 1024 | tf_op jit(solution)/shard_map/backward_product/pallas_call | solution.py:382
  166.8 2.4 %collective-permute-start.40 = (bf16[256,384]{1,0:T(8,128)(2,1)S(1)}, bf16[256,384]{1,0:T(8,128)(2,1)S(1)}, u32[]{:S(2)}, u32[]{:S(2)}) collective-permute-start(bf16[256,384]{1,0:T(8,128)(2,1)S(1)} %pair_sums.4), channel_id=1, source_target_pairs={{0,16},{4,20},{8,24},{12,28},{16,0},{20,4},{24,8},{28,12},{1,17},{... | collective-permute-start | bytes 589832 | tf_op jit(solution)/shard_map/ppermute | solution.py:471
  169.9 3.2 %collective-permute-start.42 = (bf16[256,384]{1,0:T(8,128)(2,1)S(1)}, bf16[256,384]{1,0:T(8,128)(2,1)S(1)}, u32[]{:S(2)}, u32[]{:S(2)}) collective-permute-start(bf16[256,384]{1,0:T(8,128)(2,1)S(1)} %get-tuple-element.308), channel_id=1, source_target_pairs={{0,24},{4,28},{8,0},{12,4},{16,8},{20,12},{24,16},{28,20},{1,25},{... | collective-permute-start | bytes 589832 | tf_op jit(solution)/shard_map/ppermute | solution.py:471
  173.2 2.5 %backward_product.7 = (bf16[256,384]{1,0:T(8,128)(2,1)S(1)}, bf16[256,384]{1,0:T(8,128)(2,1)S(1)}) custom-call(s32[3]{0:T(128)S(1)} %pad_add_fusion.where_ref, bf16[64,4096]{1,0:T(8,128)(2,1)S(1)} %hidden_grads.3.refs_0_, bf16[64,4096]{1,0:T(8,128)(2,1)S(1)} %collective-permute-done.31.refs_1_, bf16[64,4096]{1,0:T(8,128)(2,1)S(1)} %collective-permute-done.34.refs_2_, ...), custom_call_target="tpu_custom_call" | custom-call | flops 1024 | bytes 1024 | tf_op jit(solution)/shard_map/backward_product/pallas_call | solution.py:382
  176.4 7.6 %collective-permute-done.40.refs_1_ = bf16[256,384]{1,0:T(8,128)(2,1)S(1)} collective-permute-done((bf16[256,384]{1,0:T(8,128)(2,1)S(1)}, bf16[256,384]{1,0:T(8,128)(2,1)S(1)}, u32[]{:S(2)}, u32[]{:S(2)}) %collective-permute-start.40) | collective-permute-done | bytes 196640 | tf_op jit(solution)/shard_map/ppermute | solution.py:471
  184.1 1.4 final_sum.3
  (73 shorter events, 17.2 us)
Async XLA Ops:
  1.9 14.1 %collective-permute-start = (bf16[256,384]{1,0:T(8,128)(2,1)S(1)}, bf16[256,384]{1,0:T(8,128)(2,1)S(1)}, u32[]{:S(2)}, u32[]{:S(2)}) collective-permute-start(bf16[256,384]{1,0:T(8,128)(2,1)S(1)} %get-tuple-element.158.own_ref), channel_id=1, source_target_pairs={{0,16},{4,20},{8,24},{12,28},{16,0},{20,4},{24,8},{28,12},{1,17},{... | collective-permute-start | bytes 589832 | tf_op jit(solution)/shard_map/ppermute | solution.py:471
  6.0 10.0 %collective-permute-start.1 = (bf16[256,384]{1,0:T(8,128)(2,1)S(1)}, bf16[256,384]{1,0:T(8,128)(2,1)S(1)}, u32[]{:S(2)}, u32[]{:S(2)}) collective-permute-start(bf16[256,384]{1,0:T(8,128)(2,1)S(1)} %get-tuple-element.158.own_ref), channel_id=1, source_target_pairs={{0,8},{4,12},{8,0},{12,4},{16,24},{20,28},{24,16},{28,20},{1,9},{5... | collective-permute-start | bytes 589832 | tf_op jit(solution)/shard_map/ppermute | solution.py:476
  7.6 20.3 %collective-permute-start.2 = (bf16[256,384]{1,0:T(8,128)(2,1)S(1)}, bf16[256,384]{1,0:T(8,128)(2,1)S(1)}, u32[]{:S(2)}, u32[]{:S(2)}) collective-permute-start(bf16[256,384]{1,0:T(8,128)(2,1)S(1)} %get-tuple-element.158.own_ref), channel_id=1, source_target_pairs={{8,16},{12,20},{16,8},{20,12},{9,17},{13,21},{17,9},{21,13},{10,18... | collective-permute-start | bytes 589832 | tf_op jit(solution)/shard_map/ppermute | solution.py:476
  8.2 0.7 copy-start.1
  8.9 12.4 %copy-start.2 = (f32[24,16]{0,1:T(8,128)S(1)}, f32[24,16]{0,1:T(8,128)}, u32[]{:S(2)}) copy-start(f32[24,16]{0,1:T(8,128)} %param.13) | copy-start | bytes 4612
  16.0 11.9 %collective-permute-start.3 = (bf16[256,384]{1,0:T(8,128)(2,1)S(1)}, bf16[256,384]{1,0:T(8,128)(2,1)S(1)}, u32[]{:S(2)}, u32[]{:S(2)}) collective-permute-start(bf16[256,384]{1,0:T(8,128)(2,1)S(1)} %collective-permute-done.two_ref), channel_id=1, source_target_pairs={{8,0},{12,4},{16,24},{20,28},{9,1},{13,5},{17,25},{21,29},{10,2},{... | collective-permute-start | bytes 589832 | tf_op jit(solution)/shard_map/ppermute | solution.py:476
  17.3 12.7 %collective-permute-start.4 = (bf16[256,384]{1,0:T(8,128)(2,1)S(1)}, bf16[256,384]{1,0:T(8,128)(2,1)S(1)}, u32[]{:S(2)}, u32[]{:S(2)}) collective-permute-start(bf16[256,384]{1,0:T(8,128)(2,1)S(1)} %get-tuple-element.162.own_ref), channel_id=1, source_target_pairs={{0,16},{4,20},{8,24},{12,28},{16,0},{20,4},{24,8},{28,12},{1,17},{... | collective-permute-start | bytes 589832 | tf_op jit(solution)/shard_map/ppermute | solution.py:471
  21.3 10.7 %collective-permute-start.5 = (bf16[256,384]{1,0:T(8,128)(2,1)S(1)}, bf16[256,384]{1,0:T(8,128)(2,1)S(1)}, u32[]{:S(2)}, u32[]{:S(2)}) collective-permute-start(bf16[256,384]{1,0:T(8,128)(2,1)S(1)} %get-tuple-element.162.own_ref), channel_id=1, source_target_pairs={{0,8},{4,12},{8,0},{12,4},{16,24},{20,28},{24,16},{28,20},{1,9},{5... | collective-permute-start | bytes 589832 | tf_op jit(solution)/shard_map/ppermute | solution.py:476
  32.6 17.6 %copy-start = (f32[16,24]{1,0:T(8,128)S(1)}, f32[16,24]{1,0:T(8,128)}, u32[]{:S(2)}) copy-start(f32[16,24]{1,0:T(8,128)} %scale_ref.3) | copy-start | bytes 4612
  32.6 2.4 %collective-permute-start.6 = (bf16[256,1536]{1,0:T(8,128)(2,1)S(1)}, bf16[256,1536]{1,0:T(8,128)(2,1)S(1)}, u32[]{:S(2)}, u32[]{:S(2)}) collective-permute-start(bf16[256,1536]{1,0:T(8,128)(2,1)S(1)} %join.4.refs_0_), channel_id=1, source_target_pairs={{0,4},{4,0},{8,12},{12,8},{16,20},{20,16},{24,28},{28,24},{1,5},{5... | collective-permute-start | bytes 2359304 | tf_op jit(solution)/shard_map/ppermute | solution.py:468
  32.7 9.8 %collective-permute-start.7 = (bf16[256,384]{1,0:T(8,128)(2,1)S(1)}, bf16[256,384]{1,0:T(8,128)(2,1)S(1)}, u32[]{:S(2)}, u32[]{:S(2)}) collective-permute-start(bf16[256,384]{1,0:T(8,128)(2,1)S(1)} %get-tuple-element.162.own_ref), channel_id=1, source_target_pairs={{8,16},{12,20},{16,8},{20,12},{9,17},{13,21},{17,9},{21,13},{10,18... | collective-permute-start | bytes 589832 | tf_op jit(solution)/shard_map/ppermute | solution.py:476
  33.4 10.2 %collective-permute-start.8 = (bf16[256,384]{1,0:T(8,128)(2,1)S(1)}, bf16[256,384]{1,0:T(8,128)(2,1)S(1)}, u32[]{:S(2)}, u32[]{:S(2)}) collective-permute-start(bf16[256,384]{1,0:T(8,128)(2,1)S(1)} %collective-permute-done.4.two_ref), channel_id=1, source_target_pairs={{8,0},{12,4},{16,24},{20,28},{9,1},{13,5},{17,25},{21,29},{10,2},{... | collective-permute-start | bytes 589832 | tf_op jit(solution)/shard_map/ppermute | solution.py:476
  43.6 16.2 %collective-permute-start.10 = (bf16[128,4096]{1,0:T(8,128)(2,1)S(1)}, bf16[128,4096]{1,0:T(8,128)(2,1)S(1)}, u32[]{:S(2)}, u32[]{:S(2)}) collective-permute-start(bf16[128,4096]{1,0:T(8,128)(2,1)S(1)} %get-tuple-element.185), channel_id=1, source_target_pairs={{0,1},{1,0},{2,3},{3,2},{4,6},{5,7},{6,4},{7,5},{8,9},{9,8},{10,11... | collective-permute-start | bytes 3145736 | tf_op jit(solution)/shard_map/ppermute | solution.py:465
  45.7 4.5 %collective-permute-start.9 = (bf16[256,1536]{1,0:T(8,128)(2,1)S(1)}, bf16[256,1536]{1,0:T(8,128)(2,1)S(1)}, u32[]{:S(2)}, u32[]{:S(2)}) collective-permute-start(bf16[256,1536]{1,0:T(8,128)(2,1)S(1)} %join.5.refs_0_), channel_id=1, source_target_pairs={{0,4},{4,0},{8,12},{12,8},{16,20},{20,16},{24,28},{28,24},{1,5},{5... | collective-permute-start | bytes 2359304 | tf_op jit(solution)/shard_map/ppermute | solution.py:468
  45.8 13.7 %collective-permute-start.11 = (bf16[256,384]{1,0:T(8,128)(2,1)S(1)}, bf16[256,384]{1,0:T(8,128)(2,1)S(1)}, u32[]{:S(2)}, u32[]{:S(2)}) collective-permute-start(bf16[256,384]{1,0:T(8,128)(2,1)S(1)} %get-tuple-element.188.own_ref), channel_id=1, source_target_pairs={{0,16},{4,20},{8,24},{12,28},{16,0},{20,4},{24,8},{28,12},{1,17},{... | collective-permute-start | bytes 589832 | tf_op jit(solution)/shard_map/ppermute | solution.py:471
  49.5 10.3 %collective-permute-start.12 = (bf16[256,384]{1,0:T(8,128)(2,1)S(1)}, bf16[256,384]{1,0:T(8,128)(2,1)S(1)}, u32[]{:S(2)}, u32[]{:S(2)}) collective-permute-start(bf16[256,384]{1,0:T(8,128)(2,1)S(1)} %get-tuple-element.188.own_ref), channel_id=1, source_target_pairs={{0,8},{4,12},{8,0},{12,4},{16,24},{20,28},{24,16},{28,20},{1,9},{5... | collective-permute-start | bytes 589832 | tf_op jit(solution)/shard_map/ppermute | solution.py:476
  49.5 15.9 %collective-permute-start.13 = (bf16[256,384]{1,0:T(8,128)(2,1)S(1)}, bf16[256,384]{1,0:T(8,128)(2,1)S(1)}, u32[]{:S(2)}, u32[]{:S(2)}) collective-permute-start(bf16[256,384]{1,0:T(8,128)(2,1)S(1)} %get-tuple-element.188.own_ref), channel_id=1, source_target_pairs={{8,16},{12,20},{16,8},{20,12},{9,17},{13,21},{17,9},{21,13},{10,18... | collective-permute-start | bytes 589832 | tf_op jit(solution)/shard_map/ppermute | solution.py:476
  59.8 13.0 %collective-permute-start.14 = (bf16[256,384]{1,0:T(8,128)(2,1)S(1)}, bf16[256,384]{1,0:T(8,128)(2,1)S(1)}, u32[]{:S(2)}, u32[]{:S(2)}) collective-permute-start(bf16[256,384]{1,0:T(8,128)(2,1)S(1)} %collective-permute-done.11.two_ref), channel_id=1, source_target_pairs={{8,0},{12,4},{16,24},{20,28},{9,1},{13,5},{17,25},{21,29},{10,2},{... | collective-permute-start | bytes 589832 | tf_op jit(solution)/shard_map/ppermute | solution.py:476
  61.1 14.2 %collective-permute-start.17 = (bf16[256,384]{1,0:T(8,128)(2,1)S(1)}, bf16[256,384]{1,0:T(8,128)(2,1)S(1)}, u32[]{:S(2)}, u32[]{:S(2)}) collective-permute-start(bf16[256,384]{1,0:T(8,128)(2,1)S(1)} %get-tuple-element.201.own_ref), channel_id=1, source_target_pairs={{0,16},{4,20},{8,24},{12,28},{16,0},{20,4},{24,8},{28,12},{1,17},{... | collective-permute-start | bytes 589832 | tf_op jit(solution)/shard_map/ppermute | solution.py:471
  64.0 12.3 %collective-permute-start.18 = (bf16[256,384]{1,0:T(8,128)(2,1)S(1)}, bf16[256,384]{1,0:T(8,128)(2,1)S(1)}, u32[]{:S(2)}, u32[]{:S(2)}) collective-permute-start(bf16[256,384]{1,0:T(8,128)(2,1)S(1)} %get-tuple-element.201.own_ref), channel_id=1, source_target_pairs={{0,8},{4,12},{8,0},{12,4},{16,24},{20,28},{24,16},{28,20},{1,9},{5... | collective-permute-start | bytes 589832 | tf_op jit(solution)/shard_map/ppermute | solution.py:476
  64.0 12.3 %collective-permute-start.16 = (bf16[128,2048]{1,0:T(8,128)(2,1)S(1)}, bf16[128,2048]{1,0:T(8,128)(2,1)S(1)}, u32[]{:S(2)}, u32[]{:S(2)}) collective-permute-start(bf16[128,2048]{1,0:T(8,128)(2,1)S(1)} %get-tuple-element.198), channel_id=1, source_target_pairs={{0,1},{1,0},{2,3},{3,2},{4,6},{5,7},{6,4},{7,5},{8,9},{9,8},{10,11... | collective-permute-start | bytes 1572872 | tf_op jit(solution)/shard_map/ppermute | solution.py:465
  73.5 2.8 %collective-permute-start.15 = (bf16[256,1536]{1,0:T(8,128)(2,1)S(1)}, bf16[256,1536]{1,0:T(8,128)(2,1)S(1)}, u32[]{:S(2)}, u32[]{:S(2)}) collective-permute-start(bf16[256,1536]{1,0:T(8,128)(2,1)S(1)} %join.6.refs_0_), channel_id=1, source_target_pairs={{0,4},{4,0},{8,12},{12,8},{16,20},{20,16},{24,28},{28,24},{1,5},{5... | collective-permute-start | bytes 2359304 | tf_op jit(solution)/shard_map/ppermute | solution.py:468
  73.7 13.9 %collective-permute-start.21 = (bf16[64,4096]{1,0:T(8,128)(2,1)S(1)}, bf16[64,4096]{1,0:T(8,128)(2,1)S(1)}, u32[]{:S(2)}, u32[]{:S(2)}) collective-permute-start(bf16[64,4096]{1,0:T(8,128)(2,1)S(1)} %add_convert_fusion.1), channel_id=1, source_target_pairs={{0,2},{1,3},{2,0},{3,1},{4,5},{5,4},{6,7},{7,6},{8,10},{9,11},{10,... | collective-permute-start | bytes 1572872 | tf_op jit(solution)/shard_map/ppermute | solution.py:465
  76.4 11.3 %collective-permute-start.22 = (bf16[64,2048]{1,0:T(8,128)(2,1)S(1)}, bf16[64,2048]{1,0:T(8,128)(2,1)S(1)}, u32[]{:S(2)}, u32[]{:S(2)}) collective-permute-start(bf16[64,2048]{1,0:T(8,128)(2,1)S(1)} %add_convert_fusion.3), channel_id=1, source_target_pairs={{0,2},{1,3},{2,0},{3,1},{4,5},{5,4},{6,7},{7,6},{8,10},{9,11},{10,... | collective-permute-start | bytes 786440 | tf_op jit(solution)/shard_map/ppermute | solution.py:465
  77.9 9.7 %collective-permute-start.19 = (bf16[256,384]{1,0:T(8,128)(2,1)S(1)}, bf16[256,384]{1,0:T(8,128)(2,1)S(1)}, u32[]{:S(2)}, u32[]{:S(2)}) collective-permute-start(bf16[256,384]{1,0:T(8,128)(2,1)S(1)} %get-tuple-element.201.own_ref), channel_id=1, source_target_pairs={{8,16},{12,20},{16,8},{20,12},{9,17},{13,21},{17,9},{21,13},{10,18... | collective-permute-start | bytes 589832 | tf_op jit(solution)/shard_map/ppermute | solution.py:476
  78.6 9.0 %collective-permute-start.20 = (bf16[256,384]{1,0:T(8,128)(2,1)S(1)}, bf16[256,384]{1,0:T(8,128)(2,1)S(1)}, u32[]{:S(2)}, u32[]{:S(2)}) collective-permute-start(bf16[256,384]{1,0:T(8,128)(2,1)S(1)} %collective-permute-done.17.two_ref), channel_id=1, source_target_pairs={{8,0},{12,4},{16,24},{20,28},{9,1},{13,5},{17,25},{21,29},{10,2},{... | collective-permute-start | bytes 589832 | tf_op jit(solution)/shard_map/ppermute | solution.py:476
  88.3 2.4 %collective-permute-start.23 = (bf16[256,1536]{1,0:T(8,128)(2,1)S(1)}, bf16[256,1536]{1,0:T(8,128)(2,1)S(1)}, u32[]{:S(2)}, u32[]{:S(2)}) collective-permute-start(bf16[256,1536]{1,0:T(8,128)(2,1)S(1)} %join.7.refs_0_), channel_id=1, source_target_pairs={{0,4},{4,0},{8,12},{12,8},{16,20},{20,16},{24,28},{28,24},{1,5},{5... | collective-permute-start | bytes 2359304 | tf_op jit(solution)/shard_map/ppermute | solution.py:468
  88.4 20.5 %collective-permute-start.25 = (bf16[128,4096]{1,0:T(8,128)(2,1)S(1)}, bf16[128,4096]{1,0:T(8,128)(2,1)S(1)}, u32[]{:S(2)}, u32[]{:S(2)}) collective-permute-start(bf16[128,4096]{1,0:T(8,128)(2,1)S(1)} %get-tuple-element.228), channel_id=1, source_target_pairs={{0,1},{1,0},{2,3},{3,2},{4,6},{5,7},{6,4},{7,5},{8,9},{9,8},{10,11... | collective-permute-start | bytes 3145736 | tf_op jit(solution)/shard_map/ppermute | solution.py:465
  90.6 23.8 %collective-permute-start.24 = (bf16[64,4096]{1,0:T(8,128)(2,1)S(1)}, bf16[64,4096]{1,0:T(8,128)(2,1)S(1)}, u32[]{:S(2)}, u32[]{:S(2)}) collective-permute-start(bf16[64,4096]{1,0:T(8,128)(2,1)S(1)} %hidden_grads.2.refs_0_), channel_id=1, source_target_pairs={{0,1},{1,0},{2,3},{3,2},{4,6},{5,7},{6,4},{7,5},{8,9},{9,8},{10,11... | collective-permute-start | bytes 1572872 | tf_op jit(solution)/shard_map/ppermute | solution.py:465
  91.5 25.2 %collective-permute-start.26 = (bf16[64,4096]{1,0:T(8,128)(2,1)S(1)}, bf16[64,4096]{1,0:T(8,128)(2,1)S(1)}, u32[]{:S(2)}, u32[]{:S(2)}) collective-permute-start(bf16[64,4096]{1,0:T(8,128)(2,1)S(1)} %hidden_grads.2.refs_0_), channel_id=1, source_target_pairs={{0,2},{1,3},{2,0},{3,1},{4,5},{5,4},{6,7},{7,6},{8,10},{9,11},{10,... | collective-permute-start | bytes 1572872 | tf_op jit(solution)/shard_map/ppermute | solution.py:465
  99.5 24.0 %collective-permute-start.28 = (bf16[128,2048]{1,0:T(8,128)(2,1)S(1)}, bf16[128,2048]{1,0:T(8,128)(2,1)S(1)}, u32[]{:S(2)}, u32[]{:S(2)}) collective-permute-start(bf16[128,2048]{1,0:T(8,128)(2,1)S(1)} %get-tuple-element.241), channel_id=1, source_target_pairs={{0,1},{1,0},{2,3},{3,2},{4,6},{5,7},{6,4},{7,5},{8,9},{9,8},{10,11... | collective-permute-start | bytes 1572872 | tf_op jit(solution)/shard_map/ppermute | solution.py:465
  114.5 10.7 %collective-permute-start.27 = (bf16[64,4096]{1,0:T(8,128)(2,1)S(1)}, bf16[64,4096]{1,0:T(8,128)(2,1)S(1)}, u32[]{:S(2)}, u32[]{:S(2)}) collective-permute-start(bf16[64,4096]{1,0:T(8,128)(2,1)S(1)} %collective-permute-done.24.refs_1_), channel_id=1, source_target_pairs={{0,2},{1,3},{2,0},{3,1},{4,5},{5,4},{6,7},{7,6},{8,10},{9,11},{10,... | collective-permute-start | bytes 1572872 | tf_op jit(solution)/shard_map/ppermute | solution.py:465
  115.1 18.1 %collective-permute-start.30 = (bf16[64,4096]{1,0:T(8,128)(2,1)S(1)}, bf16[64,4096]{1,0:T(8,128)(2,1)S(1)}, u32[]{:S(2)}, u32[]{:S(2)}) collective-permute-start(bf16[64,4096]{1,0:T(8,128)(2,1)S(1)} %add_convert_fusion), channel_id=1, source_target_pairs={{0,2},{1,3},{2,0},{3,1},{4,5},{5,4},{6,7},{7,6},{8,10},{9,11},{10,... | collective-permute-start | bytes 1572872 | tf_op jit(solution)/shard_map/ppermute | solution.py:465
  125.2 8.4 %collective-permute-start.29 = (bf16[64,2048]{1,0:T(8,128)(2,1)S(1)}, bf16[64,2048]{1,0:T(8,128)(2,1)S(1)}, u32[]{:S(2)}, u32[]{:S(2)}) collective-permute-start(bf16[64,2048]{1,0:T(8,128)(2,1)S(1)} %add_convert_fusion.2), channel_id=1, source_target_pairs={{0,2},{1,3},{2,0},{3,1},{4,5},{5,4},{6,7},{7,6},{8,10},{9,11},{10,... | collective-permute-start | bytes 786440 | tf_op jit(solution)/shard_map/ppermute | solution.py:465
  133.6 2.7 %collective-permute-start.32 = (bf16[256,1536]{1,0:T(8,128)(2,1)S(1)}, bf16[256,1536]{1,0:T(8,128)(2,1)S(1)}, u32[]{:S(2)}, u32[]{:S(2)}) collective-permute-start(bf16[256,1536]{1,0:T(8,128)(2,1)S(1)} %get-tuple-element.266), channel_id=1, source_target_pairs={{0,4},{4,0},{8,12},{12,8},{16,20},{20,16},{24,28},{28,24},{1,5},{5... | collective-permute-start | bytes 2359304 | tf_op jit(solution)/shard_map/ppermute | solution.py:468
  134.9 11.3 %collective-permute-start.31 = (bf16[64,4096]{1,0:T(8,128)(2,1)S(1)}, bf16[64,4096]{1,0:T(8,128)(2,1)S(1)}, u32[]{:S(2)}, u32[]{:S(2)}) collective-permute-start(bf16[64,4096]{1,0:T(8,128)(2,1)S(1)} %hidden_grads.3.refs_0_), channel_id=1, source_target_pairs={{0,1},{1,0},{2,3},{3,2},{4,6},{5,7},{6,4},{7,5},{8,9},{9,8},{10,11... | collective-permute-start | bytes 1572872 | tf_op jit(solution)/shard_map/ppermute | solution.py:465
  136.4 12.6 %collective-permute-start.33 = (bf16[256,384]{1,0:T(8,128)(2,1)S(1)}, bf16[256,384]{1,0:T(8,128)(2,1)S(1)}, u32[]{:S(2)}, u32[]{:S(2)}) collective-permute-start(bf16[256,384]{1,0:T(8,128)(2,1)S(1)} %get-tuple-element.267), channel_id=1, source_target_pairs={{0,16},{4,20},{8,24},{12,28},{16,0},{20,4},{24,8},{28,12},{1,17},{... | collective-permute-start | bytes 589832 | tf_op jit(solution)/shard_map/ppermute | solution.py:471
  139.7 14.1 %collective-permute-start.34 = (bf16[64,4096]{1,0:T(8,128)(2,1)S(1)}, bf16[64,4096]{1,0:T(8,128)(2,1)S(1)}, u32[]{:S(2)}, u32[]{:S(2)}) collective-permute-start(bf16[64,4096]{1,0:T(8,128)(2,1)S(1)} %hidden_grads.3.refs_0_), channel_id=1, source_target_pairs={{0,2},{1,3},{2,0},{3,1},{4,5},{5,4},{6,7},{7,6},{8,10},{9,11},{10,... | collective-permute-start | bytes 1572872 | tf_op jit(solution)/shard_map/ppermute | solution.py:465
  149.0 10.5 %collective-permute-start.35 = (bf16[64,4096]{1,0:T(8,128)(2,1)S(1)}, bf16[64,4096]{1,0:T(8,128)(2,1)S(1)}, u32[]{:S(2)}, u32[]{:S(2)}) collective-permute-start(bf16[64,4096]{1,0:T(8,128)(2,1)S(1)} %collective-permute-done.31.refs_1_), channel_id=1, source_target_pairs={{0,2},{1,3},{2,0},{3,1},{4,5},{5,4},{6,7},{7,6},{8,10},{9,11},{10,... | collective-permute-start | bytes 1572872 | tf_op jit(solution)/shard_map/ppermute | solution.py:465
  149.9 9.6 %collective-permute-start.36 = (bf16[256,384]{1,0:T(8,128)(2,1)S(1)}, bf16[256,384]{1,0:T(8,128)(2,1)S(1)}, u32[]{:S(2)}, u32[]{:S(2)}) collective-permute-start(bf16[256,384]{1,0:T(8,128)(2,1)S(1)} %get-tuple-element.270), channel_id=1, source_target_pairs={{0,8},{4,12},{8,16},{12,20},{16,24},{20,28},{24,0},{28,4},{1,9},{5... | collective-permute-start | bytes 589832 | tf_op jit(solution)/shard_map/ppermute | solution.py:471
  152.8 13.4 %collective-permute-start.38 = (bf16[256,384]{1,0:T(8,128)(2,1)S(1)}, bf16[256,384]{1,0:T(8,128)(2,1)S(1)}, u32[]{:S(2)}, u32[]{:S(2)}) collective-permute-start(bf16[256,384]{1,0:T(8,128)(2,1)S(1)} %get-tuple-element.283), channel_id=1, source_target_pairs={{0,24},{4,28},{8,0},{12,4},{16,8},{20,12},{24,16},{28,20},{1,25},{... | collective-permute-start | bytes 589832 | tf_op jit(solution)/shard_map/ppermute | solution.py:471
  162.0 4.2 %collective-permute-start.37 = (bf16[256,384]{1,0:T(8,128)(2,1)S(1)}, bf16[256,384]{1,0:T(8,128)(2,1)S(1)}, u32[]{:S(2)}, u32[]{:S(2)}) collective-permute-start(bf16[256,384]{1,0:T(8,128)(2,1)S(1)} %get-tuple-element.278), channel_id=1, source_target_pairs={{0,4},{4,0},{8,12},{12,8},{16,20},{20,16},{24,28},{28,24},{1,5},{5... | collective-permute-start | bytes 589832 | tf_op jit(solution)/shard_map/ppermute | solution.py:468
  166.2 3.0 %collective-permute-start.39 = (bf16[256,768]{1,0:T(8,128)(2,1)S(1)}, bf16[256,768]{1,0:T(8,128)(2,1)S(1)}, u32[]{:S(2)}, u32[]{:S(2)}) collective-permute-start(bf16[256,768]{1,0:T(8,128)(2,1)S(1)} %get-tuple-element.285), channel_id=1, source_target_pairs={{0,4},{4,0},{8,12},{12,8},{16,20},{20,16},{24,28},{28,24},{1,5},{5... | collective-permute-start | bytes 1179656 | tf_op jit(solution)/shard_map/ppermute | solution.py:468
  166.8 17.2 %collective-permute-start.40 = (bf16[256,384]{1,0:T(8,128)(2,1)S(1)}, bf16[256,384]{1,0:T(8,128)(2,1)S(1)}, u32[]{:S(2)}, u32[]{:S(2)}) collective-permute-start(bf16[256,384]{1,0:T(8,128)(2,1)S(1)} %pair_sums.4), channel_id=1, source_target_pairs={{0,16},{4,20},{8,24},{12,28},{16,0},{20,4},{24,8},{28,12},{1,17},{... | collective-permute-start | bytes 589832 | tf_op jit(solution)/shard_map/ppermute | solution.py:471
  169.3 14.7 %collective-permute-start.41 = (bf16[256,384]{1,0:T(8,128)(2,1)S(1)}, bf16[256,384]{1,0:T(8,128)(2,1)S(1)}, u32[]{:S(2)}, u32[]{:S(2)}) collective-permute-start(bf16[256,384]{1,0:T(8,128)(2,1)S(1)} %get-tuple-element.307), channel_id=1, source_target_pairs={{0,8},{4,12},{8,16},{12,20},{16,24},{20,28},{24,0},{28,4},{1,9},{5... | collective-permute-start | bytes 589832 | tf_op jit(solution)/shard_map/ppermute | solution.py:471
  169.9 14.1 %collective-permute-start.42 = (bf16[256,384]{1,0:T(8,128)(2,1)S(1)}, bf16[256,384]{1,0:T(8,128)(2,1)S(1)}, u32[]{:S(2)}, u32[]{:S(2)}) collective-permute-start(bf16[256,384]{1,0:T(8,128)(2,1)S(1)} %get-tuple-element.308), channel_id=1, source_target_pairs={{0,24},{4,28},{8,0},{12,4},{16,8},{20,12},{24,16},{28,20},{1,25},{... | collective-permute-start | bytes 589832 | tf_op jit(solution)/shard_map/ppermute | solution.py:471
  175.6 8.4 %collective-permute-start.43 = (bf16[256,384]{1,0:T(8,128)(2,1)S(1)}, bf16[256,384]{1,0:T(8,128)(2,1)S(1)}, u32[]{:S(2)}, u32[]{:S(2)}) collective-permute-start(bf16[256,384]{1,0:T(8,128)(2,1)S(1)} %get-tuple-element.310), channel_id=1, source_target_pairs={{0,4},{4,0},{8,12},{12,8},{16,20},{20,16},{24,28},{28,24},{1,5},{5... | collective-permute-start | bytes 589832 | tf_op jit(solution)/shard_map/ppermute | solution.py:468
